TPU v7x, 32 devices: a whole 2x2x4 slice. The times are simulated.
32 devices in a mesh: dp: 4 (over z), expert: 8 (over y, x, core).
Axes of the slice: x: 2, y: 2, z: 4, core: 2. Of those that a mesh axis runs over, the one named last changes fastest.
Arguments:
- route_ids: int32 [4096, 8], P(('dp', 'expert')), may hold values from 0 to 127, all different within a row; in each aligned block of 128 rows (0 to 127, 128 to 255, ...) at most 16 rows name the same one
- route_probs: float32 [4096, 8], P(('dp', 'expert')), may hold values from 0.05 to 0.6
- capacity: int32 [8], replicated, may hold values from 4 to 16, as said below
- hot_lists: int32 [4, 4], P('dp'), may hold values from 0 to 7, as said below
- gate_up: bfloat16 [4, 8, 128, 1536], P('dp', 'expert'), may hold values from -6 to 6
- w_quant: bfloat16 [8, 768, 4096], P('expert'), may hold values from -0.21875 to 0.21875
- w_scale: float32 [8, 6, 32], P('expert'), may hold values from 0.5 to 2
- d_out: bfloat16 [4096, 4096], P(('dp', 'expert')), may hold values from -6 to 6
Outputs:
- combined: bfloat16 [4096, 4096], P(('dp', 'expert'))
- d_probs: float32 [4096, 8], P(('dp', 'expert'))
- d_gate_up: bfloat16 [4, 8, 128, 1536], P('dp', 'expert')
- d_w_down: bfloat16 [8, 4096, 768], P('expert', 'dp')
Inputs may be any that keep to these rules, and one draw needn't show every extreme that they name: `route_ids`: each row names 8 different experts; among the rows of one device no expert is named more than 16 times, a bound that some block reaches. `capacity`: each entry is a multiple of 4; some expert has exactly 16. `hot_lists`: each row names 4 different experts among the 8 computed ones.
All inputs are finite; a program needn't handle non-finite values.
Results may differ from a plain program's by a relative error of at most 0.017.
Values may be sent and summed in bfloat16 or wider, within the bound.
No kernel may reach another device: no remote copies, remote signals or barrier semaphores. Data moves between devices by JAX's collectives and lax.ppermute only.
A program may use at most 128 MiB of HBM per device.

v0:
```python
import functools

import jax
import jax.numpy as jnp
from jax import lax
from jax.experimental import pallas as pl
from jax.experimental.pallas import tpu as pltpu
from jax.sharding import PartitionSpec as P

QB = 128
CAP = 16
VMEM_LIMIT = 24 * 1024 * 1024

bf16 = jnp.bfloat16
f32 = jnp.float32

SMALL = pl.CostEstimate(flops=1024, bytes_accessed=1024, transcendentals=0)

VMEM = pl.BlockSpec(memory_space=pltpu.VMEM)
ANY = pl.BlockSpec(memory_space=pl.ANY)
HBM = pl.BlockSpec(memory_space=pltpu.HBM)


def params():
    return pltpu.CompilerParams(vmem_limit_bytes=VMEM_LIMIT)


def hbm(value):
    return pltpu.with_memory_space_constraint(value, pltpu.HBM)


def chunks(total, size):
    return [pl.ds(start, size) for start in range(0, total, size)]


def dispatch_kernel(
    flight, groups, gate_up_hbm, cap_hbm, hot_hbm, ids_hbm, probs_hbm, dout_hbm,
    hidden_hbm, own_ref, rows_hbm,
    gate_up, cap_ref, hot_ref, ids_ref, probs_ref, dout, hidden, rows,
    gate_sem, hidden_sem, small_sems, in_sems, out_sems
):
    topk, tokens = ids_ref.shape
    slots = flight * CAP
    group = lax.axis_index("dp")
    share = dout_hbm.shape[1] // groups
    small = [
        pltpu.make_async_copy(src, dst, small_sems.at[i])
        for i, (src, dst) in enumerate(
            [(ids_hbm, ids_ref), (probs_hbm, probs_ref), (cap_hbm, cap_ref), (hot_hbm, hot_ref)]
        )
    ]
    loads = [
        pltpu.make_async_copy(
            dout_hbm.at[:, pl.ds(pl.multiple_of((group ^ j) * share, share), share)],
            dout.at[j],
            in_sems.at[j],
        )
        for j in range(groups)
    ]
    gate_copy = pltpu.make_async_copy(gate_up_hbm, gate_up, gate_sem)
    for copy in [gate_copy] + small + loads:
        copy.start()
    gate_copy.wait()
    hid = hidden.shape[1]
    gate = gate_up[:, :hid].astype(f32)
    up = gate_up[:, hid:].astype(f32)
    hidden[...] = (gate * jax.nn.sigmoid(gate) * up).astype(bf16)
    hidden_copy = pltpu.make_async_copy(hidden, hidden_hbm, hidden_sem)
    hidden_copy.start()
    for copy in small:
        copy.wait()
    row = lax.broadcasted_iota(jnp.int32, (slots, 1), 0)
    row_expert = row // CAP
    row_rank = (row % CAP).astype(f32)
    limit = jnp.zeros((slots, 1), jnp.int32)
    for e in range(flight):
        hot = hot_ref[0, 0] == e
        for h in range(1, hot_ref.shape[1]):
            hot = jnp.logical_or(hot, hot_ref[0, h] == e)
        limit = jnp.where(row_expert == e, jnp.where(hot, CAP, cap_ref[e]), limit)
    limit = limit.astype(f32)
    named = jnp.zeros((slots, tokens), f32)
    weight = jnp.zeros((slots, tokens), f32)
    for k in range(topk):
        hit = ids_ref[k : k + 1, :] == row_expert
        named = jnp.where(hit, 1.0, named)
        weight = jnp.where(hit, probs_ref[k : k + 1, :], weight)
    first = lax.broadcasted_iota(jnp.int32, (tokens, tokens), 0)
    second = lax.broadcasted_iota(jnp.int32, (tokens, tokens), 1)
    before = (first < second).astype(f32).astype(bf16)
    rank = jnp.dot(named.astype(bf16), before, preferred_element_type=f32)
    owns = (named > 0.0) & (rank == row_rank) & (rank < limit)
    own_weight = jnp.where(owns, weight, 0.0)
    own_ref[...] = own_weight
    owner = jnp.where(owns, 1.0, 0.0).astype(bf16)
    slot_weight = jnp.sum(own_weight, axis=1, keepdims=True)
    stores = []
    for j in range(groups):
        loads[j].wait()
        part = jnp.dot(owner, dout[j], preferred_element_type=f32)
        rows[j] = (part * slot_weight).astype(bf16).reshape(flight, CAP, share)
        stores.append(pltpu.make_async_copy(rows.at[j], rows_hbm.at[:, j], out_sems.at[j]))
        stores[j].start()
    for copy in stores:
        copy.wait()
    hidden_copy.wait()


def dispatch(gate_up, capacity, hot_row, ids, probs, d_out, flight, groups):
    tokens, width = d_out.shape
    rows, double = gate_up.shape
    slots = flight * CAP
    share = width // groups
    return pl.pallas_call(
        functools.partial(dispatch_kernel, flight, groups),
        out_shape=(
            pltpu.HBM((rows, double // 2), bf16),
            jax.ShapeDtypeStruct((slots, tokens), f32),
            pltpu.HBM((flight, groups, CAP, share), bf16),
        ),
        in_specs=[HBM] * 6,
        out_specs=(HBM, VMEM, HBM),
        scratch_shapes=[
            pltpu.VMEM((rows, double), bf16),
            pltpu.SMEM(capacity.shape, jnp.int32),
            pltpu.SMEM(hot_row.shape, jnp.int32),
            pltpu.VMEM(ids.shape, jnp.int32),
            pltpu.VMEM(probs.shape, f32),
            pltpu.VMEM((groups, tokens, share), bf16),
            pltpu.VMEM((rows, double // 2), bf16),
            pltpu.VMEM((groups, flight, CAP, share), bf16),
            pltpu.SemaphoreType.DMA,
            pltpu.SemaphoreType.DMA,
            pltpu.SemaphoreType.DMA((4,)),
            pltpu.SemaphoreType.DMA((groups,)),
            pltpu.SemaphoreType.DMA((groups,)),
        ],
        compiler_params=params(),
        cost_estimate=SMALL,
        name="dispatch",
    )(hbm(gate_up), hbm(capacity), hbm(hot_row), hbm(ids), hbm(probs), hbm(d_out))


def forward_kernel(
    flight, block, scale_hbm, hidden_hbm, quant_hbm, weight_hbm, out_hbm,
    scale_ref, hidden, quant, weight, out, small_sems, in_sems, out_sems, weight_sems
):
    hid, width = quant.shape
    steps = chunks(width, block)
    small = [
        pltpu.make_async_copy(scale_hbm, scale_ref, small_sems.at[0]),
        pltpu.make_async_copy(hidden_hbm, hidden, small_sems.at[1]),
    ]
    loads = [
        pltpu.make_async_copy(quant_hbm.at[:, cols], quant.at[:, cols], in_sems.at[c])
        for c, cols in enumerate(steps)
    ]
    for copy in small + loads:
        copy.start()
    for copy in small:
        copy.wait()
    stores = []
    for c, cols in enumerate(steps):
        loads[c].wait()
        for i in range(hid // QB):
            for j in range(block // QB):
                at = (pl.ds(i * QB, QB), pl.ds(c * block + j * QB, QB))
                scale = scale_ref[i, 0, c * (block // QB) + j]
                weight[at] = (quant[at].astype(f32) * scale).astype(bf16)
        stores.append(
            pltpu.make_async_copy(weight.at[:, cols], weight_hbm.at[:, cols], weight_sems.at[c])
        )
        stores[-1].start()
        part = jnp.dot(hidden[...], weight[:, cols], preferred_element_type=f32)
        out[:, :, cols] = part.astype(bf16).reshape(flight, CAP, block)
        stores.append(
            pltpu.make_async_copy(out.at[:, :, cols], out_hbm.at[:, :, cols], out_sems.at[c])
        )
        stores[-1].start()
    for copy in stores:
        copy.wait()


def forward(scale, hidden, quant, flight, block=512):
    hid, width = quant.shape
    return pl.pallas_call(
        functools.partial(forward_kernel, flight, block),
        out_shape=(
            pltpu.HBM((hid, width), bf16),
            pltpu.HBM((flight, CAP, width), bf16),
        ),
        in_specs=[HBM, HBM, HBM],
        out_specs=(HBM, HBM),
        scratch_shapes=[
            pltpu.SMEM(scale.shape, f32),
            pltpu.VMEM(hidden.shape, bf16),
            pltpu.VMEM((hid, width), bf16),
            pltpu.VMEM((hid, width), bf16),
            pltpu.VMEM((flight, CAP, width), bf16),
            pltpu.SemaphoreType.DMA((2,)),
            pltpu.SemaphoreType.DMA((width // block,)),
            pltpu.SemaphoreType.DMA((width // block,)),
            pltpu.SemaphoreType.DMA((width // block,)),
        ],
        compiler_params=params(),
        cost_estimate=SMALL,
        name="expert_forward",
    )(hbm(scale), hbm(hidden), hbm(quant))


def split_kernel(groups, out_ref, rows_ref, *refs):
    pieces, sems = refs[groups:-1], refs[-1]
    copies = [
        pltpu.make_async_copy(rows_ref.at[:, j], pieces[j - 1], sems.at[j - 1])
        for j in range(1, groups)
    ]
    for copy in copies:
        copy.start()
    for copy in copies:
        copy.wait()


def split(expert_out, rows, ties):
    flight, groups, cap, share = rows.shape
    return pl.pallas_call(
        functools.partial(split_kernel, groups),
        out_shape=(pltpu.HBM(expert_out.shape, bf16),)
        + (pltpu.HBM((flight, cap, share), bf16),) * (groups - 1),
        in_specs=[HBM] + [ANY] * groups,
        out_specs=(HBM,) * groups,
        scratch_shapes=[pltpu.SemaphoreType.DMA((groups - 1,))],
        input_output_aliases={0: 0},
        compiler_params=params(),
        cost_estimate=SMALL,
        name="split",
    )(hbm(expert_out), rows, *ties)


def backward_kernel(
    gate_up_hbm, weight_hbm, rows_ref, tie_ref, out_ref, gate_up, weight, acc, gate_sem, sems
):
    flight, groups, cap, share = rows_ref.shape
    group = lax.axis_index("dp")
    loads = [
        pltpu.make_async_copy(
            weight_hbm.at[:, pl.ds(pl.multiple_of((group ^ j) * share, share), share)],
            weight.at[j],
            sems.at[j],
        )
        for j in range(groups)
    ]
    gate_copy = pltpu.make_async_copy(gate_up_hbm, gate_up, gate_sem)
    for copy in loads + [gate_copy]:
        copy.start()
    hid = acc.shape[1]
    for j in range(groups):
        loads[j].wait()
        part = lax.dot_general(
            rows_ref[:, j].reshape(flight * cap, share),
            weight[j],
            (((1,), (1,)), ((), ())),
            preferred_element_type=f32,
        )
        if j == 0:
            acc[...] = part
        else:
            acc[...] += part
    gate_copy.wait()
    gate = gate_up[:, :hid].astype(f32)
    up = gate_up[:, hid:].astype(f32)
    sig = jax.nn.sigmoid(gate)
    d_hidden = acc[...]
    out_ref[:, :hid] = (d_hidden * up * sig * (1.0 + gate * (1.0 - sig))).astype(bf16)
    out_ref[:, hid:] = (d_hidden * (gate * sig)).astype(bf16)


def backward(gate_up, weight, rows, tie):
    slots, double = gate_up.shape
    hid, width = weight.shape
    groups = rows.shape[1]
    return pl.pallas_call(
        backward_kernel,
        out_shape=jax.ShapeDtypeStruct((slots, double), bf16),
        in_specs=[HBM, HBM, VMEM, ANY],
        out_specs=VMEM,
        scratch_shapes=[
            pltpu.VMEM((slots, double), bf16),
            pltpu.VMEM((groups, hid, width // groups), bf16),
            pltpu.VMEM((slots, hid), f32),
            pltpu.SemaphoreType.DMA,
            pltpu.SemaphoreType.DMA((groups,)),
        ],
        compiler_params=params(),
        cost_estimate=SMALL,
        name="expert_backward",
    )(hbm(gate_up), hbm(weight), rows, hbm(tie))


def combine_kernel(
    block, ids_hbm, own_ref, dout_hbm, ret_ref, out_ref, dprobs_ref, ids_ref, dout, sems
):
    copies = [
        pltpu.make_async_copy(ids_hbm, ids_ref, sems.at[0]),
        pltpu.make_async_copy(dout_hbm, dout, sems.at[1]),
    ]
    for copy in copies:
        copy.start()
    topk, tokens = ids_ref.shape
    slots = own_ref.shape[0]
    width = dout.shape[1]
    own = own_ref[...]
    turned = own.T
    high = turned.astype(bf16)
    low = (turned - high.astype(f32)).astype(bf16)
    total = jnp.zeros((slots, tokens), f32)
    for copy in copies:
        copy.wait()
    for cols in chunks(width, block):
        here = ret_ref[:, :, cols].reshape(slots, block)
        out = jnp.dot(high, here, preferred_element_type=f32)
        out = out + jnp.dot(low, here, preferred_element_type=f32)
        out_ref[:, cols] = out.astype(bf16)
        total = total + lax.dot_general(
            here, dout[:, cols], (((1,), (1,)), ((), ())), preferred_element_type=f32
        )
    inner = jnp.where(own > 0.0, total, 0.0)
    row_expert = lax.broadcasted_iota(jnp.int32, (slots, 1), 0) // CAP
    for k in range(topk):
        mine = jnp.where(ids_ref[k : k + 1, :] == row_expert, inner, 0.0)
        dprobs_ref[k : k + 1, :] = jnp.sum(mine, axis=0, keepdims=True)


def combine(ids, own, d_out, returned, block=1024):
    tokens, width = d_out.shape
    return pl.pallas_call(
        functools.partial(combine_kernel, block),
        out_shape=(
            jax.ShapeDtypeStruct((tokens, width), bf16),
            jax.ShapeDtypeStruct(ids.shape, f32),
        ),
        in_specs=[HBM, VMEM, HBM, VMEM],
        out_specs=(VMEM, VMEM),
        scratch_shapes=[
            pltpu.VMEM(ids.shape, jnp.int32),
            pltpu.VMEM((tokens, width), bf16),
            pltpu.SemaphoreType.DMA((2,)),
        ],
        compiler_params=params(),
        cost_estimate=SMALL,
        name="combine",
    )(hbm(ids), own, hbm(d_out), returned)


def weight_grad_kernel(groups, block, rows_ref, *refs):
    part_refs, hid_refs = refs[: groups - 1], refs[groups - 1 : 2 * groups - 1]
    out_hbm, grads, hidden, out, sems, out_sems = refs[2 * groups - 1 :]
    flight, cap, share = part_refs[0].shape
    slots = flight * cap
    copies = []
    for j in range(groups):
        src = rows_ref.at[:, 0] if j == 0 else part_refs[j - 1]
        copies.append(
            pltpu.make_async_copy(src, grads.at[pl.ds(j * flight, flight)], sems.at[2 * j])
        )
        copies.append(
            pltpu.make_async_copy(
                hid_refs[j], hidden.at[pl.ds(j * slots, slots)], sems.at[2 * j + 1]
            )
        )
    for copy in copies:
        copy.start()
    for copy in copies:
        copy.wait()
    stores = []
    for c, cols in enumerate(chunks(share, block)):
        out[cols, :] = lax.dot_general(
            grads[:, :, cols].reshape(groups * slots, block),
            hidden[...],
            (((0,), (0,)), ((), ())),
            preferred_element_type=f32,
        ).astype(bf16)
        stores.append(pltpu.make_async_copy(out.at[cols], out_hbm.at[cols], out_sems.at[c]))
        stores[c].start()
    for copy in stores:
        copy.wait()


def weight_grad(rows, parts, hiddens, block=256):
    flight, groups, cap, share = rows.shape
    slots, hid = hiddens[0].shape
    return pl.pallas_call(
        functools.partial(weight_grad_kernel, groups, block),
        out_shape=pltpu.HBM((share, hid), bf16),
        in_specs=[ANY] * (2 * groups),
        out_specs=HBM,
        scratch_shapes=[
            pltpu.VMEM((groups * flight, cap, share), bf16),
            pltpu.VMEM((groups * slots, hid), bf16),
            pltpu.VMEM((share, hid), bf16),
            pltpu.SemaphoreType.DMA((2 * groups,)),
            pltpu.SemaphoreType.DMA((share // block,)),
        ],
        compiler_params=params(),
        cost_estimate=SMALL,
        name="weight_grad",
    )(rows, *parts, hbm(hiddens[0]), *hiddens[1:])


def swap(value, axis, j):
    size = lax.axis_size(axis)
    return lax.ppermute(value, axis, [(i, i ^ j) for i in range(size)])


def exchange(value):
    return lax.all_to_all(value, "expert", split_axis=0, concat_axis=0, tiled=True)


def shards(route_ids, route_probs, capacity, hot_lists, gate_up, w_quant, w_scale, d_out):
    flight = lax.axis_size("expert")
    groups = lax.axis_size("dp")
    gate_up = gate_up[0, 0]
    ids, probs = route_ids.T, route_probs.T
    hidden, own, rows = dispatch(gate_up, capacity, hot_lists, ids, probs, d_out, flight, groups)
    arrived = exchange(rows)
    hiddens = [hidden] + [swap(hidden, "dp", j) for j in range(1, groups)]
    weight, expert_out = forward(w_scale.transpose(1, 0, 2), hidden, w_quant[0], flight)
    expert_out, *pieces = split(expert_out, arrived, hiddens[1:])
    returned = exchange(expert_out)
    parts = [swap(pieces[j - 1], "dp", j) for j in range(1, groups)]
    d_gate_up = backward(gate_up, weight, arrived, pieces[0])
    combined, d_probs = combine(ids, own, d_out, returned)
    d_weight = weight_grad(arrived, parts, hiddens)
    return (combined, d_probs.T, d_gate_up[None, None], d_weight[None])


def solution(mesh):
    placed = (
        P(("dp", "expert"), None),
        P(("dp", "expert"), None),
        P(),
        P("dp", None),
        P("dp", "expert", None, None),
        P("expert", None, None),
        P("expert", None, None),
        P(("dp", "expert"), None),
    )
    return jax.shard_map(
        shards,
        mesh=mesh,
        in_specs=placed,
        out_specs=(
            P(("dp", "expert"), None),
            P(("dp", "expert"), None),
            P("dp", "expert", None, None),
            P("expert", "dp", None),
        ),
        check_vma=False,
    )
```

profile of v0, /device:TPU:11, one launch (start us, length us, event | category | flops | bytes accessed | tf_op | source)
XLA Modules:
  0.0 65.7 jit_solution(2850222278222939794)
XLA Ops:
  0.6 3.4 %dispatch.1 = (bf16[128,768]{1,0:T(8,128)(2,1)}, f32[128,128]{1,0:T(8,128)S(1)}, bf16[8,4,16,1024]{3,2,1,0:T(8,128)(2,1)}) custom-call(bf16[128,1536]{1,0:T(8,128)(2,1)} %bitcast.9, s32[8]{0:T(128)} %cap_hbm.1, s32[1,4]{1,0:T(1,128)} %hot_hbm.1, s32[8,128]{1,0:T(8,128)} %bitcast.13, f32[8,128]{1,0:T(8,128)} %bitcast.15, bf16[128,4096]{1,0:T(8,128)(2,1)} %dout_hbm.3), custom_call_target="tpu_custom_call" | custom-call | flops 1024 | bytes 1024 | tf_op jit(solution)/shard_map/dispatch/pallas_call | solution.py:114
  4.0 4.6 %all-to-all-start = ((bf16[8,4,16,1024]{3,2,1,0:T(8,128)(2,1)}), bf16[8,4,16,1024]{3,2,1,0:T(8,128)(2,1)S(1)}, u32[]{:S(2)}, u32[]{:S(2)}) async-start(bf16[8,4,16,1024]{3,2,1,0:T(8,128)(2,1)} %get-tuple-element.18), calls=%async_computation | async-start | bytes 2097152 | tf_op jit(solution)/shard_map/all_to_all | solution.py:415
  8.6 1.3 %collective-permute-start.2 = (bf16[128,768]{1,0:T(8,128)(2,1)}, bf16[128,768]{1,0:T(8,128)(2,1)S(1)}, u32[]{:S(2)}, u32[]{:S(2)}) collective-permute-start(bf16[128,768]{1,0:T(8,128)(2,1)} %get-tuple-element.16.hidden_hbm.refs_3_), channel_id=1, source_target_pairs={{0,24},{8,16},{16,8},{24,0},{1,25},{9,17},{17,9},{25,1},{2,26},{10... | collective-permute-start | bytes 589832 | tf_op jit(solution)/shard_map/ppermute | solution.py:411
  9.9 1.0 %collective-permute-start.1 = (bf16[128,768]{1,0:T(8,128)(2,1)}, bf16[128,768]{1,0:T(8,128)(2,1)S(1)}, u32[]{:S(2)}, u32[]{:S(2)}) collective-permute-start(bf16[128,768]{1,0:T(8,128)(2,1)} %get-tuple-element.16.hidden_hbm.refs_3_), channel_id=1, source_target_pairs={{0,16},{8,24},{16,0},{24,8},{1,17},{9,25},{17,1},{25,9},{2,18},{10... | collective-permute-start | bytes 589832 | tf_op jit(solution)/shard_map/ppermute | solution.py:411
  10.9 1.2 %collective-permute-start = (bf16[128,768]{1,0:T(8,128)(2,1)}, bf16[128,768]{1,0:T(8,128)(2,1)S(1)}, u32[]{:S(2)}, u32[]{:S(2)}) collective-permute-start(bf16[128,768]{1,0:T(8,128)(2,1)} %get-tuple-element.16.hidden_hbm.refs_3_), channel_id=1, source_target_pairs={{0,8},{8,0},{16,24},{24,16},{1,9},{9,1},{17,25},{25,17},{2,10},{10... | collective-permute-start | bytes 589832 | tf_op jit(solution)/shard_map/ppermute | solution.py:411
  12.1 7.3 %expert_forward.1 = (bf16[768,4096]{1,0:T(8,128)(2,1)}, bf16[8,16,4096]{2,1,0:T(8,128)(2,1)}) custom-call(f32[6,1,32]{2,1,0:T(1,128)} %bitcast.16, bf16[128,768]{1,0:T(8,128)(2,1)} %get-tuple-element.16.hidden_hbm.refs_3_, bf16[768,4096]{1,0:T(8,128)(2,1)} %bitcast.8), custom_call_target="tpu_custom_call" | custom-call | flops 1024 | bytes 1024 | tf_op jit(solution)/shard_map/expert_forward/pallas_call | solution.py:186
  19.4 3.9 %collective-permute-done.2.refs_2_.refs_6_ = bf16[128,768]{1,0:T(8,128)(2,1)S(1)} collective-permute-done((bf16[128,768]{1,0:T(8,128)(2,1)}, bf16[128,768]{1,0:T(8,128)(2,1)S(1)}, u32[]{:S(2)}, u32[]{:S(2)}) %collective-permute-start.2) | collective-permute-done | bytes 196640 | tf_op jit(solution)/shard_map/ppermute | solution.py:411
  23.3 3.4 %collective-permute-done.1.refs_1_.refs_5_ = bf16[128,768]{1,0:T(8,128)(2,1)S(1)} collective-permute-done((bf16[128,768]{1,0:T(8,128)(2,1)}, bf16[128,768]{1,0:T(8,128)(2,1)S(1)}, u32[]{:S(2)}, u32[]{:S(2)}) %collective-permute-start.1) | collective-permute-done | bytes 196640 | tf_op jit(solution)/shard_map/ppermute | solution.py:411
  26.8 0.0 collective-permute-done.refs_0_.refs_4_
  26.8 0.0 all-to-all-done.rows_ref
  26.8 0.9 %split.1 = (bf16[8,16,4096]{2,1,0:T(8,128)(2,1)}, bf16[8,16,1024]{2,1,0:T(8,128)(2,1)}, bf16[8,16,1024]{2,1,0:T(8,128)(2,1)}, bf16[8,16,1024]{2,1,0:T(8,128)(2,1)}) custom-call(bf16[8,16,4096]{2,1,0:T(8,128)(2,1)} %get-tuple-element.17.out_ref, bf16[8,4,16,1024]{3,2,1,0:T(8,128)(2,1)S(1)} %all-to-all-done.rows_ref, ...), custom_call_target="tpu_custom_call", output_to_operand_aliasing={{0}: (0, {})} | custom-call | flops 1024 | bytes 1024 | tf_op jit(solution)/shard_map/split/pallas_call | solution.py:225
  27.7 5.0 %all-to-all-start.1 = ((bf16[8,16,4096]{2,1,0:T(8,128)(2,1)}), bf16[8,16,4096]{2,1,0:T(8,128)(2,1)S(1)}, u32[]{:S(2)}, u32[]{:S(2)}) async-start(bf16[8,16,4096]{2,1,0:T(8,128)(2,1)} %get-tuple-element.19), calls=%async_computation.1 | async-start | bytes 2097152 | tf_op jit(solution)/shard_map/all_to_all | solution.py:415
  32.7 3.0 %collective-permute-start.4 = (bf16[8,16,1024]{2,1,0:T(8,128)(2,1)}, bf16[8,16,1024]{2,1,0:T(8,128)(2,1)S(1)}, u32[]{:S(2)}, u32[]{:S(2)}) collective-permute-start(bf16[8,16,1024]{2,1,0:T(8,128)(2,1)} %get-tuple-element.24), channel_id=1, source_target_pairs={{0,16},{8,24},{16,0},{24,8},{1,17},{9,25},{17,1},{25,9},{2,18},{10... | collective-permute-start | bytes 786440 | tf_op jit(solution)/shard_map/ppermute | solution.py:411
  35.7 0.2 collective-permute-start.5
  35.9 1.0 %collective-permute-start.3 = (bf16[8,16,1024]{2,1,0:T(8,128)(2,1)}, bf16[8,16,1024]{2,1,0:T(8,128)(2,1)S(1)}, u32[]{:S(2)}, u32[]{:S(2)}) collective-permute-start(bf16[8,16,1024]{2,1,0:T(8,128)(2,1)} %get-tuple-element.23.tie_ref), channel_id=1, source_target_pairs={{0,8},{8,0},{16,24},{24,16},{1,9},{9,1},{17,25},{25,17},{2,10},{10... | collective-permute-start | bytes 786440 | tf_op jit(solution)/shard_map/ppermute | solution.py:411
  36.9 5.5 %expert_backward.1 = bf16[128,1536]{1,0:T(8,128)(2,1)} custom-call(bf16[128,1536]{1,0:T(8,128)(2,1)} %bitcast.10, bf16[768,4096]{1,0:T(8,128)(2,1)} %get-tuple-element.22.weight_hbm, bf16[8,4,16,1024]{3,2,1,0:T(8,128)(2,1)S(1)} %all-to-all-done.rows_ref, bf16[8,16,1024]{2,1,0:T(8,128)(2,1)} %get-tuple-element.23.tie_ref), custom_call_target="tpu_custom_call" | custom-call | flops 1024 | bytes 1024 | tf_op jit(solution)/shard_map/expert_backward/pallas_call | solution.py:281
  42.4 9.6 %collective-permute-done.4.refs_1_ = bf16[8,16,1024]{2,1,0:T(8,128)(2,1)S(1)} collective-permute-done((bf16[8,16,1024]{2,1,0:T(8,128)(2,1)}, bf16[8,16,1024]{2,1,0:T(8,128)(2,1)S(1)}, u32[]{:S(2)}, u32[]{:S(2)}) %collective-permute-start.4) | collective-permute-done | bytes 262176 | tf_op jit(solution)/shard_map/ppermute | solution.py:411
  52.0 7.5 %collective-permute-done.5.refs_2_ = bf16[8,16,1024]{2,1,0:T(8,128)(2,1)S(1)} collective-permute-done((bf16[8,16,1024]{2,1,0:T(8,128)(2,1)}, bf16[8,16,1024]{2,1,0:T(8,128)(2,1)S(1)}, u32[]{:S(2)}, u32[]{:S(2)}) %collective-permute-start.5) | collective-permute-done | bytes 262176 | tf_op jit(solution)/shard_map/ppermute | solution.py:411
  59.6 0.0 collective-permute-done.3.refs_0_
  59.6 2.8 %weight_grad.1 = bf16[1024,768]{1,0:T(8,128)(2,1)} custom-call(bf16[8,4,16,1024]{3,2,1,0:T(8,128)(2,1)S(1)} %all-to-all-done.rows_ref, bf16[8,16,1024]{2,1,0:T(8,128)(2,1)S(1)} %collective-permute-done.3.refs_0_, bf16[8,16,1024]{2,1,0:T(8,128)(2,1)S(1)} %collective-permute-done.4.refs_1_, bf16[8,16,1024]{2,1,0:T(8,128)(2,1)S(1)} %collective-permute-done.5.refs_2_, ...), custom_call_target="tpu_custom_call" | custom-call | flops 1024 | bytes 1024 | tf_op jit(solution)/shard_map/weight_grad/pallas_call | solution.py:391
  62.4 0.0 all-to-all-done.1.ret_ref
  62.4 3.2 %combine.1 = (bf16[128,4096]{1,0:T(8,128)(2,1)}, f32[8,128]{1,0:T(8,128)}) custom-call(s32[8,128]{1,0:T(8,128)} %bitcast.14, f32[128,128]{1,0:T(8,128)S(1)} %get-tuple-element.15.own_ref, bf16[128,4096]{1,0:T(8,128)(2,1)} %dout_hbm.3, bf16[8,16,4096]{2,1,0:T(8,128)(2,1)S(1)} %all-to-all-done.1.ret_ref), custom_call_target="tpu_custom_call" | custom-call | flops 1024 | bytes 1024 | tf_op jit(solution)/shard_map/combine/pallas_call | solution.py:335
Async XLA Ops:
  4.0 22.8 %all-to-all-start = ((bf16[8,4,16,1024]{3,2,1,0:T(8,128)(2,1)}), bf16[8,4,16,1024]{3,2,1,0:T(8,128)(2,1)S(1)}, u32[]{:S(2)}, u32[]{:S(2)}) async-start(bf16[8,4,16,1024]{3,2,1,0:T(8,128)(2,1)} %get-tuple-element.18), calls=%async_computation | async-start | bytes 2097152 | tf_op jit(solution)/shard_map/all_to_all | solution.py:415
  8.6 14.8 %collective-permute-start.2 = (bf16[128,768]{1,0:T(8,128)(2,1)}, bf16[128,768]{1,0:T(8,128)(2,1)S(1)}, u32[]{:S(2)}, u32[]{:S(2)}) collective-permute-start(bf16[128,768]{1,0:T(8,128)(2,1)} %get-tuple-element.16.hidden_hbm.refs_3_), channel_id=1, source_target_pairs={{0,24},{8,16},{16,8},{24,0},{1,25},{9,17},{17,9},{25,1},{2,26},{10... | collective-permute-start | bytes 589832 | tf_op jit(solution)/shard_map/ppermute | solution.py:411
  9.9 16.9 %collective-permute-start.1 = (bf16[128,768]{1,0:T(8,128)(2,1)}, bf16[128,768]{1,0:T(8,128)(2,1)S(1)}, u32[]{:S(2)}, u32[]{:S(2)}) collective-permute-start(bf16[128,768]{1,0:T(8,128)(2,1)} %get-tuple-element.16.hidden_hbm.refs_3_), channel_id=1, source_target_pairs={{0,16},{8,24},{16,0},{24,8},{1,17},{9,25},{17,1},{25,9},{2,18},{10... | collective-permute-start | bytes 589832 | tf_op jit(solution)/shard_map/ppermute | solution.py:411
  10.9 15.9 %collective-permute-start = (bf16[128,768]{1,0:T(8,128)(2,1)}, bf16[128,768]{1,0:T(8,128)(2,1)S(1)}, u32[]{:S(2)}, u32[]{:S(2)}) collective-permute-start(bf16[128,768]{1,0:T(8,128)(2,1)} %get-tuple-element.16.hidden_hbm.refs_3_), channel_id=1, source_target_pairs={{0,8},{8,0},{16,24},{24,16},{1,9},{9,1},{17,25},{25,17},{2,10},{10... | collective-permute-start | bytes 589832 | tf_op jit(solution)/shard_map/ppermute | solution.py:411
  27.7 34.8 %all-to-all-start.1 = ((bf16[8,16,4096]{2,1,0:T(8,128)(2,1)}), bf16[8,16,4096]{2,1,0:T(8,128)(2,1)S(1)}, u32[]{:S(2)}, u32[]{:S(2)}) async-start(bf16[8,16,4096]{2,1,0:T(8,128)(2,1)} %get-tuple-element.19), calls=%async_computation.1 | async-start | bytes 2097152 | tf_op jit(solution)/shard_map/all_to_all | solution.py:415
  32.7 19.3 %collective-permute-start.4 = (bf16[8,16,1024]{2,1,0:T(8,128)(2,1)}, bf16[8,16,1024]{2,1,0:T(8,128)(2,1)S(1)}, u32[]{:S(2)}, u32[]{:S(2)}) collective-permute-start(bf16[8,16,1024]{2,1,0:T(8,128)(2,1)} %get-tuple-element.24), channel_id=1, source_target_pairs={{0,16},{8,24},{16,0},{24,8},{1,17},{9,25},{17,1},{25,9},{2,18},{10... | collective-permute-start | bytes 786440 | tf_op jit(solution)/shard_map/ppermute | solution.py:411
  35.7 23.9 %collective-permute-start.5 = (bf16[8,16,1024]{2,1,0:T(8,128)(2,1)}, bf16[8,16,1024]{2,1,0:T(8,128)(2,1)S(1)}, u32[]{:S(2)}, u32[]{:S(2)}) collective-permute-start(bf16[8,16,1024]{2,1,0:T(8,128)(2,1)} %get-tuple-element.25), channel_id=1, source_target_pairs={{0,24},{8,16},{16,8},{24,0},{1,25},{9,17},{17,9},{25,1},{2,26},{10... | collective-permute-start | bytes 786440 | tf_op jit(solution)/shard_map/ppermute | solution.py:411
  35.9 23.7 %collective-permute-start.3 = (bf16[8,16,1024]{2,1,0:T(8,128)(2,1)}, bf16[8,16,1024]{2,1,0:T(8,128)(2,1)S(1)}, u32[]{:S(2)}, u32[]{:S(2)}) collective-permute-start(bf16[8,16,1024]{2,1,0:T(8,128)(2,1)} %get-tuple-element.23.tie_ref), channel_id=1, source_target_pairs={{0,8},{8,0},{16,24},{24,16},{1,9},{9,1},{17,25},{25,17},{2,10},{10... | collective-permute-start | bytes 786440 | tf_op jit(solution)/shard_map/ppermute | solution.py:411
where the time goes:
time: 66 us; the launch traced here: 65.7 us
  waiting for transfers between devices  24.5 us (37%)
  Pallas kernels  23.2 us (35%)
  starting transfers between devices  17.3 us (26%)
  between operations  0.69 us (1%)
    ppermute x6, waiting for transfers between devices, swap(): return lax.ppermute(value, axis, [(i, i ^ j) for i in range(size)])  24.5 us
    all_to_all x2, starting transfers between devices, exchange(): lax.all_to_all(value, 'expert', split_axis=0, concat_axis=0, tiled=True)  9.62 us
    ppermute x6, starting transfers between devices, swap(): return lax.ppermute(value, axis, [(i, i ^ j) for i in range(size)])  7.68 us
    pallas_call x1, Pallas kernels, forward(): pl.pallas_call(functools.partial(forward_kernel, flight, block), out_shap...  7.32 us
    pallas_call x1, Pallas kernels, backward(): pl.pallas_call(backward_kernel, out_shape=jax.ShapeDtypeStruct((slots, do...  5.54 us
    pallas_call x1, Pallas kernels, dispatch(): pl.pallas_call(functools.partial(dispatch_kernel, flight, groups), out_sh...  3.36 us
    pallas_call x1, Pallas kernels, combine(): pl.pallas_call(functools.partial(combine_kernel, block), out_shape=(jax.S...  3.24 us
    pallas_call x1, Pallas kernels, weight_grad(): pl.pallas_call(functools.partial(weight_grad_kernel, groups, block), out_...  2.83 us
  transfers between devices with their start and end apart: 8, of which 4 were waited for; matrix products, arithmetic and copies ran while one was open for 0% of the time, Pallas kernels for 24%

commit v1 on v0

--- a/solution.py
+++ b/solution.py
@@ -208,8 +208,8 @@
     )(hbm(scale), hbm(hidden), hbm(quant))
 
 
-def split_kernel(groups, out_ref, rows_ref, *refs):
-    pieces, sems = refs[groups:-1], refs[-1]
+def split_kernel(groups, ties, out_ref, rows_ref, *refs):
+    pieces, sems = refs[ties + 1 : -1], refs[-1]
     copies = [
         pltpu.make_async_copy(rows_ref.at[:, j], pieces[j - 1], sems.at[j - 1])
         for j in range(1, groups)
@@ -223,10 +223,10 @@
 def split(expert_out, rows, ties):
     flight, groups, cap, share = rows.shape
     return pl.pallas_call(
-        functools.partial(split_kernel, groups),
+        functools.partial(split_kernel, groups, len(ties)),
         out_shape=(pltpu.HBM(expert_out.shape, bf16),)
         + (pltpu.HBM((flight, cap, share), bf16),) * (groups - 1),
-        in_specs=[HBM] + [ANY] * groups,
+        in_specs=[HBM] + [ANY] * (1 + len(ties)),
         out_specs=(HBM,) * groups,
         scratch_shapes=[pltpu.SemaphoreType.DMA((groups - 1,))],
         input_output_aliases={0: 0},
@@ -280,7 +280,7 @@
     groups = rows.shape[1]
     return pl.pallas_call(
         backward_kernel,
-        out_shape=jax.ShapeDtypeStruct((slots, double), bf16),
+        out_shape=pltpu.HBM((slots, double), bf16),
         in_specs=[HBM, HBM, VMEM, ANY],
         out_specs=VMEM,
         scratch_shapes=[
@@ -335,8 +335,8 @@
     return pl.pallas_call(
         functools.partial(combine_kernel, block),
         out_shape=(
-            jax.ShapeDtypeStruct((tokens, width), bf16),
-            jax.ShapeDtypeStruct(ids.shape, f32),
+            pltpu.HBM((tokens, width), bf16),
+            pltpu.HBM(ids.shape, f32),
         ),
         in_specs=[HBM, VMEM, HBM, VMEM],
         out_specs=(VMEM, VMEM),
@@ -351,7 +351,7 @@
     )(hbm(ids), own, hbm(d_out), returned)
 
 
-def weight_grad_kernel(groups, block, rows_ref, *refs):
+def weight_grad_kernel(groups, block, tie_ref, rows_ref, *refs):
     part_refs, hid_refs = refs[: groups - 1], refs[groups - 1 : 2 * groups - 1]
     out_hbm, grads, hidden, out, sems, out_sems = refs[2 * groups - 1 :]
     flight, cap, share = part_refs[0].shape
@@ -385,13 +385,13 @@
         copy.wait()
 
 
-def weight_grad(rows, parts, hiddens, block=256):
+def weight_grad(tie, rows, parts, hiddens, block=256):
     flight, groups, cap, share = rows.shape
     slots, hid = hiddens[0].shape
     return pl.pallas_call(
         functools.partial(weight_grad_kernel, groups, block),
         out_shape=pltpu.HBM((share, hid), bf16),
-        in_specs=[ANY] * (2 * groups),
+        in_specs=[ANY] * (1 + 2 * groups),
         out_specs=HBM,
         scratch_shapes=[
             pltpu.VMEM((groups * flight, cap, share), bf16),
@@ -403,7 +403,7 @@
         compiler_params=params(),
         cost_estimate=SMALL,
         name="weight_grad",
-    )(rows, *parts, hbm(hiddens[0]), *hiddens[1:])
+    )(tie, rows, *parts, hbm(hiddens[0]), *hiddens[1:])
 
 
 def swap(value, axis, j):
@@ -422,14 +422,23 @@
     ids, probs = route_ids.T, route_probs.T
     hidden, own, rows = dispatch(gate_up, capacity, hot_lists, ids, probs, d_out, flight, groups)
     arrived = exchange(rows)
-    hiddens = [hidden] + [swap(hidden, "dp", j) for j in range(1, groups)]
+    hiddens, late = {0: hidden}, set()
+    bit = groups // 2
+    while bit:
+        for j in sorted(hiddens):
+            hiddens[j ^ bit] = swap(hiddens[j], "dp", bit)
+            if j:
+                late.add(j ^ bit)
+        bit //= 2
+    early = [hiddens[j] for j in range(1, groups) if j not in late]
+    hiddens = [hiddens[j] for j in range(groups)]
     weight, expert_out = forward(w_scale.transpose(1, 0, 2), hidden, w_quant[0], flight)
-    expert_out, *pieces = split(expert_out, arrived, hiddens[1:])
+    expert_out, *pieces = split(expert_out, arrived, early)
     returned = exchange(expert_out)
     parts = [swap(pieces[j - 1], "dp", j) for j in range(1, groups)]
     d_gate_up = backward(gate_up, weight, arrived, pieces[0])
     combined, d_probs = combine(ids, own, d_out, returned)
-    d_weight = weight_grad(arrived, parts, hiddens)
+    d_weight = weight_grad(d_probs, arrived, parts, hiddens)
     return (combined, d_probs.T, d_gate_up[None, None], d_weight[None])
 
 

time: 66 us -> 58.6 us (0.89)
  the two profiles are of different devices: /device:TPU:11 before, /device:TPU:10 now
where the time goes in v1:
time: 58.6 us; the launch traced here: 58.3 us
  Pallas kernels  23.1 us (39%)
  starting transfers between devices  17.1 us (29%)
  waiting for transfers between devices  16.7 us (28%)
  local copies, waits for them, and re-layouts  0.69 us (1%)
  between operations  0.69 us (1%)
    ppermute x6, waiting for transfers between devices, swap(): return lax.ppermute(value, axis, [(i, i ^ j) for i in range(size)])  11.8 us
    all_to_all x2, starting transfers between devices, exchange(): lax.all_to_all(value, 'expert', split_axis=0, concat_axis=0, tiled=True)  9.26 us
    ppermute x6, starting transfers between devices, swap(): return lax.ppermute(value, axis, [(i, i ^ j) for i in range(size)])  7.87 us
    pallas_call x1, Pallas kernels, forward(): pl.pallas_call(functools.partial(forward_kernel, flight, block), out_shap...  7.19 us
    pallas_call x1, Pallas kernels, backward(): pl.pallas_call(backward_kernel, out_shape=pltpu.HBM((slots, double), bf16...  5.55 us
    all_to_all x2, waiting for transfers between devices, exchange(): lax.all_to_all(value, 'expert', split_axis=0, concat_axis=0, tiled=True)  4.93 us
    pallas_call x1, Pallas kernels, dispatch(): pl.pallas_call(functools.partial(dispatch_kernel, flight, groups), out_sh...  3.36 us
    pallas_call x1, Pallas kernels, combine(): pl.pallas_call(functools.partial(combine_kernel, block), out_shape=(pltpu...  3.24 us
  transfers between devices with their start and end apart: 8, of which 5 were waited for; matrix products, arithmetic and copies ran while one was open for 0% of the time, Pallas kernels for 27%

profile of v1, /device:TPU:10, one launch (start us, length us, event | category | flops | bytes accessed | tf_op | source)
XLA Modules:
  0.0 58.3 jit_solution(15252218449780168166)
XLA Ops:
  0.6 3.4 %dispatch.1 = (bf16[128,768]{1,0:T(8,128)(2,1)}, f32[128,128]{1,0:T(8,128)S(1)}, bf16[8,4,16,1024]{3,2,1,0:T(8,128)(2,1)}) custom-call(bf16[128,1536]{1,0:T(8,128)(2,1)} %bitcast.10, s32[8]{0:T(128)} %cap_hbm.1, s32[1,4]{1,0:T(1,128)} %hot_hbm.1, s32[8,128]{1,0:T(8,128)} %bitcast.14, f32[8,128]{1,0:T(8,128)} %bitcast.16, bf16[128,4096]{1,0:T(8,128)(2,1)} %dout_hbm.3), custom_call_target="tpu_custom_call" | custom-call | flops 1024 | bytes 1024 | tf_op jit(solution)/shard_map/dispatch/pallas_call | solution.py:114
  4.0 4.3 %all-to-all-start = ((bf16[8,4,16,1024]{3,2,1,0:T(8,128)(2,1)}), bf16[8,4,16,1024]{3,2,1,0:T(8,128)(2,1)S(1)}, u32[]{:S(2)}, u32[]{:S(2)}) async-start(bf16[8,4,16,1024]{3,2,1,0:T(8,128)(2,1)} %get-tuple-element.18), calls=%async_computation | async-start | bytes 2097152 | tf_op jit(solution)/shard_map/all_to_all | solution.py:415
  8.3 0.4 collective-permute-start
  8.7 2.6 %collective-permute-start.1 = (bf16[128,768]{1,0:T(8,128)(2,1)}, bf16[128,768]{1,0:T(8,128)(2,1)S(1)}, u32[]{:S(2)}, u32[]{:S(2)}) collective-permute-start(bf16[128,768]{1,0:T(8,128)(2,1)} %get-tuple-element.16.hidden_hbm.refs_3_), channel_id=1, source_target_pairs={{0,16},{8,24},{16,0},{24,8},{1,17},{9,25},{17,1},{25,9},{2,18},{10... | collective-permute-start | bytes 589832 | tf_op jit(solution)/shard_map/ppermute | solution.py:411
  11.3 7.2 %expert_forward.1 = (bf16[768,4096]{1,0:T(8,128)(2,1)}, bf16[8,16,4096]{2,1,0:T(8,128)(2,1)}) custom-call(f32[6,1,32]{2,1,0:T(1,128)} %bitcast.17, bf16[128,768]{1,0:T(8,128)(2,1)} %get-tuple-element.16.hidden_hbm.refs_3_, bf16[768,4096]{1,0:T(8,128)(2,1)} %bitcast.9), custom_call_target="tpu_custom_call" | custom-call | flops 1024 | bytes 1024 | tf_op jit(solution)/shard_map/expert_forward/pallas_call | solution.py:186
  18.5 0.0 collective-permute-done.refs_0_.refs_4_
  18.5 2.2 %collective-permute-done.1.refs_1_.refs_5_ = bf16[128,768]{1,0:T(8,128)(2,1)S(1)} collective-permute-done((bf16[128,768]{1,0:T(8,128)(2,1)}, bf16[128,768]{1,0:T(8,128)(2,1)S(1)}, u32[]{:S(2)}, u32[]{:S(2)}) %collective-permute-start.1) | collective-permute-done | bytes 196640 | tf_op jit(solution)/shard_map/ppermute | solution.py:411
  20.8 1.4 %all-to-all-done.rows_ref = bf16[8,4,16,1024]{3,2,1,0:T(8,128)(2,1)S(1)} async-done(((bf16[8,4,16,1024]{3,2,1,0:T(8,128)(2,1)}), bf16[8,4,16,1024]{3,2,1,0:T(8,128)(2,1)S(1)}, u32[]{:S(2)}, u32[]{:S(2)}) %all-to-all-start) | async-done | bytes 1048608 | tf_op jit(solution)/shard_map/all_to_all | solution.py:415
  22.2 0.9 %split.1 = (bf16[8,16,4096]{2,1,0:T(8,128)(2,1)}, bf16[8,16,1024]{2,1,0:T(8,128)(2,1)}, bf16[8,16,1024]{2,1,0:T(8,128)(2,1)}, bf16[8,16,1024]{2,1,0:T(8,128)(2,1)}) custom-call(bf16[8,16,4096]{2,1,0:T(8,128)(2,1)} %get-tuple-element.17.out_ref, bf16[8,4,16,1024]{3,2,1,0:T(8,128)(2,1)S(1)} %all-to-all-done.rows_ref, ...), custom_call_target="tpu_custom_call", output_to_operand_aliasing={{0}: (0, {})} | custom-call | flops 1024 | bytes 1024 | tf_op jit(solution)/shard_map/split/pallas_call | solution.py:225
  23.1 5.0 %all-to-all-start.1 = ((bf16[8,16,4096]{2,1,0:T(8,128)(2,1)}), bf16[8,16,4096]{2,1,0:T(8,128)(2,1)S(1)}, u32[]{:S(2)}, u32[]{:S(2)}) async-start(bf16[8,16,4096]{2,1,0:T(8,128)(2,1)} %get-tuple-element.19), calls=%async_computation.1 | async-start | bytes 2097152 | tf_op jit(solution)/shard_map/all_to_all | solution.py:415
  28.1 0.4 collective-permute-start.2
  28.6 2.6 %collective-permute-start.3 = (bf16[8,16,1024]{2,1,0:T(8,128)(2,1)}, bf16[8,16,1024]{2,1,0:T(8,128)(2,1)S(1)}, u32[]{:S(2)}, u32[]{:S(2)}) collective-permute-start(bf16[8,16,1024]{2,1,0:T(8,128)(2,1)} %get-tuple-element.24), channel_id=1, source_target_pairs={{0,16},{8,24},{16,0},{24,8},{1,17},{9,25},{17,1},{25,9},{2,18},{10... | collective-permute-start | bytes 786440 | tf_op jit(solution)/shard_map/ppermute | solution.py:411
  31.1 0.4 collective-permute-start.4
  31.6 1.3 %collective-permute-start.5 = (bf16[128,768]{1,0:T(8,128)(2,1)S(1)}, bf16[128,768]{1,0:T(8,128)(2,1)S(1)}, u32[]{:S(2)}, u32[]{:S(2)}) collective-permute-start(bf16[128,768]{1,0:T(8,128)(2,1)S(1)} %collective-permute-done.1.refs_1_.refs_5_), channel_id=1, source_target_pairs={{0,8},{8,0},{16,24},{24,16},{1,9},{9,1},{17,25},{25,17},{2,10},{10... | collective-permute-start | bytes 589832 | tf_op jit(solution)/shard_map/ppermute | solution.py:411
  32.9 5.5 %expert_backward.1 = bf16[128,1536]{1,0:T(8,128)(2,1)} custom-call(bf16[128,1536]{1,0:T(8,128)(2,1)} %bitcast.11, bf16[768,4096]{1,0:T(8,128)(2,1)} %get-tuple-element.22.weight_hbm, bf16[8,4,16,1024]{3,2,1,0:T(8,128)(2,1)S(1)} %all-to-all-done.rows_ref, bf16[8,16,1024]{2,1,0:T(8,128)(2,1)} %get-tuple-element.23.tie_ref), custom_call_target="tpu_custom_call" | custom-call | flops 1024 | bytes 1024 | tf_op jit(solution)/shard_map/expert_backward/pallas_call | solution.py:281
  38.5 3.5 %all-to-all-done.1.ret_ref = bf16[8,16,4096]{2,1,0:T(8,128)(2,1)S(1)} async-done(((bf16[8,16,4096]{2,1,0:T(8,128)(2,1)}), bf16[8,16,4096]{2,1,0:T(8,128)(2,1)S(1)}, u32[]{:S(2)}, u32[]{:S(2)}) %all-to-all-start.1) | async-done | bytes 1048608 | tf_op jit(solution)/shard_map/all_to_all | solution.py:415
  42.0 3.2 %combine.1 = (bf16[128,4096]{1,0:T(8,128)(2,1)}, f32[8,128]{1,0:T(8,128)}) custom-call(s32[8,128]{1,0:T(8,128)} %bitcast.15, f32[128,128]{1,0:T(8,128)S(1)} %get-tuple-element.15.own_ref, bf16[128,4096]{1,0:T(8,128)(2,1)} %dout_hbm.3, bf16[8,16,4096]{2,1,0:T(8,128)(2,1)S(1)} %all-to-all-done.1.ret_ref), custom_call_target="tpu_custom_call" | custom-call | flops 1024 | bytes 1024 | tf_op jit(solution)/shard_map/combine/pallas_call | solution.py:335
  45.3 6.9 %collective-permute-done.5.refs_6_ = bf16[128,768]{1,0:T(8,128)(2,1)S(1)} collective-permute-done((bf16[128,768]{1,0:T(8,128)(2,1)S(1)}, bf16[128,768]{1,0:T(8,128)(2,1)S(1)}, u32[]{:S(2)}, u32[]{:S(2)}) %collective-permute-start.5) | collective-permute-done | bytes 196640 | tf_op jit(solution)/shard_map/ppermute | solution.py:411
  52.2 0.0 collective-permute-done.2.refs_0_
  52.2 0.0 collective-permute-done.3.refs_1_
  52.2 2.6 %collective-permute-done.4.refs_2_ = bf16[8,16,1024]{2,1,0:T(8,128)(2,1)S(1)} collective-permute-done((bf16[8,16,1024]{2,1,0:T(8,128)(2,1)}, bf16[8,16,1024]{2,1,0:T(8,128)(2,1)S(1)}, u32[]{:S(2)}, u32[]{:S(2)}) %collective-permute-start.4) | collective-permute-done | bytes 262176 | tf_op jit(solution)/shard_map/ppermute | solution.py:411
  54.8 0.0 copy-start
  54.8 0.7 %copy-done = f32[8,128]{1,0:T(8,128)S(1)} copy-done((f32[8,128]{1,0:T(8,128)S(1)}, f32[8,128]{1,0:T(8,128)}, u32[]{:S(2)}) %copy-start) | copy-done | bytes 4120
  55.5 2.8 %weight_grad.1 = bf16[1024,768]{1,0:T(8,128)(2,1)} custom-call(f32[8,128]{1,0:T(8,128)S(1)} %copy-done, bf16[8,4,16,1024]{3,2,1,0:T(8,128)(2,1)S(1)} %all-to-all-done.rows_ref, bf16[8,16,1024]{2,1,0:T(8,128)(2,1)S(1)} %collective-permute-done.2.refs_0_, bf16[8,16,1024]{2,1,0:T(8,128)(2,1)S(1)} %collective-permute-done.3.refs_1_, ...), custom_call_target="tpu_custom_call" | custom-call | flops 1024 | bytes 1024 | tf_op jit(solution)/shard_map/weight_grad/pallas_call | solution.py:391
Async XLA Ops:
  4.0 18.2 %all-to-all-start = ((bf16[8,4,16,1024]{3,2,1,0:T(8,128)(2,1)}), bf16[8,4,16,1024]{3,2,1,0:T(8,128)(2,1)S(1)}, u32[]{:S(2)}, u32[]{:S(2)}) async-start(bf16[8,4,16,1024]{3,2,1,0:T(8,128)(2,1)} %get-tuple-element.18), calls=%async_computation | async-start | bytes 2097152 | tf_op jit(solution)/shard_map/all_to_all | solution.py:415
  8.3 10.2 %collective-permute-start = (bf16[128,768]{1,0:T(8,128)(2,1)}, bf16[128,768]{1,0:T(8,128)(2,1)S(1)}, u32[]{:S(2)}, u32[]{:S(2)}) collective-permute-start(bf16[128,768]{1,0:T(8,128)(2,1)} %get-tuple-element.16.hidden_hbm.refs_3_), channel_id=1, source_target_pairs={{0,8},{8,0},{16,24},{24,16},{1,9},{9,1},{17,25},{25,17},{2,10},{10... | collective-permute-start | bytes 589832 | tf_op jit(solution)/shard_map/ppermute | solution.py:411
  8.7 12.0 %collective-permute-start.1 = (bf16[128,768]{1,0:T(8,128)(2,1)}, bf16[128,768]{1,0:T(8,128)(2,1)S(1)}, u32[]{:S(2)}, u32[]{:S(2)}) collective-permute-start(bf16[128,768]{1,0:T(8,128)(2,1)} %get-tuple-element.16.hidden_hbm.refs_3_), channel_id=1, source_target_pairs={{0,16},{8,24},{16,0},{24,8},{1,17},{9,25},{17,1},{25,9},{2,18},{10... | collective-permute-start | bytes 589832 | tf_op jit(solution)/shard_map/ppermute | solution.py:411
  23.1 18.9 %all-to-all-start.1 = ((bf16[8,16,4096]{2,1,0:T(8,128)(2,1)}), bf16[8,16,4096]{2,1,0:T(8,128)(2,1)S(1)}, u32[]{:S(2)}, u32[]{:S(2)}) async-start(bf16[8,16,4096]{2,1,0:T(8,128)(2,1)} %get-tuple-element.19), calls=%async_computation.1 | async-start | bytes 2097152 | tf_op jit(solution)/shard_map/all_to_all | solution.py:415
  28.1 24.1 %collective-permute-start.2 = (bf16[8,16,1024]{2,1,0:T(8,128)(2,1)}, bf16[8,16,1024]{2,1,0:T(8,128)(2,1)S(1)}, u32[]{:S(2)}, u32[]{:S(2)}) collective-permute-start(bf16[8,16,1024]{2,1,0:T(8,128)(2,1)} %get-tuple-element.23.tie_ref), channel_id=1, source_target_pairs={{0,8},{8,0},{16,24},{24,16},{1,9},{9,1},{17,25},{25,17},{2,10},{10... | collective-permute-start | bytes 786440 | tf_op jit(solution)/shard_map/ppermute | solution.py:411
  28.6 23.7 %collective-permute-start.3 = (bf16[8,16,1024]{2,1,0:T(8,128)(2,1)}, bf16[8,16,1024]{2,1,0:T(8,128)(2,1)S(1)}, u32[]{:S(2)}, u32[]{:S(2)}) collective-permute-start(bf16[8,16,1024]{2,1,0:T(8,128)(2,1)} %get-tuple-element.24), channel_id=1, source_target_pairs={{0,16},{8,24},{16,0},{24,8},{1,17},{9,25},{17,1},{25,9},{2,18},{10... | collective-permute-start | bytes 786440 | tf_op jit(solution)/shard_map/ppermute | solution.py:411
  31.1 23.7 %collective-permute-start.4 = (bf16[8,16,1024]{2,1,0:T(8,128)(2,1)}, bf16[8,16,1024]{2,1,0:T(8,128)(2,1)S(1)}, u32[]{:S(2)}, u32[]{:S(2)}) collective-permute-start(bf16[8,16,1024]{2,1,0:T(8,128)(2,1)} %get-tuple-element.25), channel_id=1, source_target_pairs={{0,24},{8,16},{16,8},{24,0},{1,25},{9,17},{17,9},{25,1},{2,26},{10... | collective-permute-start | bytes 786440 | tf_op jit(solution)/shard_map/ppermute | solution.py:411
  31.6 20.6 %collective-permute-start.5 = (bf16[128,768]{1,0:T(8,128)(2,1)S(1)}, bf16[128,768]{1,0:T(8,128)(2,1)S(1)}, u32[]{:S(2)}, u32[]{:S(2)}) collective-permute-start(bf16[128,768]{1,0:T(8,128)(2,1)S(1)} %collective-permute-done.1.refs_1_.refs_5_), channel_id=1, source_target_pairs={{0,8},{8,0},{16,24},{24,16},{1,9},{9,1},{17,25},{25,17},{2,10},{10... | collective-permute-start | bytes 589832 | tf_op jit(solution)/shard_map/ppermute | solution.py:411
  54.8 0.7 %copy-start = (f32[8,128]{1,0:T(8,128)S(1)}, f32[8,128]{1,0:T(8,128)}, u32[]{:S(2)}) copy-start(f32[8,128]{1,0:T(8,128)} %get-tuple-element.21.tie_ref) | copy-start | bytes 12292

commit v2 on v1

v2 whole, which is shorter than its diff:
```python
import functools

import jax
import jax.numpy as jnp
from jax import lax
from jax.experimental import pallas as pl
from jax.experimental.pallas import tpu as pltpu
from jax.sharding import PartitionSpec as P

QB = 128
CAP = 16
VMEM_LIMIT = 30 * 1024 * 1024

bf16 = jnp.bfloat16
f32 = jnp.float32

SMALL = pl.CostEstimate(flops=1024, bytes_accessed=1024, transcendentals=0)

VMEM = pl.BlockSpec(memory_space=pltpu.VMEM)
ANY = pl.BlockSpec(memory_space=pl.ANY)
HBM = pl.BlockSpec(memory_space=pltpu.HBM)


def params():
    return pltpu.CompilerParams(vmem_limit_bytes=VMEM_LIMIT)


def hbm(value):
    return pltpu.with_memory_space_constraint(value, pltpu.HBM)


def chunks(total, size):
    return [pl.ds(start, size) for start in range(0, total, size)]


def block_place(me, r, flight):
    half = flight // 2
    return me ^ (2 * (r % half) + r // half)


def dispatch_kernel(flight, groups, gate_up_hbm, cap_hbm, hot_hbm, ids_hbm, probs_hbm, dout_hbm, *refs):
    half = flight // 2
    hidden_hbm, own_ref, *chips = refs[: 2 + half]
    gate_up, cap_ref, hot_ref, ids_ref, probs_ref, dout, hidden, rows = refs[2 + half : 10 + half]
    gate_sems, hidden_sem, small_sems, in_sems, out_sems = refs[10 + half :]
    topk, tokens = ids_ref.shape
    slots = flight * CAP
    me, group = lax.axis_index("expert"), lax.axis_index("dp")
    share = dout_hbm.shape[1] // groups
    small = [
        pltpu.make_async_copy(src, dst, small_sems.at[i])
        for i, (src, dst) in enumerate(
            [(ids_hbm, ids_ref), (probs_hbm, probs_ref), (cap_hbm, cap_ref), (hot_hbm, hot_ref)]
        )
    ]
    loads = [
        pltpu.make_async_copy(
            dout_hbm.at[:, pl.ds(pl.multiple_of((group ^ j) * share, share), share)],
            dout.at[j],
            in_sems.at[j],
        )
        for j in range(groups)
    ]
    gates = [
        pltpu.make_async_copy(
            gate_up_hbm.at[pl.ds(pl.multiple_of(block_place(me, r, flight) * CAP, CAP), CAP)],
            gate_up.at[pl.ds(r * CAP, CAP)],
            gate_sems.at[r],
        )
        for r in range(flight)
    ]
    for copy in gates + small + loads:
        copy.start()
    for copy in gates:
        copy.wait()
    hid = hidden.shape[1]
    gate = gate_up[:, :hid].astype(f32)
    up = gate_up[:, hid:].astype(f32)
    hidden[...] = (gate * jax.nn.sigmoid(gate) * up).astype(bf16)
    hidden_copy = pltpu.make_async_copy(hidden, hidden_hbm, hidden_sem)
    hidden_copy.start()
    for copy in small:
        copy.wait()
    row = lax.broadcasted_iota(jnp.int32, (slots, 1), 0)
    row_expert = row // CAP
    row_rank = (row % CAP).astype(f32)
    limit = jnp.zeros((slots, 1), jnp.int32)
    for e in range(flight):
        hot = hot_ref[0, 0] == e
        for h in range(1, hot_ref.shape[1]):
            hot = jnp.logical_or(hot, hot_ref[0, h] == e)
        limit = jnp.where(row_expert == e, jnp.where(hot, CAP, cap_ref[e]), limit)
    limit = limit.astype(f32)
    named = jnp.zeros((slots, tokens), f32)
    weight = jnp.zeros((slots, tokens), f32)
    for k in range(topk):
        hit = ids_ref[k : k + 1, :] == row_expert
        named = jnp.where(hit, 1.0, named)
        weight = jnp.where(hit, probs_ref[k : k + 1, :], weight)
    first = lax.broadcasted_iota(jnp.int32, (tokens, tokens), 0)
    second = lax.broadcasted_iota(jnp.int32, (tokens, tokens), 1)
    before = (first < second).astype(f32).astype(bf16)
    rank = jnp.dot(named.astype(bf16), before, preferred_element_type=f32)
    owns = (named > 0.0) & (rank == row_rank) & (rank < limit)
    own_weight = jnp.where(owns, weight, 0.0)
    own_ref[...] = own_weight
    owner = jnp.where(owns, 1.0, 0.0).astype(bf16)
    slot_weight = jnp.sum(own_weight, axis=1, keepdims=True)
    stores = []
    for j in range(groups):
        loads[j].wait()
        part = jnp.dot(owner, dout[j], preferred_element_type=f32)
        rows[j] = (part * slot_weight).astype(bf16).reshape(flight, CAP, share)
        for c in range(half):
            for k in range(2):
                copy = pltpu.make_async_copy(
                    rows.at[j, me ^ (2 * c + k)], chips[c].at[k, j], out_sems.at[j, 2 * c + k]
                )
                copy.start()
                stores.append(copy)
    for copy in stores:
        copy.wait()
    hidden_copy.wait()


def dispatch(gate_up, capacity, hot_row, ids, probs, d_out, flight, groups):
    tokens, width = d_out.shape
    rows, double = gate_up.shape
    slots = flight * CAP
    share = width // groups
    half = flight // 2
    return pl.pallas_call(
        functools.partial(dispatch_kernel, flight, groups),
        out_shape=(
            pltpu.HBM((rows, double // 2), bf16),
            jax.ShapeDtypeStruct((slots, tokens), f32),
        )
        + (pltpu.HBM((2, groups, CAP, share), bf16),) * half,
        in_specs=[HBM] * 6,
        out_specs=(HBM, VMEM) + (HBM,) * half,
        scratch_shapes=[
            pltpu.VMEM((rows, double), bf16),
            pltpu.SMEM(capacity.shape, jnp.int32),
            pltpu.SMEM(hot_row.shape, jnp.int32),
            pltpu.VMEM(ids.shape, jnp.int32),
            pltpu.VMEM(probs.shape, f32),
            pltpu.VMEM((groups, tokens, share), bf16),
            pltpu.VMEM((rows, double // 2), bf16),
            pltpu.VMEM((groups, flight, CAP, share), bf16),
            pltpu.SemaphoreType.DMA((flight,)),
            pltpu.SemaphoreType.DMA,
            pltpu.SemaphoreType.DMA((4,)),
            pltpu.SemaphoreType.DMA((groups,)),
            pltpu.SemaphoreType.DMA((groups, flight)),
        ],
        compiler_params=params(),
        cost_estimate=SMALL,
        name="dispatch",
    )(hbm(gate_up), hbm(capacity), hbm(hot_row), hbm(ids), hbm(probs), hbm(d_out))


def dequant(weight, quant, scale, first):
    hid, block = quant.shape
    for i in range(hid // QB):
        for j in range(block // QB):
            at = (pl.ds(i * QB, QB), pl.ds(j * QB, QB))
            weight[at] = (quant[at].astype(f32) * scale[i, 0, first + j]).astype(bf16)


def forward_kernel(
    flight, block, scale_hbm, hidden_hbm, quant_hbm, out_hbm,
    scale, hidden, quant, weight, out, scale_sem, hidden_sems, in_sems, out_sems
):
    steps, hid, _ = quant.shape
    me = lax.axis_index("expert")
    loads = [
        pltpu.make_async_copy(quant_hbm.at[:, pl.ds(c * block, block)], quant.at[c], in_sems.at[c])
        for c in range(steps)
    ]
    small = [pltpu.make_async_copy(scale_hbm, scale, scale_sem)]
    for r in range(flight):
        place = pl.multiple_of(block_place(me, r, flight) * CAP, CAP)
        small.append(
            pltpu.make_async_copy(
                hidden_hbm.at[pl.ds(r * CAP, CAP)], hidden.at[pl.ds(place, CAP)], hidden_sems.at[r]
            )
        )
    for copy in loads[:1] + small + loads[1:]:
        copy.start()
    for copy in small:
        copy.wait()
    stores = []
    for c in range(steps + 1):
        if c < steps:
            loads[c].wait()
            dequant(weight.at[c], quant.at[c], scale, c * (block // QB))
        if c > 0:
            cols = pl.ds((c - 1) * block, block)
            part = jnp.dot(hidden[...], weight[c - 1], preferred_element_type=f32)
            out[:, :, cols] = part.astype(bf16).reshape(flight, CAP, block)
            copy = pltpu.make_async_copy(
                out.at[:, :, cols], out_hbm.at[:, :, cols], out_sems.at[c - 1]
            )
            copy.start()
            stores.append(copy)
    for copy in stores:
        copy.wait()


def forward(scale, hidden, quant, flight, block=512):
    hid, width = quant.shape
    steps = width // block
    return pl.pallas_call(
        functools.partial(forward_kernel, flight, block),
        out_shape=pltpu.HBM((flight, CAP, width), bf16),
        in_specs=[HBM, HBM, HBM],
        out_specs=HBM,
        scratch_shapes=[
            pltpu.SMEM(scale.shape, f32),
            pltpu.VMEM(hidden.shape, bf16),
            pltpu.VMEM((steps, hid, block), bf16),
            pltpu.VMEM((steps, hid, block), bf16),
            pltpu.VMEM((flight, CAP, width), bf16),
            pltpu.SemaphoreType.DMA,
            pltpu.SemaphoreType.DMA((flight,)),
            pltpu.SemaphoreType.DMA((steps,)),
            pltpu.SemaphoreType.DMA((steps,)),
        ],
        compiler_params=params(),
        cost_estimate=SMALL,
        name="expert_forward",
    )(hbm(scale), hbm(hidden), hbm(quant))


def copy_all(pairs, sems):
    copies = [pltpu.make_async_copy(src, dst, sems.at[i]) for i, (src, dst) in enumerate(pairs)]
    for copy in copies:
        copy.start()
    for copy in copies:
        copy.wait()


def sibling_kernel(half, *refs):
    chips, ties, (out_ref, sems) = refs[:half], refs[half:-2], refs[-2:]
    copy_all([(chips[c].at[1], out_ref.at[c]) for c in range(half)], sems)


def sibling_rows(chips, ties):
    half = len(chips)
    return pl.pallas_call(
        functools.partial(sibling_kernel, half),
        out_shape=pltpu.HBM((half,) + chips[0].shape[1:], bf16),
        in_specs=[ANY] * (half + len(ties)),
        out_specs=HBM,
        scratch_shapes=[pltpu.SemaphoreType.DMA((half,))],
        compiler_params=params(),
        cost_estimate=SMALL,
        name="sibling_rows",
    )(hbm(chips[0]), *chips[1:], *ties)


def split_kernel(half, groups, *refs):
    chips, swapped = refs[:half], refs[half]
    pieces, sems = refs[half + 1 : -1], refs[-1]
    pairs = []
    for j in range(1, groups):
        pairs.append((swapped.at[:, j], pieces[j - 1].at[pl.ds(half, half)]))
        for c in range(half):
            pairs.append((chips[c].at[0, j], pieces[j - 1].at[c]))
    copy_all(pairs, sems)


def split(chips, swapped):
    half, groups, cap, share = swapped.shape
    return pl.pallas_call(
        functools.partial(split_kernel, half, groups),
        out_shape=(pltpu.HBM((2 * half, cap, share), bf16),) * (groups - 1),
        in_specs=[ANY] * (half + 1),
        out_specs=(HBM,) * (groups - 1),
        scratch_shapes=[pltpu.SemaphoreType.DMA(((groups - 1) * (half + 1),))],
        compiler_params=params(),
        cost_estimate=SMALL,
        name="split",
    )(hbm(chips[0]), *chips[1:], swapped)


def backward_kernel(flight, groups, scale_hbm, gate_up_hbm, quant_hbm, tie_ref, swapped, *refs):
    half = flight // 2
    chips, out_hbm = refs[:half], refs[half]
    scale, gate_up, rows, quant, weight, acc, out = refs[half + 1 : half + 8]
    scale_sem, gate_sems, row_sems, in_sems, out_sems = refs[half + 8 :]
    me, group = lax.axis_index("expert"), lax.axis_index("dp")
    slots, hid = acc.shape
    share = quant.shape[2]

    def place(r):
        return pl.ds(pl.multiple_of(block_place(me, r, flight) * CAP, CAP), CAP)

    loads = [
        pltpu.make_async_copy(
            quant_hbm.at[:, pl.ds(pl.multiple_of((group ^ j) * share, share), share)],
            quant.at[j],
            in_sems.at[j],
        )
        for j in range(groups)
    ]
    gates = [
        pltpu.make_async_copy(
            gate_up_hbm.at[place(r)], gate_up.at[pl.ds(r * CAP, CAP)], gate_sems.at[r]
        )
        for r in range(flight)
    ]
    small = [pltpu.make_async_copy(scale_hbm, scale, scale_sem)]
    for r in range(flight):
        src = chips[r].at[0] if r < half else swapped.at[r - half]
        small.append(
            pltpu.make_async_copy(src, rows.at[:, pl.ds(r * CAP, CAP), :], row_sems.at[r])
        )
    for copy in loads[:1] + small + loads[1:] + gates:
        copy.start()
    for copy in small:
        copy.wait()
    for j in range(groups + 1):
        if j < groups:
            loads[j].wait()
            dequant(weight.at[j], quant.at[j], scale, (group ^ j) * (share // QB))
        if j > 0:
            part = lax.dot_general(
                rows[j - 1], weight[j - 1], (((1,), (1,)), ((), ())), preferred_element_type=f32
            )
            if j == 1:
                acc[...] = part
            else:
                acc[...] += part
    for copy in gates:
        copy.wait()
    gate = gate_up[:, :hid].astype(f32)
    up = gate_up[:, hid:].astype(f32)
    sig = jax.nn.sigmoid(gate)
    d_hidden = acc[...]
    out[:, :hid] = (d_hidden * up * sig * (1.0 + gate * (1.0 - sig))).astype(bf16)
    out[:, hid:] = (d_hidden * (gate * sig)).astype(bf16)
    copy_all([(out.at[pl.ds(r * CAP, CAP)], out_hbm.at[place(r)]) for r in range(flight)], out_sems)


def backward(scale, gate_up, quant, tie, chips, swapped):
    slots, double = gate_up.shape
    hid, width = quant.shape
    half, groups, cap, share = swapped.shape
    flight = 2 * half
    return pl.pallas_call(
        functools.partial(backward_kernel, flight, groups),
        out_shape=pltpu.HBM((slots, double), bf16),
        in_specs=[HBM, HBM, HBM, HBM] + [ANY] * (1 + half),
        out_specs=HBM,
        scratch_shapes=[
            pltpu.SMEM(scale.shape, f32),
            pltpu.VMEM((slots, double), bf16),
            pltpu.VMEM((groups, slots, share), bf16),
            pltpu.VMEM((groups, hid, share), bf16),
            pltpu.VMEM((groups, hid, share), bf16),
            pltpu.VMEM((slots, hid), f32),
            pltpu.VMEM((slots, double), bf16),
            pltpu.SemaphoreType.DMA,
            pltpu.SemaphoreType.DMA((flight,)),
            pltpu.SemaphoreType.DMA((flight,)),
            pltpu.SemaphoreType.DMA((groups,)),
            pltpu.SemaphoreType.DMA((flight,)),
        ],
        compiler_params=params(),
        cost_estimate=SMALL,
        name="expert_backward",
    )(hbm(scale), hbm(gate_up), hbm(quant), hbm(tie), swapped, hbm(chips[0]), *chips[1:])


def combine_kernel(
    block, ids_hbm, own_ref, dout_hbm, ret_ref, out_ref, dprobs_ref, ids_ref, dout, sems
):
    copies = [
        pltpu.make_async_copy(ids_hbm, ids_ref, sems.at[0]),
        pltpu.make_async_copy(dout_hbm, dout, sems.at[1]),
    ]
    for copy in copies:
        copy.start()
    topk, tokens = ids_ref.shape
    slots = own_ref.shape[0]
    width = dout.shape[1]
    own = own_ref[...]
    turned = own.T
    high = turned.astype(bf16)
    low = (turned - high.astype(f32)).astype(bf16)
    total = jnp.zeros((slots, tokens), f32)
    for copy in copies:
        copy.wait()
    for cols in chunks(width, block):
        here = ret_ref[:, :, cols].reshape(slots, block)
        out = jnp.dot(high, here, preferred_element_type=f32)
        out = out + jnp.dot(low, here, preferred_element_type=f32)
        out_ref[:, cols] = out.astype(bf16)
        total = total + lax.dot_general(
            here, dout[:, cols], (((1,), (1,)), ((), ())), preferred_element_type=f32
        )
    inner = jnp.where(own > 0.0, total, 0.0)
    row_expert = lax.broadcasted_iota(jnp.int32, (slots, 1), 0) // CAP
    for k in range(topk):
        mine = jnp.where(ids_ref[k : k + 1, :] == row_expert, inner, 0.0)
        dprobs_ref[k : k + 1, :] = jnp.sum(mine, axis=0, keepdims=True)


def combine(ids, own, d_out, returned, block=1024):
    tokens, width = d_out.shape
    return pl.pallas_call(
        functools.partial(combine_kernel, block),
        out_shape=(
            pltpu.HBM((tokens, width), bf16),
            pltpu.HBM(ids.shape, f32),
        ),
        in_specs=[HBM, VMEM, HBM, VMEM],
        out_specs=(VMEM, VMEM),
        scratch_shapes=[
            pltpu.VMEM(ids.shape, jnp.int32),
            pltpu.VMEM((tokens, width), bf16),
            pltpu.SemaphoreType.DMA((2,)),
        ],
        compiler_params=params(),
        cost_estimate=SMALL,
        name="combine",
    )(hbm(ids), own, hbm(d_out), returned)


def weight_grad_kernel(half, groups, block, tie_ref, swapped, *refs):
    chips, parts = refs[:half], refs[half : half + groups - 1]
    hid_refs = refs[half + groups - 1 : half + 2 * groups - 1]
    out_hbm, grads, hidden, out, sems, out_sems = refs[half + 2 * groups - 1 :]
    cap, share = parts[0].shape[1:]
    slots = 2 * half * cap
    pairs = [(chips[c].at[0, 0], grads.at[c]) for c in range(half)]
    pairs.append((swapped.at[:, 0], grads.at[pl.ds(half, half)]))
    for j in range(groups):
        pairs.append((hid_refs[j], hidden.at[pl.ds(j * slots, slots)]))
        if j:
            pairs.append((parts[j - 1], grads.at[pl.ds(2 * half * j, 2 * half)]))
    copy_all(pairs, sems)
    stores = []
    for c, cols in enumerate(chunks(share, block)):
        out[cols, :] = lax.dot_general(
            grads[:, :, cols].reshape(groups * slots, block),
            hidden[...],
            (((0,), (0,)), ((), ())),
            preferred_element_type=f32,
        ).astype(bf16)
        stores.append(pltpu.make_async_copy(out.at[cols], out_hbm.at[cols], out_sems.at[c]))
        stores[c].start()
    for copy in stores:
        copy.wait()


def weight_grad(tie, chips, swapped, parts, hiddens, block=256):
    half, groups, cap, share = swapped.shape
    slots, hid = hiddens[0].shape
    return pl.pallas_call(
        functools.partial(weight_grad_kernel, half, groups, block),
        out_shape=pltpu.HBM((share, hid), bf16),
        in_specs=[HBM] + [ANY] * (half + 2 * groups),
        out_specs=HBM,
        scratch_shapes=[
            pltpu.VMEM((groups * 2 * half, cap, share), bf16),
            pltpu.VMEM((groups * slots, hid), bf16),
            pltpu.VMEM((share, hid), bf16),
            pltpu.SemaphoreType.DMA((half + 2 * groups,)),
            pltpu.SemaphoreType.DMA((share // block,)),
        ],
        compiler_params=params(),
        cost_estimate=SMALL,
        name="weight_grad",
    )(hbm(tie), swapped, hbm(chips[0]), *chips[1:], *parts, hbm(hiddens[0]), *hiddens[1:])


def swap(value, axis, j):
    size = lax.axis_size(axis)
    return lax.ppermute(value, axis, [(i, i ^ j) for i in range(size)])


def shards(route_ids, route_probs, capacity, hot_lists, gate_up, w_quant, w_scale, d_out):
    flight = lax.axis_size("expert")
    groups = lax.axis_size("dp")
    gate_up = gate_up[0, 0]
    ids, probs = route_ids.T, route_probs.T
    scale = w_scale.transpose(1, 0, 2)
    hidden, own, *chips = dispatch(
        gate_up, capacity, hot_lists, ids, probs, d_out, flight, groups
    )
    chips = chips[:1] + [swap(chips[c], "expert", 2 * c) for c in range(1, flight // 2)]
    hiddens, late = {0: hidden}, set()
    bit = groups // 2
    while bit:
        for j in sorted(hiddens):
            hiddens[j ^ bit] = swap(hiddens[j], "dp", bit)
            if j:
                late.add(j ^ bit)
        bit //= 2
    early = [hiddens[j] for j in range(1, groups) if j not in late]
    hiddens = [hiddens[j] for j in range(groups)]
    expert_out = forward(scale, hidden, w_quant[0], flight)
    returned = lax.all_to_all(expert_out, "expert", split_axis=0, concat_axis=0, tiled=True)
    swapped = swap(sibling_rows(chips, [hbm(expert_out)] + early), "expert", 1)
    pieces = split(chips, swapped)
    parts = [swap(pieces[j - 1], "dp", j) for j in range(1, groups)]
    d_gate_up = backward(scale, gate_up, w_quant[0], pieces[0], chips, swapped)
    combined, d_probs = combine(ids, own, d_out, returned)
    d_weight = weight_grad(d_probs, chips, swapped, parts, hiddens)
    return (combined, d_probs.T, d_gate_up[None, None], d_weight[None])


def solution(mesh):
    placed = (
        P(("dp", "expert"), None),
        P(("dp", "expert"), None),
        P(),
        P("dp", None),
        P("dp", "expert", None, None),
        P("expert", None, None),
        P("expert", None, None),
        P(("dp", "expert"), None),
    )
    return jax.shard_map(
        shards,
        mesh=mesh,
        in_specs=placed,
        out_specs=(
            P(("dp", "expert"), None),
            P(("dp", "expert"), None),
            P("dp", "expert", None, None),
            P("expert", "dp", None),
        ),
        check_vma=False,
    )
```

time: 58.6 us -> 65.8 us (1.12)
  the two profiles are of different devices: /device:TPU:10 before, /device:TPU:0 now
where the time goes in v2:
time: 65.8 us; the launch traced here: 65.5 us
  Pallas kernels  32.9 us (50%)
  starting transfers between devices  18.3 us (28%)
  waiting for transfers between devices  12.1 us (18%)
  local copies, waits for them, and re-layouts  1.45 us (2%)
  between operations  0.75 us (1%)
    ppermute x10, starting transfers between devices, swap(): return lax.ppermute(value, axis, [(i, i ^ j) for i in range(size)])  14.6 us
    ppermute x10, waiting for transfers between devices, swap(): return lax.ppermute(value, axis, [(i, i ^ j) for i in range(size)])  12.1 us
    pallas_call x1, Pallas kernels, backward(): pl.pallas_call(functools.partial(backward_kernel, flight, groups), out_sh...  7.18 us
    pallas_call x1, Pallas kernels, forward(): pl.pallas_call(functools.partial(forward_kernel, flight, block), out_shap...  5.92 us
    pallas_call x1, Pallas kernels, sibling_rows(): pl.pallas_call(functools.partial(sibling_kernel, half), out_shape=pltpu.H...  5.11 us
    pallas_call x1, Pallas kernels, split(): pl.pallas_call(functools.partial(split_kernel, half, groups), out_shape=(...  4.22 us
    all_to_all x1, starting transfers between devices, shards(): lax.all_to_all(expert_out, 'expert', split_axis=0, concat_axis=0, tiled=T...  3.75 us
    pallas_call x1, Pallas kernels, dispatch(): pl.pallas_call(functools.partial(dispatch_kernel, flight, groups), out_sh...  3.62 us
  transfers between devices with their start and end apart: 11, of which 2 were waited for; matrix products, arithmetic and copies ran while one was open for 0% of the time, Pallas kernels for 39%

profile of v2, /device:TPU:0, one launch (start us, length us, event | category | flops | bytes accessed | tf_op | source)
XLA Modules:
  0.0 65.5 jit_solution(16177052438135302261)
XLA Ops:
  0.6 3.6 %dispatch.1 = (bf16[128,768]{1,0:T(8,128)(2,1)}, f32[128,128]{1,0:T(8,128)S(1)}, bf16[2,4,16,1024]{3,2,1,0:T(8,128)(2,1)}, bf16[2,4,16,1024]{3,2,1,0:T(8,128)(2,...) custom-call(bf16[128,1536]{1,0:T(8,128)(2,1)} %bitcast.11, s32[8]{0:T(128)} %cap_hbm.1, ...), custom_call_target="tpu_custom_call" | custom-call | flops 1024 | bytes 1024 | tf_op jit(solution)/shard_map/dispatch/pallas_call | solution.py:132
  4.3 0.6 copy-done
  4.9 2.9 %collective-permute-start = (bf16[2,4,16,1024]{3,2,1,0:T(8,128)(2,1)}, bf16[2,4,16,1024]{3,2,1,0:T(8,128)(2,1)S(1)}, u32[]{:S(2)}, u32[]{:S(2)}) collective-permute-start(bf16[2,4,16,1024]{3,2,1,0:T(8,128)(2,1)} %get-tuple-element.20), channel_id=1, source_target_pairs={{0,2},{1,3},{2,0},{3,1},{4,6},{5,7},{6,4},{7,5},{8,10},{9,11},{10,... | collective-permute-start | bytes 786440 | tf_op jit(solution)/shard_map/ppermute | solution.py:481
  7.8 1.5 %collective-permute-start.1 = (bf16[2,4,16,1024]{3,2,1,0:T(8,128)(2,1)}, bf16[2,4,16,1024]{3,2,1,0:T(8,128)(2,1)S(1)}, u32[]{:S(2)}, u32[]{:S(2)}) collective-permute-start(bf16[2,4,16,1024]{3,2,1,0:T(8,128)(2,1)} %get-tuple-element.21), channel_id=1, source_target_pairs={{0,4},{1,5},{2,6},{3,7},{4,0},{5,1},{6,2},{7,3},{8,12},{9,13},{10,... | collective-permute-start | bytes 786440 | tf_op jit(solution)/shard_map/ppermute | solution.py:481
  9.3 0.0 collective-permute-start.2
  9.3 3.1 %collective-permute-start.4 = (bf16[128,768]{1,0:T(8,128)(2,1)}, bf16[128,768]{1,0:T(8,128)(2,1)S(1)}, u32[]{:S(2)}, u32[]{:S(2)}) collective-permute-start(bf16[128,768]{1,0:T(8,128)(2,1)} %get-tuple-element.16.hidden_hbm.refs_7_), channel_id=1, source_target_pairs={{0,16},{8,24},{16,0},{24,8},{1,17},{9,25},{17,1},{25,9},{2,18},{10... | collective-permute-start | bytes 589832 | tf_op jit(solution)/shard_map/ppermute | solution.py:481
  12.4 1.6 %collective-permute-start.3 = (bf16[128,768]{1,0:T(8,128)(2,1)}, bf16[128,768]{1,0:T(8,128)(2,1)S(1)}, u32[]{:S(2)}, u32[]{:S(2)}) collective-permute-start(bf16[128,768]{1,0:T(8,128)(2,1)} %get-tuple-element.16.hidden_hbm.refs_7_), channel_id=1, source_target_pairs={{0,8},{8,0},{16,24},{24,16},{1,9},{9,1},{17,25},{25,17},{2,10},{10... | collective-permute-start | bytes 589832 | tf_op jit(solution)/shard_map/ppermute | solution.py:481
  14.0 5.9 %expert_forward.1.refs_4_ = bf16[8,16,4096]{2,1,0:T(8,128)(2,1)} custom-call(f32[6,1,32]{2,1,0:T(1,128)} %bitcast.16, bf16[128,768]{1,0:T(8,128)(2,1)} %get-tuple-element.16.hidden_hbm.refs_7_, bf16[768,4096]{1,0:T(8,128)(2,1)} %bitcast.8), custom_call_target="tpu_custom_call" | custom-call | flops 1024 | bytes 1024 | tf_op jit(solution)/shard_map/expert_forward/pallas_call | solution.py:213
  19.9 3.8 %all-to-all-start = ((bf16[8,16,4096]{2,1,0:T(8,128)(2,1)}), bf16[8,16,4096]{2,1,0:T(8,128)(2,1)S(1)}, u32[]{:S(2)}, u32[]{:S(2)}) async-start(bf16[8,16,4096]{2,1,0:T(8,128)(2,1)} %expert_forward.1.refs_4_), calls=%async_computation | async-start | bytes 2097152 | tf_op jit(solution)/shard_map/all_to_all | solution.py:505
  23.7 0.0 collective-permute-done.4.refs_6_.refs_9_
  23.7 0.0 collective-permute-done.refs_1_
  23.7 5.1 %sibling_rows.1 = bf16[4,4,16,1024]{3,2,1,0:T(8,128)(2,1)} custom-call(bf16[2,4,16,1024]{3,2,1,0:T(8,128)(2,1)} %get-tuple-element.19.refs_0_, bf16[2,4,16,1024]{3,2,1,0:T(8,128)(2,1)S(1)} %collective-permute-done.refs_1_, bf16[2,4,16,1024]{3,2,1,0:T(8,128)(2,1)S(1)} %collective-permute-done.1.refs_2_, ...), custom_call_target="tpu_custom_call" | custom-call | flops 1024 | bytes 1024 | tf_op jit(solution)/shard_map/sibling_rows/pallas_call | solution.py:250
  28.8 0.6 collective-permute-start.5
  29.4 1.7 %collective-permute-done.5.refs_4_.swapped = bf16[4,4,16,1024]{3,2,1,0:T(8,128)(2,1)S(1)} collective-permute-done((bf16[4,4,16,1024]{3,2,1,0:T(8,128)(2,1)}, bf16[4,4,16,1024]{3,2,1,0:T(8,128)(2,1)S(1)}, u32[]{:S(2)}, u32[]{:S(2)}) %collective-permute-start.5) | collective-permute-done | bytes 524320 | tf_op jit(solution)/shard_map/ppermute | solution.py:481
  31.1 4.2 %split.1 = (bf16[8,16,1024]{2,1,0:T(8,128)(2,1)}, bf16[8,16,1024]{2,1,0:T(8,128)(2,1)}, bf16[8,16,1024]{2,1,0:T(8,128)(2,1)}) custom-call(bf16[2,4,16,1024]{3,2,1,0:T(8,128)(2,1)} %get-tuple-element.19.refs_0_, bf16[2,4,16,1024]{3,2,1,0:T(8,128)(2,1)S(1)} %collective-permute-done.refs_1_, bf16[2,4,16,1024]{3,2,1,0:T(8,128)(2,1)S(1)} %collective-permute-done.1.refs_2_, ...), custom_call_target="tpu_custom_call" | custom-call | flops 1024 | bytes 1024 | tf_op jit(solution)/shard_map/split/pallas_call | solution.py:275
  35.4 0.4 collective-permute-start.7
  35.8 2.5 %collective-permute-start.8 = (bf16[8,16,1024]{2,1,0:T(8,128)(2,1)}, bf16[8,16,1024]{2,1,0:T(8,128)(2,1)S(1)}, u32[]{:S(2)}, u32[]{:S(2)}) collective-permute-start(bf16[8,16,1024]{2,1,0:T(8,128)(2,1)} %get-tuple-element.25), channel_id=1, source_target_pairs={{0,24},{8,16},{16,8},{24,0},{1,25},{9,17},{17,9},{25,1},{2,26},{10... | collective-permute-start | bytes 786440 | tf_op jit(solution)/shard_map/ppermute | solution.py:481
  38.3 0.7 %collective-permute-start.6 = (bf16[8,16,1024]{2,1,0:T(8,128)(2,1)}, bf16[8,16,1024]{2,1,0:T(8,128)(2,1)S(1)}, u32[]{:S(2)}, u32[]{:S(2)}) collective-permute-start(bf16[8,16,1024]{2,1,0:T(8,128)(2,1)} %get-tuple-element.23.tie_ref), channel_id=1, source_target_pairs={{0,8},{8,0},{16,24},{24,16},{1,9},{9,1},{17,25},{25,17},{2,10},{10... | collective-permute-start | bytes 786440 | tf_op jit(solution)/shard_map/ppermute | solution.py:481
  38.9 1.3 %collective-permute-start.9 = (bf16[128,768]{1,0:T(8,128)(2,1)S(1)}, bf16[128,768]{1,0:T(8,128)(2,1)}, u32[]{:S(2)}, u32[]{:S(2)}) collective-permute-start(bf16[128,768]{1,0:T(8,128)(2,1)S(1)} %collective-permute-done.4.refs_6_.refs_9_), channel_id=1, source_target_pairs={{0,8},{8,0},{16,24},{24,16},{1,9},{9,1},{17,25},{25,17},{2,10},{10... | collective-permute-start | bytes 589832 | tf_op jit(solution)/shard_map/ppermute | solution.py:481
  40.3 7.2 %expert_backward.1 = bf16[128,1536]{1,0:T(8,128)(2,1)} custom-call(f32[6,1,32]{2,1,0:T(1,128)} %bitcast.17, bf16[128,1536]{1,0:T(8,128)(2,1)} %bitcast.12, bf16[768,4096]{1,0:T(8,128)(2,1)} %bitcast.9, bf16[8,16,1024]{2,1,0:T(8,128)(2,1)} %get-tuple-element.23.tie_ref, bf16[4,4,16,1024]{3,2,1,0:T(8,128)(2,1)S(1)} %collective-permute-done.5.refs_4_.swapped, ...), custom_call_target="tpu_custom_call" | custom-call | flops 1024 | bytes 1024 | tf_op jit(solution)/shard_map/expert_backward/pallas_call | solution.py:351
  47.5 0.8 %copy-done.1 = f32[128,128]{1,0:T(8,128)S(1)} copy-done((f32[128,128]{1,0:T(8,128)S(1)}, f32[128,128]{1,0:T(8,128)}, u32[]{:S(2)}) %copy-start.1) | copy-done | bytes 65560
  48.3 3.2 %combine.1 = (bf16[128,4096]{1,0:T(8,128)(2,1)}, f32[8,128]{1,0:T(8,128)}) custom-call(s32[8,128]{1,0:T(8,128)} %bitcast.15, f32[128,128]{1,0:T(8,128)S(1)} %copy-done.1, bf16[128,4096]{1,0:T(8,128)(2,1)} %dout_hbm.3, bf16[8,16,4096]{2,1,0:T(8,128)(2,1)S(1)} %all-to-all-done.ret_ref), custom_call_target="tpu_custom_call" | custom-call | flops 1024 | bytes 1024 | tf_op jit(solution)/shard_map/combine/pallas_call | solution.py:412
  51.6 10.4 %collective-permute-done.9.refs_10_ = bf16[128,768]{1,0:T(8,128)(2,1)} collective-permute-done((bf16[128,768]{1,0:T(8,128)(2,1)S(1)}, bf16[128,768]{1,0:T(8,128)(2,1)}, u32[]{:S(2)}, u32[]{:S(2)}) %collective-permute-start.9) | collective-permute-done | bytes 196640 | tf_op jit(solution)/shard_map/ppermute | solution.py:481
  61.9 3.6 %weight_grad.1 = bf16[1024,768]{1,0:T(8,128)(2,1)} custom-call(f32[8,128]{1,0:T(8,128)} %get-tuple-element.18.tie_ref, bf16[4,4,16,1024]{3,2,1,0:T(8,128)(2,1)S(1)} %collective-permute-done.5.refs_4_.swapped, bf16[2,4,16,1024]{3,2,1,0:T(8,128)(2,1)} %get-tuple-element.19.refs_0_, bf16[2,4,16,1024]{3,2,1,0:T(8,128)(2,1)S(1)} %collective-permute-done.refs_1_, ...), custom_call_target="tpu_custom_call" | custom-call | flops 1024 | bytes 1024 | tf_op jit(solution)/shard_map/weight_grad/pallas_call | solution.py:461
  (9 shorter events, 0.0 us)
Async XLA Ops:
  4.3 0.6 copy-start
  4.9 18.8 %collective-permute-start = (bf16[2,4,16,1024]{3,2,1,0:T(8,128)(2,1)}, bf16[2,4,16,1024]{3,2,1,0:T(8,128)(2,1)S(1)}, u32[]{:S(2)}, u32[]{:S(2)}) collective-permute-start(bf16[2,4,16,1024]{3,2,1,0:T(8,128)(2,1)} %get-tuple-element.20), channel_id=1, source_target_pairs={{0,2},{1,3},{2,0},{3,1},{4,6},{5,7},{6,4},{7,5},{8,10},{9,11},{10,... | collective-permute-start | bytes 786440 | tf_op jit(solution)/shard_map/ppermute | solution.py:481
  7.8 15.9 %collective-permute-start.1 = (bf16[2,4,16,1024]{3,2,1,0:T(8,128)(2,1)}, bf16[2,4,16,1024]{3,2,1,0:T(8,128)(2,1)S(1)}, u32[]{:S(2)}, u32[]{:S(2)}) collective-permute-start(bf16[2,4,16,1024]{3,2,1,0:T(8,128)(2,1)} %get-tuple-element.21), channel_id=1, source_target_pairs={{0,4},{1,5},{2,6},{3,7},{4,0},{5,1},{6,2},{7,3},{8,12},{9,13},{10,... | collective-permute-start | bytes 786440 | tf_op jit(solution)/shard_map/ppermute | solution.py:481
  9.3 14.4 %collective-permute-start.2 = (bf16[2,4,16,1024]{3,2,1,0:T(8,128)(2,1)}, bf16[2,4,16,1024]{3,2,1,0:T(8,128)(2,1)S(1)}, u32[]{:S(2)}, u32[]{:S(2)}) collective-permute-start(bf16[2,4,16,1024]{3,2,1,0:T(8,128)(2,1)} %get-tuple-element.22), channel_id=1, source_target_pairs={{0,6},{1,7},{2,4},{3,5},{4,2},{5,3},{6,0},{7,1},{8,14},{9,15},{10,... | collective-permute-start | bytes 786440 | tf_op jit(solution)/shard_map/ppermute | solution.py:481
  9.3 14.3 %collective-permute-start.4 = (bf16[128,768]{1,0:T(8,128)(2,1)}, bf16[128,768]{1,0:T(8,128)(2,1)S(1)}, u32[]{:S(2)}, u32[]{:S(2)}) collective-permute-start(bf16[128,768]{1,0:T(8,128)(2,1)} %get-tuple-element.16.hidden_hbm.refs_7_), channel_id=1, source_target_pairs={{0,16},{8,24},{16,0},{24,8},{1,17},{9,25},{17,1},{25,9},{2,18},{10... | collective-permute-start | bytes 589832 | tf_op jit(solution)/shard_map/ppermute | solution.py:481
  12.4 11.3 %collective-permute-start.3 = (bf16[128,768]{1,0:T(8,128)(2,1)}, bf16[128,768]{1,0:T(8,128)(2,1)S(1)}, u32[]{:S(2)}, u32[]{:S(2)}) collective-permute-start(bf16[128,768]{1,0:T(8,128)(2,1)} %get-tuple-element.16.hidden_hbm.refs_7_), channel_id=1, source_target_pairs={{0,8},{8,0},{16,24},{24,16},{1,9},{9,1},{17,25},{25,17},{2,10},{10... | collective-permute-start | bytes 589832 | tf_op jit(solution)/shard_map/ppermute | solution.py:481
  19.9 27.6 %all-to-all-start = ((bf16[8,16,4096]{2,1,0:T(8,128)(2,1)}), bf16[8,16,4096]{2,1,0:T(8,128)(2,1)S(1)}, u32[]{:S(2)}, u32[]{:S(2)}) async-start(bf16[8,16,4096]{2,1,0:T(8,128)(2,1)} %expert_forward.1.refs_4_), calls=%async_computation | async-start | bytes 2097152 | tf_op jit(solution)/shard_map/all_to_all | solution.py:505
  28.8 2.3 %collective-permute-start.5 = (bf16[4,4,16,1024]{3,2,1,0:T(8,128)(2,1)}, bf16[4,4,16,1024]{3,2,1,0:T(8,128)(2,1)S(1)}, u32[]{:S(2)}, u32[]{:S(2)}) collective-permute-start(bf16[4,4,16,1024]{3,2,1,0:T(8,128)(2,1)} %sibling_rows.1), channel_id=1, source_target_pairs={{0,1},{1,0},{2,3},{3,2},{4,5},{5,4},{6,7},{7,6},{8,9},{9,8},{10,11... | collective-permute-start | bytes 1572872 | tf_op jit(solution)/shard_map/ppermute | solution.py:481
  35.4 26.6 %collective-permute-start.7 = (bf16[8,16,1024]{2,1,0:T(8,128)(2,1)}, bf16[8,16,1024]{2,1,0:T(8,128)(2,1)S(1)}, u32[]{:S(2)}, u32[]{:S(2)}) collective-permute-start(bf16[8,16,1024]{2,1,0:T(8,128)(2,1)} %get-tuple-element.24), channel_id=1, source_target_pairs={{0,16},{8,24},{16,0},{24,8},{1,17},{9,25},{17,1},{25,9},{2,18},{10... | collective-permute-start | bytes 786440 | tf_op jit(solution)/shard_map/ppermute | solution.py:481
  35.8 26.2 %collective-permute-start.8 = (bf16[8,16,1024]{2,1,0:T(8,128)(2,1)}, bf16[8,16,1024]{2,1,0:T(8,128)(2,1)S(1)}, u32[]{:S(2)}, u32[]{:S(2)}) collective-permute-start(bf16[8,16,1024]{2,1,0:T(8,128)(2,1)} %get-tuple-element.25), channel_id=1, source_target_pairs={{0,24},{8,16},{16,8},{24,0},{1,25},{9,17},{17,9},{25,1},{2,26},{10... | collective-permute-start | bytes 786440 | tf_op jit(solution)/shard_map/ppermute | solution.py:481
  38.3 23.7 %collective-permute-start.6 = (bf16[8,16,1024]{2,1,0:T(8,128)(2,1)}, bf16[8,16,1024]{2,1,0:T(8,128)(2,1)S(1)}, u32[]{:S(2)}, u32[]{:S(2)}) collective-permute-start(bf16[8,16,1024]{2,1,0:T(8,128)(2,1)} %get-tuple-element.23.tie_ref), channel_id=1, source_target_pairs={{0,8},{8,0},{16,24},{24,16},{1,9},{9,1},{17,25},{25,17},{2,10},{10... | collective-permute-start | bytes 786440 | tf_op jit(solution)/shard_map/ppermute | solution.py:481
  38.9 23.0 %collective-permute-start.9 = (bf16[128,768]{1,0:T(8,128)(2,1)S(1)}, bf16[128,768]{1,0:T(8,128)(2,1)}, u32[]{:S(2)}, u32[]{:S(2)}) collective-permute-start(bf16[128,768]{1,0:T(8,128)(2,1)S(1)} %collective-permute-done.4.refs_6_.refs_9_), channel_id=1, source_target_pairs={{0,8},{8,0},{16,24},{24,16},{1,9},{9,1},{17,25},{25,17},{2,10},{10... | collective-permute-start | bytes 589832 | tf_op jit(solution)/shard_map/ppermute | solution.py:481
  47.5 0.8 %copy-start.1 = (f32[128,128]{1,0:T(8,128)S(1)}, f32[128,128]{1,0:T(8,128)}, u32[]{:S(2)}) copy-start(f32[128,128]{1,0:T(8,128)} %copy-done) | copy-start | bytes 196612

commit v3 on v2

--- a/solution.py
+++ b/solution.py
@@ -40,9 +40,10 @@
 
 def dispatch_kernel(flight, groups, gate_up_hbm, cap_hbm, hot_hbm, ids_hbm, probs_hbm, dout_hbm, *refs):
     half = flight // 2
-    hidden_hbm, own_ref, *chips = refs[: 2 + half]
-    gate_up, cap_ref, hot_ref, ids_ref, probs_ref, dout, hidden, rows = refs[2 + half : 10 + half]
-    gate_sems, hidden_sem, small_sems, in_sems, out_sems = refs[10 + half :]
+    hidden_hbm, own_hbm, *chips = refs[: 2 + half]
+    gate_up, cap_ref, hot_ref, ids_ref, probs_ref, dout = refs[2 + half : 8 + half]
+    hidden, own_ref, rows = refs[8 + half : 11 + half]
+    gate_sems, keep_sems, small_sems, in_sems, out_sems = refs[11 + half :]
     topk, tokens = ids_ref.shape
     slots = flight * CAP
     me, group = lax.axis_index("expert"), lax.axis_index("dp")
@@ -77,7 +78,7 @@
     gate = gate_up[:, :hid].astype(f32)
     up = gate_up[:, hid:].astype(f32)
     hidden[...] = (gate * jax.nn.sigmoid(gate) * up).astype(bf16)
-    hidden_copy = pltpu.make_async_copy(hidden, hidden_hbm, hidden_sem)
+    hidden_copy = pltpu.make_async_copy(hidden, hidden_hbm, keep_sems.at[0])
     hidden_copy.start()
     for copy in small:
         copy.wait()
@@ -104,6 +105,8 @@
     owns = (named > 0.0) & (rank == row_rank) & (rank < limit)
     own_weight = jnp.where(owns, weight, 0.0)
     own_ref[...] = own_weight
+    own_copy = pltpu.make_async_copy(own_ref, own_hbm, keep_sems.at[1])
+    own_copy.start()
     owner = jnp.where(owns, 1.0, 0.0).astype(bf16)
     slot_weight = jnp.sum(own_weight, axis=1, keepdims=True)
     stores = []
@@ -121,6 +124,7 @@
     for copy in stores:
         copy.wait()
     hidden_copy.wait()
+    own_copy.wait()
 
 
 def dispatch(gate_up, capacity, hot_row, ids, probs, d_out, flight, groups):
@@ -133,11 +137,11 @@
         functools.partial(dispatch_kernel, flight, groups),
         out_shape=(
             pltpu.HBM((rows, double // 2), bf16),
-            jax.ShapeDtypeStruct((slots, tokens), f32),
+            pltpu.HBM((slots, tokens), f32),
         )
         + (pltpu.HBM((2, groups, CAP, share), bf16),) * half,
         in_specs=[HBM] * 6,
-        out_specs=(HBM, VMEM) + (HBM,) * half,
+        out_specs=(HBM, HBM) + (HBM,) * half,
         scratch_shapes=[
             pltpu.VMEM((rows, double), bf16),
             pltpu.SMEM(capacity.shape, jnp.int32),
@@ -146,9 +150,10 @@
             pltpu.VMEM(probs.shape, f32),
             pltpu.VMEM((groups, tokens, share), bf16),
             pltpu.VMEM((rows, double // 2), bf16),
+            pltpu.VMEM((slots, tokens), f32),
             pltpu.VMEM((groups, flight, CAP, share), bf16),
             pltpu.SemaphoreType.DMA((flight,)),
-            pltpu.SemaphoreType.DMA,
+            pltpu.SemaphoreType.DMA((2,)),
             pltpu.SemaphoreType.DMA((4,)),
             pltpu.SemaphoreType.DMA((groups,)),
             pltpu.SemaphoreType.DMA((groups, flight)),
@@ -164,7 +169,9 @@
     for i in range(hid // QB):
         for j in range(block // QB):
             at = (pl.ds(i * QB, QB), pl.ds(j * QB, QB))
-            weight[at] = (quant[at].astype(f32) * scale[i, 0, first + j]).astype(bf16)
+            factor = jnp.full((CAP, QB), scale[i, 0, first + j], f32).astype(bf16)
+            part = quant[at].reshape(QB // CAP, CAP, QB) * factor[None]
+            weight[at] = part.reshape(QB, QB)
 
 
 def forward_kernel(
@@ -249,9 +256,9 @@
     half = len(chips)
     return pl.pallas_call(
         functools.partial(sibling_kernel, half),
-        out_shape=pltpu.HBM((half,) + chips[0].shape[1:], bf16),
+        out_shape=pltpu.VMEM((half,) + chips[0].shape[1:], bf16),
         in_specs=[ANY] * (half + len(ties)),
-        out_specs=HBM,
+        out_specs=VMEM,
         scratch_shapes=[pltpu.SemaphoreType.DMA((half,))],
         compiler_params=params(),
         cost_estimate=SMALL,
@@ -274,9 +281,9 @@
     half, groups, cap, share = swapped.shape
     return pl.pallas_call(
         functools.partial(split_kernel, half, groups),
-        out_shape=(pltpu.HBM((2 * half, cap, share), bf16),) * (groups - 1),
+        out_shape=(pltpu.VMEM((2 * half, cap, share), bf16),) * (groups - 1),
         in_specs=[ANY] * (half + 1),
-        out_specs=(HBM,) * (groups - 1),
+        out_specs=(VMEM,) * (groups - 1),
         scratch_shapes=[pltpu.SemaphoreType.DMA(((groups - 1) * (half + 1),))],
         compiler_params=params(),
         cost_estimate=SMALL,
@@ -351,7 +358,7 @@
     return pl.pallas_call(
         functools.partial(backward_kernel, flight, groups),
         out_shape=pltpu.HBM((slots, double), bf16),
-        in_specs=[HBM, HBM, HBM, HBM] + [ANY] * (1 + half),
+        in_specs=[HBM, HBM, HBM] + [ANY] * (2 + half),
         out_specs=HBM,
         scratch_shapes=[
             pltpu.SMEM(scale.shape, f32),
@@ -370,28 +377,30 @@
         compiler_params=params(),
         cost_estimate=SMALL,
         name="expert_backward",
-    )(hbm(scale), hbm(gate_up), hbm(quant), hbm(tie), swapped, hbm(chips[0]), *chips[1:])
+    )(hbm(scale), hbm(gate_up), hbm(quant), tie, swapped, hbm(chips[0]), *chips[1:])
 
 
 def combine_kernel(
-    block, ids_hbm, own_ref, dout_hbm, ret_ref, out_ref, dprobs_ref, ids_ref, dout, sems
+    block, ids_hbm, own_hbm, dout_hbm, ret_ref, out_ref, dprobs_ref, ids_ref, own_ref, dout, sems
 ):
     copies = [
         pltpu.make_async_copy(ids_hbm, ids_ref, sems.at[0]),
-        pltpu.make_async_copy(dout_hbm, dout, sems.at[1]),
+        pltpu.make_async_copy(own_hbm, own_ref, sems.at[1]),
+        pltpu.make_async_copy(dout_hbm, dout, sems.at[2]),
     ]
     for copy in copies:
         copy.start()
     topk, tokens = ids_ref.shape
     slots = own_ref.shape[0]
     width = dout.shape[1]
+    copies[1].wait()
     own = own_ref[...]
     turned = own.T
     high = turned.astype(bf16)
     low = (turned - high.astype(f32)).astype(bf16)
     total = jnp.zeros((slots, tokens), f32)
-    for copy in copies:
-        copy.wait()
+    copies[0].wait()
+    copies[2].wait()
     for cols in chunks(width, block):
         here = ret_ref[:, :, cols].reshape(slots, block)
         out = jnp.dot(high, here, preferred_element_type=f32)
@@ -415,17 +424,18 @@
             pltpu.HBM((tokens, width), bf16),
             pltpu.HBM(ids.shape, f32),
         ),
-        in_specs=[HBM, VMEM, HBM, VMEM],
+        in_specs=[HBM, HBM, HBM, VMEM],
         out_specs=(VMEM, VMEM),
         scratch_shapes=[
             pltpu.VMEM(ids.shape, jnp.int32),
+            pltpu.VMEM(own.shape, f32),
             pltpu.VMEM((tokens, width), bf16),
-            pltpu.SemaphoreType.DMA((2,)),
+            pltpu.SemaphoreType.DMA((3,)),
         ],
         compiler_params=params(),
         cost_estimate=SMALL,
         name="combine",
-    )(hbm(ids), own, hbm(d_out), returned)
+    )(hbm(ids), hbm(own), hbm(d_out), returned)
 
 
 def weight_grad_kernel(half, groups, block, tie_ref, swapped, *refs):

time: 65.8 us -> 59.5 us (0.904)
  Pallas kernels: 32.9 us -> 27.1 us
  local copies, waits for them, and re-layouts: 1.45 us -> 0 us
  waiting for transfers between devices: 12.1 us -> 12.9 us
    pallas_call x1, Pallas kernels: 5.11 us -> 0.95 us  [sibling_rows(): pl.pallas_call(functools.partial(sibling_kernel, half), out_shape=pltpu.V...]
    pallas_call x1, Pallas kernels: 4.22 us -> 2.17 us  [split(): pl.pallas_call(functools.partial(split_kernel, half, groups), out_shape=(...]
    unnamed x4 -> x0, local copies, waits for them, and re-layouts: 1.45 us -> none
    ppermute x10, waiting for transfers between devices: 12.1 us -> 12.8 us  [swap(): return lax.ppermute(value, axis, [(i, i ^ j) for i in range(size)])]
  transfers between devices with their start and end apart: 11 -> 11, of which waited for: 2 -> 2; matrix products, arithmetic and copies ran while one was open for 0% -> 0% of each run, Pallas kernels for 39% -> 34%
where the time goes in v3:
time: 59.5 us; the launch traced here: 59.1 us
  Pallas kernels  27.1 us (46%)
  starting transfers between devices  18.4 us (31%)
  waiting for transfers between devices  12.9 us (22%)
  between operations  0.73 us (1%)
    ppermute x10, starting transfers between devices, swap(): return lax.ppermute(value, axis, [(i, i ^ j) for i in range(size)])  14.6 us
    ppermute x10, waiting for transfers between devices, swap(): return lax.ppermute(value, axis, [(i, i ^ j) for i in range(size)])  12.8 us
    pallas_call x1, Pallas kernels, backward(): pl.pallas_call(functools.partial(backward_kernel, flight, groups), out_sh...  7.04 us
    pallas_call x1, Pallas kernels, forward(): pl.pallas_call(functools.partial(forward_kernel, flight, block), out_shap...  6.44 us
    all_to_all x1, starting transfers between devices, shards(): lax.all_to_all(expert_out, 'expert', split_axis=0, concat_axis=0, tiled=T...  3.73 us
    pallas_call x1, Pallas kernels, dispatch(): pl.pallas_call(functools.partial(dispatch_kernel, flight, groups), out_sh...  3.63 us
    pallas_call x1, Pallas kernels, weight_grad(): pl.pallas_call(functools.partial(weight_grad_kernel, half, groups, block)...  3.58 us
    pallas_call x1, Pallas kernels, combine(): pl.pallas_call(functools.partial(combine_kernel, block), out_shape=(pltpu...  3.29 us
  transfers between devices with their start and end apart: 11, of which 2 were waited for; matrix products, arithmetic and copies ran while one was open for 0% of the time, Pallas kernels for 34%

profile of v3, /device:TPU:0, one launch (start us, length us, event | category | flops | bytes accessed | tf_op | source)
XLA Modules:
  0.0 59.1 jit_solution(10989656302229897789)
XLA Ops:
  0.6 3.6 %dispatch.1 = (bf16[128,768]{1,0:T(8,128)(2,1)}, f32[128,128]{1,0:T(8,128)}, bf16[2,4,16,1024]{3,2,1,0:T(8,128)(2,1)}, bf16[2,4,16,1024]{3,2,1,0:T(8,128)(2,1)},...) custom-call(bf16[128,1536]{1,0:T(8,128)(2,1)} %bitcast.11, s32[8]{0:T(128)} %cap_hbm.1, ...), custom_call_target="tpu_custom_call" | custom-call | flops 1024 | bytes 1024 | tf_op jit(solution)/shard_map/dispatch/pallas_call | solution.py:136
  4.3 3.0 %collective-permute-start = (bf16[2,4,16,1024]{3,2,1,0:T(8,128)(2,1)}, bf16[2,4,16,1024]{3,2,1,0:T(8,128)(2,1)S(1)}, u32[]{:S(2)}, u32[]{:S(2)}) collective-permute-start(bf16[2,4,16,1024]{3,2,1,0:T(8,128)(2,1)} %get-tuple-element.20), channel_id=1, source_target_pairs={{0,2},{1,3},{2,0},{3,1},{4,6},{5,7},{6,4},{7,5},{8,10},{9,11},{10,... | collective-permute-start | bytes 786440 | tf_op jit(solution)/shard_map/ppermute | solution.py:491
  7.3 1.5 %collective-permute-start.1 = (bf16[2,4,16,1024]{3,2,1,0:T(8,128)(2,1)}, bf16[2,4,16,1024]{3,2,1,0:T(8,128)(2,1)S(1)}, u32[]{:S(2)}, u32[]{:S(2)}) collective-permute-start(bf16[2,4,16,1024]{3,2,1,0:T(8,128)(2,1)} %get-tuple-element.21), channel_id=1, source_target_pairs={{0,4},{1,5},{2,6},{3,7},{4,0},{5,1},{6,2},{7,3},{8,12},{9,13},{10,... | collective-permute-start | bytes 786440 | tf_op jit(solution)/shard_map/ppermute | solution.py:491
  8.8 0.0 collective-permute-start.2
  8.8 3.0 %collective-permute-start.4 = (bf16[128,768]{1,0:T(8,128)(2,1)}, bf16[128,768]{1,0:T(8,128)(2,1)S(1)}, u32[]{:S(2)}, u32[]{:S(2)}) collective-permute-start(bf16[128,768]{1,0:T(8,128)(2,1)} %get-tuple-element.16.hidden_hbm.refs_7_), channel_id=1, source_target_pairs={{0,16},{8,24},{16,0},{24,8},{1,17},{9,25},{17,1},{25,9},{2,18},{10... | collective-permute-start | bytes 589832 | tf_op jit(solution)/shard_map/ppermute | solution.py:491
  11.9 1.6 %collective-permute-start.3 = (bf16[128,768]{1,0:T(8,128)(2,1)}, bf16[128,768]{1,0:T(8,128)(2,1)S(1)}, u32[]{:S(2)}, u32[]{:S(2)}) collective-permute-start(bf16[128,768]{1,0:T(8,128)(2,1)} %get-tuple-element.16.hidden_hbm.refs_7_), channel_id=1, source_target_pairs={{0,8},{8,0},{16,24},{24,16},{1,9},{9,1},{17,25},{25,17},{2,10},{10... | collective-permute-start | bytes 589832 | tf_op jit(solution)/shard_map/ppermute | solution.py:491
  13.4 6.4 %expert_forward.1.refs_4_ = bf16[8,16,4096]{2,1,0:T(8,128)(2,1)} custom-call(f32[6,1,32]{2,1,0:T(1,128)} %bitcast.16, bf16[128,768]{1,0:T(8,128)(2,1)} %get-tuple-element.16.hidden_hbm.refs_7_, bf16[768,4096]{1,0:T(8,128)(2,1)} %bitcast.8), custom_call_target="tpu_custom_call" | custom-call | flops 1024 | bytes 1024 | tf_op jit(solution)/shard_map/expert_forward/pallas_call | solution.py:220
  19.9 3.7 %all-to-all-start = ((bf16[8,16,4096]{2,1,0:T(8,128)(2,1)}), bf16[8,16,4096]{2,1,0:T(8,128)(2,1)S(1)}, u32[]{:S(2)}, u32[]{:S(2)}) async-start(bf16[8,16,4096]{2,1,0:T(8,128)(2,1)} %expert_forward.1.refs_4_), calls=%async_computation | async-start | bytes 2097152 | tf_op jit(solution)/shard_map/all_to_all | solution.py:515
  23.6 0.0 collective-permute-done.4.refs_6_.refs_9_
  23.6 0.0 collective-permute-done.3.refs_5_.refs_8_
  23.7 0.0 collective-permute-done.1.refs_2_
  23.7 0.0 collective-permute-done.2.refs_3_
  23.7 0.9 %sibling_rows.1 = bf16[4,4,16,1024]{3,2,1,0:T(8,128)(2,1)S(1)} custom-call(bf16[2,4,16,1024]{3,2,1,0:T(8,128)(2,1)} %get-tuple-element.19.refs_0_, bf16[2,4,16,1024]{3,2,1,0:T(8,128)(2,1)S(1)} %collective-permute-done.refs_1_, bf16[2,4,16,1024]{3,2,1,0:T(8,128)(2,1)S(1)} %collective-permute-done.1.refs_2_, ...), custom_call_target="tpu_custom_call" | custom-call | flops 1024 | bytes 1024 | tf_op jit(solution)/shard_map/sibling_rows/pallas_call | solution.py:257
  24.6 0.6 collective-permute-start.5
  25.2 1.5 %collective-permute-done.5.refs_4_.swapped = bf16[4,4,16,1024]{3,2,1,0:T(8,128)(2,1)S(1)} collective-permute-done((bf16[4,4,16,1024]{3,2,1,0:T(8,128)(2,1)S(1)}, bf16[4,4,16,1024]{3,2,1,0:T(8,128)(2,1)S(1)}, u32[]{:S(2)}, u32[]{:S(2)}) %collective-permute-start.5) | collective-permute-done | bytes 524320 | tf_op jit(solution)/shard_map/ppermute | solution.py:491
  26.7 2.2 %split.1 = (bf16[8,16,1024]{2,1,0:T(8,128)(2,1)}, bf16[8,16,1024]{2,1,0:T(8,128)(2,1)}, bf16[8,16,1024]{2,1,0:T(8,128)(2,1)}) custom-call(bf16[2,4,16,1024]{3,2,1,0:T(8,128)(2,1)} %get-tuple-element.19.refs_0_, bf16[2,4,16,1024]{3,2,1,0:T(8,128)(2,1)S(1)} %collective-permute-done.refs_1_, bf16[2,4,16,1024]{3,2,1,0:T(8,128)(2,1)S(1)} %collective-permute-done.1.refs_2_, ...), custom_call_target="tpu_custom_call" | custom-call | flops 1024 | bytes 1024 | tf_op jit(solution)/shard_map/split/pallas_call | solution.py:282
  28.9 0.4 collective-permute-start.7
  29.3 2.5 %collective-permute-start.8 = (bf16[8,16,1024]{2,1,0:T(8,128)(2,1)}, bf16[8,16,1024]{2,1,0:T(8,128)(2,1)S(1)}, u32[]{:S(2)}, u32[]{:S(2)}) collective-permute-start(bf16[8,16,1024]{2,1,0:T(8,128)(2,1)} %get-tuple-element.25), channel_id=1, source_target_pairs={{0,24},{8,16},{16,8},{24,0},{1,25},{9,17},{17,9},{25,1},{2,26},{10... | collective-permute-start | bytes 786440 | tf_op jit(solution)/shard_map/ppermute | solution.py:491
  31.8 0.7 %collective-permute-start.6 = (bf16[8,16,1024]{2,1,0:T(8,128)(2,1)}, bf16[8,16,1024]{2,1,0:T(8,128)(2,1)S(1)}, u32[]{:S(2)}, u32[]{:S(2)}) collective-permute-start(bf16[8,16,1024]{2,1,0:T(8,128)(2,1)} %get-tuple-element.23.tie_ref), channel_id=1, source_target_pairs={{0,8},{8,0},{16,24},{24,16},{1,9},{9,1},{17,25},{25,17},{2,10},{10... | collective-permute-start | bytes 786440 | tf_op jit(solution)/shard_map/ppermute | solution.py:491
  32.5 1.3 %collective-permute-start.9 = (bf16[128,768]{1,0:T(8,128)(2,1)S(1)}, bf16[128,768]{1,0:T(8,128)(2,1)}, u32[]{:S(2)}, u32[]{:S(2)}) collective-permute-start(bf16[128,768]{1,0:T(8,128)(2,1)S(1)} %collective-permute-done.4.refs_6_.refs_9_), channel_id=1, source_target_pairs={{0,8},{8,0},{16,24},{24,16},{1,9},{9,1},{17,25},{25,17},{2,10},{10... | collective-permute-start | bytes 589832 | tf_op jit(solution)/shard_map/ppermute | solution.py:491
  33.8 7.0 %expert_backward.1 = bf16[128,1536]{1,0:T(8,128)(2,1)} custom-call(f32[6,1,32]{2,1,0:T(1,128)} %bitcast.17, bf16[128,1536]{1,0:T(8,128)(2,1)} %bitcast.12, bf16[768,4096]{1,0:T(8,128)(2,1)} %bitcast.9, bf16[8,16,1024]{2,1,0:T(8,128)(2,1)} %get-tuple-element.23.tie_ref, bf16[4,4,16,1024]{3,2,1,0:T(8,128)(2,1)S(1)} %collective-permute-done.5.refs_4_.swapped, ...), custom_call_target="tpu_custom_call" | custom-call | flops 1024 | bytes 1024 | tf_op jit(solution)/shard_map/expert_backward/pallas_call | solution.py:358
  40.9 3.3 %combine.1 = (bf16[128,4096]{1,0:T(8,128)(2,1)}, f32[8,128]{1,0:T(8,128)}) custom-call(s32[8,128]{1,0:T(8,128)} %bitcast.15, f32[128,128]{1,0:T(8,128)} %get-tuple-element.15.own_hbm, bf16[128,4096]{1,0:T(8,128)(2,1)} %dout_hbm.3, bf16[8,16,4096]{2,1,0:T(8,128)(2,1)S(1)} %all-to-all-done.ret_ref), custom_call_target="tpu_custom_call" | custom-call | flops 1024 | bytes 1024 | tf_op jit(solution)/shard_map/combine/pallas_call | solution.py:421
  44.2 11.3 %collective-permute-done.9.refs_10_ = bf16[128,768]{1,0:T(8,128)(2,1)} collective-permute-done((bf16[128,768]{1,0:T(8,128)(2,1)S(1)}, bf16[128,768]{1,0:T(8,128)(2,1)}, u32[]{:S(2)}, u32[]{:S(2)}) %collective-permute-start.9) | collective-permute-done | bytes 196640 | tf_op jit(solution)/shard_map/ppermute | solution.py:491
  55.5 3.6 %weight_grad.1 = bf16[1024,768]{1,0:T(8,128)(2,1)} custom-call(f32[8,128]{1,0:T(8,128)} %get-tuple-element.18.tie_ref, bf16[4,4,16,1024]{3,2,1,0:T(8,128)(2,1)S(1)} %collective-permute-done.5.refs_4_.swapped, bf16[2,4,16,1024]{3,2,1,0:T(8,128)(2,1)} %get-tuple-element.19.refs_0_, bf16[2,4,16,1024]{3,2,1,0:T(8,128)(2,1)S(1)} %collective-permute-done.refs_1_, ...), custom_call_target="tpu_custom_call" | custom-call | flops 1024 | bytes 1024 | tf_op jit(solution)/shard_map/weight_grad/pallas_call | solution.py:471
  (5 shorter events, 0.0 us)
Async XLA Ops:
  4.3 19.4 %collective-permute-start = (bf16[2,4,16,1024]{3,2,1,0:T(8,128)(2,1)}, bf16[2,4,16,1024]{3,2,1,0:T(8,128)(2,1)S(1)}, u32[]{:S(2)}, u32[]{:S(2)}) collective-permute-start(bf16[2,4,16,1024]{3,2,1,0:T(8,128)(2,1)} %get-tuple-element.20), channel_id=1, source_target_pairs={{0,2},{1,3},{2,0},{3,1},{4,6},{5,7},{6,4},{7,5},{8,10},{9,11},{10,... | collective-permute-start | bytes 786440 | tf_op jit(solution)/shard_map/ppermute | solution.py:491
  7.3 16.4 %collective-permute-start.1 = (bf16[2,4,16,1024]{3,2,1,0:T(8,128)(2,1)}, bf16[2,4,16,1024]{3,2,1,0:T(8,128)(2,1)S(1)}, u32[]{:S(2)}, u32[]{:S(2)}) collective-permute-start(bf16[2,4,16,1024]{3,2,1,0:T(8,128)(2,1)} %get-tuple-element.21), channel_id=1, source_target_pairs={{0,4},{1,5},{2,6},{3,7},{4,0},{5,1},{6,2},{7,3},{8,12},{9,13},{10,... | collective-permute-start | bytes 786440 | tf_op jit(solution)/shard_map/ppermute | solution.py:491
  8.8 14.9 %collective-permute-start.2 = (bf16[2,4,16,1024]{3,2,1,0:T(8,128)(2,1)}, bf16[2,4,16,1024]{3,2,1,0:T(8,128)(2,1)S(1)}, u32[]{:S(2)}, u32[]{:S(2)}) collective-permute-start(bf16[2,4,16,1024]{3,2,1,0:T(8,128)(2,1)} %get-tuple-element.22), channel_id=1, source_target_pairs={{0,6},{1,7},{2,4},{3,5},{4,2},{5,3},{6,0},{7,1},{8,14},{9,15},{10,... | collective-permute-start | bytes 786440 | tf_op jit(solution)/shard_map/ppermute | solution.py:491
  8.8 14.8 %collective-permute-start.4 = (bf16[128,768]{1,0:T(8,128)(2,1)}, bf16[128,768]{1,0:T(8,128)(2,1)S(1)}, u32[]{:S(2)}, u32[]{:S(2)}) collective-permute-start(bf16[128,768]{1,0:T(8,128)(2,1)} %get-tuple-element.16.hidden_hbm.refs_7_), channel_id=1, source_target_pairs={{0,16},{8,24},{16,0},{24,8},{1,17},{9,25},{17,1},{25,9},{2,18},{10... | collective-permute-start | bytes 589832 | tf_op jit(solution)/shard_map/ppermute | solution.py:491
  11.9 11.8 %collective-permute-start.3 = (bf16[128,768]{1,0:T(8,128)(2,1)}, bf16[128,768]{1,0:T(8,128)(2,1)S(1)}, u32[]{:S(2)}, u32[]{:S(2)}) collective-permute-start(bf16[128,768]{1,0:T(8,128)(2,1)} %get-tuple-element.16.hidden_hbm.refs_7_), channel_id=1, source_target_pairs={{0,8},{8,0},{16,24},{24,16},{1,9},{9,1},{17,25},{25,17},{2,10},{10... | collective-permute-start | bytes 589832 | tf_op jit(solution)/shard_map/ppermute | solution.py:491
  19.9 21.0 %all-to-all-start = ((bf16[8,16,4096]{2,1,0:T(8,128)(2,1)}), bf16[8,16,4096]{2,1,0:T(8,128)(2,1)S(1)}, u32[]{:S(2)}, u32[]{:S(2)}) async-start(bf16[8,16,4096]{2,1,0:T(8,128)(2,1)} %expert_forward.1.refs_4_), calls=%async_computation | async-start | bytes 2097152 | tf_op jit(solution)/shard_map/all_to_all | solution.py:515
  24.6 2.1 %collective-permute-start.5 = (bf16[4,4,16,1024]{3,2,1,0:T(8,128)(2,1)S(1)}, bf16[4,4,16,1024]{3,2,1,0:T(8,128)(2,1)S(1)}, u32[]{:S(2)}, u32[]{:S(2)}) collective-permute-start(bf16[4,4,16,1024]{3,2,1,0:T(8,128)(2,1)S(1)} %sibling_rows.1), channel_id=1, source_target_pairs={{0,1},{1,0},{2,3},{3,2},{4,5},{5,4},{6,7},{7,6},{8,9},{9,8},{10,11... | collective-permute-start | bytes 1572872 | tf_op jit(solution)/shard_map/ppermute | solution.py:491
  28.9 26.6 %collective-permute-start.7 = (bf16[8,16,1024]{2,1,0:T(8,128)(2,1)}, bf16[8,16,1024]{2,1,0:T(8,128)(2,1)S(1)}, u32[]{:S(2)}, u32[]{:S(2)}) collective-permute-start(bf16[8,16,1024]{2,1,0:T(8,128)(2,1)} %get-tuple-element.24), channel_id=1, source_target_pairs={{0,16},{8,24},{16,0},{24,8},{1,17},{9,25},{17,1},{25,9},{2,18},{10... | collective-permute-start | bytes 786440 | tf_op jit(solution)/shard_map/ppermute | solution.py:491
  29.3 26.1 %collective-permute-start.8 = (bf16[8,16,1024]{2,1,0:T(8,128)(2,1)}, bf16[8,16,1024]{2,1,0:T(8,128)(2,1)S(1)}, u32[]{:S(2)}, u32[]{:S(2)}) collective-permute-start(bf16[8,16,1024]{2,1,0:T(8,128)(2,1)} %get-tuple-element.25), channel_id=1, source_target_pairs={{0,24},{8,16},{16,8},{24,0},{1,25},{9,17},{17,9},{25,1},{2,26},{10... | collective-permute-start | bytes 786440 | tf_op jit(solution)/shard_map/ppermute | solution.py:491
  31.8 23.7 %collective-permute-start.6 = (bf16[8,16,1024]{2,1,0:T(8,128)(2,1)}, bf16[8,16,1024]{2,1,0:T(8,128)(2,1)S(1)}, u32[]{:S(2)}, u32[]{:S(2)}) collective-permute-start(bf16[8,16,1024]{2,1,0:T(8,128)(2,1)} %get-tuple-element.23.tie_ref), channel_id=1, source_target_pairs={{0,8},{8,0},{16,24},{24,16},{1,9},{9,1},{17,25},{25,17},{2,10},{10... | collective-permute-start | bytes 786440 | tf_op jit(solution)/shard_map/ppermute | solution.py:491
  32.5 23.0 %collective-permute-start.9 = (bf16[128,768]{1,0:T(8,128)(2,1)S(1)}, bf16[128,768]{1,0:T(8,128)(2,1)}, u32[]{:S(2)}, u32[]{:S(2)}) collective-permute-start(bf16[128,768]{1,0:T(8,128)(2,1)S(1)} %collective-permute-done.4.refs_6_.refs_9_), channel_id=1, source_target_pairs={{0,8},{8,0},{16,24},{24,16},{1,9},{9,1},{17,25},{25,17},{2,10},{10... | collective-permute-start | bytes 589832 | tf_op jit(solution)/shard_map/ppermute | solution.py:491

commit v4 on v3

v4 whole, which is shorter than its diff:
```python
import functools

import jax
import jax.numpy as jnp
from jax import lax
from jax.experimental import pallas as pl
from jax.experimental.pallas import tpu as pltpu
from jax.sharding import PartitionSpec as P

QB = 128
CAP = 16
VMEM_LIMIT = 24 * 1024 * 1024

bf16 = jnp.bfloat16
f32 = jnp.float32

SMALL = pl.CostEstimate(flops=1024, bytes_accessed=1024, transcendentals=0)

VMEM = pl.BlockSpec(memory_space=pltpu.VMEM)
ANY = pl.BlockSpec(memory_space=pl.ANY)
HBM = pl.BlockSpec(memory_space=pltpu.HBM)


def params():
    return pltpu.CompilerParams(vmem_limit_bytes=VMEM_LIMIT)


def hbm(value):
    return pltpu.with_memory_space_constraint(value, pltpu.HBM)


def chunks(total, size):
    return [pl.ds(start, size) for start in range(0, total, size)]


def block_place(me, r, flight):
    half = flight // 2
    return me ^ (2 * (r % half) + r // half)


def dispatch_kernel(flight, groups, gate_up_hbm, cap_hbm, hot_hbm, ids_hbm, probs_hbm, dout_hbm, *refs):
    half = flight // 2
    own_hbm, hidden_ref, *chips = refs[: 2 + half]
    gate_up, cap_ref, hot_ref, ids_ref, probs_ref, dout, own_ref = refs[2 + half : 9 + half]
    gate_sems, own_sem, small_sems, in_sems = refs[9 + half :]
    topk, tokens = ids_ref.shape
    slots = flight * CAP
    me, group = lax.axis_index("expert"), lax.axis_index("dp")
    share = dout_hbm.shape[1] // groups
    small = [
        pltpu.make_async_copy(src, dst, small_sems.at[i])
        for i, (src, dst) in enumerate(
            [(ids_hbm, ids_ref), (probs_hbm, probs_ref), (cap_hbm, cap_ref), (hot_hbm, hot_ref)]
        )
    ]
    loads = [
        pltpu.make_async_copy(
            dout_hbm.at[:, pl.ds(pl.multiple_of((group ^ j) * share, share), share)],
            dout.at[j],
            in_sems.at[j],
        )
        for j in range(groups)
    ]
    gates = [
        pltpu.make_async_copy(
            gate_up_hbm.at[pl.ds(pl.multiple_of(block_place(me, r, flight) * CAP, CAP), CAP)],
            gate_up.at[pl.ds(r * CAP, CAP)],
            gate_sems.at[r],
        )
        for r in range(flight)
    ]
    for copy in small + loads + gates:
        copy.start()
    for copy in small:
        copy.wait()
    row = lax.broadcasted_iota(jnp.int32, (slots, 1), 0)
    row_expert = block_place(me, row // CAP, flight)
    row_rank = (row % CAP).astype(f32)
    limit = jnp.zeros((slots, 1), jnp.int32)
    for e in range(flight):
        hot = hot_ref[0, 0] == e
        for h in range(1, hot_ref.shape[1]):
            hot = jnp.logical_or(hot, hot_ref[0, h] == e)
        limit = jnp.where(row_expert == e, jnp.where(hot, CAP, cap_ref[e]), limit)
    limit = limit.astype(f32)
    named = jnp.zeros((slots, tokens), f32)
    weight = jnp.zeros((slots, tokens), f32)
    for k in range(topk):
        hit = ids_ref[k : k + 1, :] == row_expert
        named = jnp.where(hit, 1.0, named)
        weight = jnp.where(hit, probs_ref[k : k + 1, :], weight)
    first = lax.broadcasted_iota(jnp.int32, (tokens, tokens), 0)
    second = lax.broadcasted_iota(jnp.int32, (tokens, tokens), 1)
    before = (first < second).astype(f32).astype(bf16)
    rank = jnp.dot(named.astype(bf16), before, preferred_element_type=f32)
    owns = (named > 0.0) & (rank == row_rank) & (rank < limit)
    own_weight = jnp.where(owns, weight, 0.0)
    own_ref[...] = own_weight
    own_copy = pltpu.make_async_copy(own_ref, own_hbm, own_sem)
    own_copy.start()
    owner = jnp.where(owns, 1.0, 0.0).astype(bf16)
    slot_weight = jnp.sum(own_weight, axis=1, keepdims=True)
    for copy in loads:
        copy.wait()
    for j in range(groups):
        part = jnp.dot(owner, dout[j], preferred_element_type=f32)
        part = (part * slot_weight).astype(bf16)
        for r in range(flight):
            chips[r % half][r // half, j] = part[r * CAP : (r + 1) * CAP, :]
    for copy in gates:
        copy.wait()
    hid = hidden_ref.shape[1]
    gate = gate_up[:, :hid].astype(f32)
    up = gate_up[:, hid:].astype(f32)
    hidden_ref[...] = (gate * jax.nn.sigmoid(gate) * up).astype(bf16)
    own_copy.wait()


def dispatch(gate_up, capacity, hot_row, ids, probs, d_out, flight, groups):
    tokens, width = d_out.shape
    rows, double = gate_up.shape
    slots = flight * CAP
    share = width // groups
    half = flight // 2
    return pl.pallas_call(
        functools.partial(dispatch_kernel, flight, groups),
        out_shape=(pltpu.HBM((slots, tokens), f32), pltpu.VMEM((rows, double // 2), bf16))
        + (pltpu.VMEM((2, groups, CAP, share), bf16),) * half,
        in_specs=[HBM] * 6,
        out_specs=(HBM, VMEM) + (VMEM,) * half,
        scratch_shapes=[
            pltpu.VMEM((rows, double), bf16),
            pltpu.SMEM(capacity.shape, jnp.int32),
            pltpu.SMEM(hot_row.shape, jnp.int32),
            pltpu.VMEM(ids.shape, jnp.int32),
            pltpu.VMEM(probs.shape, f32),
            pltpu.VMEM((groups, tokens, share), bf16),
            pltpu.VMEM((slots, tokens), f32),
            pltpu.SemaphoreType.DMA((flight,)),
            pltpu.SemaphoreType.DMA,
            pltpu.SemaphoreType.DMA((4,)),
            pltpu.SemaphoreType.DMA((groups,)),
        ],
        compiler_params=params(),
        cost_estimate=SMALL,
        name="dispatch",
    )(hbm(gate_up), hbm(capacity), hbm(hot_row), hbm(ids), hbm(probs), hbm(d_out))


def forward_kernel(
    flight, block, hidden_ref, scale_hbm, quant_hbm, out_hbm,
    scale, hidden, quant, out, scale_sem, in_sems, out_sems
):
    steps, hid, _ = quant.shape
    me = lax.axis_index("expert")
    loads = [
        pltpu.make_async_copy(quant_hbm.at[:, pl.ds(c * block, block)], quant.at[c], in_sems.at[c])
        for c in range(steps)
    ]
    small = pltpu.make_async_copy(scale_hbm, scale, scale_sem)
    for copy in [small] + loads:
        copy.start()
    for r in range(flight):
        place = pl.multiple_of(block_place(me, r, flight) * CAP, CAP)
        hidden[pl.ds(place, CAP), :] = hidden_ref[pl.ds(r * CAP, CAP), :]
    small.wait()
    stores = []
    for c in range(steps):
        cols = pl.ds(c * block, block)
        loads[c].wait()
        total = [None] * (block // QB)
        for i in range(hid // QB):
            part = jnp.dot(
                hidden[:, i * QB : (i + 1) * QB],
                quant[c, i * QB : (i + 1) * QB, :],
                preferred_element_type=f32,
            )
            for j in range(block // QB):
                scaled = part[:, j * QB : (j + 1) * QB] * scale[i, 0, c * (block // QB) + j]
                total[j] = scaled if i == 0 else total[j] + scaled
        for j in range(block // QB):
            at = pl.ds(c * block + j * QB, QB)
            out[:, :, at] = total[j].astype(bf16).reshape(flight, CAP, QB)
        stores.append(
            pltpu.make_async_copy(out.at[:, :, cols], out_hbm.at[:, :, cols], out_sems.at[c])
        )
        stores[c].start()
    for copy in stores:
        copy.wait()


def forward(scale, hidden, quant, flight, block=512):
    hid, width = quant.shape
    steps = width // block
    return pl.pallas_call(
        functools.partial(forward_kernel, flight, block),
        out_shape=pltpu.HBM((flight, CAP, width), bf16),
        in_specs=[VMEM, HBM, HBM],
        out_specs=HBM,
        scratch_shapes=[
            pltpu.SMEM(scale.shape, f32),
            pltpu.VMEM(hidden.shape, bf16),
            pltpu.VMEM((steps, hid, block), bf16),
            pltpu.VMEM((flight, CAP, width), bf16),
            pltpu.SemaphoreType.DMA,
            pltpu.SemaphoreType.DMA((steps,)),
            pltpu.SemaphoreType.DMA((steps,)),
        ],
        compiler_params=params(),
        cost_estimate=SMALL,
        name="expert_forward",
    )(hidden, hbm(scale), hbm(quant))


def sibling_kernel(half, *refs):
    chips, out_ref = refs[:half], refs[-1]
    for c in range(half):
        out_ref[c] = chips[c][1]


def sibling_rows(chips, ties):
    half = len(chips)
    return pl.pallas_call(
        functools.partial(sibling_kernel, half),
        out_shape=pltpu.VMEM((half,) + chips[0].shape[1:], bf16),
        in_specs=[VMEM] * half + [ANY] * len(ties),
        out_specs=VMEM,
        compiler_params=params(),
        cost_estimate=SMALL,
        name="sibling_rows",
    )(*chips, *ties)


def split_kernel(half, groups, *refs):
    chips, swapped, pieces = refs[:half], refs[half], refs[half + 1 :]
    for j in range(1, groups):
        for c in range(half):
            pieces[j - 1][c] = chips[c][0, j]
            pieces[j - 1][half + c] = swapped[c, j]


def split(chips, swapped):
    half, groups, cap, share = swapped.shape
    return pl.pallas_call(
        functools.partial(split_kernel, half, groups),
        out_shape=(pltpu.VMEM((2 * half, cap, share), bf16),) * (groups - 1),
        in_specs=[VMEM] * (half + 1),
        out_specs=(VMEM,) * (groups - 1),
        compiler_params=params(),
        cost_estimate=SMALL,
        name="split",
    )(*chips, swapped)


def backward_kernel(flight, groups, scale_hbm, gate_up_hbm, quant_hbm, tie_ref, swapped, *refs):
    half = flight // 2
    chips, out_hbm = refs[:half], refs[half]
    scale, gate_up, rows, quant, acc, out = refs[half + 1 : half + 7]
    scale_sem, gate_sems, in_sems, out_sems = refs[half + 7 :]
    me, group = lax.axis_index("expert"), lax.axis_index("dp")
    slots, hid = acc.shape
    share = quant.shape[2]

    def place(r):
        return pl.ds(pl.multiple_of(block_place(me, r, flight) * CAP, CAP), CAP)

    loads = [
        pltpu.make_async_copy(
            quant_hbm.at[:, pl.ds(pl.multiple_of((group ^ j) * share, share), share)],
            quant.at[j],
            in_sems.at[j],
        )
        for j in range(groups)
    ]
    gates = [
        pltpu.make_async_copy(
            gate_up_hbm.at[place(r)], gate_up.at[pl.ds(r * CAP, CAP)], gate_sems.at[r]
        )
        for r in range(flight)
    ]
    small = pltpu.make_async_copy(scale_hbm, scale, scale_sem)
    for copy in [small] + loads + gates:
        copy.start()
    for c in range(half):
        rows[:, c * CAP : (c + 1) * CAP, :] = chips[c][0]
        rows[:, (half + c) * CAP : (half + c + 1) * CAP, :] = swapped[c]
    small.wait()
    for j in range(groups):
        loads[j].wait()
        for b in range(share // QB):
            cols = slice(b * QB, (b + 1) * QB)
            part = lax.dot_general(
                rows[j, :, cols],
                quant[j, :, cols],
                (((1,), (1,)), ((), ())),
                preferred_element_type=f32,
            )
            for i in range(hid // QB):
                at = (slice(None), slice(i * QB, (i + 1) * QB))
                scaled = part[at] * scale[i, 0, (group ^ j) * (share // QB) + b]
                if j == 0 and b == 0:
                    acc[at] = scaled
                else:
                    acc[at] += scaled
    for copy in gates:
        copy.wait()
    gate = gate_up[:, :hid].astype(f32)
    up = gate_up[:, hid:].astype(f32)
    sig = jax.nn.sigmoid(gate)
    d_hidden = acc[...]
    out[:, :hid] = (d_hidden * up * sig * (1.0 + gate * (1.0 - sig))).astype(bf16)
    out[:, hid:] = (d_hidden * (gate * sig)).astype(bf16)
    stores = [
        pltpu.make_async_copy(out.at[pl.ds(r * CAP, CAP)], out_hbm.at[place(r)], out_sems.at[r])
        for r in range(flight)
    ]
    for copy in stores:
        copy.start()
    for copy in stores:
        copy.wait()


def backward(scale, gate_up, quant, tie, chips, swapped):
    slots, double = gate_up.shape
    hid, width = quant.shape
    half, groups, cap, share = swapped.shape
    flight = 2 * half
    return pl.pallas_call(
        functools.partial(backward_kernel, flight, groups),
        out_shape=pltpu.HBM((slots, double), bf16),
        in_specs=[HBM, HBM, HBM, ANY] + [VMEM] * (1 + half),
        out_specs=HBM,
        scratch_shapes=[
            pltpu.SMEM(scale.shape, f32),
            pltpu.VMEM((slots, double), bf16),
            pltpu.VMEM((groups, slots, share), bf16),
            pltpu.VMEM((groups, hid, share), bf16),
            pltpu.VMEM((slots, hid), f32),
            pltpu.VMEM((slots, double), bf16),
            pltpu.SemaphoreType.DMA,
            pltpu.SemaphoreType.DMA((flight,)),
            pltpu.SemaphoreType.DMA((groups,)),
            pltpu.SemaphoreType.DMA((flight,)),
        ],
        compiler_params=params(),
        cost_estimate=SMALL,
        name="expert_backward",
    )(hbm(scale), hbm(gate_up), hbm(quant), tie, swapped, *chips)


def combine_kernel(
    block, ids_hbm, own_hbm, dout_hbm, ret_ref, out_ref, dprobs_ref, ids_ref, own_ref, dout, sems
):
    copies = [
        pltpu.make_async_copy(ids_hbm, ids_ref, sems.at[0]),
        pltpu.make_async_copy(own_hbm, own_ref, sems.at[1]),
        pltpu.make_async_copy(dout_hbm, dout, sems.at[2]),
    ]
    for copy in copies:
        copy.start()
    topk, tokens = ids_ref.shape
    slots = own_ref.shape[0]
    width = dout.shape[1]
    flight = slots // CAP
    me = lax.axis_index("expert")
    copies[1].wait()
    own = own_ref[...]
    turned = own.T
    high = turned.astype(bf16)
    low = (turned - high.astype(f32)).astype(bf16)
    total = jnp.zeros((slots, tokens), f32)
    copies[0].wait()
    copies[2].wait()
    for cols in chunks(width, block):
        here = jnp.concatenate(
            [ret_ref[block_place(me, r, flight), :, cols] for r in range(flight)], axis=0
        )
        out = jnp.dot(high, here, preferred_element_type=f32)
        out = out + jnp.dot(low, here, preferred_element_type=f32)
        out_ref[:, cols] = out.astype(bf16)
        total = total + lax.dot_general(
            here, dout[:, cols], (((1,), (1,)), ((), ())), preferred_element_type=f32
        )
    inner = jnp.where(own > 0.0, total, 0.0)
    row_expert = block_place(me, lax.broadcasted_iota(jnp.int32, (slots, 1), 0) // CAP, flight)
    for k in range(topk):
        mine = jnp.where(ids_ref[k : k + 1, :] == row_expert, inner, 0.0)
        dprobs_ref[k : k + 1, :] = jnp.sum(mine, axis=0, keepdims=True)


def combine(ids, own, d_out, returned, block=1024):
    tokens, width = d_out.shape
    return pl.pallas_call(
        functools.partial(combine_kernel, block),
        out_shape=(
            pltpu.HBM((tokens, width), bf16),
            pltpu.HBM(ids.shape, f32),
        ),
        in_specs=[HBM, HBM, HBM, VMEM],
        out_specs=(VMEM, VMEM),
        scratch_shapes=[
            pltpu.VMEM(ids.shape, jnp.int32),
            pltpu.VMEM(own.shape, f32),
            pltpu.VMEM((tokens, width), bf16),
            pltpu.SemaphoreType.DMA((3,)),
        ],
        compiler_params=params(),
        cost_estimate=SMALL,
        name="combine",
    )(hbm(ids), hbm(own), hbm(d_out), returned)


def weight_grad_kernel(half, groups, block, tie_ref, swapped, *refs):
    chips, parts = refs[:half], refs[half : half + groups - 1]
    hid_refs = refs[half + groups - 1 : half + 2 * groups - 1]
    out_hbm, hidden, out, out_sems = refs[half + 2 * groups - 1 :]
    cap, share = parts[0].shape[1:]
    slots = 2 * half * cap
    for j in range(groups):
        hidden[j * slots : (j + 1) * slots, :] = hid_refs[j][...]
    stores = []
    for n, cols in enumerate(chunks(share, block)):
        grads = [chips[c][0, 0, :, cols] for c in range(half)]
        grads += [swapped[c, 0, :, cols] for c in range(half)]
        grads += [part[:, :, cols].reshape(slots, block) for part in parts]
        out[cols, :] = lax.dot_general(
            jnp.concatenate(grads, axis=0),
            hidden[...],
            (((0,), (0,)), ((), ())),
            preferred_element_type=f32,
        ).astype(bf16)
        stores.append(pltpu.make_async_copy(out.at[cols], out_hbm.at[cols], out_sems.at[n]))
        stores[n].start()
    for copy in stores:
        copy.wait()


def weight_grad(tie, chips, swapped, parts, hiddens, block=256):
    half, groups, cap, share = swapped.shape
    slots, hid = hiddens[0].shape
    return pl.pallas_call(
        functools.partial(weight_grad_kernel, half, groups, block),
        out_shape=pltpu.HBM((share, hid), bf16),
        in_specs=[HBM] + [VMEM] * (half + 2 * groups),
        out_specs=HBM,
        scratch_shapes=[
            pltpu.VMEM((groups * slots, hid), bf16),
            pltpu.VMEM((share, hid), bf16),
            pltpu.SemaphoreType.DMA((share // block,)),
        ],
        compiler_params=params(),
        cost_estimate=SMALL,
        name="weight_grad",
    )(hbm(tie), swapped, *chips, *parts, *hiddens)


def swap(value, axis, j):
    size = lax.axis_size(axis)
    return lax.ppermute(value, axis, [(i, i ^ j) for i in range(size)])


def shards(route_ids, route_probs, capacity, hot_lists, gate_up, w_quant, w_scale, d_out):
    flight = lax.axis_size("expert")
    groups = lax.axis_size("dp")
    gate_up = gate_up[0, 0]
    ids, probs = route_ids.T, route_probs.T
    scale = w_scale.transpose(1, 0, 2)
    own, hidden, *chips = dispatch(
        gate_up, capacity, hot_lists, ids, probs, d_out, flight, groups
    )
    chips = chips[:1] + [swap(chips[c], "expert", 2 * c) for c in range(1, flight // 2)]
    hiddens, late = {0: hidden}, set()
    bit = groups // 2
    while bit:
        for j in sorted(hiddens):
            hiddens[j ^ bit] = swap(hiddens[j], "dp", bit)
            if j:
                late.add(j ^ bit)
        bit //= 2
    early = [hiddens[j] for j in range(1, groups) if j not in late]
    hiddens = [hiddens[j] for j in range(groups)]
    expert_out = forward(scale, hidden, w_quant[0], flight)
    returned = lax.all_to_all(expert_out, "expert", split_axis=0, concat_axis=0, tiled=True)
    swapped = swap(sibling_rows(chips, [hbm(expert_out)] + early), "expert", 1)
    pieces = split(chips, swapped)
    parts = [swap(pieces[j - 1], "dp", j) for j in range(1, groups)]
    d_gate_up = backward(scale, gate_up, w_quant[0], pieces[0], chips, swapped)
    combined, d_probs = combine(ids, own, d_out, returned)
    d_weight = weight_grad(d_probs, chips, swapped, parts, hiddens)
    return (combined, d_probs.T, d_gate_up[None, None], d_weight[None])


def solution(mesh):
    placed = (
        P(("dp", "expert"), None),
        P(("dp", "expert"), None),
        P(),
        P("dp", None),
        P("dp", "expert", None, None),
        P("expert", None, None),
        P("expert", None, None),
        P(("dp", "expert"), None),
    )
    return jax.shard_map(
        shards,
        mesh=mesh,
        in_specs=placed,
        out_specs=(
            P(("dp", "expert"), None),
            P(("dp", "expert"), None),
            P("dp", "expert", None, None),
            P("expert", "dp", None),
        ),
        check_vma=False,
    )
```

time: 59.5 us -> 53.2 us (0.89)
  Pallas kernels: 27.1 us -> 19.3 us
  waiting for transfers between devices: 12.9 us -> 14.6 us
    all_to_all x1, waiting for transfers between devices: 0.01 us -> 2.17 us  [shards(): lax.all_to_all(expert_out, 'expert', split_axis=0, concat_axis=0, tiled=T...]
    pallas_call x1, Pallas kernels: 7.04 us -> 5.25 us  [backward(): pl.pallas_call(functools.partial(backward_kernel, flight, groups), out_sh...]
    pallas_call x1, Pallas kernels: 6.44 us -> 4.79 us  [forward(): pl.pallas_call(functools.partial(forward_kernel, flight, block), out_shap...]
    pallas_call x1, Pallas kernels: 3.63 us -> 2.09 us  [dispatch(): pl.pallas_call(functools.partial(dispatch_kernel, flight, groups), out_sh...]
    pallas_call x1, Pallas kernels: 2.17 us -> 0.93 us  [split(): pl.pallas_call(functools.partial(split_kernel, half, groups), out_shape=(...]
    pallas_call x1, Pallas kernels: 0.95 us -> 0.04 us  [sibling_rows(): pl.pallas_call(functools.partial(sibling_kernel, half), out_shape=pltpu.V...]
    pallas_call x1, Pallas kernels: 3.58 us -> 2.89 us  [weight_grad(): pl.pallas_call(functools.partial(weight_grad_kernel, half, groups, block)...]
  transfers between devices with their start and end apart: 11 -> 11, of which waited for: 2 -> 3; matrix products, arithmetic and copies ran while one was open for 0% -> 0% of each run, Pallas kernels for 34% -> 27%
where the time goes in v4:
time: 53.2 us; the launch traced here: 53 us
  Pallas kernels  19.3 us (36%)
  starting transfers between devices  18.3 us (34%)
  waiting for transfers between devices  14.6 us (27%)
  between operations  0.72 us (1%)
    ppermute x10, starting transfers between devices, swap(): return lax.ppermute(value, axis, [(i, i ^ j) for i in range(size)])  14.6 us
    ppermute x10, waiting for transfers between devices, swap(): return lax.ppermute(value, axis, [(i, i ^ j) for i in range(size)])  12.5 us
    pallas_call x1, Pallas kernels, backward(): pl.pallas_call(functools.partial(backward_kernel, flight, groups), out_sh...  5.25 us
    pallas_call x1, Pallas kernels, forward(): pl.pallas_call(functools.partial(forward_kernel, flight, block), out_shap...  4.79 us
    all_to_all x1, starting transfers between devices, shards(): lax.all_to_all(expert_out, 'expert', split_axis=0, concat_axis=0, tiled=T...  3.73 us
    pallas_call x1, Pallas kernels, combine(): pl.pallas_call(functools.partial(combine_kernel, block), out_shape=(pltpu...  3.29 us
    pallas_call x1, Pallas kernels, weight_grad(): pl.pallas_call(functools.partial(weight_grad_kernel, half, groups, block)...  2.89 us
    all_to_all x1, waiting for transfers between devices, shards(): lax.all_to_all(expert_out, 'expert', split_axis=0, concat_axis=0, tiled=T...  2.17 us
  transfers between devices with their start and end apart: 11, of which 3 were waited for; matrix products, arithmetic and copies ran while one was open for 0% of the time, Pallas kernels for 27%

profile of v4, /device:TPU:0, one launch (start us, length us, event | category | flops | bytes accessed | tf_op | source)
XLA Modules:
  0.0 53.0 jit_solution(2390381064409721392)
XLA Ops:
  0.6 2.1 %dispatch.1 = (f32[128,128]{1,0:T(8,128)}, bf16[128,768]{1,0:T(8,128)(2,1)S(1)}, bf16[2,4,16,1024]{3,2,1,0:T(8,128)(2,1)S(1)}, bf16[2,4,16,1024]{3,2,1,0:T(8,128...) custom-call(bf16[128,1536]{1,0:T(8,128)(2,1)} %bitcast.11, s32[8]{0:T(128)} %cap_hbm.1, ...), custom_call_target="tpu_custom_call" | custom-call | flops 1024 | bytes 1024 | tf_op jit(solution)/shard_map/dispatch/pallas_call | solution.py:125
  2.7 3.0 %collective-permute-start = (bf16[2,4,16,1024]{3,2,1,0:T(8,128)(2,1)S(1)}, bf16[2,4,16,1024]{3,2,1,0:T(8,128)(2,1)S(1)}, u32[]{:S(2)}, u32[]{:S(2)}) collective-permute-start(bf16[2,4,16,1024]{3,2,1,0:T(8,128)(2,1)S(1)} %get-tuple-element.20), channel_id=1, source_target_pairs={{0,2},{1,3},{2,0},{3,1},{4,6},{5,7},{6,4},{7,5},{8,10},{9,11},{10,... | collective-permute-start | bytes 786440 | tf_op jit(solution)/shard_map/ppermute | solution.py:459
  5.7 1.5 %collective-permute-start.1 = (bf16[2,4,16,1024]{3,2,1,0:T(8,128)(2,1)S(1)}, bf16[2,4,16,1024]{3,2,1,0:T(8,128)(2,1)S(1)}, u32[]{:S(2)}, u32[]{:S(2)}) collective-permute-start(bf16[2,4,16,1024]{3,2,1,0:T(8,128)(2,1)S(1)} %get-tuple-element.21), channel_id=1, source_target_pairs={{0,4},{1,5},{2,6},{3,7},{4,0},{5,1},{6,2},{7,3},{8,12},{9,13},{10,... | collective-permute-start | bytes 786440 | tf_op jit(solution)/shard_map/ppermute | solution.py:459
  7.2 0.0 collective-permute-start.2
  7.3 3.0 %collective-permute-start.4 = (bf16[128,768]{1,0:T(8,128)(2,1)S(1)}, bf16[128,768]{1,0:T(8,128)(2,1)S(1)}, u32[]{:S(2)}, u32[]{:S(2)}) collective-permute-start(bf16[128,768]{1,0:T(8,128)(2,1)S(1)} %get-tuple-element.16.hidden_ref.refs_7_), channel_id=1, source_target_pairs={{0,16},{8,24},{16,0},{24,8},{1,17},{9,25},{17,1},{25,9},{2,18},{10... | collective-permute-start | bytes 589832 | tf_op jit(solution)/shard_map/ppermute | solution.py:459
  10.3 1.6 %collective-permute-start.3 = (bf16[128,768]{1,0:T(8,128)(2,1)S(1)}, bf16[128,768]{1,0:T(8,128)(2,1)S(1)}, u32[]{:S(2)}, u32[]{:S(2)}) collective-permute-start(bf16[128,768]{1,0:T(8,128)(2,1)S(1)} %get-tuple-element.16.hidden_ref.refs_7_), channel_id=1, source_target_pairs={{0,8},{8,0},{16,24},{24,16},{1,9},{9,1},{17,25},{25,17},{2,10},{10... | collective-permute-start | bytes 589832 | tf_op jit(solution)/shard_map/ppermute | solution.py:459
  11.9 4.8 %expert_forward.1.refs_4_ = bf16[8,16,4096]{2,1,0:T(8,128)(2,1)} custom-call(bf16[128,768]{1,0:T(8,128)(2,1)S(1)} %get-tuple-element.16.hidden_ref.refs_7_, f32[6,1,32]{2,1,0:T(1,128)} %bitcast.16, bf16[768,4096]{1,0:T(8,128)(2,1)} %bitcast.8), custom_call_target="tpu_custom_call" | custom-call | flops 1024 | bytes 1024 | tf_op jit(solution)/shard_map/expert_forward/pallas_call | solution.py:195
  16.7 3.7 %all-to-all-start = ((bf16[8,16,4096]{2,1,0:T(8,128)(2,1)}), bf16[8,16,4096]{2,1,0:T(8,128)(2,1)S(1)}, u32[]{:S(2)}, u32[]{:S(2)}) async-start(bf16[8,16,4096]{2,1,0:T(8,128)(2,1)} %expert_forward.1.refs_4_), calls=%async_computation | async-start | bytes 2097152 | tf_op jit(solution)/shard_map/all_to_all | solution.py:483
  20.4 0.0 collective-permute-done.4.refs_6_.refs_9_
  20.4 0.0 collective-permute-done.1.refs_2_
  20.5 0.0 collective-permute-done.2.refs_3_
  20.5 0.6 %collective-permute-start.5 = (bf16[4,4,16,1024]{3,2,1,0:T(8,128)(2,1)S(1)}, bf16[4,4,16,1024]{3,2,1,0:T(8,128)(2,1)S(1)}, u32[]{:S(2)}, u32[]{:S(2)}) collective-permute-start(bf16[4,4,16,1024]{3,2,1,0:T(8,128)(2,1)S(1)} %sibling_rows.1), channel_id=1, source_target_pairs={{0,1},{1,0},{2,3},{3,2},{4,5},{5,4},{6,7},{7,6},{8,9},{9,8},{10,11... | collective-permute-start | bytes 1572872 | tf_op jit(solution)/shard_map/ppermute | solution.py:459
  21.1 1.5 %collective-permute-done.5.refs_4_.swapped = bf16[4,4,16,1024]{3,2,1,0:T(8,128)(2,1)S(1)} collective-permute-done((bf16[4,4,16,1024]{3,2,1,0:T(8,128)(2,1)S(1)}, bf16[4,4,16,1024]{3,2,1,0:T(8,128)(2,1)S(1)}, u32[]{:S(2)}, u32[]{:S(2)}) %collective-permute-start.5) | collective-permute-done | bytes 524320 | tf_op jit(solution)/shard_map/ppermute | solution.py:459
  22.6 0.9 %split.1 = (bf16[8,16,1024]{2,1,0:T(8,128)(2,1)}, bf16[8,16,1024]{2,1,0:T(8,128)(2,1)}, bf16[8,16,1024]{2,1,0:T(8,128)(2,1)}) custom-call(bf16[2,4,16,1024]{3,2,1,0:T(8,128)(2,1)S(1)} %get-tuple-element.19.refs_0_, bf16[2,4,16,1024]{3,2,1,0:T(8,128)(2,1)S(1)} %collective-permute-done.refs_1_, bf16[2,4,16,1024]{3,2,1,0:T(8,128)(2,1)S(1)} %collective-permute-done.1.refs_2_, ...), custom_call_target="tpu_custom_call" | custom-call | flops 1024 | bytes 1024 | tf_op jit(solution)/shard_map/split/pallas_call | solution.py:244
  23.5 1.1 %collective-permute-start.7 = (bf16[8,16,1024]{2,1,0:T(8,128)(2,1)}, bf16[8,16,1024]{2,1,0:T(8,128)(2,1)S(1)}, u32[]{:S(2)}, u32[]{:S(2)}) collective-permute-start(bf16[8,16,1024]{2,1,0:T(8,128)(2,1)} %get-tuple-element.24), channel_id=1, source_target_pairs={{0,16},{8,24},{16,0},{24,8},{1,17},{9,25},{17,1},{25,9},{2,18},{10... | collective-permute-start | bytes 786440 | tf_op jit(solution)/shard_map/ppermute | solution.py:459
  24.7 1.7 %collective-permute-start.8 = (bf16[8,16,1024]{2,1,0:T(8,128)(2,1)}, bf16[8,16,1024]{2,1,0:T(8,128)(2,1)}, u32[]{:S(2)}, u32[]{:S(2)}) collective-permute-start(bf16[8,16,1024]{2,1,0:T(8,128)(2,1)} %get-tuple-element.25), channel_id=1, source_target_pairs={{0,24},{8,16},{16,8},{24,0},{1,25},{9,17},{17,9},{25,1},{2,26},{10... | collective-permute-start | bytes 786440 | tf_op jit(solution)/shard_map/ppermute | solution.py:459
  26.4 0.7 %collective-permute-start.6 = (bf16[8,16,1024]{2,1,0:T(8,128)(2,1)}, bf16[8,16,1024]{2,1,0:T(8,128)(2,1)}, u32[]{:S(2)}, u32[]{:S(2)}) collective-permute-start(bf16[8,16,1024]{2,1,0:T(8,128)(2,1)} %get-tuple-element.23.tie_ref), channel_id=1, source_target_pairs={{0,8},{8,0},{16,24},{24,16},{1,9},{9,1},{17,25},{25,17},{2,10},{10... | collective-permute-start | bytes 786440 | tf_op jit(solution)/shard_map/ppermute | solution.py:459
  27.0 1.3 %collective-permute-start.9 = (bf16[128,768]{1,0:T(8,128)(2,1)S(1)}, bf16[128,768]{1,0:T(8,128)(2,1)}, u32[]{:S(2)}, u32[]{:S(2)}) collective-permute-start(bf16[128,768]{1,0:T(8,128)(2,1)S(1)} %collective-permute-done.4.refs_6_.refs_9_), channel_id=1, source_target_pairs={{0,8},{8,0},{16,24},{24,16},{1,9},{9,1},{17,25},{25,17},{2,10},{10... | collective-permute-start | bytes 589832 | tf_op jit(solution)/shard_map/ppermute | solution.py:459
  28.4 5.3 %expert_backward.1 = bf16[128,1536]{1,0:T(8,128)(2,1)} custom-call(f32[6,1,32]{2,1,0:T(1,128)} %bitcast.17, bf16[128,1536]{1,0:T(8,128)(2,1)} %bitcast.12, bf16[768,4096]{1,0:T(8,128)(2,1)} %bitcast.9, bf16[8,16,1024]{2,1,0:T(8,128)(2,1)} %get-tuple-element.23.tie_ref, bf16[4,4,16,1024]{3,2,1,0:T(8,128)(2,1)S(1)} %collective-permute-done.5.refs_4_.swapped, ...), custom_call_target="tpu_custom_call" | custom-call | flops 1024 | bytes 1024 | tf_op jit(solution)/shard_map/expert_backward/pallas_call | solution.py:328
  33.7 2.2 %all-to-all-done.ret_ref = bf16[8,16,4096]{2,1,0:T(8,128)(2,1)S(1)} async-done(((bf16[8,16,4096]{2,1,0:T(8,128)(2,1)}), bf16[8,16,4096]{2,1,0:T(8,128)(2,1)S(1)}, u32[]{:S(2)}, u32[]{:S(2)}) %all-to-all-start) | async-done | bytes 1048608 | tf_op jit(solution)/shard_map/all_to_all | solution.py:483
  35.8 3.3 %combine.1 = (bf16[128,4096]{1,0:T(8,128)(2,1)}, f32[8,128]{1,0:T(8,128)}) custom-call(s32[8,128]{1,0:T(8,128)} %bitcast.15, f32[128,128]{1,0:T(8,128)} %get-tuple-element.15.own_hbm, bf16[128,4096]{1,0:T(8,128)(2,1)} %dout_hbm.3, bf16[8,16,4096]{2,1,0:T(8,128)(2,1)S(1)} %all-to-all-done.ret_ref), custom_call_target="tpu_custom_call" | custom-call | flops 1024 | bytes 1024 | tf_op jit(solution)/shard_map/combine/pallas_call | solution.py:393
  39.1 10.9 %collective-permute-done.9.refs_10_ = bf16[128,768]{1,0:T(8,128)(2,1)} collective-permute-done((bf16[128,768]{1,0:T(8,128)(2,1)S(1)}, bf16[128,768]{1,0:T(8,128)(2,1)}, u32[]{:S(2)}, u32[]{:S(2)}) %collective-permute-start.9) | collective-permute-done | bytes 196640 | tf_op jit(solution)/shard_map/ppermute | solution.py:459
  50.0 0.0 collective-permute-done.7.refs_5_
  50.1 2.9 %weight_grad.1 = bf16[1024,768]{1,0:T(8,128)(2,1)} custom-call(f32[8,128]{1,0:T(8,128)} %get-tuple-element.18.tie_ref, bf16[4,4,16,1024]{3,2,1,0:T(8,128)(2,1)S(1)} %collective-permute-done.5.refs_4_.swapped, bf16[2,4,16,1024]{3,2,1,0:T(8,128)(2,1)S(1)} %get-tuple-element.19.refs_0_, bf16[2,4,16,1024]{3,2,1,0:T(8,128)(2,1)S(1)} %collective-permute-done.refs_1_, ...), custom_call_target="tpu_custom_call" | custom-call | flops 1024 | bytes 1024 | tf_op jit(solution)/shard_map/weight_grad/pallas_call | solution.py:441
  (5 shorter events, 0.0 us)
Async XLA Ops:
  2.7 17.7 %collective-permute-start = (bf16[2,4,16,1024]{3,2,1,0:T(8,128)(2,1)S(1)}, bf16[2,4,16,1024]{3,2,1,0:T(8,128)(2,1)S(1)}, u32[]{:S(2)}, u32[]{:S(2)}) collective-permute-start(bf16[2,4,16,1024]{3,2,1,0:T(8,128)(2,1)S(1)} %get-tuple-element.20), channel_id=1, source_target_pairs={{0,2},{1,3},{2,0},{3,1},{4,6},{5,7},{6,4},{7,5},{8,10},{9,11},{10,... | collective-permute-start | bytes 786440 | tf_op jit(solution)/shard_map/ppermute | solution.py:459
  5.7 14.7 %collective-permute-start.1 = (bf16[2,4,16,1024]{3,2,1,0:T(8,128)(2,1)S(1)}, bf16[2,4,16,1024]{3,2,1,0:T(8,128)(2,1)S(1)}, u32[]{:S(2)}, u32[]{:S(2)}) collective-permute-start(bf16[2,4,16,1024]{3,2,1,0:T(8,128)(2,1)S(1)} %get-tuple-element.21), channel_id=1, source_target_pairs={{0,4},{1,5},{2,6},{3,7},{4,0},{5,1},{6,2},{7,3},{8,12},{9,13},{10,... | collective-permute-start | bytes 786440 | tf_op jit(solution)/shard_map/ppermute | solution.py:459
  7.2 13.2 %collective-permute-start.2 = (bf16[2,4,16,1024]{3,2,1,0:T(8,128)(2,1)S(1)}, bf16[2,4,16,1024]{3,2,1,0:T(8,128)(2,1)S(1)}, u32[]{:S(2)}, u32[]{:S(2)}) collective-permute-start(bf16[2,4,16,1024]{3,2,1,0:T(8,128)(2,1)S(1)} %get-tuple-element.22), channel_id=1, source_target_pairs={{0,6},{1,7},{2,4},{3,5},{4,2},{5,3},{6,0},{7,1},{8,14},{9,15},{10,... | collective-permute-start | bytes 786440 | tf_op jit(solution)/shard_map/ppermute | solution.py:459
  7.3 13.2 %collective-permute-start.4 = (bf16[128,768]{1,0:T(8,128)(2,1)S(1)}, bf16[128,768]{1,0:T(8,128)(2,1)S(1)}, u32[]{:S(2)}, u32[]{:S(2)}) collective-permute-start(bf16[128,768]{1,0:T(8,128)(2,1)S(1)} %get-tuple-element.16.hidden_ref.refs_7_), channel_id=1, source_target_pairs={{0,16},{8,24},{16,0},{24,8},{1,17},{9,25},{17,1},{25,9},{2,18},{10... | collective-permute-start | bytes 589832 | tf_op jit(solution)/shard_map/ppermute | solution.py:459
  10.3 10.1 %collective-permute-start.3 = (bf16[128,768]{1,0:T(8,128)(2,1)S(1)}, bf16[128,768]{1,0:T(8,128)(2,1)S(1)}, u32[]{:S(2)}, u32[]{:S(2)}) collective-permute-start(bf16[128,768]{1,0:T(8,128)(2,1)S(1)} %get-tuple-element.16.hidden_ref.refs_7_), channel_id=1, source_target_pairs={{0,8},{8,0},{16,24},{24,16},{1,9},{9,1},{17,25},{25,17},{2,10},{10... | collective-permute-start | bytes 589832 | tf_op jit(solution)/shard_map/ppermute | solution.py:459
  16.7 19.1 %all-to-all-start = ((bf16[8,16,4096]{2,1,0:T(8,128)(2,1)}), bf16[8,16,4096]{2,1,0:T(8,128)(2,1)S(1)}, u32[]{:S(2)}, u32[]{:S(2)}) async-start(bf16[8,16,4096]{2,1,0:T(8,128)(2,1)} %expert_forward.1.refs_4_), calls=%async_computation | async-start | bytes 2097152 | tf_op jit(solution)/shard_map/all_to_all | solution.py:483
  20.5 2.1 %collective-permute-start.5 = (bf16[4,4,16,1024]{3,2,1,0:T(8,128)(2,1)S(1)}, bf16[4,4,16,1024]{3,2,1,0:T(8,128)(2,1)S(1)}, u32[]{:S(2)}, u32[]{:S(2)}) collective-permute-start(bf16[4,4,16,1024]{3,2,1,0:T(8,128)(2,1)S(1)} %sibling_rows.1), channel_id=1, source_target_pairs={{0,1},{1,0},{2,3},{3,2},{4,5},{5,4},{6,7},{7,6},{8,9},{9,8},{10,11... | collective-permute-start | bytes 1572872 | tf_op jit(solution)/shard_map/ppermute | solution.py:459
  23.5 26.5 %collective-permute-start.7 = (bf16[8,16,1024]{2,1,0:T(8,128)(2,1)}, bf16[8,16,1024]{2,1,0:T(8,128)(2,1)S(1)}, u32[]{:S(2)}, u32[]{:S(2)}) collective-permute-start(bf16[8,16,1024]{2,1,0:T(8,128)(2,1)} %get-tuple-element.24), channel_id=1, source_target_pairs={{0,16},{8,24},{16,0},{24,8},{1,17},{9,25},{17,1},{25,9},{2,18},{10... | collective-permute-start | bytes 786440 | tf_op jit(solution)/shard_map/ppermute | solution.py:459
  24.7 25.4 %collective-permute-start.8 = (bf16[8,16,1024]{2,1,0:T(8,128)(2,1)}, bf16[8,16,1024]{2,1,0:T(8,128)(2,1)}, u32[]{:S(2)}, u32[]{:S(2)}) collective-permute-start(bf16[8,16,1024]{2,1,0:T(8,128)(2,1)} %get-tuple-element.25), channel_id=1, source_target_pairs={{0,24},{8,16},{16,8},{24,0},{1,25},{9,17},{17,9},{25,1},{2,26},{10... | collective-permute-start | bytes 786440 | tf_op jit(solution)/shard_map/ppermute | solution.py:459
  26.4 23.7 %collective-permute-start.6 = (bf16[8,16,1024]{2,1,0:T(8,128)(2,1)}, bf16[8,16,1024]{2,1,0:T(8,128)(2,1)}, u32[]{:S(2)}, u32[]{:S(2)}) collective-permute-start(bf16[8,16,1024]{2,1,0:T(8,128)(2,1)} %get-tuple-element.23.tie_ref), channel_id=1, source_target_pairs={{0,8},{8,0},{16,24},{24,16},{1,9},{9,1},{17,25},{25,17},{2,10},{10... | collective-permute-start | bytes 786440 | tf_op jit(solution)/shard_map/ppermute | solution.py:459
  27.0 23.0 %collective-permute-start.9 = (bf16[128,768]{1,0:T(8,128)(2,1)S(1)}, bf16[128,768]{1,0:T(8,128)(2,1)}, u32[]{:S(2)}, u32[]{:S(2)}) collective-permute-start(bf16[128,768]{1,0:T(8,128)(2,1)S(1)} %collective-permute-done.4.refs_6_.refs_9_), channel_id=1, source_target_pairs={{0,8},{8,0},{16,24},{24,16},{1,9},{9,1},{17,25},{25,17},{2,10},{10... | collective-permute-start | bytes 589832 | tf_op jit(solution)/shard_map/ppermute | solution.py:459

commit v5 on v4

--- a/solution.py
+++ b/solution.py
@@ -9,7 +9,7 @@
 
 QB = 128
 CAP = 16
-VMEM_LIMIT = 24 * 1024 * 1024
+TILE = 256
 
 bf16 = jnp.bfloat16
 f32 = jnp.float32
@@ -21,8 +21,8 @@
 HBM = pl.BlockSpec(memory_space=pltpu.HBM)
 
 
-def params():
-    return pltpu.CompilerParams(vmem_limit_bytes=VMEM_LIMIT)
+def params(slots):
+    return pltpu.CompilerParams(vmem_limit_bytes=(12 + slots // 32) * 1024 * 1024)
 
 
 def hbm(value):
@@ -31,6 +31,14 @@
 
 def chunks(total, size):
     return [pl.ds(start, size) for start in range(0, total, size)]
+
+
+def bits_of(groups):
+    bits = []
+    while groups > 1:
+        groups //= 2
+        bits.append(groups)
+    return bits
 
 
 def block_place(me, r, flight):
@@ -40,13 +48,17 @@
 
 def dispatch_kernel(flight, groups, gate_up_hbm, cap_hbm, hot_hbm, ids_hbm, probs_hbm, dout_hbm, *refs):
     half = flight // 2
+    bits = bits_of(groups)
+    outs = 2 + half + len(bits)
     own_hbm, hidden_ref, *chips = refs[: 2 + half]
-    gate_up, cap_ref, hot_ref, ids_ref, probs_ref, dout, own_ref = refs[2 + half : 9 + half]
-    gate_sems, own_sem, small_sems, in_sems = refs[9 + half :]
+    messages = dict(zip(bits, refs[2 + half : outs]))
+    gate_up, cap_ref, hot_ref, ids_ref, probs_ref, dout, own_ref = refs[outs : outs + 7]
+    gate_sems, own_sem, small_sems, in_sems = refs[outs + 7 :]
     topk, tokens = ids_ref.shape
     slots = flight * CAP
     me, group = lax.axis_index("expert"), lax.axis_index("dp")
     share = dout_hbm.shape[1] // groups
+    hid = hidden_ref.shape[1]
     small = [
         pltpu.make_async_copy(src, dst, small_sems.at[i])
         for i, (src, dst) in enumerate(
@@ -89,9 +101,9 @@
         hit = ids_ref[k : k + 1, :] == row_expert
         named = jnp.where(hit, 1.0, named)
         weight = jnp.where(hit, probs_ref[k : k + 1, :], weight)
-    first = lax.broadcasted_iota(jnp.int32, (tokens, tokens), 0)
-    second = lax.broadcasted_iota(jnp.int32, (tokens, tokens), 1)
-    before = (first < second).astype(f32).astype(bf16)
+    earlier = lax.broadcasted_iota(jnp.int32, (tokens, tokens), 0)
+    later = lax.broadcasted_iota(jnp.int32, (tokens, tokens), 1)
+    before = (earlier < later).astype(f32).astype(bf16)
     rank = jnp.dot(named.astype(bf16), before, preferred_element_type=f32)
     owns = (named > 0.0) & (rank == row_rank) & (rank < limit)
     own_weight = jnp.where(owns, weight, 0.0)
@@ -107,12 +119,22 @@
         part = (part * slot_weight).astype(bf16)
         for r in range(flight):
             chips[r % half][r // half, j] = part[r * CAP : (r + 1) * CAP, :]
+        for bit in bits:
+            if bit <= j < 2 * bit:
+                first = flight * (hid // TILE) + (j - bit) * (share // TILE)
+                for q in range(share // TILE):
+                    messages[bit][first + q] = part[:CAP, q * TILE : (q + 1) * TILE]
     for copy in gates:
         copy.wait()
-    hid = hidden_ref.shape[1]
-    gate = gate_up[:, :hid].astype(f32)
-    up = gate_up[:, hid:].astype(f32)
-    hidden_ref[...] = (gate * jax.nn.sigmoid(gate) * up).astype(bf16)
+    for r in range(flight):
+        at = slice(r * CAP, (r + 1) * CAP)
+        gate = gate_up[at, :hid].astype(f32)
+        up = gate_up[at, hid:].astype(f32)
+        block = (gate * jax.nn.sigmoid(gate) * up).astype(bf16)
+        hidden_ref[at, :] = block
+        for bit in bits:
+            for q in range(hid // TILE):
+                messages[bit][r * (hid // TILE) + q] = block[:, q * TILE : (q + 1) * TILE]
     own_copy.wait()
 
 
@@ -125,9 +147,13 @@
     return pl.pallas_call(
         functools.partial(dispatch_kernel, flight, groups),
         out_shape=(pltpu.HBM((slots, tokens), f32), pltpu.VMEM((rows, double // 2), bf16))
-        + (pltpu.VMEM((2, groups, CAP, share), bf16),) * half,
+        + (pltpu.VMEM((2, groups, CAP, share), bf16),) * half
+        + tuple(
+            pltpu.VMEM((flight * (double // 2 // TILE) + bit * (share // TILE), CAP, TILE), bf16)
+            for bit in bits_of(groups)
+        ),
         in_specs=[HBM] * 6,
-        out_specs=(HBM, VMEM) + (VMEM,) * half,
+        out_specs=(HBM, VMEM) + (VMEM,) * (half + len(bits_of(groups))),
         scratch_shapes=[
             pltpu.VMEM((rows, double), bf16),
             pltpu.SMEM(capacity.shape, jnp.int32),
@@ -141,7 +167,7 @@
             pltpu.SemaphoreType.DMA((4,)),
             pltpu.SemaphoreType.DMA((groups,)),
         ],
-        compiler_params=params(),
+        compiler_params=params(slots),
         cost_estimate=SMALL,
         name="dispatch",
     )(hbm(gate_up), hbm(capacity), hbm(hot_row), hbm(ids), hbm(probs), hbm(d_out))
@@ -206,7 +232,7 @@
             pltpu.SemaphoreType.DMA((steps,)),
             pltpu.SemaphoreType.DMA((steps,)),
         ],
-        compiler_params=params(),
+        compiler_params=params(flight * CAP),
         cost_estimate=SMALL,
         name="expert_forward",
     )(hidden, hbm(scale), hbm(quant))
@@ -225,31 +251,32 @@
         out_shape=pltpu.VMEM((half,) + chips[0].shape[1:], bf16),
         in_specs=[VMEM] * half + [ANY] * len(ties),
         out_specs=VMEM,
-        compiler_params=params(),
+        compiler_params=params(2 * half * CAP),
         cost_estimate=SMALL,
         name="sibling_rows",
     )(*chips, *ties)
 
 
 def split_kernel(half, groups, *refs):
-    chips, swapped, pieces = refs[:half], refs[half], refs[half + 1 :]
+    chips, swapped, pieces = refs[: half - 1], refs[half - 1], refs[1 - groups :]
     for j in range(1, groups):
         for c in range(half):
-            pieces[j - 1][c] = chips[c][0, j]
-            pieces[j - 1][half + c] = swapped[c, j]
+            if c:
+                pieces[j - 1][c - 1] = chips[c - 1][0, j]
+            pieces[j - 1][half - 1 + c] = swapped[c, j]
 
 
 def split(chips, swapped):
     half, groups, cap, share = swapped.shape
     return pl.pallas_call(
         functools.partial(split_kernel, half, groups),
-        out_shape=(pltpu.VMEM((2 * half, cap, share), bf16),) * (groups - 1),
-        in_specs=[VMEM] * (half + 1),
+        out_shape=(pltpu.VMEM((2 * half - 1, cap, share), bf16),) * (groups - 1),
+        in_specs=[VMEM] * half,
         out_specs=(VMEM,) * (groups - 1),
-        compiler_params=params(),
+        compiler_params=params(2 * half * CAP),
         cost_estimate=SMALL,
         name="split",
-    )(*chips, swapped)
+    )(*chips[1:], swapped)
 
 
 def backward_kernel(flight, groups, scale_hbm, gate_up_hbm, quant_hbm, tie_ref, swapped, *refs):
@@ -342,7 +369,7 @@
             pltpu.SemaphoreType.DMA((groups,)),
             pltpu.SemaphoreType.DMA((flight,)),
         ],
-        compiler_params=params(),
+        compiler_params=params(slots),
         cost_estimate=SMALL,
         name="expert_backward",
     )(hbm(scale), hbm(gate_up), hbm(quant), tie, swapped, *chips)
@@ -404,25 +431,40 @@
             pltpu.VMEM((tokens, width), bf16),
             pltpu.SemaphoreType.DMA((3,)),
         ],
-        compiler_params=params(),
+        compiler_params=params(own.shape[0]),
         cost_estimate=SMALL,
         name="combine",
     )(hbm(ids), hbm(own), hbm(d_out), returned)
 
 
-def weight_grad_kernel(half, groups, block, tie_ref, swapped, *refs):
+def weight_grad_kernel(half, groups, block, tie_ref, swapped, hidden_ref, *refs):
     chips, parts = refs[:half], refs[half : half + groups - 1]
-    hid_refs = refs[half + groups - 1 : half + 2 * groups - 1]
-    out_hbm, hidden, out, out_sems = refs[half + 2 * groups - 1 :]
+    messages = refs[half + groups - 1 : half + 2 * groups - 2]
+    out_hbm, hidden, own, out, out_sems = refs[half + 2 * groups - 2 :]
     cap, share = parts[0].shape[1:]
-    slots = 2 * half * cap
-    for j in range(groups):
-        hidden[j * slots : (j + 1) * slots, :] = hid_refs[j][...]
+    flight = 2 * half
+    slots = flight * cap
+    wide = hidden_ref.shape[1] // TILE
+    hidden[:slots, :] = hidden_ref[...]
+    for j in range(1, groups):
+        bit = max(b for b in bits_of(groups) if b <= j)
+        message = messages[j - 1]
+        for r in range(flight):
+            for q in range(wide):
+                hidden[
+                    j * slots + r * cap : j * slots + (r + 1) * cap, q * TILE : (q + 1) * TILE
+                ] = message[r * wide + q]
+        for q in range(share // TILE):
+            own[j - 1, :, q * TILE : (q + 1) * TILE] = message[
+                flight * wide + (j - bit) * (share // TILE) + q
+            ]
     stores = []
     for n, cols in enumerate(chunks(share, block)):
         grads = [chips[c][0, 0, :, cols] for c in range(half)]
         grads += [swapped[c, 0, :, cols] for c in range(half)]
-        grads += [part[:, :, cols].reshape(slots, block) for part in parts]
+        for j in range(1, groups):
+            grads.append(own[j - 1, :, cols])
+            grads.append(parts[j - 1][:, :, cols].reshape(slots - cap, block))
         out[cols, :] = lax.dot_general(
             jnp.concatenate(grads, axis=0),
             hidden[...],
@@ -435,9 +477,9 @@
         copy.wait()
 
 
-def weight_grad(tie, chips, swapped, parts, hiddens, block=256):
+def weight_grad(tie, chips, swapped, hidden, parts, messages, block=256):
     half, groups, cap, share = swapped.shape
-    slots, hid = hiddens[0].shape
+    slots, hid = hidden.shape
     return pl.pallas_call(
         functools.partial(weight_grad_kernel, half, groups, block),
         out_shape=pltpu.HBM((share, hid), bf16),
@@ -445,13 +487,14 @@
         out_specs=HBM,
         scratch_shapes=[
             pltpu.VMEM((groups * slots, hid), bf16),
+            pltpu.VMEM((groups - 1, cap, share), bf16),
             pltpu.VMEM((share, hid), bf16),
             pltpu.SemaphoreType.DMA((share // block,)),
         ],
-        compiler_params=params(),
+        compiler_params=params(slots),
         cost_estimate=SMALL,
         name="weight_grad",
-    )(hbm(tie), swapped, *chips, *parts, *hiddens)
+    )(hbm(tie), swapped, hidden, *chips, *parts, *messages)
 
 
 def swap(value, axis, j):
@@ -465,20 +508,18 @@
     gate_up = gate_up[0, 0]
     ids, probs = route_ids.T, route_probs.T
     scale = w_scale.transpose(1, 0, 2)
-    own, hidden, *chips = dispatch(
+    own, hidden, *rest = dispatch(
         gate_up, capacity, hot_lists, ids, probs, d_out, flight, groups
     )
-    chips = chips[:1] + [swap(chips[c], "expert", 2 * c) for c in range(1, flight // 2)]
-    hiddens, late = {0: hidden}, set()
-    bit = groups // 2
-    while bit:
-        for j in sorted(hiddens):
-            hiddens[j ^ bit] = swap(hiddens[j], "dp", bit)
-            if j:
-                late.add(j ^ bit)
-        bit //= 2
-    early = [hiddens[j] for j in range(1, groups) if j not in late]
-    hiddens = [hiddens[j] for j in range(groups)]
+    half, bits = flight // 2, bits_of(groups)
+    chips = rest[:1] + [swap(rest[c], "expert", 2 * c) for c in range(1, half)]
+    messages, early = {}, []
+    for bit, message in zip(bits, rest[half:]):
+        for j in sorted(messages):
+            messages[j ^ bit] = swap(messages[j], "dp", bit)
+        messages[bit] = swap(message, "dp", bit)
+        early.append(messages[bit])
+    messages = [messages[j] for j in range(1, groups)]
     expert_out = forward(scale, hidden, w_quant[0], flight)
     returned = lax.all_to_all(expert_out, "expert", split_axis=0, concat_axis=0, tiled=True)
     swapped = swap(sibling_rows(chips, [hbm(expert_out)] + early), "expert", 1)
@@ -486,7 +527,7 @@
     parts = [swap(pieces[j - 1], "dp", j) for j in range(1, groups)]
     d_gate_up = backward(scale, gate_up, w_quant[0], pieces[0], chips, swapped)
     combined, d_probs = combine(ids, own, d_out, returned)
-    d_weight = weight_grad(d_probs, chips, swapped, parts, hiddens)
+    d_weight = weight_grad(d_probs, chips, swapped, hidden, parts, messages)
     return (combined, d_probs.T, d_gate_up[None, None], d_weight[None])
 
 

time: 53.2 us -> 50.6 us (0.951)
  the two profiles are of different devices: /device:TPU:0 before, /device:TPU:18 now
where the time goes in v5:
time: 50.6 us; the launch traced here: 50.4 us
  Pallas kernels  20.1 us (40%)
  starting transfers between devices  17.4 us (34%)
  waiting for transfers between devices  12.2 us (24%)
  between operations  0.72 us (1%)
    ppermute x10, starting transfers between devices, swap(): return lax.ppermute(value, axis, [(i, i ^ j) for i in range(size)])  13.1 us
    ppermute x10, waiting for transfers between devices, swap(): return lax.ppermute(value, axis, [(i, i ^ j) for i in range(size)])  12.2 us
    pallas_call x1, Pallas kernels, backward(): pl.pallas_call(functools.partial(backward_kernel, flight, groups), out_sh...  5.25 us
    pallas_call x1, Pallas kernels, forward(): pl.pallas_call(functools.partial(forward_kernel, flight, block), out_shap...  4.78 us
    all_to_all x1, starting transfers between devices, shards(): lax.all_to_all(expert_out, 'expert', split_axis=0, concat_axis=0, tiled=T...  4.27 us
    pallas_call x1, Pallas kernels, combine(): pl.pallas_call(functools.partial(combine_kernel, block), out_shape=(pltpu...  3.29 us
    pallas_call x1, Pallas kernels, weight_grad(): pl.pallas_call(functools.partial(weight_grad_kernel, half, groups, block)...  2.98 us
    pallas_call x1, Pallas kernels, dispatch(): pl.pallas_call(functools.partial(dispatch_kernel, flight, groups), out_sh...  2.88 us
  transfers between devices with their start and end apart: 11, of which 3 were waited for; matrix products, arithmetic and copies ran while one was open for 0% of the time, Pallas kernels for 28%

profile of v5, /device:TPU:18, one launch (start us, length us, event | category | flops | bytes accessed | tf_op | source)
XLA Modules:
  0.0 50.4 jit_solution(17947887719803663679)
XLA Ops:
  0.6 2.9 %dispatch.1 = (f32[128,128]{1,0:T(8,128)}, bf16[128,768]{1,0:T(8,128)(2,1)S(1)}, bf16[2,4,16,1024]{3,2,1,0:T(8,128)(2,1)S(1)}, bf16[2,4,16,1024]{3,2,1,0:T(8,128...) custom-call(bf16[128,1536]{1,0:T(8,128)(2,1)} %bitcast.10, ...), custom_call_target="tpu_custom_call" | custom-call | flops 1024 | bytes 1024 | tf_op jit(solution)/shard_map/dispatch/pallas_call | solution.py:147
  3.5 0.6 %collective-permute-start = (bf16[2,4,16,1024]{3,2,1,0:T(8,128)(2,1)}, bf16[2,4,16,1024]{3,2,1,0:T(8,128)(2,1)S(1)}, u32[]{:S(2)}, u32[]{:S(2)}) collective-permute-start(bf16[2,4,16,1024]{3,2,1,0:T(8,128)(2,1)} %get-tuple-element.21), channel_id=1, source_target_pairs={{0,2},{1,3},{2,0},{3,1},{4,6},{5,7},{6,4},{7,5},{8,10},{9,11},{10,... | collective-permute-start | bytes 786440 | tf_op jit(solution)/shard_map/ppermute | solution.py:502
  4.1 1.5 %collective-permute-start.1 = (bf16[2,4,16,1024]{3,2,1,0:T(8,128)(2,1)}, bf16[2,4,16,1024]{3,2,1,0:T(8,128)(2,1)S(1)}, u32[]{:S(2)}, u32[]{:S(2)}) collective-permute-start(bf16[2,4,16,1024]{3,2,1,0:T(8,128)(2,1)} %get-tuple-element.22), channel_id=1, source_target_pairs={{0,4},{1,5},{2,6},{3,7},{4,0},{5,1},{6,2},{7,3},{8,12},{9,13},{10,... | collective-permute-start | bytes 786440 | tf_op jit(solution)/shard_map/ppermute | solution.py:502
  5.6 1.4 %collective-permute-start.2 = (bf16[2,4,16,1024]{3,2,1,0:T(8,128)(2,1)S(1)}, bf16[2,4,16,1024]{3,2,1,0:T(8,128)(2,1)S(1)}, u32[]{:S(2)}, u32[]{:S(2)}) collective-permute-start(bf16[2,4,16,1024]{3,2,1,0:T(8,128)(2,1)S(1)} %get-tuple-element.23), channel_id=1, source_target_pairs={{0,6},{1,7},{2,4},{3,5},{4,2},{5,3},{6,0},{7,1},{8,14},{9,15},{10,... | collective-permute-start | bytes 786440 | tf_op jit(solution)/shard_map/ppermute | solution.py:502
  7.1 0.3 collective-permute-start.3
  7.4 1.6 %collective-permute-start.4 = (bf16[28,16,256]{2,1,0:T(8,128)(2,1)S(1)}, bf16[28,16,256]{2,1,0:T(8,128)(2,1)S(1)}, u32[]{:S(2)}, u32[]{:S(2)}) collective-permute-start(bf16[28,16,256]{2,1,0:T(8,128)(2,1)S(1)} %get-tuple-element.26), channel_id=1, source_target_pairs={{0,8},{8,0},{16,24},{24,16},{1,9},{9,1},{17,25},{25,17},{2,10},{10... | collective-permute-start | bytes 688136 | tf_op jit(solution)/shard_map/ppermute | solution.py:502
  9.0 4.8 %expert_forward.1.refs_4_ = bf16[8,16,4096]{2,1,0:T(8,128)(2,1)} custom-call(bf16[128,768]{1,0:T(8,128)(2,1)S(1)} %get-tuple-element.18.hidden_ref, f32[6,1,32]{2,1,0:T(1,128)} %bitcast.16, bf16[768,4096]{1,0:T(8,128)(2,1)} %bitcast.8), custom_call_target="tpu_custom_call" | custom-call | flops 1024 | bytes 1024 | tf_op jit(solution)/shard_map/expert_forward/pallas_call | solution.py:221
  13.8 4.3 %all-to-all-start = ((bf16[8,16,4096]{2,1,0:T(8,128)(2,1)}), bf16[8,16,4096]{2,1,0:T(8,128)(2,1)S(1)}, u32[]{:S(2)}, u32[]{:S(2)}) async-start(bf16[8,16,4096]{2,1,0:T(8,128)(2,1)} %expert_forward.1.refs_4_), calls=%async_computation | async-start | bytes 2097152 | tf_op jit(solution)/shard_map/all_to_all | solution.py:524
  18.0 1.1 %collective-permute-done.4.refs_6_.refs_7_ = bf16[28,16,256]{2,1,0:T(8,128)(2,1)S(1)} collective-permute-done((bf16[28,16,256]{2,1,0:T(8,128)(2,1)S(1)}, bf16[28,16,256]{2,1,0:T(8,128)(2,1)S(1)}, u32[]{:S(2)}, u32[]{:S(2)}) %collective-permute-start.4) | collective-permute-done | bytes 229408 | tf_op jit(solution)/shard_map/ppermute | solution.py:502
  19.1 0.0 collective-permute-done.refs_1_.refs_0_
  19.1 0.0 collective-permute-done.1.refs_2_.refs_1_
  19.2 0.1 collective-permute-start.5
  19.3 3.2 %collective-permute-start.9 = (bf16[32,16,256]{2,1,0:T(8,128)(2,1)S(1)}, bf16[32,16,256]{2,1,0:T(8,128)(2,1)}, u32[]{:S(2)}, u32[]{:S(2)}) collective-permute-start(bf16[32,16,256]{2,1,0:T(8,128)(2,1)S(1)} %collective-permute-done.3.refs_5_.refs_8_), channel_id=1, source_target_pairs={{0,8},{8,0},{16,24},{24,16},{1,9},{9,1},{17,25},{25,17},{2,10},{10... | collective-permute-start | bytes 786440 | tf_op jit(solution)/shard_map/ppermute | solution.py:502
  22.4 0.9 %split.1 = (bf16[7,16,1024]{2,1,0:T(8,128)(2,1)}, bf16[7,16,1024]{2,1,0:T(8,128)(2,1)}, bf16[7,16,1024]{2,1,0:T(8,128)(2,1)}) custom-call(bf16[2,4,16,1024]{3,2,1,0:T(8,128)(2,1)S(1)} %collective-permute-done.refs_1_.refs_0_, bf16[2,4,16,1024]{3,2,1,0:T(8,128)(2,1)S(1)} %collective-permute-done.1.refs_2_.refs_1_, ...), custom_call_target="tpu_custom_call" | custom-call | flops 1024 | bytes 1024 | tf_op jit(solution)/shard_map/split/pallas_call | solution.py:271
  23.3 0.7 %collective-permute-start.7 = (bf16[7,16,1024]{2,1,0:T(8,128)(2,1)}, bf16[7,16,1024]{2,1,0:T(8,128)(2,1)S(1)}, u32[]{:S(2)}, u32[]{:S(2)}) collective-permute-start(bf16[7,16,1024]{2,1,0:T(8,128)(2,1)} %get-tuple-element.28), channel_id=1, source_target_pairs={{0,16},{8,24},{16,0},{24,8},{1,17},{9,25},{17,1},{25,9},{2,18},{10... | collective-permute-start | bytes 688136 | tf_op jit(solution)/shard_map/ppermute | solution.py:502
  24.0 2.6 %collective-permute-start.8 = (bf16[7,16,1024]{2,1,0:T(8,128)(2,1)}, bf16[7,16,1024]{2,1,0:T(8,128)(2,1)}, u32[]{:S(2)}, u32[]{:S(2)}) collective-permute-start(bf16[7,16,1024]{2,1,0:T(8,128)(2,1)} %get-tuple-element.29), channel_id=1, source_target_pairs={{0,24},{8,16},{16,8},{24,0},{1,25},{9,17},{17,9},{25,1},{2,26},{10... | collective-permute-start | bytes 688136 | tf_op jit(solution)/shard_map/ppermute | solution.py:502
  26.6 1.1 %collective-permute-start.6 = (bf16[7,16,1024]{2,1,0:T(8,128)(2,1)}, bf16[7,16,1024]{2,1,0:T(8,128)(2,1)}, u32[]{:S(2)}, u32[]{:S(2)}) collective-permute-start(bf16[7,16,1024]{2,1,0:T(8,128)(2,1)} %get-tuple-element.27.tie_ref), channel_id=1, source_target_pairs={{0,8},{8,0},{16,24},{24,16},{1,9},{9,1},{17,25},{25,17},{2,10},{10... | collective-permute-start | bytes 688136 | tf_op jit(solution)/shard_map/ppermute | solution.py:502
  27.7 5.3 %expert_backward.1 = bf16[128,1536]{1,0:T(8,128)(2,1)} custom-call(f32[6,1,32]{2,1,0:T(1,128)} %bitcast.17, bf16[128,1536]{1,0:T(8,128)(2,1)} %bitcast.11, bf16[768,4096]{1,0:T(8,128)(2,1)} %bitcast.9, bf16[7,16,1024]{2,1,0:T(8,128)(2,1)} %get-tuple-element.27.tie_ref, bf16[4,4,16,1024]{3,2,1,0:T(8,128)(2,1)S(1)} %collective-permute-done.5.refs_3_.swapped, ...), custom_call_target="tpu_custom_call" | custom-call | flops 1024 | bytes 1024 | tf_op jit(solution)/shard_map/expert_backward/pallas_call | solution.py:355
  33.0 0.0 all-to-all-done.ret_ref
  33.0 3.3 %combine.1 = (bf16[128,4096]{1,0:T(8,128)(2,1)}, f32[8,128]{1,0:T(8,128)}) custom-call(s32[8,128]{1,0:T(8,128)} %bitcast.15, f32[128,128]{1,0:T(8,128)} %get-tuple-element.17.own_hbm, bf16[128,4096]{1,0:T(8,128)(2,1)} %dout_hbm.3, bf16[8,16,4096]{2,1,0:T(8,128)(2,1)S(1)} %all-to-all-done.ret_ref), custom_call_target="tpu_custom_call" | custom-call | flops 1024 | bytes 1024 | tf_op jit(solution)/shard_map/combine/pallas_call | solution.py:420
  36.3 0.0 collective-permute-done.9.refs_9_
  36.3 3.9 %collective-permute-done.7.refs_5_ = bf16[7,16,1024]{2,1,0:T(8,128)(2,1)S(1)} collective-permute-done((bf16[7,16,1024]{2,1,0:T(8,128)(2,1)}, bf16[7,16,1024]{2,1,0:T(8,128)(2,1)S(1)}, u32[]{:S(2)}, u32[]{:S(2)}) %collective-permute-start.7) | collective-permute-done | bytes 229408 | tf_op jit(solution)/shard_map/ppermute | solution.py:502
  40.2 7.2 %collective-permute-done.8.refs_6_ = bf16[7,16,1024]{2,1,0:T(8,128)(2,1)} collective-permute-done((bf16[7,16,1024]{2,1,0:T(8,128)(2,1)}, bf16[7,16,1024]{2,1,0:T(8,128)(2,1)}, u32[]{:S(2)}, u32[]{:S(2)}) %collective-permute-start.8) | collective-permute-done | bytes 229408 | tf_op jit(solution)/shard_map/ppermute | solution.py:502
  47.4 3.0 %weight_grad.1 = bf16[1024,768]{1,0:T(8,128)(2,1)} custom-call(f32[8,128]{1,0:T(8,128)} %get-tuple-element.20.tie_ref, bf16[4,4,16,1024]{3,2,1,0:T(8,128)(2,1)S(1)} %collective-permute-done.5.refs_3_.swapped, bf16[128,768]{1,0:T(8,128)(2,1)S(1)} %get-tuple-element.18.hidden_ref, bf16[2,4,16,1024]{3,2,1,0:T(8,128)(2,1)S(1)} %get-tuple-element.24.refs_0_, ...), custom_call_target="tpu_custom_call" | custom-call | flops 1024 | bytes 1024 | tf_op jit(solution)/shard_map/weight_grad/pallas_call | solution.py:483
  (5 shorter events, 0.0 us)
Async XLA Ops:
  3.5 15.6 %collective-permute-start = (bf16[2,4,16,1024]{3,2,1,0:T(8,128)(2,1)}, bf16[2,4,16,1024]{3,2,1,0:T(8,128)(2,1)S(1)}, u32[]{:S(2)}, u32[]{:S(2)}) collective-permute-start(bf16[2,4,16,1024]{3,2,1,0:T(8,128)(2,1)} %get-tuple-element.21), channel_id=1, source_target_pairs={{0,2},{1,3},{2,0},{3,1},{4,6},{5,7},{6,4},{7,5},{8,10},{9,11},{10,... | collective-permute-start | bytes 786440 | tf_op jit(solution)/shard_map/ppermute | solution.py:502
  4.1 15.0 %collective-permute-start.1 = (bf16[2,4,16,1024]{3,2,1,0:T(8,128)(2,1)}, bf16[2,4,16,1024]{3,2,1,0:T(8,128)(2,1)S(1)}, u32[]{:S(2)}, u32[]{:S(2)}) collective-permute-start(bf16[2,4,16,1024]{3,2,1,0:T(8,128)(2,1)} %get-tuple-element.22), channel_id=1, source_target_pairs={{0,4},{1,5},{2,6},{3,7},{4,0},{5,1},{6,2},{7,3},{8,12},{9,13},{10,... | collective-permute-start | bytes 786440 | tf_op jit(solution)/shard_map/ppermute | solution.py:502
  5.6 13.5 %collective-permute-start.2 = (bf16[2,4,16,1024]{3,2,1,0:T(8,128)(2,1)S(1)}, bf16[2,4,16,1024]{3,2,1,0:T(8,128)(2,1)S(1)}, u32[]{:S(2)}, u32[]{:S(2)}) collective-permute-start(bf16[2,4,16,1024]{3,2,1,0:T(8,128)(2,1)S(1)} %get-tuple-element.23), channel_id=1, source_target_pairs={{0,6},{1,7},{2,4},{3,5},{4,2},{5,3},{6,0},{7,1},{8,14},{9,15},{10,... | collective-permute-start | bytes 786440 | tf_op jit(solution)/shard_map/ppermute | solution.py:502
  7.1 12.1 %collective-permute-start.3 = (bf16[32,16,256]{2,1,0:T(8,128)(2,1)S(1)}, bf16[32,16,256]{2,1,0:T(8,128)(2,1)S(1)}, u32[]{:S(2)}, u32[]{:S(2)}) collective-permute-start(bf16[32,16,256]{2,1,0:T(8,128)(2,1)S(1)} %get-tuple-element.25), channel_id=1, source_target_pairs={{0,16},{8,24},{16,0},{24,8},{1,17},{9,25},{17,1},{25,9},{2,18},{10... | collective-permute-start | bytes 786440 | tf_op jit(solution)/shard_map/ppermute | solution.py:502
  7.4 11.7 %collective-permute-start.4 = (bf16[28,16,256]{2,1,0:T(8,128)(2,1)S(1)}, bf16[28,16,256]{2,1,0:T(8,128)(2,1)S(1)}, u32[]{:S(2)}, u32[]{:S(2)}) collective-permute-start(bf16[28,16,256]{2,1,0:T(8,128)(2,1)S(1)} %get-tuple-element.26), channel_id=1, source_target_pairs={{0,8},{8,0},{16,24},{24,16},{1,9},{9,1},{17,25},{25,17},{2,10},{10... | collective-permute-start | bytes 688136 | tf_op jit(solution)/shard_map/ppermute | solution.py:502
  13.8 19.2 %all-to-all-start = ((bf16[8,16,4096]{2,1,0:T(8,128)(2,1)}), bf16[8,16,4096]{2,1,0:T(8,128)(2,1)S(1)}, u32[]{:S(2)}, u32[]{:S(2)}) async-start(bf16[8,16,4096]{2,1,0:T(8,128)(2,1)} %expert_forward.1.refs_4_), calls=%async_computation | async-start | bytes 2097152 | tf_op jit(solution)/shard_map/all_to_all | solution.py:524
  19.2 3.2 %collective-permute-start.5 = (bf16[4,4,16,1024]{3,2,1,0:T(8,128)(2,1)S(1)}, bf16[4,4,16,1024]{3,2,1,0:T(8,128)(2,1)S(1)}, u32[]{:S(2)}, u32[]{:S(2)}) collective-permute-start(bf16[4,4,16,1024]{3,2,1,0:T(8,128)(2,1)S(1)} %sibling_rows.1), channel_id=1, source_target_pairs={{0,1},{1,0},{2,3},{3,2},{4,5},{5,4},{6,7},{7,6},{8,9},{9,8},{10,11... | collective-permute-start | bytes 1572872 | tf_op jit(solution)/shard_map/ppermute | solution.py:502
  19.3 17.0 %collective-permute-start.9 = (bf16[32,16,256]{2,1,0:T(8,128)(2,1)S(1)}, bf16[32,16,256]{2,1,0:T(8,128)(2,1)}, u32[]{:S(2)}, u32[]{:S(2)}) collective-permute-start(bf16[32,16,256]{2,1,0:T(8,128)(2,1)S(1)} %collective-permute-done.3.refs_5_.refs_8_), channel_id=1, source_target_pairs={{0,8},{8,0},{16,24},{24,16},{1,9},{9,1},{17,25},{25,17},{2,10},{10... | collective-permute-start | bytes 786440 | tf_op jit(solution)/shard_map/ppermute | solution.py:502
  23.3 16.9 %collective-permute-start.7 = (bf16[7,16,1024]{2,1,0:T(8,128)(2,1)}, bf16[7,16,1024]{2,1,0:T(8,128)(2,1)S(1)}, u32[]{:S(2)}, u32[]{:S(2)}) collective-permute-start(bf16[7,16,1024]{2,1,0:T(8,128)(2,1)} %get-tuple-element.28), channel_id=1, source_target_pairs={{0,16},{8,24},{16,0},{24,8},{1,17},{9,25},{17,1},{25,9},{2,18},{10... | collective-permute-start | bytes 688136 | tf_op jit(solution)/shard_map/ppermute | solution.py:502
  24.0 23.4 %collective-permute-start.8 = (bf16[7,16,1024]{2,1,0:T(8,128)(2,1)}, bf16[7,16,1024]{2,1,0:T(8,128)(2,1)}, u32[]{:S(2)}, u32[]{:S(2)}) collective-permute-start(bf16[7,16,1024]{2,1,0:T(8,128)(2,1)} %get-tuple-element.29), channel_id=1, source_target_pairs={{0,24},{8,16},{16,8},{24,0},{1,25},{9,17},{17,9},{25,1},{2,26},{10... | collective-permute-start | bytes 688136 | tf_op jit(solution)/shard_map/ppermute | solution.py:502
  26.6 20.8 %collective-permute-start.6 = (bf16[7,16,1024]{2,1,0:T(8,128)(2,1)}, bf16[7,16,1024]{2,1,0:T(8,128)(2,1)}, u32[]{:S(2)}, u32[]{:S(2)}) collective-permute-start(bf16[7,16,1024]{2,1,0:T(8,128)(2,1)} %get-tuple-element.27.tie_ref), channel_id=1, source_target_pairs={{0,8},{8,0},{16,24},{24,16},{1,9},{9,1},{17,25},{25,17},{2,10},{10... | collective-permute-start | bytes 688136 | tf_op jit(solution)/shard_map/ppermute | solution.py:502

commit v6 on v5

--- a/solution.py
+++ b/solution.py
@@ -238,45 +238,46 @@
     )(hidden, hbm(scale), hbm(quant))
 
 
-def sibling_kernel(half, *refs):
-    chips, out_ref = refs[:half], refs[-1]
+def sort_kernel(half, groups, ties, *refs):
+    chips, (sibling, *pieces) = refs[:half], refs[half + ties :]
     for c in range(half):
-        out_ref[c] = chips[c][1]
-
-
-def sibling_rows(chips, ties):
+        sibling[c] = chips[c][1]
+        for j in range(1, groups):
+            if c:
+                pieces[j - 1][c - 1] = chips[c][0, j]
+
+
+def sort_rows(chips, ties):
     half = len(chips)
-    return pl.pallas_call(
-        functools.partial(sibling_kernel, half),
-        out_shape=pltpu.VMEM((half,) + chips[0].shape[1:], bf16),
+    _, groups, cap, share = chips[0].shape
+    return pl.pallas_call(
+        functools.partial(sort_kernel, half, groups, len(ties)),
+        out_shape=(pltpu.VMEM((half, groups, cap, share), bf16),)
+        + (pltpu.VMEM((half - 1, cap, share), bf16),) * (groups - 1),
         in_specs=[VMEM] * half + [ANY] * len(ties),
-        out_specs=VMEM,
+        out_specs=(VMEM,) * groups,
         compiler_params=params(2 * half * CAP),
         cost_estimate=SMALL,
-        name="sibling_rows",
+        name="sort_rows",
     )(*chips, *ties)
 
 
-def split_kernel(half, groups, *refs):
-    chips, swapped, pieces = refs[: half - 1], refs[half - 1], refs[1 - groups :]
+def split_kernel(groups, swapped, *pieces):
     for j in range(1, groups):
-        for c in range(half):
-            if c:
-                pieces[j - 1][c - 1] = chips[c - 1][0, j]
-            pieces[j - 1][half - 1 + c] = swapped[c, j]
-
-
-def split(chips, swapped):
+        pieces[j - 1][...] = swapped[:, j]
+
+
+def split(swapped):
     half, groups, cap, share = swapped.shape
     return pl.pallas_call(
-        functools.partial(split_kernel, half, groups),
-        out_shape=(pltpu.VMEM((2 * half - 1, cap, share), bf16),) * (groups - 1),
-        in_specs=[VMEM] * half,
+        functools.partial(split_kernel, groups),
+        out_shape=(pltpu.VMEM((half, cap, share), bf16),) * (groups - 1),
+        in_specs=[VMEM],
         out_specs=(VMEM,) * (groups - 1),
         compiler_params=params(2 * half * CAP),
         cost_estimate=SMALL,
         name="split",
-    )(*chips[1:], swapped)
+    )(swapped)
 
 
 def backward_kernel(flight, groups, scale_hbm, gate_up_hbm, quant_hbm, tie_ref, swapped, *refs):
@@ -376,12 +377,13 @@
 
 
 def combine_kernel(
-    block, ids_hbm, own_hbm, dout_hbm, ret_ref, out_ref, dprobs_ref, ids_ref, own_ref, dout, sems
+    block, ids_hbm, own_hbm, dout_hbm, ret_hbm, out_ref, dprobs_ref, ids_ref, own_ref, dout, ret_ref, sems
 ):
     copies = [
         pltpu.make_async_copy(ids_hbm, ids_ref, sems.at[0]),
         pltpu.make_async_copy(own_hbm, own_ref, sems.at[1]),
         pltpu.make_async_copy(dout_hbm, dout, sems.at[2]),
+        pltpu.make_async_copy(ret_hbm, ret_ref, sems.at[3]),
     ]
     for copy in copies:
         copy.start()
@@ -396,8 +398,8 @@
     high = turned.astype(bf16)
     low = (turned - high.astype(f32)).astype(bf16)
     total = jnp.zeros((slots, tokens), f32)
-    copies[0].wait()
-    copies[2].wait()
+    for copy in (copies[0], copies[2], copies[3]):
+        copy.wait()
     for cols in chunks(width, block):
         here = jnp.concatenate(
             [ret_ref[block_place(me, r, flight), :, cols] for r in range(flight)], axis=0
@@ -423,24 +425,25 @@
             pltpu.HBM((tokens, width), bf16),
             pltpu.HBM(ids.shape, f32),
         ),
-        in_specs=[HBM, HBM, HBM, VMEM],
+        in_specs=[HBM, HBM, HBM, HBM],
         out_specs=(VMEM, VMEM),
         scratch_shapes=[
             pltpu.VMEM(ids.shape, jnp.int32),
             pltpu.VMEM(own.shape, f32),
             pltpu.VMEM((tokens, width), bf16),
-            pltpu.SemaphoreType.DMA((3,)),
+            pltpu.VMEM(returned.shape, bf16),
+            pltpu.SemaphoreType.DMA((4,)),
         ],
         compiler_params=params(own.shape[0]),
         cost_estimate=SMALL,
         name="combine",
-    )(hbm(ids), hbm(own), hbm(d_out), returned)
+    )(hbm(ids), hbm(own), hbm(d_out), hbm(returned))
 
 
 def weight_grad_kernel(half, groups, block, tie_ref, swapped, hidden_ref, *refs):
-    chips, parts = refs[:half], refs[half : half + groups - 1]
-    messages = refs[half + groups - 1 : half + 2 * groups - 2]
-    out_hbm, hidden, own, out, out_sems = refs[half + 2 * groups - 2 :]
+    others = groups - 1
+    chips, parts, refs = refs[:half], refs[half : half + 2 * others], refs[half + 2 * others :]
+    messages, (out_hbm, hidden, own, out, out_sems) = refs[:others], refs[others:]
     cap, share = parts[0].shape[1:]
     flight = 2 * half
     slots = flight * cap
@@ -464,7 +467,8 @@
         grads += [swapped[c, 0, :, cols] for c in range(half)]
         for j in range(1, groups):
             grads.append(own[j - 1, :, cols])
-            grads.append(parts[j - 1][:, :, cols].reshape(slots - cap, block))
+            grads.append(parts[j - 1][:, :, cols].reshape(slots // 2 - cap, block))
+            grads.append(parts[others + j - 1][:, :, cols].reshape(slots // 2, block))
         out[cols, :] = lax.dot_general(
             jnp.concatenate(grads, axis=0),
             hidden[...],
@@ -483,7 +487,7 @@
     return pl.pallas_call(
         functools.partial(weight_grad_kernel, half, groups, block),
         out_shape=pltpu.HBM((share, hid), bf16),
-        in_specs=[HBM] + [VMEM] * (half + 2 * groups),
+        in_specs=[HBM] + [VMEM] * (half + 3 * groups - 1),
         out_specs=HBM,
         scratch_shapes=[
             pltpu.VMEM((groups * slots, hid), bf16),
@@ -522,10 +526,12 @@
     messages = [messages[j] for j in range(1, groups)]
     expert_out = forward(scale, hidden, w_quant[0], flight)
     returned = lax.all_to_all(expert_out, "expert", split_axis=0, concat_axis=0, tiled=True)
-    swapped = swap(sibling_rows(chips, [hbm(expert_out)] + early), "expert", 1)
-    pieces = split(chips, swapped)
-    parts = [swap(pieces[j - 1], "dp", j) for j in range(1, groups)]
-    d_gate_up = backward(scale, gate_up, w_quant[0], pieces[0], chips, swapped)
+    sibling, *direct = sort_rows(chips, [hbm(expert_out)] + early)
+    swapped = swap(sibling, "expert", 1)
+    handed = split(swapped)
+    parts = [swap(direct[j - 1], "dp", j) for j in range(1, groups)]
+    parts += [swap(handed[j - 1], "dp", j) for j in range(1, groups)]
+    d_gate_up = backward(scale, gate_up, w_quant[0], handed[0], chips, swapped)
     combined, d_probs = combine(ids, own, d_out, returned)
     d_weight = weight_grad(d_probs, chips, swapped, hidden, parts, messages)
     return (combined, d_probs.T, d_gate_up[None, None], d_weight[None])

time: 50.6 us -> 57.3 us (1.13)
  the two profiles are of different devices: /device:TPU:18 before, /device:TPU:0 now
where the time goes in v6:
time: 57.3 us; the launch traced here: 57.1 us
  starting transfers between devices  23.8 us (42%)
  Pallas kernels  18.9 us (33%)
  waiting for transfers between devices  13.6 us (24%)
  between operations  0.74 us (1%)
    ppermute x13, starting transfers between devices, swap(): return lax.ppermute(value, axis, [(i, i ^ j) for i in range(size)])  19.5 us
    ppermute x13, waiting for transfers between devices, swap(): return lax.ppermute(value, axis, [(i, i ^ j) for i in range(size)])  13.6 us
    pallas_call x1, Pallas kernels, backward(): pl.pallas_call(functools.partial(backward_kernel, flight, groups), out_sh...  5.25 us
    pallas_call x1, Pallas kernels, forward(): pl.pallas_call(functools.partial(forward_kernel, flight, block), out_shap...  4.79 us
    all_to_all x1, starting transfers between devices, shards(): lax.all_to_all(expert_out, 'expert', split_axis=0, concat_axis=0, tiled=T...  4.28 us
    pallas_call x1, Pallas kernels, combine(): pl.pallas_call(functools.partial(combine_kernel, block), out_shape=(pltpu...  3.63 us
    pallas_call x1, Pallas kernels, dispatch(): pl.pallas_call(functools.partial(dispatch_kernel, flight, groups), out_sh...  2.09 us
    pallas_call x1, Pallas kernels, weight_grad(): pl.pallas_call(functools.partial(weight_grad_kernel, half, groups, block)...  1.81 us
  transfers between devices with their start and end apart: 14, of which 2 were waited for; matrix products, arithmetic and copies ran while one was open for 0% of the time, Pallas kernels for 26%

profile of v6, /device:TPU:0, one launch (start us, length us, event | category | flops | bytes accessed | tf_op | source)
XLA Modules:
  0.0 57.1 jit_solution(18119795389105989514)
XLA Ops:
  0.6 2.1 %dispatch.1 = (f32[128,128]{1,0:T(8,128)}, bf16[128,768]{1,0:T(8,128)(2,1)S(1)}, bf16[2,4,16,1024]{3,2,1,0:T(8,128)(2,1)S(1)}, bf16[2,4,16,1024]{3,2,1,0:T(8,128...) custom-call(bf16[128,1536]{1,0:T(8,128)(2,1)} %bitcast.10, ...), custom_call_target="tpu_custom_call" | custom-call | flops 1024 | bytes 1024 | tf_op jit(solution)/shard_map/dispatch/pallas_call | solution.py:147
  2.7 3.0 %collective-permute-start = (bf16[2,4,16,1024]{3,2,1,0:T(8,128)(2,1)S(1)}, bf16[2,4,16,1024]{3,2,1,0:T(8,128)(2,1)S(1)}, u32[]{:S(2)}, u32[]{:S(2)}) collective-permute-start(bf16[2,4,16,1024]{3,2,1,0:T(8,128)(2,1)S(1)} %get-tuple-element.26), channel_id=1, source_target_pairs={{0,2},{1,3},{2,0},{3,1},{4,6},{5,7},{6,4},{7,5},{8,10},{9,11},{10,... | collective-permute-start | bytes 786440 | tf_op jit(solution)/shard_map/ppermute | solution.py:506
  5.7 1.5 %collective-permute-start.1 = (bf16[2,4,16,1024]{3,2,1,0:T(8,128)(2,1)S(1)}, bf16[2,4,16,1024]{3,2,1,0:T(8,128)(2,1)S(1)}, u32[]{:S(2)}, u32[]{:S(2)}) collective-permute-start(bf16[2,4,16,1024]{3,2,1,0:T(8,128)(2,1)S(1)} %get-tuple-element.27), channel_id=1, source_target_pairs={{0,4},{1,5},{2,6},{3,7},{4,0},{5,1},{6,2},{7,3},{8,12},{9,13},{10,... | collective-permute-start | bytes 786440 | tf_op jit(solution)/shard_map/ppermute | solution.py:506
  7.3 0.0 collective-permute-start.2
  7.3 3.0 %collective-permute-start.3 = (bf16[32,16,256]{2,1,0:T(8,128)(2,1)S(1)}, bf16[32,16,256]{2,1,0:T(8,128)(2,1)S(1)}, u32[]{:S(2)}, u32[]{:S(2)}) collective-permute-start(bf16[32,16,256]{2,1,0:T(8,128)(2,1)S(1)} %get-tuple-element.29), channel_id=1, source_target_pairs={{0,16},{8,24},{16,0},{24,8},{1,17},{9,25},{17,1},{25,9},{2,18},{10... | collective-permute-start | bytes 786440 | tf_op jit(solution)/shard_map/ppermute | solution.py:506
  10.3 4.8 %expert_forward.1.refs_4_ = bf16[8,16,4096]{2,1,0:T(8,128)(2,1)} custom-call(bf16[128,768]{1,0:T(8,128)(2,1)S(1)} %get-tuple-element.22.hidden_ref, f32[6,1,32]{2,1,0:T(1,128)} %bitcast.16, bf16[768,4096]{1,0:T(8,128)(2,1)} %bitcast.8), custom_call_target="tpu_custom_call" | custom-call | flops 1024 | bytes 1024 | tf_op jit(solution)/shard_map/expert_forward/pallas_call | solution.py:221
  15.1 4.3 %all-to-all-start = ((bf16[8,16,4096]{2,1,0:T(8,128)(2,1)}), bf16[8,16,4096]{2,1,0:T(8,128)(2,1)}, u32[]{:S(2)}, u32[]{:S(2)}) async-start(bf16[8,16,4096]{2,1,0:T(8,128)(2,1)} %expert_forward.1.refs_4_), calls=%async_computation | async-start | bytes 2097152 | tf_op jit(solution)/shard_map/all_to_all | solution.py:528
  19.4 1.6 %collective-permute-start.4 = (bf16[28,16,256]{2,1,0:T(8,128)(2,1)S(1)}, bf16[28,16,256]{2,1,0:T(8,128)(2,1)S(1)}, u32[]{:S(2)}, u32[]{:S(2)}) collective-permute-start(bf16[28,16,256]{2,1,0:T(8,128)(2,1)S(1)} %get-tuple-element.30), channel_id=1, source_target_pairs={{0,8},{8,0},{16,24},{24,16},{1,9},{9,1},{17,25},{25,17},{2,10},{10... | collective-permute-start | bytes 688136 | tf_op jit(solution)/shard_map/ppermute | solution.py:506
  21.0 6.2 %collective-permute-done.4.refs_6_.refs_10_ = bf16[28,16,256]{2,1,0:T(8,128)(2,1)S(1)} collective-permute-done((bf16[28,16,256]{2,1,0:T(8,128)(2,1)S(1)}, bf16[28,16,256]{2,1,0:T(8,128)(2,1)S(1)}, u32[]{:S(2)}, u32[]{:S(2)}) %collective-permute-start.4) | collective-permute-done | bytes 229408 | tf_op jit(solution)/shard_map/ppermute | solution.py:506
  27.3 0.0 collective-permute-done.2.refs_3_
  27.3 0.0 collective-permute-done.3.refs_5_.refs_11_
  27.3 0.7 %sort_rows.1 = (bf16[4,4,16,1024]{3,2,1,0:T(8,128)(2,1)S(1)}, bf16[3,16,1024]{2,1,0:T(8,128)(2,1)S(1)}, bf16[3,16,1024]{2,1,0:T(8,128)(2,1)S(1)}, bf16[3,16,1024]{2,1,0:T(8,128)(2,1)}) custom-call(bf16[2,4,16,1024]{3,2,1,0:T(8,128)(2,1)S(1)} %get-tuple-element.25.refs_0_, bf16[2,4,16,1024]{3,2,1,0:T(8,128)(2,1)S(1)} %collective-permute-done.refs_1_, ...), custom_call_target="tpu_custom_call" | custom-call | flops 1024 | bytes 1024 | tf_op jit(solution)/shard_map/sort_rows/pallas_call | solution.py:253
  28.0 1.6 %collective-permute-start.12 = (bf16[32,16,256]{2,1,0:T(8,128)(2,1)S(1)}, bf16[32,16,256]{2,1,0:T(8,128)(2,1)S(1)}, u32[]{:S(2)}, u32[]{:S(2)}) collective-permute-start(bf16[32,16,256]{2,1,0:T(8,128)(2,1)S(1)} %collective-permute-done.3.refs_5_.refs_11_), channel_id=1, source_target_pairs={{0,8},{8,0},{16,24},{24,16},{1,9},{9,1},{17,25},{25,17},{2,10},{10... | collective-permute-start | bytes 786440 | tf_op jit(solution)/shard_map/ppermute | solution.py:506
  29.6 0.5 collective-permute-start.6
  30.0 1.3 %collective-permute-start.7 = (bf16[3,16,1024]{2,1,0:T(8,128)(2,1)S(1)}, bf16[3,16,1024]{2,1,0:T(8,128)(2,1)S(1)}, u32[]{:S(2)}, u32[]{:S(2)}) collective-permute-start(bf16[3,16,1024]{2,1,0:T(8,128)(2,1)S(1)} %get-tuple-element.34), channel_id=1, source_target_pairs={{0,16},{8,24},{16,0},{24,8},{1,17},{9,25},{17,1},{25,9},{2,18},{10... | collective-permute-start | bytes 294920 | tf_op jit(solution)/shard_map/ppermute | solution.py:506
  31.3 0.0 collective-permute-done.5.swapped
  31.3 0.7 %split.1 = (bf16[4,16,1024]{2,1,0:T(8,128)(2,1)S(1)}, bf16[4,16,1024]{2,1,0:T(8,128)(2,1)}, bf16[4,16,1024]{2,1,0:T(8,128)(2,1)S(1)}) custom-call(bf16[4,4,16,1024]{3,2,1,0:T(8,128)(2,1)S(1)} %collective-permute-done.5.swapped), custom_call_target="tpu_custom_call" | custom-call | flops 1024 | bytes 1024 | tf_op jit(solution)/shard_map/split/pallas_call | solution.py:272
  32.0 1.6 %collective-permute-start.10 = (bf16[4,16,1024]{2,1,0:T(8,128)(2,1)}, bf16[4,16,1024]{2,1,0:T(8,128)(2,1)S(1)}, u32[]{:S(2)}, u32[]{:S(2)}) collective-permute-start(bf16[4,16,1024]{2,1,0:T(8,128)(2,1)} %get-tuple-element.36), channel_id=1, source_target_pairs={{0,16},{8,24},{16,0},{24,8},{1,17},{9,25},{17,1},{25,9},{2,18},{10... | collective-permute-start | bytes 393224 | tf_op jit(solution)/shard_map/ppermute | solution.py:506
  33.7 2.7 %collective-permute-start.11 = (bf16[4,16,1024]{2,1,0:T(8,128)(2,1)S(1)}, bf16[4,16,1024]{2,1,0:T(8,128)(2,1)S(1)}, u32[]{:S(2)}, u32[]{:S(2)}) collective-permute-start(bf16[4,16,1024]{2,1,0:T(8,128)(2,1)S(1)} %get-tuple-element.37), channel_id=1, source_target_pairs={{0,24},{8,16},{16,8},{24,0},{1,25},{9,17},{17,9},{25,1},{2,26},{10... | collective-permute-start | bytes 393224 | tf_op jit(solution)/shard_map/ppermute | solution.py:506
  36.4 7.4 %collective-permute-done.6.refs_4_ = bf16[3,16,1024]{2,1,0:T(8,128)(2,1)S(1)} collective-permute-done((bf16[3,16,1024]{2,1,0:T(8,128)(2,1)S(1)}, bf16[3,16,1024]{2,1,0:T(8,128)(2,1)S(1)}, u32[]{:S(2)}, u32[]{:S(2)}) %collective-permute-start.6) | collective-permute-done | bytes 98336 | tf_op jit(solution)/shard_map/ppermute | solution.py:506
  43.8 2.6 %collective-permute-start.8 = (bf16[3,16,1024]{2,1,0:T(8,128)(2,1)}, bf16[3,16,1024]{2,1,0:T(8,128)(2,1)S(1)}, u32[]{:S(2)}, u32[]{:S(2)}) collective-permute-start(bf16[3,16,1024]{2,1,0:T(8,128)(2,1)} %get-tuple-element.35), channel_id=1, source_target_pairs={{0,24},{8,16},{16,8},{24,0},{1,25},{9,17},{17,9},{25,1},{2,26},{10... | collective-permute-start | bytes 294920 | tf_op jit(solution)/shard_map/ppermute | solution.py:506
  46.3 5.2 %expert_backward.1 = bf16[128,1536]{1,0:T(8,128)(2,1)} custom-call(f32[6,1,32]{2,1,0:T(1,128)} %bitcast.17, bf16[128,1536]{1,0:T(8,128)(2,1)} %bitcast.11, bf16[768,4096]{1,0:T(8,128)(2,1)} %bitcast.9, bf16[4,16,1024]{2,1,0:T(8,128)(2,1)S(1)} %get-tuple-element.32.tie_ref, bf16[4,4,16,1024]{3,2,1,0:T(8,128)(2,1)S(1)} %collective-permute-done.5.swapped, ...), custom_call_target="tpu_custom_call" | custom-call | flops 1024 | bytes 1024 | tf_op jit(solution)/shard_map/expert_backward/pallas_call | solution.py:356
  51.6 3.6 %combine.1 = (bf16[128,4096]{1,0:T(8,128)(2,1)}, f32[8,128]{1,0:T(8,128)}) custom-call(s32[8,128]{1,0:T(8,128)} %bitcast.15, f32[128,128]{1,0:T(8,128)} %get-tuple-element.21.own_hbm, bf16[128,4096]{1,0:T(8,128)(2,1)} %dout_hbm.3, bf16[8,16,4096]{2,1,0:T(8,128)(2,1)} %all-to-all-done.ret_hbm), custom_call_target="tpu_custom_call" | custom-call | flops 1024 | bytes 1024 | tf_op jit(solution)/shard_map/combine/pallas_call | solution.py:422
  55.3 1.8 %weight_grad.1 = bf16[1024,768]{1,0:T(8,128)(2,1)} custom-call(f32[8,128]{1,0:T(8,128)} %get-tuple-element.24.tie_ref, bf16[4,4,16,1024]{3,2,1,0:T(8,128)(2,1)S(1)} %collective-permute-done.5.swapped, bf16[128,768]{1,0:T(8,128)(2,1)S(1)} %get-tuple-element.22.hidden_ref, bf16[2,4,16,1024]{3,2,1,0:T(8,128)(2,1)S(1)} %get-tuple-element.25.refs_0_, ...), custom_call_target="tpu_custom_call" | custom-call | flops 1024 | bytes 1024 | tf_op jit(solution)/shard_map/weight_grad/pallas_call | solution.py:487
  (11 shorter events, 0.0 us)
Async XLA Ops:
  2.7 24.6 %collective-permute-start = (bf16[2,4,16,1024]{3,2,1,0:T(8,128)(2,1)S(1)}, bf16[2,4,16,1024]{3,2,1,0:T(8,128)(2,1)S(1)}, u32[]{:S(2)}, u32[]{:S(2)}) collective-permute-start(bf16[2,4,16,1024]{3,2,1,0:T(8,128)(2,1)S(1)} %get-tuple-element.26), channel_id=1, source_target_pairs={{0,2},{1,3},{2,0},{3,1},{4,6},{5,7},{6,4},{7,5},{8,10},{9,11},{10,... | collective-permute-start | bytes 786440 | tf_op jit(solution)/shard_map/ppermute | solution.py:506
  5.7 21.6 %collective-permute-start.1 = (bf16[2,4,16,1024]{3,2,1,0:T(8,128)(2,1)S(1)}, bf16[2,4,16,1024]{3,2,1,0:T(8,128)(2,1)S(1)}, u32[]{:S(2)}, u32[]{:S(2)}) collective-permute-start(bf16[2,4,16,1024]{3,2,1,0:T(8,128)(2,1)S(1)} %get-tuple-element.27), channel_id=1, source_target_pairs={{0,4},{1,5},{2,6},{3,7},{4,0},{5,1},{6,2},{7,3},{8,12},{9,13},{10,... | collective-permute-start | bytes 786440 | tf_op jit(solution)/shard_map/ppermute | solution.py:506
  7.3 20.0 %collective-permute-start.2 = (bf16[2,4,16,1024]{3,2,1,0:T(8,128)(2,1)S(1)}, bf16[2,4,16,1024]{3,2,1,0:T(8,128)(2,1)S(1)}, u32[]{:S(2)}, u32[]{:S(2)}) collective-permute-start(bf16[2,4,16,1024]{3,2,1,0:T(8,128)(2,1)S(1)} %get-tuple-element.28), channel_id=1, source_target_pairs={{0,6},{1,7},{2,4},{3,5},{4,2},{5,3},{6,0},{7,1},{8,14},{9,15},{10,... | collective-permute-start | bytes 786440 | tf_op jit(solution)/shard_map/ppermute | solution.py:506
  7.3 20.0 %collective-permute-start.3 = (bf16[32,16,256]{2,1,0:T(8,128)(2,1)S(1)}, bf16[32,16,256]{2,1,0:T(8,128)(2,1)S(1)}, u32[]{:S(2)}, u32[]{:S(2)}) collective-permute-start(bf16[32,16,256]{2,1,0:T(8,128)(2,1)S(1)} %get-tuple-element.29), channel_id=1, source_target_pairs={{0,16},{8,24},{16,0},{24,8},{1,17},{9,25},{17,1},{25,9},{2,18},{10... | collective-permute-start | bytes 786440 | tf_op jit(solution)/shard_map/ppermute | solution.py:506
  15.1 36.5 %all-to-all-start = ((bf16[8,16,4096]{2,1,0:T(8,128)(2,1)}), bf16[8,16,4096]{2,1,0:T(8,128)(2,1)}, u32[]{:S(2)}, u32[]{:S(2)}) async-start(bf16[8,16,4096]{2,1,0:T(8,128)(2,1)} %expert_forward.1.refs_4_), calls=%async_computation | async-start | bytes 2097152 | tf_op jit(solution)/shard_map/all_to_all | solution.py:528
  19.4 7.9 %collective-permute-start.4 = (bf16[28,16,256]{2,1,0:T(8,128)(2,1)S(1)}, bf16[28,16,256]{2,1,0:T(8,128)(2,1)S(1)}, u32[]{:S(2)}, u32[]{:S(2)}) collective-permute-start(bf16[28,16,256]{2,1,0:T(8,128)(2,1)S(1)} %get-tuple-element.30), channel_id=1, source_target_pairs={{0,8},{8,0},{16,24},{24,16},{1,9},{9,1},{17,25},{25,17},{2,10},{10... | collective-permute-start | bytes 688136 | tf_op jit(solution)/shard_map/ppermute | solution.py:506
  28.0 3.3 %collective-permute-start.5 = (bf16[4,4,16,1024]{3,2,1,0:T(8,128)(2,1)S(1)}, bf16[4,4,16,1024]{3,2,1,0:T(8,128)(2,1)S(1)}, u32[]{:S(2)}, u32[]{:S(2)}) collective-permute-start(bf16[4,4,16,1024]{3,2,1,0:T(8,128)(2,1)S(1)} %get-tuple-element.31), channel_id=1, source_target_pairs={{0,1},{1,0},{2,3},{3,2},{4,5},{5,4},{6,7},{7,6},{8,9},{9,8},{10,11... | collective-permute-start | bytes 1572872 | tf_op jit(solution)/shard_map/ppermute | solution.py:506
  28.0 27.2 %collective-permute-start.12 = (bf16[32,16,256]{2,1,0:T(8,128)(2,1)S(1)}, bf16[32,16,256]{2,1,0:T(8,128)(2,1)S(1)}, u32[]{:S(2)}, u32[]{:S(2)}) collective-permute-start(bf16[32,16,256]{2,1,0:T(8,128)(2,1)S(1)} %collective-permute-done.3.refs_5_.refs_11_), channel_id=1, source_target_pairs={{0,8},{8,0},{16,24},{24,16},{1,9},{9,1},{17,25},{25,17},{2,10},{10... | collective-permute-start | bytes 786440 | tf_op jit(solution)/shard_map/ppermute | solution.py:506
  29.6 14.2 %collective-permute-start.6 = (bf16[3,16,1024]{2,1,0:T(8,128)(2,1)S(1)}, bf16[3,16,1024]{2,1,0:T(8,128)(2,1)S(1)}, u32[]{:S(2)}, u32[]{:S(2)}) collective-permute-start(bf16[3,16,1024]{2,1,0:T(8,128)(2,1)S(1)} %get-tuple-element.33), channel_id=1, source_target_pairs={{0,8},{8,0},{16,24},{24,16},{1,9},{9,1},{17,25},{25,17},{2,10},{10... | collective-permute-start | bytes 294920 | tf_op jit(solution)/shard_map/ppermute | solution.py:506
  30.0 13.7 %collective-permute-start.7 = (bf16[3,16,1024]{2,1,0:T(8,128)(2,1)S(1)}, bf16[3,16,1024]{2,1,0:T(8,128)(2,1)S(1)}, u32[]{:S(2)}, u32[]{:S(2)}) collective-permute-start(bf16[3,16,1024]{2,1,0:T(8,128)(2,1)S(1)} %get-tuple-element.34), channel_id=1, source_target_pairs={{0,16},{8,24},{16,0},{24,8},{1,17},{9,25},{17,1},{25,9},{2,18},{10... | collective-permute-start | bytes 294920 | tf_op jit(solution)/shard_map/ppermute | solution.py:506
  32.0 23.2 %collective-permute-start.10 = (bf16[4,16,1024]{2,1,0:T(8,128)(2,1)}, bf16[4,16,1024]{2,1,0:T(8,128)(2,1)S(1)}, u32[]{:S(2)}, u32[]{:S(2)}) collective-permute-start(bf16[4,16,1024]{2,1,0:T(8,128)(2,1)} %get-tuple-element.36), channel_id=1, source_target_pairs={{0,16},{8,24},{16,0},{24,8},{1,17},{9,25},{17,1},{25,9},{2,18},{10... | collective-permute-start | bytes 393224 | tf_op jit(solution)/shard_map/ppermute | solution.py:506
  33.7 21.6 %collective-permute-start.11 = (bf16[4,16,1024]{2,1,0:T(8,128)(2,1)S(1)}, bf16[4,16,1024]{2,1,0:T(8,128)(2,1)S(1)}, u32[]{:S(2)}, u32[]{:S(2)}) collective-permute-start(bf16[4,16,1024]{2,1,0:T(8,128)(2,1)S(1)} %get-tuple-element.37), channel_id=1, source_target_pairs={{0,24},{8,16},{16,8},{24,0},{1,25},{9,17},{17,9},{25,1},{2,26},{10... | collective-permute-start | bytes 393224 | tf_op jit(solution)/shard_map/ppermute | solution.py:506
  43.8 11.5 %collective-permute-start.9 = (bf16[4,16,1024]{2,1,0:T(8,128)(2,1)S(1)}, bf16[4,16,1024]{2,1,0:T(8,128)(2,1)S(1)}, u32[]{:S(2)}, u32[]{:S(2)}) collective-permute-start(bf16[4,16,1024]{2,1,0:T(8,128)(2,1)S(1)} %get-tuple-element.32.tie_ref), channel_id=1, source_target_pairs={{0,8},{8,0},{16,24},{24,16},{1,9},{9,1},{17,25},{25,17},{2,10},{10... | collective-permute-start | bytes 393224 | tf_op jit(solution)/shard_map/ppermute | solution.py:506
  43.8 11.5 %collective-permute-start.8 = (bf16[3,16,1024]{2,1,0:T(8,128)(2,1)}, bf16[3,16,1024]{2,1,0:T(8,128)(2,1)S(1)}, u32[]{:S(2)}, u32[]{:S(2)}) collective-permute-start(bf16[3,16,1024]{2,1,0:T(8,128)(2,1)} %get-tuple-element.35), channel_id=1, source_target_pairs={{0,24},{8,16},{16,8},{24,0},{1,25},{9,17},{17,9},{25,1},{2,26},{10... | collective-permute-start | bytes 294920 | tf_op jit(solution)/shard_map/ppermute | solution.py:506

commit v7 on v6

--- a/solution.py
+++ b/solution.py
@@ -242,9 +242,9 @@
     chips, (sibling, *pieces) = refs[:half], refs[half + ties :]
     for c in range(half):
         sibling[c] = chips[c][1]
-        for j in range(1, groups):
+        for j in range(2, groups):
             if c:
-                pieces[j - 1][c - 1] = chips[c][0, j]
+                pieces[j - 2][c - 1] = chips[c][0, j]
 
 
 def sort_rows(chips, ties):
@@ -253,31 +253,46 @@
     return pl.pallas_call(
         functools.partial(sort_kernel, half, groups, len(ties)),
         out_shape=(pltpu.VMEM((half, groups, cap, share), bf16),)
-        + (pltpu.VMEM((half - 1, cap, share), bf16),) * (groups - 1),
+        + (pltpu.VMEM((half - 1, cap, share), bf16),) * (groups - 2),
         in_specs=[VMEM] * half + [ANY] * len(ties),
-        out_specs=(VMEM,) * groups,
+        out_specs=(VMEM,) * (groups - 1),
         compiler_params=params(2 * half * CAP),
         cost_estimate=SMALL,
         name="sort_rows",
     )(*chips, *ties)
 
 
-def split_kernel(groups, swapped, *pieces):
-    for j in range(1, groups):
-        pieces[j - 1][...] = swapped[:, j]
-
-
-def split(swapped):
+def split_kernel(half, groups, count, swapped, *refs):
+    chips, messages = refs[: half - 1], refs[half - 1 : half - 1 + count]
+    near, *pieces = refs[half - 1 + count :]
+    wide = swapped.shape[3] // TILE
+    for j in range(2, groups):
+        pieces[j - 2][...] = swapped[:, j]
+    for r in range(2 * half - 1):
+        for q in range(wide):
+            cols = slice(q * TILE, (q + 1) * TILE)
+            near[r * wide + q] = (
+                chips[r][0, 1, :, cols] if r < half - 1 else swapped[r - half + 1, 1, :, cols]
+            )
+    first = (2 * half - 1) * wide
+    for message in messages:
+        near[first : first + message.shape[0]] = message[...]
+        first += message.shape[0]
+
+
+def split(swapped, chips, messages):
     half, groups, cap, share = swapped.shape
-    return pl.pallas_call(
-        functools.partial(split_kernel, groups),
-        out_shape=(pltpu.VMEM((half, cap, share), bf16),) * (groups - 1),
-        in_specs=[VMEM],
+    tiles = (2 * half - 1) * (share // TILE) + sum(message.shape[0] for message in messages)
+    return pl.pallas_call(
+        functools.partial(split_kernel, half, groups, len(messages)),
+        out_shape=(pltpu.VMEM((tiles, cap, TILE), bf16),)
+        + (pltpu.VMEM((half, cap, share), bf16),) * (groups - 2),
+        in_specs=[VMEM] * (half + len(messages)),
         out_specs=(VMEM,) * (groups - 1),
         compiler_params=params(2 * half * CAP),
         cost_estimate=SMALL,
         name="split",
-    )(swapped)
+    )(swapped, *chips[1:], *messages)
 
 
 def backward_kernel(flight, groups, scale_hbm, gate_up_hbm, quant_hbm, tie_ref, swapped, *refs):
@@ -440,26 +455,33 @@
     )(hbm(ids), hbm(own), hbm(d_out), hbm(returned))
 
 
-def weight_grad_kernel(half, groups, block, tie_ref, swapped, hidden_ref, *refs):
-    others = groups - 1
-    chips, parts, refs = refs[:half], refs[half : half + 2 * others], refs[half + 2 * others :]
-    messages, (out_hbm, hidden, own, out, out_sems) = refs[:others], refs[others:]
-    cap, share = parts[0].shape[1:]
+def weight_grad_kernel(half, groups, block, tie_ref, swapped, hidden_ref, near, *refs):
+    chips, refs = refs[:half], refs[half:]
+    direct, handed, refs = refs[: groups - 2], refs[groups - 2 : 2 * groups - 4], refs[2 * groups - 4 :]
+    messages, (out_hbm, hidden, own, rows, out, out_sems) = refs[: groups // 2], refs[groups // 2 :]
+    cap, share = rows.shape[1:]
     flight = 2 * half
     slots = flight * cap
-    wide = hidden_ref.shape[1] // TILE
+    wide, tall = hidden_ref.shape[1] // TILE, share // TILE
+    for r in range(flight - 1):
+        for q in range(tall):
+            rows[r, :, q * TILE : (q + 1) * TILE] = near[r * tall + q]
     hidden[:slots, :] = hidden_ref[...]
+    passed = (flight - 1) * tall
     for j in range(1, groups):
         bit = max(b for b in bits_of(groups) if b <= j)
-        message = messages[j - 1]
+        message, first = messages[j // 2], 0
+        if j > 1 and j % 2:
+            message, first = near, passed
+            passed += messages[j // 2].shape[0]
         for r in range(flight):
             for q in range(wide):
                 hidden[
                     j * slots + r * cap : j * slots + (r + 1) * cap, q * TILE : (q + 1) * TILE
-                ] = message[r * wide + q]
-        for q in range(share // TILE):
+                ] = message[first + r * wide + q]
+        for q in range(tall):
             own[j - 1, :, q * TILE : (q + 1) * TILE] = message[
-                flight * wide + (j - bit) * (share // TILE) + q
+                first + flight * wide + (j - bit) * tall + q
             ]
     stores = []
     for n, cols in enumerate(chunks(share, block)):
@@ -467,8 +489,11 @@
         grads += [swapped[c, 0, :, cols] for c in range(half)]
         for j in range(1, groups):
             grads.append(own[j - 1, :, cols])
-            grads.append(parts[j - 1][:, :, cols].reshape(slots // 2 - cap, block))
-            grads.append(parts[others + j - 1][:, :, cols].reshape(slots // 2, block))
+            if j == 1:
+                grads.append(rows[:, :, cols].reshape(slots - cap, block))
+            else:
+                grads.append(direct[j - 2][:, :, cols].reshape(slots // 2 - cap, block))
+                grads.append(handed[j - 2][:, :, cols].reshape(slots // 2, block))
         out[cols, :] = lax.dot_general(
             jnp.concatenate(grads, axis=0),
             hidden[...],
@@ -481,24 +506,26 @@
         copy.wait()
 
 
-def weight_grad(tie, chips, swapped, hidden, parts, messages, block=256):
+def weight_grad(tie, chips, swapped, hidden, near, direct, handed, messages, block=256):
     half, groups, cap, share = swapped.shape
     slots, hid = hidden.shape
+    operands = [swapped, hidden, near, *chips, *direct, *handed, *messages]
     return pl.pallas_call(
         functools.partial(weight_grad_kernel, half, groups, block),
         out_shape=pltpu.HBM((share, hid), bf16),
-        in_specs=[HBM] + [VMEM] * (half + 3 * groups - 1),
+        in_specs=[HBM] + [VMEM] * len(operands),
         out_specs=HBM,
         scratch_shapes=[
             pltpu.VMEM((groups * slots, hid), bf16),
             pltpu.VMEM((groups - 1, cap, share), bf16),
+            pltpu.VMEM((2 * half - 1, cap, share), bf16),
             pltpu.VMEM((share, hid), bf16),
             pltpu.SemaphoreType.DMA((share // block,)),
         ],
         compiler_params=params(slots),
         cost_estimate=SMALL,
         name="weight_grad",
-    )(hbm(tie), swapped, hidden, *chips, *parts, *messages)
+    )(hbm(tie), *operands)
 
 
 def swap(value, axis, j):
@@ -519,21 +546,26 @@
     chips = rest[:1] + [swap(rest[c], "expert", 2 * c) for c in range(1, half)]
     messages, early = {}, []
     for bit, message in zip(bits, rest[half:]):
-        for j in sorted(messages):
-            messages[j ^ bit] = swap(messages[j], "dp", bit)
+        if bit > 1:
+            for j in sorted(messages):
+                messages[j ^ bit] = swap(messages[j], "dp", bit)
         messages[bit] = swap(message, "dp", bit)
         early.append(messages[bit])
-    messages = [messages[j] for j in range(1, groups)]
+    passed = [messages[j] for j in range(2, groups, 2)]
     expert_out = forward(scale, hidden, w_quant[0], flight)
     returned = lax.all_to_all(expert_out, "expert", split_axis=0, concat_axis=0, tiled=True)
     sibling, *direct = sort_rows(chips, [hbm(expert_out)] + early)
     swapped = swap(sibling, "expert", 1)
-    handed = split(swapped)
-    parts = [swap(direct[j - 1], "dp", j) for j in range(1, groups)]
-    parts += [swap(handed[j - 1], "dp", j) for j in range(1, groups)]
-    d_gate_up = backward(scale, gate_up, w_quant[0], handed[0], chips, swapped)
+    near, *handed = split(swapped, chips, passed)
+    tie = near
+    near = swap(near, "dp", 1)
+    direct = [swap(direct[j - 2], "dp", j) for j in range(2, groups)]
+    handed = [swap(handed[j - 2], "dp", j) for j in range(2, groups)]
+    d_gate_up = backward(scale, gate_up, w_quant[0], tie, chips, swapped)
     combined, d_probs = combine(ids, own, d_out, returned)
-    d_weight = weight_grad(d_probs, chips, swapped, hidden, parts, messages)
+    d_weight = weight_grad(
+        d_probs, chips, swapped, hidden, near, direct, handed, [messages[1]] + passed
+    )
     return (combined, d_probs.T, d_gate_up[None, None], d_weight[None])
 
 

time: 57.3 us -> 56.1 us (0.979)
  starting transfers between devices: 23.8 us -> 21.4 us
  local copies, waits for them, and re-layouts: 0 us -> 1.27 us
    ppermute x13 -> x11, starting transfers between devices: 19.5 us -> 17.1 us  [swap(): return lax.ppermute(value, axis, [(i, i ^ j) for i in range(size)])]
    ppermute x13 -> x11, waiting for transfers between devices: 13.6 us -> 11.8 us  [swap(): return lax.ppermute(value, axis, [(i, i ^ j) for i in range(size)])]
    all_to_all x1, waiting for transfers between devices: 0.01 us -> 1.45 us  [shards(): lax.all_to_all(expert_out, 'expert', split_axis=0, concat_axis=0, tiled=T...]
    unnamed x0 -> x4, local copies, waits for them, and re-layouts: none -> 1.27 us
    pallas_call x1, Pallas kernels: 1.81 us -> 2.74 us  [weight_grad(): pl.pallas_call(functools.partial(weight_grad_kernel, half, groups, block)...]
    pallas_call x1, Pallas kernels: 0.71 us -> 0.05 us  [sort_rows(): pl.pallas_call(functools.partial(sort_kernel, half, groups, len(ties)), o...]
  transfers between devices with their start and end apart: 14 -> 12, of which waited for: 2 -> 5; matrix products, arithmetic and copies ran while one was open for 0% -> 0% of each run, Pallas kernels for 26% -> 26%
where the time goes in v7:
time: 56.1 us; the launch traced here: 55.9 us
  starting transfers between devices  21.4 us (38%)
  Pallas kernels  19.3 us (34%)
  waiting for transfers between devices  13.2 us (24%)
  local copies, waits for them, and re-layouts  1.27 us (2%)
  between operations  0.71 us (1%)
    ppermute x11, starting transfers between devices, swap(): return lax.ppermute(value, axis, [(i, i ^ j) for i in range(size)])  17.1 us
    ppermute x11, waiting for transfers between devices, swap(): return lax.ppermute(value, axis, [(i, i ^ j) for i in range(size)])  11.8 us
    pallas_call x1, Pallas kernels, backward(): pl.pallas_call(functools.partial(backward_kernel, flight, groups), out_sh...  5.24 us
    pallas_call x1, Pallas kernels, forward(): pl.pallas_call(functools.partial(forward_kernel, flight, block), out_shap...  4.78 us
    all_to_all x1, starting transfers between devices, shards(): lax.all_to_all(expert_out, 'expert', split_axis=0, concat_axis=0, tiled=T...  4.27 us
    pallas_call x1, Pallas kernels, combine(): pl.pallas_call(functools.partial(combine_kernel, block), out_shape=(pltpu...  3.63 us
    pallas_call x1, Pallas kernels, weight_grad(): pl.pallas_call(functools.partial(weight_grad_kernel, half, groups, block)...  2.74 us
    pallas_call x1, Pallas kernels, dispatch(): pl.pallas_call(functools.partial(dispatch_kernel, flight, groups), out_sh...  2.09 us
  transfers between devices with their start and end apart: 12, of which 5 were waited for; matrix products, arithmetic and copies ran while one was open for 0% of the time, Pallas kernels for 26%

profile of v7, /device:TPU:0, one launch (start us, length us, event | category | flops | bytes accessed | tf_op | source)
XLA Modules:
  0.0 55.9 jit_solution(5746797057290073913)
XLA Ops:
  0.6 2.1 %dispatch.1 = (f32[128,128]{1,0:T(8,128)}, bf16[128,768]{1,0:T(8,128)(2,1)S(1)}, bf16[2,4,16,1024]{3,2,1,0:T(8,128)(2,1)S(1)}, bf16[2,4,16,1024]{3,2,1,0:T(8,128...) custom-call(bf16[128,1536]{1,0:T(8,128)(2,1)} %bitcast.11, ...), custom_call_target="tpu_custom_call" | custom-call | flops 1024 | bytes 1024 | tf_op jit(solution)/shard_map/dispatch/pallas_call | solution.py:147
  2.7 3.0 %collective-permute-start = (bf16[2,4,16,1024]{3,2,1,0:T(8,128)(2,1)S(1)}, bf16[2,4,16,1024]{3,2,1,0:T(8,128)(2,1)S(1)}, u32[]{:S(2)}, u32[]{:S(2)}) collective-permute-start(bf16[2,4,16,1024]{3,2,1,0:T(8,128)(2,1)S(1)} %get-tuple-element.25), channel_id=1, source_target_pairs={{0,2},{1,3},{2,0},{3,1},{4,6},{5,7},{6,4},{7,5},{8,10},{9,11},{10,... | collective-permute-start | bytes 786440 | tf_op jit(solution)/shard_map/ppermute | solution.py:533
  5.7 1.5 %collective-permute-start.1 = (bf16[2,4,16,1024]{3,2,1,0:T(8,128)(2,1)S(1)}, bf16[2,4,16,1024]{3,2,1,0:T(8,128)(2,1)S(1)}, u32[]{:S(2)}, u32[]{:S(2)}) collective-permute-start(bf16[2,4,16,1024]{3,2,1,0:T(8,128)(2,1)S(1)} %get-tuple-element.26), channel_id=1, source_target_pairs={{0,4},{1,5},{2,6},{3,7},{4,0},{5,1},{6,2},{7,3},{8,12},{9,13},{10,... | collective-permute-start | bytes 786440 | tf_op jit(solution)/shard_map/ppermute | solution.py:533
  7.3 0.0 collective-permute-start.2
  7.3 3.0 %collective-permute-start.3 = (bf16[32,16,256]{2,1,0:T(8,128)(2,1)S(1)}, bf16[32,16,256]{2,1,0:T(8,128)(2,1)S(1)}, u32[]{:S(2)}, u32[]{:S(2)}) collective-permute-start(bf16[32,16,256]{2,1,0:T(8,128)(2,1)S(1)} %get-tuple-element.28), channel_id=1, source_target_pairs={{0,16},{8,24},{16,0},{24,8},{1,17},{9,25},{17,1},{25,9},{2,18},{10... | collective-permute-start | bytes 786440 | tf_op jit(solution)/shard_map/ppermute | solution.py:533
  10.3 1.6 %collective-permute-start.4 = (bf16[28,16,256]{2,1,0:T(8,128)(2,1)S(1)}, bf16[28,16,256]{2,1,0:T(8,128)(2,1)S(1)}, u32[]{:S(2)}, u32[]{:S(2)}) collective-permute-start(bf16[28,16,256]{2,1,0:T(8,128)(2,1)S(1)} %get-tuple-element.29), channel_id=1, source_target_pairs={{0,8},{8,0},{16,24},{24,16},{1,9},{9,1},{17,25},{25,17},{2,10},{10... | collective-permute-start | bytes 688136 | tf_op jit(solution)/shard_map/ppermute | solution.py:533
  11.9 4.8 %expert_forward.1.refs_4_ = bf16[8,16,4096]{2,1,0:T(8,128)(2,1)} custom-call(bf16[128,768]{1,0:T(8,128)(2,1)S(1)} %get-tuple-element.21.hidden_ref, f32[6,1,32]{2,1,0:T(1,128)} %bitcast.16, bf16[768,4096]{1,0:T(8,128)(2,1)} %bitcast.8), custom_call_target="tpu_custom_call" | custom-call | flops 1024 | bytes 1024 | tf_op jit(solution)/shard_map/expert_forward/pallas_call | solution.py:221
  16.7 3.3 %collective-permute-done.4.refs_6_.refs_8_ = bf16[28,16,256]{2,1,0:T(8,128)(2,1)S(1)} collective-permute-done((bf16[28,16,256]{2,1,0:T(8,128)(2,1)S(1)}, bf16[28,16,256]{2,1,0:T(8,128)(2,1)S(1)}, u32[]{:S(2)}, u32[]{:S(2)}) %collective-permute-start.4) | collective-permute-done | bytes 229408 | tf_op jit(solution)/shard_map/ppermute | solution.py:533
  20.0 1.4 %collective-permute-done.3.refs_5_.refs_3_.refs_9_ = bf16[32,16,256]{2,1,0:T(8,128)(2,1)S(1)} collective-permute-done((bf16[32,16,256]{2,1,0:T(8,128)(2,1)S(1)}, bf16[32,16,256]{2,1,0:T(8,128)(2,1)S(1)}, u32[]{:S(2)}, u32[]{:S(2)}) %collective-permute-start.3) | collective-permute-done | bytes 262176 | tf_op jit(solution)/shard_map/ppermute | solution.py:533
  21.5 0.6 %copy-done = bf16[3,16,1024]{2,1,0:T(8,128)(2,1)} copy-done((bf16[3,16,1024]{2,1,0:T(8,128)(2,1)}, bf16[3,16,1024]{2,1,0:T(8,128)(2,1)S(1)}, u32[]{:S(2)}) %copy-start) | copy-done | bytes 98328
  22.1 0.6 %copy-done.1 = bf16[3,16,1024]{2,1,0:T(8,128)(2,1)} copy-done((bf16[3,16,1024]{2,1,0:T(8,128)(2,1)}, bf16[3,16,1024]{2,1,0:T(8,128)(2,1)S(1)}, u32[]{:S(2)}) %copy-start.1) | copy-done | bytes 98328
  22.7 4.3 %all-to-all-start = ((bf16[8,16,4096]{2,1,0:T(8,128)(2,1)}), bf16[8,16,4096]{2,1,0:T(8,128)(2,1)}, u32[]{:S(2)}, u32[]{:S(2)}) async-start(bf16[8,16,4096]{2,1,0:T(8,128)(2,1)} %expert_forward.1.refs_4_), calls=%async_computation | async-start | bytes 2097152 | tf_op jit(solution)/shard_map/all_to_all | solution.py:556
  27.0 0.8 %split.1 = (bf16[60,16,256]{2,1,0:T(8,128)(2,1)S(1)}, bf16[4,16,1024]{2,1,0:T(8,128)(2,1)}, bf16[4,16,1024]{2,1,0:T(8,128)(2,1)}) custom-call(bf16[4,4,16,1024]{3,2,1,0:T(8,128)(2,1)S(1)} %collective-permute-done.5.swapped, bf16[2,4,16,1024]{3,2,1,0:T(8,128)(2,1)S(1)} %collective-permute-done.refs_1_.refs_0_, ...), custom_call_target="tpu_custom_call" | custom-call | flops 1024 | bytes 1024 | tf_op jit(solution)/shard_map/split/pallas_call | solution.py:286
  27.8 1.1 %collective-permute-start.6 = (bf16[60,16,256]{2,1,0:T(8,128)(2,1)S(1)}, bf16[60,16,256]{2,1,0:T(8,128)(2,1)S(1)}, u32[]{:S(2)}, u32[]{:S(2)}) collective-permute-start(bf16[60,16,256]{2,1,0:T(8,128)(2,1)S(1)} %get-tuple-element.31.tie_ref), channel_id=1, source_target_pairs={{0,8},{8,0},{16,24},{24,16},{1,9},{9,1},{17,25},{25,17},{2,10},{10... | collective-permute-start | bytes 1474568 | tf_op jit(solution)/shard_map/ppermute | solution.py:533
  28.9 3.0 %collective-permute-start.9 = (bf16[4,16,1024]{2,1,0:T(8,128)(2,1)}, bf16[4,16,1024]{2,1,0:T(8,128)(2,1)S(1)}, u32[]{:S(2)}, u32[]{:S(2)}) collective-permute-start(bf16[4,16,1024]{2,1,0:T(8,128)(2,1)} %get-tuple-element.34), channel_id=1, source_target_pairs={{0,16},{8,24},{16,0},{24,8},{1,17},{9,25},{17,1},{25,9},{2,18},{10... | collective-permute-start | bytes 393224 | tf_op jit(solution)/shard_map/ppermute | solution.py:533
  31.9 0.3 collective-permute-start.10
  32.2 1.2 %collective-permute-start.7 = (bf16[3,16,1024]{2,1,0:T(8,128)(2,1)}, bf16[3,16,1024]{2,1,0:T(8,128)(2,1)}, u32[]{:S(2)}, u32[]{:S(2)}) collective-permute-start(bf16[3,16,1024]{2,1,0:T(8,128)(2,1)} %copy-done.1), channel_id=1, source_target_pairs={{0,16},{8,24},{16,0},{24,8},{1,17},{9,25},{17,1},{25,9},{2,18},{10... | collective-permute-start | bytes 294920 | tf_op jit(solution)/shard_map/ppermute | solution.py:533
  33.4 2.4 %collective-permute-start.8 = (bf16[3,16,1024]{2,1,0:T(8,128)(2,1)}, bf16[3,16,1024]{2,1,0:T(8,128)(2,1)}, u32[]{:S(2)}, u32[]{:S(2)}) collective-permute-start(bf16[3,16,1024]{2,1,0:T(8,128)(2,1)} %copy-done), channel_id=1, source_target_pairs={{0,24},{8,16},{16,8},{24,0},{1,25},{9,17},{17,9},{25,1},{2,26},{10... | collective-permute-start | bytes 294920 | tf_op jit(solution)/shard_map/ppermute | solution.py:533
  35.7 5.2 %expert_backward.1 = bf16[128,1536]{1,0:T(8,128)(2,1)} custom-call(f32[6,1,32]{2,1,0:T(1,128)} %bitcast.17, bf16[128,1536]{1,0:T(8,128)(2,1)} %bitcast.12, bf16[768,4096]{1,0:T(8,128)(2,1)} %bitcast.9, bf16[60,16,256]{2,1,0:T(8,128)(2,1)S(1)} %get-tuple-element.31.tie_ref, bf16[4,4,16,1024]{3,2,1,0:T(8,128)(2,1)S(1)} %collective-permute-done.5.swapped, ...), custom_call_target="tpu_custom_call" | custom-call | flops 1024 | bytes 1024 | tf_op jit(solution)/shard_map/expert_backward/pallas_call | solution.py:371
  41.0 1.4 %all-to-all-done.ret_hbm = bf16[8,16,4096]{2,1,0:T(8,128)(2,1)} async-done(((bf16[8,16,4096]{2,1,0:T(8,128)(2,1)}), bf16[8,16,4096]{2,1,0:T(8,128)(2,1)}, u32[]{:S(2)}, u32[]{:S(2)}) %all-to-all-start) | async-done | bytes 1048608 | tf_op jit(solution)/shard_map/all_to_all | solution.py:556
  42.4 3.6 %combine.1 = (bf16[128,4096]{1,0:T(8,128)(2,1)}, f32[8,128]{1,0:T(8,128)}) custom-call(s32[8,128]{1,0:T(8,128)} %bitcast.15, f32[128,128]{1,0:T(8,128)} %get-tuple-element.20.own_hbm, bf16[128,4096]{1,0:T(8,128)(2,1)} %dout_hbm.3, bf16[8,16,4096]{2,1,0:T(8,128)(2,1)} %all-to-all-done.ret_hbm), custom_call_target="tpu_custom_call" | custom-call | flops 1024 | bytes 1024 | tf_op jit(solution)/shard_map/combine/pallas_call | solution.py:437
  46.1 2.3 %collective-permute-done.7.refs_4_ = bf16[3,16,1024]{2,1,0:T(8,128)(2,1)} collective-permute-done((bf16[3,16,1024]{2,1,0:T(8,128)(2,1)}, bf16[3,16,1024]{2,1,0:T(8,128)(2,1)}, u32[]{:S(2)}, u32[]{:S(2)}) %collective-permute-start.7) | collective-permute-done | bytes 98336 | tf_op jit(solution)/shard_map/ppermute | solution.py:533
  48.4 4.8 %collective-permute-done.8.refs_5_ = bf16[3,16,1024]{2,1,0:T(8,128)(2,1)} collective-permute-done((bf16[3,16,1024]{2,1,0:T(8,128)(2,1)}, bf16[3,16,1024]{2,1,0:T(8,128)(2,1)}, u32[]{:S(2)}, u32[]{:S(2)}) %collective-permute-start.8) | collective-permute-done | bytes 98336 | tf_op jit(solution)/shard_map/ppermute | solution.py:533
  53.1 2.7 %weight_grad.1 = bf16[1024,768]{1,0:T(8,128)(2,1)} custom-call(f32[8,128]{1,0:T(8,128)} %get-tuple-element.23.tie_ref, bf16[4,4,16,1024]{3,2,1,0:T(8,128)(2,1)S(1)} %collective-permute-done.5.swapped, bf16[128,768]{1,0:T(8,128)(2,1)S(1)} %get-tuple-element.21.hidden_ref, bf16[60,16,256]{2,1,0:T(8,128)(2,1)S(1)} %collective-permute-done.6.near, ...), custom_call_target="tpu_custom_call" | custom-call | flops 1024 | bytes 1024 | tf_op jit(solution)/shard_map/weight_grad/pallas_call | solution.py:513
  (11 shorter events, 0.1 us)
Async XLA Ops:
  2.7 17.3 %collective-permute-start = (bf16[2,4,16,1024]{3,2,1,0:T(8,128)(2,1)S(1)}, bf16[2,4,16,1024]{3,2,1,0:T(8,128)(2,1)S(1)}, u32[]{:S(2)}, u32[]{:S(2)}) collective-permute-start(bf16[2,4,16,1024]{3,2,1,0:T(8,128)(2,1)S(1)} %get-tuple-element.25), channel_id=1, source_target_pairs={{0,2},{1,3},{2,0},{3,1},{4,6},{5,7},{6,4},{7,5},{8,10},{9,11},{10,... | collective-permute-start | bytes 786440 | tf_op jit(solution)/shard_map/ppermute | solution.py:533
  5.7 14.3 %collective-permute-start.1 = (bf16[2,4,16,1024]{3,2,1,0:T(8,128)(2,1)S(1)}, bf16[2,4,16,1024]{3,2,1,0:T(8,128)(2,1)S(1)}, u32[]{:S(2)}, u32[]{:S(2)}) collective-permute-start(bf16[2,4,16,1024]{3,2,1,0:T(8,128)(2,1)S(1)} %get-tuple-element.26), channel_id=1, source_target_pairs={{0,4},{1,5},{2,6},{3,7},{4,0},{5,1},{6,2},{7,3},{8,12},{9,13},{10,... | collective-permute-start | bytes 786440 | tf_op jit(solution)/shard_map/ppermute | solution.py:533
  7.3 12.8 %collective-permute-start.2 = (bf16[2,4,16,1024]{3,2,1,0:T(8,128)(2,1)S(1)}, bf16[2,4,16,1024]{3,2,1,0:T(8,128)(2,1)S(1)}, u32[]{:S(2)}, u32[]{:S(2)}) collective-permute-start(bf16[2,4,16,1024]{3,2,1,0:T(8,128)(2,1)S(1)} %get-tuple-element.27), channel_id=1, source_target_pairs={{0,6},{1,7},{2,4},{3,5},{4,2},{5,3},{6,0},{7,1},{8,14},{9,15},{10,... | collective-permute-start | bytes 786440 | tf_op jit(solution)/shard_map/ppermute | solution.py:533
  7.3 14.1 %collective-permute-start.3 = (bf16[32,16,256]{2,1,0:T(8,128)(2,1)S(1)}, bf16[32,16,256]{2,1,0:T(8,128)(2,1)S(1)}, u32[]{:S(2)}, u32[]{:S(2)}) collective-permute-start(bf16[32,16,256]{2,1,0:T(8,128)(2,1)S(1)} %get-tuple-element.28), channel_id=1, source_target_pairs={{0,16},{8,24},{16,0},{24,8},{1,17},{9,25},{17,1},{25,9},{2,18},{10... | collective-permute-start | bytes 786440 | tf_op jit(solution)/shard_map/ppermute | solution.py:533
  10.3 9.7 %collective-permute-start.4 = (bf16[28,16,256]{2,1,0:T(8,128)(2,1)S(1)}, bf16[28,16,256]{2,1,0:T(8,128)(2,1)S(1)}, u32[]{:S(2)}, u32[]{:S(2)}) collective-permute-start(bf16[28,16,256]{2,1,0:T(8,128)(2,1)S(1)} %get-tuple-element.29), channel_id=1, source_target_pairs={{0,8},{8,0},{16,24},{24,16},{1,9},{9,1},{17,25},{25,17},{2,10},{10... | collective-permute-start | bytes 688136 | tf_op jit(solution)/shard_map/ppermute | solution.py:533
  21.4 0.6 %copy-start = (bf16[3,16,1024]{2,1,0:T(8,128)(2,1)}, bf16[3,16,1024]{2,1,0:T(8,128)(2,1)S(1)}, u32[]{:S(2)}) copy-start(bf16[3,16,1024]{2,1,0:T(8,128)(2,1)S(1)} %get-tuple-element.33) | copy-start | bytes 294916
  22.1 0.6 %copy-start.1 = (bf16[3,16,1024]{2,1,0:T(8,128)(2,1)}, bf16[3,16,1024]{2,1,0:T(8,128)(2,1)S(1)}, u32[]{:S(2)}) copy-start(bf16[3,16,1024]{2,1,0:T(8,128)(2,1)S(1)} %get-tuple-element.32) | copy-start | bytes 294916
  22.7 4.3 %collective-permute-start.5 = (bf16[4,4,16,1024]{3,2,1,0:T(8,128)(2,1)S(1)}, bf16[4,4,16,1024]{3,2,1,0:T(8,128)(2,1)S(1)}, u32[]{:S(2)}, u32[]{:S(2)}) collective-permute-start(bf16[4,4,16,1024]{3,2,1,0:T(8,128)(2,1)S(1)} %get-tuple-element.30), channel_id=1, source_target_pairs={{0,1},{1,0},{2,3},{3,2},{4,5},{5,4},{6,7},{7,6},{8,9},{9,8},{10,11... | collective-permute-start | bytes 1572872 | tf_op jit(solution)/shard_map/ppermute | solution.py:533
  22.7 19.7 %all-to-all-start = ((bf16[8,16,4096]{2,1,0:T(8,128)(2,1)}), bf16[8,16,4096]{2,1,0:T(8,128)(2,1)}, u32[]{:S(2)}, u32[]{:S(2)}) async-start(bf16[8,16,4096]{2,1,0:T(8,128)(2,1)} %expert_forward.1.refs_4_), calls=%async_computation | async-start | bytes 2097152 | tf_op jit(solution)/shard_map/all_to_all | solution.py:556
  27.8 25.4 %collective-permute-start.6 = (bf16[60,16,256]{2,1,0:T(8,128)(2,1)S(1)}, bf16[60,16,256]{2,1,0:T(8,128)(2,1)S(1)}, u32[]{:S(2)}, u32[]{:S(2)}) collective-permute-start(bf16[60,16,256]{2,1,0:T(8,128)(2,1)S(1)} %get-tuple-element.31.tie_ref), channel_id=1, source_target_pairs={{0,8},{8,0},{16,24},{24,16},{1,9},{9,1},{17,25},{25,17},{2,10},{10... | collective-permute-start | bytes 1474568 | tf_op jit(solution)/shard_map/ppermute | solution.py:533
  28.9 24.2 %collective-permute-start.9 = (bf16[4,16,1024]{2,1,0:T(8,128)(2,1)}, bf16[4,16,1024]{2,1,0:T(8,128)(2,1)S(1)}, u32[]{:S(2)}, u32[]{:S(2)}) collective-permute-start(bf16[4,16,1024]{2,1,0:T(8,128)(2,1)} %get-tuple-element.34), channel_id=1, source_target_pairs={{0,16},{8,24},{16,0},{24,8},{1,17},{9,25},{17,1},{25,9},{2,18},{10... | collective-permute-start | bytes 393224 | tf_op jit(solution)/shard_map/ppermute | solution.py:533
  31.9 21.2 %collective-permute-start.10 = (bf16[4,16,1024]{2,1,0:T(8,128)(2,1)}, bf16[4,16,1024]{2,1,0:T(8,128)(2,1)S(1)}, u32[]{:S(2)}, u32[]{:S(2)}) collective-permute-start(bf16[4,16,1024]{2,1,0:T(8,128)(2,1)} %get-tuple-element.35), channel_id=1, source_target_pairs={{0,24},{8,16},{16,8},{24,0},{1,25},{9,17},{17,9},{25,1},{2,26},{10... | collective-permute-start | bytes 393224 | tf_op jit(solution)/shard_map/ppermute | solution.py:533
  32.2 16.2 %collective-permute-start.7 = (bf16[3,16,1024]{2,1,0:T(8,128)(2,1)}, bf16[3,16,1024]{2,1,0:T(8,128)(2,1)}, u32[]{:S(2)}, u32[]{:S(2)}) collective-permute-start(bf16[3,16,1024]{2,1,0:T(8,128)(2,1)} %copy-done.1), channel_id=1, source_target_pairs={{0,16},{8,24},{16,0},{24,8},{1,17},{9,25},{17,1},{25,9},{2,18},{10... | collective-permute-start | bytes 294920 | tf_op jit(solution)/shard_map/ppermute | solution.py:533
  33.4 19.8 %collective-permute-start.8 = (bf16[3,16,1024]{2,1,0:T(8,128)(2,1)}, bf16[3,16,1024]{2,1,0:T(8,128)(2,1)}, u32[]{:S(2)}, u32[]{:S(2)}) collective-permute-start(bf16[3,16,1024]{2,1,0:T(8,128)(2,1)} %copy-done), channel_id=1, source_target_pairs={{0,24},{8,16},{16,8},{24,0},{1,25},{9,17},{17,9},{25,1},{2,26},{10... | collective-permute-start | bytes 294920 | tf_op jit(solution)/shard_map/ppermute | solution.py:533

commit v8 on v7

--- a/solution.py
+++ b/solution.py
@@ -119,11 +119,10 @@
         part = (part * slot_weight).astype(bf16)
         for r in range(flight):
             chips[r % half][r // half, j] = part[r * CAP : (r + 1) * CAP, :]
-        for bit in bits:
-            if bit <= j < 2 * bit:
-                first = flight * (hid // TILE) + (j - bit) * (share // TILE)
-                for q in range(share // TILE):
-                    messages[bit][first + q] = part[:CAP, q * TILE : (q + 1) * TILE]
+        if j in bits:
+            for q in range(share // TILE):
+                at = flight * (hid // TILE) + q
+                messages[j][at] = part[:CAP, q * TILE : (q + 1) * TILE]
     for copy in gates:
         copy.wait()
     for r in range(flight):
@@ -149,8 +148,8 @@
         out_shape=(pltpu.HBM((slots, tokens), f32), pltpu.VMEM((rows, double // 2), bf16))
         + (pltpu.VMEM((2, groups, CAP, share), bf16),) * half
         + tuple(
-            pltpu.VMEM((flight * (double // 2 // TILE) + bit * (share // TILE), CAP, TILE), bf16)
-            for bit in bits_of(groups)
+            pltpu.VMEM((flight * (double // 2 // TILE) + share // TILE, CAP, TILE), bf16)
+            for _ in bits_of(groups)
         ),
         in_specs=[HBM] * 6,
         out_specs=(HBM, VMEM) + (VMEM,) * (half + len(bits_of(groups))),
@@ -243,7 +242,9 @@
     for c in range(half):
         sibling[c] = chips[c][1]
         for j in range(2, groups):
-            if c:
+            if j not in bits_of(groups):
+                pieces[j - 2][c] = chips[c][0, j]
+            elif c:
                 pieces[j - 2][c - 1] = chips[c][0, j]
 
 
@@ -253,7 +254,9 @@
     return pl.pallas_call(
         functools.partial(sort_kernel, half, groups, len(ties)),
         out_shape=(pltpu.VMEM((half, groups, cap, share), bf16),)
-        + (pltpu.VMEM((half - 1, cap, share), bf16),) * (groups - 2),
+        + tuple(
+            pltpu.VMEM((half - (j in bits_of(groups)), cap, share), bf16) for j in range(2, groups)
+        ),
         in_specs=[VMEM] * half + [ANY] * len(ties),
         out_specs=(VMEM,) * (groups - 1),
         compiler_params=params(2 * half * CAP),
@@ -295,8 +298,9 @@
     )(swapped, *chips[1:], *messages)
 
 
-def backward_kernel(flight, groups, scale_hbm, gate_up_hbm, quant_hbm, tie_ref, swapped, *refs):
+def backward_kernel(flight, groups, ties, scale_hbm, gate_up_hbm, quant_hbm, *refs):
     half = flight // 2
+    swapped, *refs = refs[ties:]
     chips, out_hbm = refs[:half], refs[half]
     scale, gate_up, rows, quant, acc, out = refs[half + 1 : half + 7]
     scale_sem, gate_sems, in_sems, out_sems = refs[half + 7 :]
@@ -363,15 +367,15 @@
         copy.wait()
 
 
-def backward(scale, gate_up, quant, tie, chips, swapped):
+def backward(scale, gate_up, quant, ties, chips, swapped):
     slots, double = gate_up.shape
     hid, width = quant.shape
     half, groups, cap, share = swapped.shape
     flight = 2 * half
     return pl.pallas_call(
-        functools.partial(backward_kernel, flight, groups),
+        functools.partial(backward_kernel, flight, groups, len(ties)),
         out_shape=pltpu.HBM((slots, double), bf16),
-        in_specs=[HBM, HBM, HBM, ANY] + [VMEM] * (1 + half),
+        in_specs=[HBM] * 3 + [ANY] * len(ties) + [VMEM] * (1 + half),
         out_specs=HBM,
         scratch_shapes=[
             pltpu.SMEM(scale.shape, f32),
@@ -388,7 +392,7 @@
         compiler_params=params(slots),
         cost_estimate=SMALL,
         name="expert_backward",
-    )(hbm(scale), hbm(gate_up), hbm(quant), tie, swapped, *chips)
+    )(hbm(scale), hbm(gate_up), hbm(quant), *ties, swapped, *chips)
 
 
 def combine_kernel(
@@ -469,7 +473,6 @@
     hidden[:slots, :] = hidden_ref[...]
     passed = (flight - 1) * tall
     for j in range(1, groups):
-        bit = max(b for b in bits_of(groups) if b <= j)
         message, first = messages[j // 2], 0
         if j > 1 and j % 2:
             message, first = near, passed
@@ -479,20 +482,20 @@
                 hidden[
                     j * slots + r * cap : j * slots + (r + 1) * cap, q * TILE : (q + 1) * TILE
                 ] = message[first + r * wide + q]
-        for q in range(tall):
-            own[j - 1, :, q * TILE : (q + 1) * TILE] = message[
-                first + flight * wide + (j - bit) * tall + q
-            ]
+        for q in range(tall if j in bits_of(groups) else 0):
+            own[j - 1, :, q * TILE : (q + 1) * TILE] = message[first + flight * wide + q]
     stores = []
     for n, cols in enumerate(chunks(share, block)):
         grads = [chips[c][0, 0, :, cols] for c in range(half)]
         grads += [swapped[c, 0, :, cols] for c in range(half)]
         for j in range(1, groups):
-            grads.append(own[j - 1, :, cols])
+            if j in bits_of(groups):
+                grads.append(own[j - 1, :, cols])
             if j == 1:
                 grads.append(rows[:, :, cols].reshape(slots - cap, block))
             else:
-                grads.append(direct[j - 2][:, :, cols].reshape(slots // 2 - cap, block))
+                count = direct[j - 2].shape[0] * cap
+                grads.append(direct[j - 2][:, :, cols].reshape(count, block))
                 grads.append(handed[j - 2][:, :, cols].reshape(slots // 2, block))
         out[cols, :] = lax.dot_general(
             jnp.concatenate(grads, axis=0),
@@ -561,7 +564,7 @@
     near = swap(near, "dp", 1)
     direct = [swap(direct[j - 2], "dp", j) for j in range(2, groups)]
     handed = [swap(handed[j - 2], "dp", j) for j in range(2, groups)]
-    d_gate_up = backward(scale, gate_up, w_quant[0], tie, chips, swapped)
+    d_gate_up = backward(scale, gate_up, w_quant[0], [tie] + direct, chips, swapped)
     combined, d_probs = combine(ids, own, d_out, returned)
     d_weight = weight_grad(
         d_probs, chips, swapped, hidden, near, direct, handed, [messages[1]] + passed

time: 56.1 us -> 64.8 us (1.16)
  waiting for transfers between devices: 13.2 us -> 22.5 us
    ppermute x11, waiting for transfers between devices: 11.8 us -> 22.5 us  [swap(): return lax.ppermute(value, axis, [(i, i ^ j) for i in range(size)])]
    all_to_all x1, waiting for transfers between devices: 1.45 us -> 0.01 us  [shards(): lax.all_to_all(expert_out, 'expert', split_axis=0, concat_axis=0, tiled=T...]
    pallas_call x1, Pallas kernels: 0.05 us -> 0.71 us  [sort_rows(): pl.pallas_call(functools.partial(sort_kernel, half, groups, len(ties)), o...]
  transfers between devices with their start and end apart: 12 -> 12, of which waited for: 5 -> 3; matrix products, arithmetic and copies ran while one was open for 0% -> 0% of each run, Pallas kernels for 26% -> 22%
where the time goes in v8:
time: 64.8 us; the launch traced here: 64.5 us
  waiting for transfers between devices  22.5 us (35%)
  starting transfers between devices  20.8 us (32%)
  Pallas kernels  19.9 us (31%)
  between operations  0.73 us (1%)
    ppermute x11, waiting for transfers between devices, swap(): return lax.ppermute(value, axis, [(i, i ^ j) for i in range(size)])  22.5 us
    ppermute x11, starting transfers between devices, swap(): return lax.ppermute(value, axis, [(i, i ^ j) for i in range(size)])  16.5 us
    pallas_call x1, Pallas kernels, backward(): pl.pallas_call(functools.partial(backward_kernel, flight, groups, len(tie...  5.24 us
    pallas_call x1, Pallas kernels, forward(): pl.pallas_call(functools.partial(forward_kernel, flight, block), out_shap...  4.78 us
    all_to_all x1, starting transfers between devices, shards(): lax.all_to_all(expert_out, 'expert', split_axis=0, concat_axis=0, tiled=T...  4.25 us
    pallas_call x1, Pallas kernels, combine(): pl.pallas_call(functools.partial(combine_kernel, block), out_shape=(pltpu...  3.63 us
    pallas_call x1, Pallas kernels, weight_grad(): pl.pallas_call(functools.partial(weight_grad_kernel, half, groups, block)...  2.71 us
    pallas_call x1, Pallas kernels, dispatch(): pl.pallas_call(functools.partial(dispatch_kernel, flight, groups), out_sh...  2.09 us
  transfers between devices with their start and end apart: 12, of which 3 were waited for; matrix products, arithmetic and copies ran while one was open for 0% of the time, Pallas kernels for 22%

profile of v8, /device:TPU:0, one launch (start us, length us, event | category | flops | bytes accessed | tf_op | source)
XLA Modules:
  0.0 64.5 jit_solution(345955800458982901)
XLA Ops:
  0.6 2.1 %dispatch.1 = (f32[128,128]{1,0:T(8,128)}, bf16[128,768]{1,0:T(8,128)(2,1)S(1)}, bf16[2,4,16,1024]{3,2,1,0:T(8,128)(2,1)S(1)}, bf16[2,4,16,1024]{3,2,1,0:T(8,128...) custom-call(bf16[128,1536]{1,0:T(8,128)(2,1)} %bitcast.10, ...), custom_call_target="tpu_custom_call" | custom-call | flops 1024 | bytes 1024 | tf_op jit(solution)/shard_map/dispatch/pallas_call | solution.py:146
  2.7 3.0 %collective-permute-start = (bf16[2,4,16,1024]{3,2,1,0:T(8,128)(2,1)S(1)}, bf16[2,4,16,1024]{3,2,1,0:T(8,128)(2,1)S(1)}, u32[]{:S(2)}, u32[]{:S(2)}) collective-permute-start(bf16[2,4,16,1024]{3,2,1,0:T(8,128)(2,1)S(1)} %get-tuple-element.25), channel_id=1, source_target_pairs={{0,2},{1,3},{2,0},{3,1},{4,6},{5,7},{6,4},{7,5},{8,10},{9,11},{10,... | collective-permute-start | bytes 786440 | tf_op jit(solution)/shard_map/ppermute | solution.py:536
  5.7 1.5 %collective-permute-start.1 = (bf16[2,4,16,1024]{3,2,1,0:T(8,128)(2,1)S(1)}, bf16[2,4,16,1024]{3,2,1,0:T(8,128)(2,1)S(1)}, u32[]{:S(2)}, u32[]{:S(2)}) collective-permute-start(bf16[2,4,16,1024]{3,2,1,0:T(8,128)(2,1)S(1)} %get-tuple-element.26), channel_id=1, source_target_pairs={{0,4},{1,5},{2,6},{3,7},{4,0},{5,1},{6,2},{7,3},{8,12},{9,13},{10,... | collective-permute-start | bytes 786440 | tf_op jit(solution)/shard_map/ppermute | solution.py:536
  7.3 0.0 collective-permute-start.2
  7.3 3.0 %collective-permute-start.3 = (bf16[28,16,256]{2,1,0:T(8,128)(2,1)S(1)}, bf16[28,16,256]{2,1,0:T(8,128)(2,1)S(1)}, u32[]{:S(2)}, u32[]{:S(2)}) collective-permute-start(bf16[28,16,256]{2,1,0:T(8,128)(2,1)S(1)} %get-tuple-element.28), channel_id=1, source_target_pairs={{0,16},{8,24},{16,0},{24,8},{1,17},{9,25},{17,1},{25,9},{2,18},{10... | collective-permute-start | bytes 688136 | tf_op jit(solution)/shard_map/ppermute | solution.py:536
  10.3 1.6 %collective-permute-start.4 = (bf16[28,16,256]{2,1,0:T(8,128)(2,1)S(1)}, bf16[28,16,256]{2,1,0:T(8,128)(2,1)S(1)}, u32[]{:S(2)}, u32[]{:S(2)}) collective-permute-start(bf16[28,16,256]{2,1,0:T(8,128)(2,1)S(1)} %get-tuple-element.29), channel_id=1, source_target_pairs={{0,8},{8,0},{16,24},{24,16},{1,9},{9,1},{17,25},{25,17},{2,10},{10... | collective-permute-start | bytes 688136 | tf_op jit(solution)/shard_map/ppermute | solution.py:536
  11.9 4.8 %expert_forward.1.refs_4_ = bf16[8,16,4096]{2,1,0:T(8,128)(2,1)} custom-call(bf16[128,768]{1,0:T(8,128)(2,1)S(1)} %get-tuple-element.21.hidden_ref, f32[6,1,32]{2,1,0:T(1,128)} %bitcast.16, bf16[768,4096]{1,0:T(8,128)(2,1)} %bitcast.8), custom_call_target="tpu_custom_call" | custom-call | flops 1024 | bytes 1024 | tf_op jit(solution)/shard_map/expert_forward/pallas_call | solution.py:220
  16.7 3.4 %collective-permute-done.3.refs_5_.refs_3_.refs_9_ = bf16[28,16,256]{2,1,0:T(8,128)(2,1)S(1)} collective-permute-done((bf16[28,16,256]{2,1,0:T(8,128)(2,1)S(1)}, bf16[28,16,256]{2,1,0:T(8,128)(2,1)S(1)}, u32[]{:S(2)}, u32[]{:S(2)}) %collective-permute-start.3) | collective-permute-done | bytes 229408 | tf_op jit(solution)/shard_map/ppermute | solution.py:536
  20.1 0.2 collective-permute-done.4.refs_6_.refs_8_
  20.3 0.0 collective-permute-done.refs_1_.refs_0_.refs_5_
  20.3 0.7 %sort_rows.1 = (bf16[4,4,16,1024]{3,2,1,0:T(8,128)(2,1)S(1)}, bf16[3,16,1024]{2,1,0:T(8,128)(2,1)S(1)}, bf16[4,16,1024]{2,1,0:T(8,128)(2,1)}) custom-call(bf16[2,4,16,1024]{3,2,1,0:T(8,128)(2,1)S(1)} %get-tuple-element.24.refs_0_.refs_4_, bf16[2,4,16,1024]{3,2,1,0:T(8,128)(2,1)S(1)} %collective-permute-done.refs_1_.refs_0_.refs_5_, ...), custom_call_target="tpu_custom_call" | custom-call | flops 1024 | bytes 1024 | tf_op jit(solution)/shard_map/sort_rows/pallas_call | solution.py:254
  21.0 0.6 copy-done
  21.6 4.2 %all-to-all-start = ((bf16[8,16,4096]{2,1,0:T(8,128)(2,1)}), bf16[8,16,4096]{2,1,0:T(8,128)(2,1)}, u32[]{:S(2)}, u32[]{:S(2)}) async-start(bf16[8,16,4096]{2,1,0:T(8,128)(2,1)} %expert_forward.1.refs_4_), calls=%async_computation | async-start | bytes 2097152 | tf_op jit(solution)/shard_map/all_to_all | solution.py:559
  25.9 0.7 %split.1 = (bf16[56,16,256]{2,1,0:T(8,128)(2,1)S(1)}, bf16[4,16,1024]{2,1,0:T(8,128)(2,1)}, bf16[4,16,1024]{2,1,0:T(8,128)(2,1)}) custom-call(bf16[4,4,16,1024]{3,2,1,0:T(8,128)(2,1)S(1)} %collective-permute-done.5.swapped.refs_3_, bf16[2,4,16,1024]{3,2,1,0:T(8,128)(2,1)S(1)} %collective-permute-done.refs_1_.refs_0_.refs_5_, ...), custom_call_target="tpu_custom_call" | custom-call | flops 1024 | bytes 1024 | tf_op jit(solution)/shard_map/split/pallas_call | solution.py:289
  26.7 1.5 %collective-permute-start.8 = (bf16[56,16,256]{2,1,0:T(8,128)(2,1)S(1)}, bf16[56,16,256]{2,1,0:T(8,128)(2,1)S(1)}, u32[]{:S(2)}, u32[]{:S(2)}) collective-permute-start(bf16[56,16,256]{2,1,0:T(8,128)(2,1)S(1)} %get-tuple-element.31.refs_0_), channel_id=1, source_target_pairs={{0,8},{8,0},{16,24},{24,16},{1,9},{9,1},{17,25},{25,17},{2,10},{10... | collective-permute-start | bytes 1376264 | tf_op jit(solution)/shard_map/ppermute | solution.py:536
  28.1 1.8 %collective-permute-start.7 = (bf16[4,16,1024]{2,1,0:T(8,128)(2,1)}, bf16[4,16,1024]{2,1,0:T(8,128)(2,1)S(1)}, u32[]{:S(2)}, u32[]{:S(2)}) collective-permute-start(bf16[4,16,1024]{2,1,0:T(8,128)(2,1)} %get-tuple-element.33), channel_id=1, source_target_pairs={{0,24},{8,16},{16,8},{24,0},{1,25},{9,17},{17,9},{25,1},{2,26},{10... | collective-permute-start | bytes 393224 | tf_op jit(solution)/shard_map/ppermute | solution.py:536
  29.9 0.6 collective-permute-start.9
  30.5 2.9 %collective-permute-start.10 = (bf16[4,16,1024]{2,1,0:T(8,128)(2,1)}, bf16[4,16,1024]{2,1,0:T(8,128)(2,1)}, u32[]{:S(2)}, u32[]{:S(2)}) collective-permute-start(bf16[4,16,1024]{2,1,0:T(8,128)(2,1)} %get-tuple-element.35), channel_id=1, source_target_pairs={{0,24},{8,16},{16,8},{24,0},{1,25},{9,17},{17,9},{25,1},{2,26},{10... | collective-permute-start | bytes 393224 | tf_op jit(solution)/shard_map/ppermute | solution.py:536
  33.4 0.6 collective-permute-start.6
  34.0 18.9 %collective-permute-done.6.refs_1_.refs_4_ = bf16[3,16,1024]{2,1,0:T(8,128)(2,1)S(1)} collective-permute-done((bf16[3,16,1024]{2,1,0:T(8,128)(2,1)}, bf16[3,16,1024]{2,1,0:T(8,128)(2,1)S(1)}, u32[]{:S(2)}, u32[]{:S(2)}) %collective-permute-start.6) | collective-permute-done | bytes 98336 | tf_op jit(solution)/shard_map/ppermute | solution.py:536
  52.9 5.2 %expert_backward.1 = bf16[128,1536]{1,0:T(8,128)(2,1)} custom-call(f32[6,1,32]{2,1,0:T(1,128)} %bitcast.17, bf16[128,1536]{1,0:T(8,128)(2,1)} %bitcast.11, bf16[768,4096]{1,0:T(8,128)(2,1)} %bitcast.9, bf16[56,16,256]{2,1,0:T(8,128)(2,1)S(1)} %get-tuple-element.31.refs_0_, bf16[3,16,1024]{2,1,0:T(8,128)(2,1)S(1)} %collective-permute-done.6.refs_1_.refs_4_, ...), custom_call_target="tpu_custom_call" | custom-call | flops 1024 | bytes 1024 | tf_op jit(solution)/shard_map/expert_backward/pallas_call | solution.py:375
  58.1 3.6 %combine.1 = (bf16[128,4096]{1,0:T(8,128)(2,1)}, f32[8,128]{1,0:T(8,128)}) custom-call(s32[8,128]{1,0:T(8,128)} %bitcast.15, f32[128,128]{1,0:T(8,128)} %get-tuple-element.20.own_hbm, bf16[128,4096]{1,0:T(8,128)(2,1)} %dout_hbm.3, bf16[8,16,4096]{2,1,0:T(8,128)(2,1)} %all-to-all-done.ret_hbm), custom_call_target="tpu_custom_call" | custom-call | flops 1024 | bytes 1024 | tf_op jit(solution)/shard_map/combine/pallas_call | solution.py:441
  61.8 0.0 collective-permute-done.9.refs_6_
  61.8 2.7 %weight_grad.1 = bf16[1024,768]{1,0:T(8,128)(2,1)} custom-call(f32[8,128]{1,0:T(8,128)} %get-tuple-element.23.tie_ref, bf16[4,4,16,1024]{3,2,1,0:T(8,128)(2,1)S(1)} %collective-permute-done.5.swapped.refs_3_, bf16[128,768]{1,0:T(8,128)(2,1)S(1)} %get-tuple-element.21.hidden_ref, bf16[56,16,256]{2,1,0:T(8,128)(2,1)S(1)} %collective-permute-done.8.near, ...), custom_call_target="tpu_custom_call" | custom-call | flops 1024 | bytes 1024 | tf_op jit(solution)/shard_map/weight_grad/pallas_call | solution.py:516
  (9 shorter events, 0.0 us)
Async XLA Ops:
  2.7 17.6 %collective-permute-start = (bf16[2,4,16,1024]{3,2,1,0:T(8,128)(2,1)S(1)}, bf16[2,4,16,1024]{3,2,1,0:T(8,128)(2,1)S(1)}, u32[]{:S(2)}, u32[]{:S(2)}) collective-permute-start(bf16[2,4,16,1024]{3,2,1,0:T(8,128)(2,1)S(1)} %get-tuple-element.25), channel_id=1, source_target_pairs={{0,2},{1,3},{2,0},{3,1},{4,6},{5,7},{6,4},{7,5},{8,10},{9,11},{10,... | collective-permute-start | bytes 786440 | tf_op jit(solution)/shard_map/ppermute | solution.py:536
  5.7 14.6 %collective-permute-start.1 = (bf16[2,4,16,1024]{3,2,1,0:T(8,128)(2,1)S(1)}, bf16[2,4,16,1024]{3,2,1,0:T(8,128)(2,1)S(1)}, u32[]{:S(2)}, u32[]{:S(2)}) collective-permute-start(bf16[2,4,16,1024]{3,2,1,0:T(8,128)(2,1)S(1)} %get-tuple-element.26), channel_id=1, source_target_pairs={{0,4},{1,5},{2,6},{3,7},{4,0},{5,1},{6,2},{7,3},{8,12},{9,13},{10,... | collective-permute-start | bytes 786440 | tf_op jit(solution)/shard_map/ppermute | solution.py:536
  7.3 13.0 %collective-permute-start.2 = (bf16[2,4,16,1024]{3,2,1,0:T(8,128)(2,1)S(1)}, bf16[2,4,16,1024]{3,2,1,0:T(8,128)(2,1)S(1)}, u32[]{:S(2)}, u32[]{:S(2)}) collective-permute-start(bf16[2,4,16,1024]{3,2,1,0:T(8,128)(2,1)S(1)} %get-tuple-element.27), channel_id=1, source_target_pairs={{0,6},{1,7},{2,4},{3,5},{4,2},{5,3},{6,0},{7,1},{8,14},{9,15},{10,... | collective-permute-start | bytes 786440 | tf_op jit(solution)/shard_map/ppermute | solution.py:536
  7.3 12.8 %collective-permute-start.3 = (bf16[28,16,256]{2,1,0:T(8,128)(2,1)S(1)}, bf16[28,16,256]{2,1,0:T(8,128)(2,1)S(1)}, u32[]{:S(2)}, u32[]{:S(2)}) collective-permute-start(bf16[28,16,256]{2,1,0:T(8,128)(2,1)S(1)} %get-tuple-element.28), channel_id=1, source_target_pairs={{0,16},{8,24},{16,0},{24,8},{1,17},{9,25},{17,1},{25,9},{2,18},{10... | collective-permute-start | bytes 688136 | tf_op jit(solution)/shard_map/ppermute | solution.py:536
  10.3 10.0 %collective-permute-start.4 = (bf16[28,16,256]{2,1,0:T(8,128)(2,1)S(1)}, bf16[28,16,256]{2,1,0:T(8,128)(2,1)S(1)}, u32[]{:S(2)}, u32[]{:S(2)}) collective-permute-start(bf16[28,16,256]{2,1,0:T(8,128)(2,1)S(1)} %get-tuple-element.29), channel_id=1, source_target_pairs={{0,8},{8,0},{16,24},{24,16},{1,9},{9,1},{17,25},{25,17},{2,10},{10... | collective-permute-start | bytes 688136 | tf_op jit(solution)/shard_map/ppermute | solution.py:536
  21.0 0.6 copy-start
  21.6 4.3 %collective-permute-start.5 = (bf16[4,4,16,1024]{3,2,1,0:T(8,128)(2,1)S(1)}, bf16[4,4,16,1024]{3,2,1,0:T(8,128)(2,1)S(1)}, u32[]{:S(2)}, u32[]{:S(2)}) collective-permute-start(bf16[4,4,16,1024]{3,2,1,0:T(8,128)(2,1)S(1)} %get-tuple-element.30), channel_id=1, source_target_pairs={{0,1},{1,0},{2,3},{3,2},{4,5},{5,4},{6,7},{7,6},{8,9},{9,8},{10,11... | collective-permute-start | bytes 1572872 | tf_op jit(solution)/shard_map/ppermute | solution.py:536
  21.6 36.5 %all-to-all-start = ((bf16[8,16,4096]{2,1,0:T(8,128)(2,1)}), bf16[8,16,4096]{2,1,0:T(8,128)(2,1)}, u32[]{:S(2)}, u32[]{:S(2)}) async-start(bf16[8,16,4096]{2,1,0:T(8,128)(2,1)} %expert_forward.1.refs_4_), calls=%async_computation | async-start | bytes 2097152 | tf_op jit(solution)/shard_map/all_to_all | solution.py:559
  26.7 35.1 %collective-permute-start.8 = (bf16[56,16,256]{2,1,0:T(8,128)(2,1)S(1)}, bf16[56,16,256]{2,1,0:T(8,128)(2,1)S(1)}, u32[]{:S(2)}, u32[]{:S(2)}) collective-permute-start(bf16[56,16,256]{2,1,0:T(8,128)(2,1)S(1)} %get-tuple-element.31.refs_0_), channel_id=1, source_target_pairs={{0,8},{8,0},{16,24},{24,16},{1,9},{9,1},{17,25},{25,17},{2,10},{10... | collective-permute-start | bytes 1376264 | tf_op jit(solution)/shard_map/ppermute | solution.py:536
  28.1 24.7 %collective-permute-start.7 = (bf16[4,16,1024]{2,1,0:T(8,128)(2,1)}, bf16[4,16,1024]{2,1,0:T(8,128)(2,1)S(1)}, u32[]{:S(2)}, u32[]{:S(2)}) collective-permute-start(bf16[4,16,1024]{2,1,0:T(8,128)(2,1)} %get-tuple-element.33), channel_id=1, source_target_pairs={{0,24},{8,16},{16,8},{24,0},{1,25},{9,17},{17,9},{25,1},{2,26},{10... | collective-permute-start | bytes 393224 | tf_op jit(solution)/shard_map/ppermute | solution.py:536
  29.9 31.8 %collective-permute-start.9 = (bf16[4,16,1024]{2,1,0:T(8,128)(2,1)}, bf16[4,16,1024]{2,1,0:T(8,128)(2,1)S(1)}, u32[]{:S(2)}, u32[]{:S(2)}) collective-permute-start(bf16[4,16,1024]{2,1,0:T(8,128)(2,1)} %get-tuple-element.34), channel_id=1, source_target_pairs={{0,16},{8,24},{16,0},{24,8},{1,17},{9,25},{17,1},{25,9},{2,18},{10... | collective-permute-start | bytes 393224 | tf_op jit(solution)/shard_map/ppermute | solution.py:536
  30.5 31.3 %collective-permute-start.10 = (bf16[4,16,1024]{2,1,0:T(8,128)(2,1)}, bf16[4,16,1024]{2,1,0:T(8,128)(2,1)}, u32[]{:S(2)}, u32[]{:S(2)}) collective-permute-start(bf16[4,16,1024]{2,1,0:T(8,128)(2,1)} %get-tuple-element.35), channel_id=1, source_target_pairs={{0,24},{8,16},{16,8},{24,0},{1,25},{9,17},{17,9},{25,1},{2,26},{10... | collective-permute-start | bytes 393224 | tf_op jit(solution)/shard_map/ppermute | solution.py:536
  33.4 19.5 %collective-permute-start.6 = (bf16[3,16,1024]{2,1,0:T(8,128)(2,1)}, bf16[3,16,1024]{2,1,0:T(8,128)(2,1)S(1)}, u32[]{:S(2)}, u32[]{:S(2)}) collective-permute-start(bf16[3,16,1024]{2,1,0:T(8,128)(2,1)} %copy-done), channel_id=1, source_target_pairs={{0,16},{8,24},{16,0},{24,8},{1,17},{9,25},{17,1},{25,9},{2,18},{10... | collective-permute-start | bytes 294920 | tf_op jit(solution)/shard_map/ppermute | solution.py:536

commit v9 on v5

--- a/solution.py
+++ b/solution.py
@@ -376,12 +376,13 @@
 
 
 def combine_kernel(
-    block, ids_hbm, own_hbm, dout_hbm, ret_ref, out_ref, dprobs_ref, ids_ref, own_ref, dout, sems
+    block, ids_hbm, own_hbm, dout_hbm, ret_hbm, out_ref, dprobs_ref, ids_ref, own_ref, dout, ret_ref, sems
 ):
     copies = [
         pltpu.make_async_copy(ids_hbm, ids_ref, sems.at[0]),
         pltpu.make_async_copy(own_hbm, own_ref, sems.at[1]),
         pltpu.make_async_copy(dout_hbm, dout, sems.at[2]),
+        pltpu.make_async_copy(ret_hbm, ret_ref, sems.at[3]),
     ]
     for copy in copies:
         copy.start()
@@ -396,8 +397,8 @@
     high = turned.astype(bf16)
     low = (turned - high.astype(f32)).astype(bf16)
     total = jnp.zeros((slots, tokens), f32)
-    copies[0].wait()
-    copies[2].wait()
+    for copy in (copies[0], copies[2], copies[3]):
+        copy.wait()
     for cols in chunks(width, block):
         here = jnp.concatenate(
             [ret_ref[block_place(me, r, flight), :, cols] for r in range(flight)], axis=0
@@ -423,18 +424,19 @@
             pltpu.HBM((tokens, width), bf16),
             pltpu.HBM(ids.shape, f32),
         ),
-        in_specs=[HBM, HBM, HBM, VMEM],
+        in_specs=[HBM, HBM, HBM, HBM],
         out_specs=(VMEM, VMEM),
         scratch_shapes=[
             pltpu.VMEM(ids.shape, jnp.int32),
             pltpu.VMEM(own.shape, f32),
             pltpu.VMEM((tokens, width), bf16),
-            pltpu.SemaphoreType.DMA((3,)),
+            pltpu.VMEM(returned.shape, bf16),
+            pltpu.SemaphoreType.DMA((4,)),
         ],
         compiler_params=params(own.shape[0]),
         cost_estimate=SMALL,
         name="combine",
-    )(hbm(ids), hbm(own), hbm(d_out), returned)
+    )(hbm(ids), hbm(own), hbm(d_out), hbm(returned))
 
 
 def weight_grad_kernel(half, groups, block, tie_ref, swapped, hidden_ref, *refs):

time: 50.6 us -> 48.5 us (0.958)
  Pallas kernels: 20.1 us -> 18.4 us
  waiting for transfers between devices: 12.2 us -> 11.4 us
    pallas_call x1, Pallas kernels: 2.98 us -> 1.8 us  [weight_grad(): pl.pallas_call(functools.partial(weight_grad_kernel, half, groups, block)...]
    ppermute x10, waiting for transfers between devices: 12.2 us -> 11.3 us  [swap(): return lax.ppermute(value, axis, [(i, i ^ j) for i in range(size)])]
    pallas_call x1, Pallas kernels: 2.88 us -> 2.09 us  [dispatch(): pl.pallas_call(functools.partial(dispatch_kernel, flight, groups), out_sh...]
  transfers between devices with their start and end apart: 11 -> 11, of which waited for: 3 -> 3; matrix products, arithmetic and copies ran while one was open for 0% -> 0% of each run, Pallas kernels for 28% -> 30%
where the time goes in v9:
time: 48.5 us; the launch traced here: 48.2 us
  Pallas kernels  18.4 us (38%)
  starting transfers between devices  17.8 us (37%)
  waiting for transfers between devices  11.4 us (24%)
  between operations  0.72 us (1%)
    ppermute x10, starting transfers between devices, swap(): return lax.ppermute(value, axis, [(i, i ^ j) for i in range(size)])  13.1 us
    ppermute x10, waiting for transfers between devices, swap(): return lax.ppermute(value, axis, [(i, i ^ j) for i in range(size)])  11.3 us
    pallas_call x1, Pallas kernels, backward(): pl.pallas_call(functools.partial(backward_kernel, flight, groups), out_sh...  5.25 us
    pallas_call x1, Pallas kernels, forward(): pl.pallas_call(functools.partial(forward_kernel, flight, block), out_shap...  4.78 us
    all_to_all x1, starting transfers between devices, shards(): lax.all_to_all(expert_out, 'expert', split_axis=0, concat_axis=0, tiled=T...  4.67 us
    pallas_call x1, Pallas kernels, combine(): pl.pallas_call(functools.partial(combine_kernel, block), out_shape=(pltpu...  3.63 us
    pallas_call x1, Pallas kernels, dispatch(): pl.pallas_call(functools.partial(dispatch_kernel, flight, groups), out_sh...  2.09 us
    pallas_call x1, Pallas kernels, weight_grad(): pl.pallas_call(functools.partial(weight_grad_kernel, half, groups, block)...  1.8 us
  transfers between devices with their start and end apart: 11, of which 3 were waited for; matrix products, arithmetic and copies ran while one was open for 0% of the time, Pallas kernels for 30%

profile of v9, /device:TPU:18, one launch (start us, length us, event | category | flops | bytes accessed | tf_op | source)
XLA Modules:
  0.0 48.2 jit_solution(7981754755969618131)
XLA Ops:
  0.6 2.1 %dispatch.1 = (f32[128,128]{1,0:T(8,128)}, bf16[128,768]{1,0:T(8,128)(2,1)S(1)}, bf16[2,4,16,1024]{3,2,1,0:T(8,128)(2,1)S(1)}, bf16[2,4,16,1024]{3,2,1,0:T(8,128...) custom-call(bf16[128,1536]{1,0:T(8,128)(2,1)} %bitcast.10, ...), custom_call_target="tpu_custom_call" | custom-call | flops 1024 | bytes 1024 | tf_op jit(solution)/shard_map/dispatch/pallas_call | solution.py:147
  2.7 0.6 %collective-permute-start = (bf16[2,4,16,1024]{3,2,1,0:T(8,128)(2,1)S(1)}, bf16[2,4,16,1024]{3,2,1,0:T(8,128)(2,1)S(1)}, u32[]{:S(2)}, u32[]{:S(2)}) collective-permute-start(bf16[2,4,16,1024]{3,2,1,0:T(8,128)(2,1)S(1)} %get-tuple-element.21), channel_id=1, source_target_pairs={{0,2},{1,3},{2,0},{3,1},{4,6},{5,7},{6,4},{7,5},{8,10},{9,11},{10,... | collective-permute-start | bytes 786440 | tf_op jit(solution)/shard_map/ppermute | solution.py:504
  3.3 1.5 %collective-permute-start.1 = (bf16[2,4,16,1024]{3,2,1,0:T(8,128)(2,1)S(1)}, bf16[2,4,16,1024]{3,2,1,0:T(8,128)(2,1)S(1)}, u32[]{:S(2)}, u32[]{:S(2)}) collective-permute-start(bf16[2,4,16,1024]{3,2,1,0:T(8,128)(2,1)S(1)} %get-tuple-element.22), channel_id=1, source_target_pairs={{0,4},{1,5},{2,6},{3,7},{4,0},{5,1},{6,2},{7,3},{8,12},{9,13},{10,... | collective-permute-start | bytes 786440 | tf_op jit(solution)/shard_map/ppermute | solution.py:504
  4.8 1.4 %collective-permute-start.2 = (bf16[2,4,16,1024]{3,2,1,0:T(8,128)(2,1)S(1)}, bf16[2,4,16,1024]{3,2,1,0:T(8,128)(2,1)S(1)}, u32[]{:S(2)}, u32[]{:S(2)}) collective-permute-start(bf16[2,4,16,1024]{3,2,1,0:T(8,128)(2,1)S(1)} %get-tuple-element.23), channel_id=1, source_target_pairs={{0,6},{1,7},{2,4},{3,5},{4,2},{5,3},{6,0},{7,1},{8,14},{9,15},{10,... | collective-permute-start | bytes 786440 | tf_op jit(solution)/shard_map/ppermute | solution.py:504
  6.3 0.3 collective-permute-start.3
  6.6 1.6 %collective-permute-start.4 = (bf16[28,16,256]{2,1,0:T(8,128)(2,1)S(1)}, bf16[28,16,256]{2,1,0:T(8,128)(2,1)S(1)}, u32[]{:S(2)}, u32[]{:S(2)}) collective-permute-start(bf16[28,16,256]{2,1,0:T(8,128)(2,1)S(1)} %get-tuple-element.26), channel_id=1, source_target_pairs={{0,8},{8,0},{16,24},{24,16},{1,9},{9,1},{17,25},{25,17},{2,10},{10... | collective-permute-start | bytes 688136 | tf_op jit(solution)/shard_map/ppermute | solution.py:504
  8.2 4.8 %expert_forward.1.refs_4_ = bf16[8,16,4096]{2,1,0:T(8,128)(2,1)} custom-call(bf16[128,768]{1,0:T(8,128)(2,1)S(1)} %get-tuple-element.18.hidden_ref, f32[6,1,32]{2,1,0:T(1,128)} %bitcast.16, bf16[768,4096]{1,0:T(8,128)(2,1)} %bitcast.8), custom_call_target="tpu_custom_call" | custom-call | flops 1024 | bytes 1024 | tf_op jit(solution)/shard_map/expert_forward/pallas_call | solution.py:221
  13.0 4.7 %all-to-all-start = ((bf16[8,16,4096]{2,1,0:T(8,128)(2,1)}), bf16[8,16,4096]{2,1,0:T(8,128)(2,1)}, u32[]{:S(2)}, u32[]{:S(2)}) async-start(bf16[8,16,4096]{2,1,0:T(8,128)(2,1)} %expert_forward.1.refs_4_), calls=%async_computation | async-start | bytes 2097152 | tf_op jit(solution)/shard_map/all_to_all | solution.py:526
  17.7 0.7 %collective-permute-done.4.refs_6_.refs_7_ = bf16[28,16,256]{2,1,0:T(8,128)(2,1)S(1)} collective-permute-done((bf16[28,16,256]{2,1,0:T(8,128)(2,1)S(1)}, bf16[28,16,256]{2,1,0:T(8,128)(2,1)S(1)}, u32[]{:S(2)}, u32[]{:S(2)}) %collective-permute-start.4) | collective-permute-done | bytes 229408 | tf_op jit(solution)/shard_map/ppermute | solution.py:504
  18.3 0.0 collective-permute-done.refs_1_.refs_0_
  18.3 0.0 collective-permute-done.3.refs_5_.refs_8_
  18.4 0.1 collective-permute-start.5
  18.5 3.2 %collective-permute-start.9 = (bf16[32,16,256]{2,1,0:T(8,128)(2,1)S(1)}, bf16[32,16,256]{2,1,0:T(8,128)(2,1)S(1)}, u32[]{:S(2)}, u32[]{:S(2)}) collective-permute-start(bf16[32,16,256]{2,1,0:T(8,128)(2,1)S(1)} %collective-permute-done.3.refs_5_.refs_8_), channel_id=1, source_target_pairs={{0,8},{8,0},{16,24},{24,16},{1,9},{9,1},{17,25},{25,17},{2,10},{10... | collective-permute-start | bytes 786440 | tf_op jit(solution)/shard_map/ppermute | solution.py:504
  21.7 0.8 %split.1 = (bf16[7,16,1024]{2,1,0:T(8,128)(2,1)S(1)}, bf16[7,16,1024]{2,1,0:T(8,128)(2,1)}, bf16[7,16,1024]{2,1,0:T(8,128)(2,1)}) custom-call(bf16[2,4,16,1024]{3,2,1,0:T(8,128)(2,1)S(1)} %collective-permute-done.refs_1_.refs_0_, bf16[2,4,16,1024]{3,2,1,0:T(8,128)(2,1)S(1)} %collective-permute-done.1.refs_2_.refs_1_, ...), custom_call_target="tpu_custom_call" | custom-call | flops 1024 | bytes 1024 | tf_op jit(solution)/shard_map/split/pallas_call | solution.py:271
  22.5 0.7 %collective-permute-start.7 = (bf16[7,16,1024]{2,1,0:T(8,128)(2,1)}, bf16[7,16,1024]{2,1,0:T(8,128)(2,1)S(1)}, u32[]{:S(2)}, u32[]{:S(2)}) collective-permute-start(bf16[7,16,1024]{2,1,0:T(8,128)(2,1)} %get-tuple-element.28), channel_id=1, source_target_pairs={{0,16},{8,24},{16,0},{24,8},{1,17},{9,25},{17,1},{25,9},{2,18},{10... | collective-permute-start | bytes 688136 | tf_op jit(solution)/shard_map/ppermute | solution.py:504
  23.2 2.6 %collective-permute-start.8 = (bf16[7,16,1024]{2,1,0:T(8,128)(2,1)}, bf16[7,16,1024]{2,1,0:T(8,128)(2,1)S(1)}, u32[]{:S(2)}, u32[]{:S(2)}) collective-permute-start(bf16[7,16,1024]{2,1,0:T(8,128)(2,1)} %get-tuple-element.29), channel_id=1, source_target_pairs={{0,24},{8,16},{16,8},{24,0},{1,25},{9,17},{17,9},{25,1},{2,26},{10... | collective-permute-start | bytes 688136 | tf_op jit(solution)/shard_map/ppermute | solution.py:504
  25.8 1.1 %collective-permute-start.6 = (bf16[7,16,1024]{2,1,0:T(8,128)(2,1)S(1)}, bf16[7,16,1024]{2,1,0:T(8,128)(2,1)S(1)}, u32[]{:S(2)}, u32[]{:S(2)}) collective-permute-start(bf16[7,16,1024]{2,1,0:T(8,128)(2,1)S(1)} %get-tuple-element.27.tie_ref), channel_id=1, source_target_pairs={{0,8},{8,0},{16,24},{24,16},{1,9},{9,1},{17,25},{25,17},{2,10},{10... | collective-permute-start | bytes 688136 | tf_op jit(solution)/shard_map/ppermute | solution.py:504
  26.9 5.3 %expert_backward.1 = bf16[128,1536]{1,0:T(8,128)(2,1)} custom-call(f32[6,1,32]{2,1,0:T(1,128)} %bitcast.17, bf16[128,1536]{1,0:T(8,128)(2,1)} %bitcast.11, bf16[768,4096]{1,0:T(8,128)(2,1)} %bitcast.9, bf16[7,16,1024]{2,1,0:T(8,128)(2,1)S(1)} %get-tuple-element.27.tie_ref, bf16[4,4,16,1024]{3,2,1,0:T(8,128)(2,1)S(1)} %collective-permute-done.5.refs_3_.swapped, ...), custom_call_target="tpu_custom_call" | custom-call | flops 1024 | bytes 1024 | tf_op jit(solution)/shard_map/expert_backward/pallas_call | solution.py:355
  32.1 0.0 all-to-all-done.ret_hbm
  32.1 3.6 %combine.1 = (bf16[128,4096]{1,0:T(8,128)(2,1)}, f32[8,128]{1,0:T(8,128)}) custom-call(s32[8,128]{1,0:T(8,128)} %bitcast.15, f32[128,128]{1,0:T(8,128)} %get-tuple-element.17.own_hbm, bf16[128,4096]{1,0:T(8,128)(2,1)} %dout_hbm.3, bf16[8,16,4096]{2,1,0:T(8,128)(2,1)} %all-to-all-done.ret_hbm), custom_call_target="tpu_custom_call" | custom-call | flops 1024 | bytes 1024 | tf_op jit(solution)/shard_map/combine/pallas_call | solution.py:421
  35.8 3.6 %collective-permute-done.7.refs_5_ = bf16[7,16,1024]{2,1,0:T(8,128)(2,1)S(1)} collective-permute-done((bf16[7,16,1024]{2,1,0:T(8,128)(2,1)}, bf16[7,16,1024]{2,1,0:T(8,128)(2,1)S(1)}, u32[]{:S(2)}, u32[]{:S(2)}) %collective-permute-start.7) | collective-permute-done | bytes 229408 | tf_op jit(solution)/shard_map/ppermute | solution.py:504
  39.4 7.1 %collective-permute-done.8.refs_6_ = bf16[7,16,1024]{2,1,0:T(8,128)(2,1)S(1)} collective-permute-done((bf16[7,16,1024]{2,1,0:T(8,128)(2,1)}, bf16[7,16,1024]{2,1,0:T(8,128)(2,1)S(1)}, u32[]{:S(2)}, u32[]{:S(2)}) %collective-permute-start.8) | collective-permute-done | bytes 229408 | tf_op jit(solution)/shard_map/ppermute | solution.py:504
  46.4 0.0 collective-permute-done.6.refs_4_
  46.4 1.8 %weight_grad.1 = bf16[1024,768]{1,0:T(8,128)(2,1)} custom-call(f32[8,128]{1,0:T(8,128)} %get-tuple-element.20.tie_ref, bf16[4,4,16,1024]{3,2,1,0:T(8,128)(2,1)S(1)} %collective-permute-done.5.refs_3_.swapped, bf16[128,768]{1,0:T(8,128)(2,1)S(1)} %get-tuple-element.18.hidden_ref, bf16[2,4,16,1024]{3,2,1,0:T(8,128)(2,1)S(1)} %get-tuple-element.24.refs_0_, ...), custom_call_target="tpu_custom_call" | custom-call | flops 1024 | bytes 1024 | tf_op jit(solution)/shard_map/weight_grad/pallas_call | solution.py:485
  (5 shorter events, 0.0 us)
Async XLA Ops:
  2.7 15.6 %collective-permute-start = (bf16[2,4,16,1024]{3,2,1,0:T(8,128)(2,1)S(1)}, bf16[2,4,16,1024]{3,2,1,0:T(8,128)(2,1)S(1)}, u32[]{:S(2)}, u32[]{:S(2)}) collective-permute-start(bf16[2,4,16,1024]{3,2,1,0:T(8,128)(2,1)S(1)} %get-tuple-element.21), channel_id=1, source_target_pairs={{0,2},{1,3},{2,0},{3,1},{4,6},{5,7},{6,4},{7,5},{8,10},{9,11},{10,... | collective-permute-start | bytes 786440 | tf_op jit(solution)/shard_map/ppermute | solution.py:504
  3.3 15.0 %collective-permute-start.1 = (bf16[2,4,16,1024]{3,2,1,0:T(8,128)(2,1)S(1)}, bf16[2,4,16,1024]{3,2,1,0:T(8,128)(2,1)S(1)}, u32[]{:S(2)}, u32[]{:S(2)}) collective-permute-start(bf16[2,4,16,1024]{3,2,1,0:T(8,128)(2,1)S(1)} %get-tuple-element.22), channel_id=1, source_target_pairs={{0,4},{1,5},{2,6},{3,7},{4,0},{5,1},{6,2},{7,3},{8,12},{9,13},{10,... | collective-permute-start | bytes 786440 | tf_op jit(solution)/shard_map/ppermute | solution.py:504
  4.8 13.5 %collective-permute-start.2 = (bf16[2,4,16,1024]{3,2,1,0:T(8,128)(2,1)S(1)}, bf16[2,4,16,1024]{3,2,1,0:T(8,128)(2,1)S(1)}, u32[]{:S(2)}, u32[]{:S(2)}) collective-permute-start(bf16[2,4,16,1024]{3,2,1,0:T(8,128)(2,1)S(1)} %get-tuple-element.23), channel_id=1, source_target_pairs={{0,6},{1,7},{2,4},{3,5},{4,2},{5,3},{6,0},{7,1},{8,14},{9,15},{10,... | collective-permute-start | bytes 786440 | tf_op jit(solution)/shard_map/ppermute | solution.py:504
  6.3 12.1 %collective-permute-start.3 = (bf16[32,16,256]{2,1,0:T(8,128)(2,1)S(1)}, bf16[32,16,256]{2,1,0:T(8,128)(2,1)S(1)}, u32[]{:S(2)}, u32[]{:S(2)}) collective-permute-start(bf16[32,16,256]{2,1,0:T(8,128)(2,1)S(1)} %get-tuple-element.25), channel_id=1, source_target_pairs={{0,16},{8,24},{16,0},{24,8},{1,17},{9,25},{17,1},{25,9},{2,18},{10... | collective-permute-start | bytes 786440 | tf_op jit(solution)/shard_map/ppermute | solution.py:504
  6.6 11.7 %collective-permute-start.4 = (bf16[28,16,256]{2,1,0:T(8,128)(2,1)S(1)}, bf16[28,16,256]{2,1,0:T(8,128)(2,1)S(1)}, u32[]{:S(2)}, u32[]{:S(2)}) collective-permute-start(bf16[28,16,256]{2,1,0:T(8,128)(2,1)S(1)} %get-tuple-element.26), channel_id=1, source_target_pairs={{0,8},{8,0},{16,24},{24,16},{1,9},{9,1},{17,25},{25,17},{2,10},{10... | collective-permute-start | bytes 688136 | tf_op jit(solution)/shard_map/ppermute | solution.py:504
  13.0 19.1 %all-to-all-start = ((bf16[8,16,4096]{2,1,0:T(8,128)(2,1)}), bf16[8,16,4096]{2,1,0:T(8,128)(2,1)}, u32[]{:S(2)}, u32[]{:S(2)}) async-start(bf16[8,16,4096]{2,1,0:T(8,128)(2,1)} %expert_forward.1.refs_4_), calls=%async_computation | async-start | bytes 2097152 | tf_op jit(solution)/shard_map/all_to_all | solution.py:526
  18.4 3.2 %collective-permute-start.5 = (bf16[4,4,16,1024]{3,2,1,0:T(8,128)(2,1)S(1)}, bf16[4,4,16,1024]{3,2,1,0:T(8,128)(2,1)S(1)}, u32[]{:S(2)}, u32[]{:S(2)}) collective-permute-start(bf16[4,4,16,1024]{3,2,1,0:T(8,128)(2,1)S(1)} %sibling_rows.1), channel_id=1, source_target_pairs={{0,1},{1,0},{2,3},{3,2},{4,5},{5,4},{6,7},{7,6},{8,9},{9,8},{10,11... | collective-permute-start | bytes 1572872 | tf_op jit(solution)/shard_map/ppermute | solution.py:504
  18.5 17.3 %collective-permute-start.9 = (bf16[32,16,256]{2,1,0:T(8,128)(2,1)S(1)}, bf16[32,16,256]{2,1,0:T(8,128)(2,1)S(1)}, u32[]{:S(2)}, u32[]{:S(2)}) collective-permute-start(bf16[32,16,256]{2,1,0:T(8,128)(2,1)S(1)} %collective-permute-done.3.refs_5_.refs_8_), channel_id=1, source_target_pairs={{0,8},{8,0},{16,24},{24,16},{1,9},{9,1},{17,25},{25,17},{2,10},{10... | collective-permute-start | bytes 786440 | tf_op jit(solution)/shard_map/ppermute | solution.py:504
  22.5 16.9 %collective-permute-start.7 = (bf16[7,16,1024]{2,1,0:T(8,128)(2,1)}, bf16[7,16,1024]{2,1,0:T(8,128)(2,1)S(1)}, u32[]{:S(2)}, u32[]{:S(2)}) collective-permute-start(bf16[7,16,1024]{2,1,0:T(8,128)(2,1)} %get-tuple-element.28), channel_id=1, source_target_pairs={{0,16},{8,24},{16,0},{24,8},{1,17},{9,25},{17,1},{25,9},{2,18},{10... | collective-permute-start | bytes 688136 | tf_op jit(solution)/shard_map/ppermute | solution.py:504
  23.2 23.3 %collective-permute-start.8 = (bf16[7,16,1024]{2,1,0:T(8,128)(2,1)}, bf16[7,16,1024]{2,1,0:T(8,128)(2,1)S(1)}, u32[]{:S(2)}, u32[]{:S(2)}) collective-permute-start(bf16[7,16,1024]{2,1,0:T(8,128)(2,1)} %get-tuple-element.29), channel_id=1, source_target_pairs={{0,24},{8,16},{16,8},{24,0},{1,25},{9,17},{17,9},{25,1},{2,26},{10... | collective-permute-start | bytes 688136 | tf_op jit(solution)/shard_map/ppermute | solution.py:504
  25.8 20.7 %collective-permute-start.6 = (bf16[7,16,1024]{2,1,0:T(8,128)(2,1)S(1)}, bf16[7,16,1024]{2,1,0:T(8,128)(2,1)S(1)}, u32[]{:S(2)}, u32[]{:S(2)}) collective-permute-start(bf16[7,16,1024]{2,1,0:T(8,128)(2,1)S(1)} %get-tuple-element.27.tie_ref), channel_id=1, source_target_pairs={{0,8},{8,0},{16,24},{24,16},{1,9},{9,1},{17,25},{25,17},{2,10},{10... | collective-permute-start | bytes 688136 | tf_op jit(solution)/shard_map/ppermute | solution.py:504

commit v10 on v9

--- a/solution.py
+++ b/solution.py
@@ -238,52 +238,51 @@
     )(hidden, hbm(scale), hbm(quant))
 
 
-def sibling_kernel(half, *refs):
-    chips, out_ref = refs[:half], refs[-1]
+def sort_kernel(half, *refs):
+    chips, (sibling, mine) = refs[:half], refs[-2:]
     for c in range(half):
-        out_ref[c] = chips[c][1]
-
-
-def sibling_rows(chips, ties):
+        sibling[c] = chips[c][1]
+        mine[c] = chips[c][0]
+
+
+def sort_rows(chips, ties):
     half = len(chips)
     return pl.pallas_call(
-        functools.partial(sibling_kernel, half),
-        out_shape=pltpu.VMEM((half,) + chips[0].shape[1:], bf16),
+        functools.partial(sort_kernel, half),
+        out_shape=(pltpu.VMEM((half,) + chips[0].shape[1:], bf16),) * 2,
         in_specs=[VMEM] * half + [ANY] * len(ties),
-        out_specs=VMEM,
+        out_specs=(VMEM, VMEM),
         compiler_params=params(2 * half * CAP),
         cost_estimate=SMALL,
-        name="sibling_rows",
+        name="sort_rows",
     )(*chips, *ties)
 
 
-def split_kernel(half, groups, *refs):
-    chips, swapped, pieces = refs[: half - 1], refs[half - 1], refs[1 - groups :]
-    for j in range(1, groups):
-        for c in range(half):
-            if c:
-                pieces[j - 1][c - 1] = chips[c - 1][0, j]
-            pieces[j - 1][half - 1 + c] = swapped[c, j]
-
-
-def split(chips, swapped):
+def split_kernel(mine, swapped, *pieces):
+    half = mine.shape[0]
+    for j, piece in enumerate(pieces, 1):
+        piece[: half - 1] = mine[1:, j]
+        piece[half - 1 :] = swapped[:, j]
+
+
+def split(mine, swapped):
     half, groups, cap, share = swapped.shape
     return pl.pallas_call(
-        functools.partial(split_kernel, half, groups),
+        split_kernel,
         out_shape=(pltpu.VMEM((2 * half - 1, cap, share), bf16),) * (groups - 1),
-        in_specs=[VMEM] * half,
+        in_specs=[VMEM, VMEM],
         out_specs=(VMEM,) * (groups - 1),
         compiler_params=params(2 * half * CAP),
         cost_estimate=SMALL,
         name="split",
-    )(*chips[1:], swapped)
-
-
-def backward_kernel(flight, groups, scale_hbm, gate_up_hbm, quant_hbm, tie_ref, swapped, *refs):
+    )(mine, swapped)
+
+
+def backward_kernel(
+    flight, groups, scale_hbm, gate_up_hbm, quant_hbm, tie_ref, mine, swapped, out_hbm,
+    scale, gate_up, rows, quant, acc, out, scale_sem, gate_sems, in_sems, out_sems
+):
     half = flight // 2
-    chips, out_hbm = refs[:half], refs[half]
-    scale, gate_up, rows, quant, acc, out = refs[half + 1 : half + 7]
-    scale_sem, gate_sems, in_sems, out_sems = refs[half + 7 :]
     me, group = lax.axis_index("expert"), lax.axis_index("dp")
     slots, hid = acc.shape
     share = quant.shape[2]
@@ -309,7 +308,7 @@
     for copy in [small] + loads + gates:
         copy.start()
     for c in range(half):
-        rows[:, c * CAP : (c + 1) * CAP, :] = chips[c][0]
+        rows[:, c * CAP : (c + 1) * CAP, :] = mine[c]
         rows[:, (half + c) * CAP : (half + c + 1) * CAP, :] = swapped[c]
     small.wait()
     for j in range(groups):
@@ -347,7 +346,7 @@
         copy.wait()
 
 
-def backward(scale, gate_up, quant, tie, chips, swapped):
+def backward(scale, gate_up, quant, tie, mine, swapped):
     slots, double = gate_up.shape
     hid, width = quant.shape
     half, groups, cap, share = swapped.shape
@@ -355,7 +354,7 @@
     return pl.pallas_call(
         functools.partial(backward_kernel, flight, groups),
         out_shape=pltpu.HBM((slots, double), bf16),
-        in_specs=[HBM, HBM, HBM, ANY] + [VMEM] * (1 + half),
+        in_specs=[HBM, HBM, HBM, ANY, VMEM, VMEM],
         out_specs=HBM,
         scratch_shapes=[
             pltpu.SMEM(scale.shape, f32),
@@ -372,7 +371,7 @@
         compiler_params=params(slots),
         cost_estimate=SMALL,
         name="expert_backward",
-    )(hbm(scale), hbm(gate_up), hbm(quant), tie, swapped, *chips)
+    )(hbm(scale), hbm(gate_up), hbm(quant), tie, mine, swapped)
 
 
 def combine_kernel(
@@ -439,10 +438,10 @@
     )(hbm(ids), hbm(own), hbm(d_out), hbm(returned))
 
 
-def weight_grad_kernel(half, groups, block, tie_ref, swapped, hidden_ref, *refs):
-    chips, parts = refs[:half], refs[half : half + groups - 1]
-    messages = refs[half + groups - 1 : half + 2 * groups - 2]
-    out_hbm, hidden, own, out, out_sems = refs[half + 2 * groups - 2 :]
+def weight_grad_kernel(groups, block, tie_ref, mine, swapped, hidden_ref, *refs):
+    parts, messages = refs[: groups - 1], refs[groups - 1 : 2 * groups - 2]
+    out_hbm, hidden, own, out, out_sems = refs[2 * groups - 2 :]
+    half = mine.shape[0]
     cap, share = parts[0].shape[1:]
     flight = 2 * half
     slots = flight * cap
@@ -462,7 +461,7 @@
             ]
     stores = []
     for n, cols in enumerate(chunks(share, block)):
-        grads = [chips[c][0, 0, :, cols] for c in range(half)]
+        grads = [mine[c, 0, :, cols] for c in range(half)]
         grads += [swapped[c, 0, :, cols] for c in range(half)]
         for j in range(1, groups):
             grads.append(own[j - 1, :, cols])
@@ -479,13 +478,13 @@
         copy.wait()
 
 
-def weight_grad(tie, chips, swapped, hidden, parts, messages, block=256):
+def weight_grad(tie, mine, swapped, hidden, parts, messages, block=256):
     half, groups, cap, share = swapped.shape
     slots, hid = hidden.shape
     return pl.pallas_call(
-        functools.partial(weight_grad_kernel, half, groups, block),
+        functools.partial(weight_grad_kernel, groups, block),
         out_shape=pltpu.HBM((share, hid), bf16),
-        in_specs=[HBM] + [VMEM] * (half + 2 * groups),
+        in_specs=[HBM] + [VMEM] * (1 + 2 * groups),
         out_specs=HBM,
         scratch_shapes=[
             pltpu.VMEM((groups * slots, hid), bf16),
@@ -496,7 +495,7 @@
         compiler_params=params(slots),
         cost_estimate=SMALL,
         name="weight_grad",
-    )(hbm(tie), swapped, hidden, *chips, *parts, *messages)
+    )(hbm(tie), mine, swapped, hidden, *parts, *messages)
 
 
 def swap(value, axis, j):
@@ -524,12 +523,13 @@
     messages = [messages[j] for j in range(1, groups)]
     expert_out = forward(scale, hidden, w_quant[0], flight)
     returned = lax.all_to_all(expert_out, "expert", split_axis=0, concat_axis=0, tiled=True)
-    swapped = swap(sibling_rows(chips, [hbm(expert_out)] + early), "expert", 1)
-    pieces = split(chips, swapped)
+    sibling, mine = sort_rows(chips, [hbm(expert_out)] + early)
+    swapped = swap(sibling, "expert", 1)
+    pieces = split(mine, swapped)
     parts = [swap(pieces[j - 1], "dp", j) for j in range(1, groups)]
-    d_gate_up = backward(scale, gate_up, w_quant[0], pieces[0], chips, swapped)
+    d_gate_up = backward(scale, gate_up, w_quant[0], pieces[0], mine, swapped)
     combined, d_probs = combine(ids, own, d_out, returned)
-    d_weight = weight_grad(d_probs, chips, swapped, hidden, parts, messages)
+    d_weight = weight_grad(d_probs, mine, swapped, hidden, parts, messages)
     return (combined, d_probs.T, d_gate_up[None, None], d_weight[None])
 
 

time: 48.5 us -> 47.6 us (0.981)
  the two profiles are of different devices: /device:TPU:18 before, /device:TPU:0 now
where the time goes in v10:
time: 47.6 us; the launch traced here: 46.8 us
  starting transfers between devices  18.9 us (40%)
  Pallas kernels  17.7 us (37%)
  waiting for transfers between devices  9.54 us (20%)
  between operations  0.73 us (2%)
    ppermute x10, starting transfers between devices, swap(): return lax.ppermute(value, axis, [(i, i ^ j) for i in range(size)])  14.6 us
    ppermute x10, waiting for transfers between devices, swap(): return lax.ppermute(value, axis, [(i, i ^ j) for i in range(size)])  6.12 us
    pallas_call x1, Pallas kernels, backward(): pl.pallas_call(functools.partial(backward_kernel, flight, groups), out_sh...  5.28 us
    pallas_call x1, Pallas kernels, forward(): pl.pallas_call(functools.partial(forward_kernel, flight, block), out_shap...  4.78 us
    all_to_all x1, starting transfers between devices, shards(): lax.all_to_all(expert_out, 'expert', split_axis=0, concat_axis=0, tiled=T...  4.27 us
    pallas_call x1, Pallas kernels, combine(): pl.pallas_call(functools.partial(combine_kernel, block), out_shape=(pltpu...  3.63 us
    all_to_all x1, waiting for transfers between devices, shards(): lax.all_to_all(expert_out, 'expert', split_axis=0, concat_axis=0, tiled=T...  3.41 us
    pallas_call x1, Pallas kernels, dispatch(): pl.pallas_call(functools.partial(dispatch_kernel, flight, groups), out_sh...  2.09 us
  transfers between devices with their start and end apart: 11, of which 5 were waited for; matrix products, arithmetic and copies ran while one was open for 0% of the time, Pallas kernels for 29%

profile of v10, /device:TPU:0, one launch (start us, length us, event | category | flops | bytes accessed | tf_op | source)
XLA Modules:
  0.0 46.8 jit_solution(9656190431009952584)
XLA Ops:
  0.6 2.1 %dispatch.1 = (f32[128,128]{1,0:T(8,128)}, bf16[128,768]{1,0:T(8,128)(2,1)S(1)}, bf16[2,4,16,1024]{3,2,1,0:T(8,128)(2,1)S(1)}, bf16[2,4,16,1024]{3,2,1,0:T(8,128...) custom-call(bf16[128,1536]{1,0:T(8,128)(2,1)} %bitcast.10, ...), custom_call_target="tpu_custom_call" | custom-call | flops 1024 | bytes 1024 | tf_op jit(solution)/shard_map/dispatch/pallas_call | solution.py:147
  2.7 3.0 %collective-permute-start = (bf16[2,4,16,1024]{3,2,1,0:T(8,128)(2,1)S(1)}, bf16[2,4,16,1024]{3,2,1,0:T(8,128)(2,1)S(1)}, u32[]{:S(2)}, u32[]{:S(2)}) collective-permute-start(bf16[2,4,16,1024]{3,2,1,0:T(8,128)(2,1)S(1)} %get-tuple-element.24), channel_id=1, source_target_pairs={{0,2},{1,3},{2,0},{3,1},{4,6},{5,7},{6,4},{7,5},{8,10},{9,11},{10,... | collective-permute-start | bytes 786440 | tf_op jit(solution)/shard_map/ppermute | solution.py:503
  5.7 1.5 %collective-permute-start.1 = (bf16[2,4,16,1024]{3,2,1,0:T(8,128)(2,1)S(1)}, bf16[2,4,16,1024]{3,2,1,0:T(8,128)(2,1)S(1)}, u32[]{:S(2)}, u32[]{:S(2)}) collective-permute-start(bf16[2,4,16,1024]{3,2,1,0:T(8,128)(2,1)S(1)} %get-tuple-element.25), channel_id=1, source_target_pairs={{0,4},{1,5},{2,6},{3,7},{4,0},{5,1},{6,2},{7,3},{8,12},{9,13},{10,... | collective-permute-start | bytes 786440 | tf_op jit(solution)/shard_map/ppermute | solution.py:503
  7.3 0.0 collective-permute-start.2
  7.3 3.0 %collective-permute-start.3 = (bf16[32,16,256]{2,1,0:T(8,128)(2,1)S(1)}, bf16[32,16,256]{2,1,0:T(8,128)(2,1)S(1)}, u32[]{:S(2)}, u32[]{:S(2)}) collective-permute-start(bf16[32,16,256]{2,1,0:T(8,128)(2,1)S(1)} %get-tuple-element.27), channel_id=1, source_target_pairs={{0,16},{8,24},{16,0},{24,8},{1,17},{9,25},{17,1},{25,9},{2,18},{10... | collective-permute-start | bytes 786440 | tf_op jit(solution)/shard_map/ppermute | solution.py:503
  10.3 1.6 %collective-permute-start.4 = (bf16[28,16,256]{2,1,0:T(8,128)(2,1)S(1)}, bf16[28,16,256]{2,1,0:T(8,128)(2,1)S(1)}, u32[]{:S(2)}, u32[]{:S(2)}) collective-permute-start(bf16[28,16,256]{2,1,0:T(8,128)(2,1)S(1)} %get-tuple-element.28), channel_id=1, source_target_pairs={{0,8},{8,0},{16,24},{24,16},{1,9},{9,1},{17,25},{25,17},{2,10},{10... | collective-permute-start | bytes 688136 | tf_op jit(solution)/shard_map/ppermute | solution.py:503
  11.9 4.8 %expert_forward.1.refs_4_ = bf16[8,16,4096]{2,1,0:T(8,128)(2,1)} custom-call(bf16[128,768]{1,0:T(8,128)(2,1)S(1)} %get-tuple-element.20.hidden_ref, f32[6,1,32]{2,1,0:T(1,128)} %bitcast.16, bf16[768,4096]{1,0:T(8,128)(2,1)} %bitcast.8), custom_call_target="tpu_custom_call" | custom-call | flops 1024 | bytes 1024 | tf_op jit(solution)/shard_map/expert_forward/pallas_call | solution.py:221
  16.7 4.3 %all-to-all-start = ((bf16[8,16,4096]{2,1,0:T(8,128)(2,1)}), bf16[8,16,4096]{2,1,0:T(8,128)(2,1)}, u32[]{:S(2)}, u32[]{:S(2)}) async-start(bf16[8,16,4096]{2,1,0:T(8,128)(2,1)} %expert_forward.1.refs_4_), calls=%async_computation | async-start | bytes 2097152 | tf_op jit(solution)/shard_map/all_to_all | solution.py:525
  21.0 0.0 collective-permute-done.4.refs_6_.refs_3_
  21.0 0.0 collective-permute-done.1.refs_2_
  21.0 0.4 collective-permute-done.3.refs_5_.refs_4_
  21.4 0.1 sort_rows.1
  21.5 0.1 collective-permute-start.5
  21.6 1.2 %collective-permute-start.9 = (bf16[32,16,256]{2,1,0:T(8,128)(2,1)S(1)}, bf16[32,16,256]{2,1,0:T(8,128)(2,1)S(1)}, u32[]{:S(2)}, u32[]{:S(2)}) collective-permute-start(bf16[32,16,256]{2,1,0:T(8,128)(2,1)S(1)} %collective-permute-done.3.refs_5_.refs_4_), channel_id=1, source_target_pairs={{0,8},{8,0},{16,24},{24,16},{1,9},{9,1},{17,25},{25,17},{2,10},{10... | collective-permute-start | bytes 786440 | tf_op jit(solution)/shard_map/ppermute | solution.py:503
  22.7 0.7 %collective-permute-done.5.swapped = bf16[4,4,16,1024]{3,2,1,0:T(8,128)(2,1)S(1)} collective-permute-done((bf16[4,4,16,1024]{3,2,1,0:T(8,128)(2,1)S(1)}, bf16[4,4,16,1024]{3,2,1,0:T(8,128)(2,1)S(1)}, u32[]{:S(2)}, u32[]{:S(2)}) %collective-permute-start.5) | collective-permute-done | bytes 524320 | tf_op jit(solution)/shard_map/ppermute | solution.py:503
  23.5 2.3 %collective-permute-start.7 = (bf16[7,16,1024]{2,1,0:T(8,128)(2,1)S(1)}, bf16[7,16,1024]{2,1,0:T(8,128)(2,1)S(1)}, u32[]{:S(2)}, u32[]{:S(2)}) collective-permute-start(bf16[7,16,1024]{2,1,0:T(8,128)(2,1)S(1)} %get-tuple-element.32), channel_id=1, source_target_pairs={{0,16},{8,24},{16,0},{24,8},{1,17},{9,25},{17,1},{25,9},{2,18},{10... | collective-permute-start | bytes 688136 | tf_op jit(solution)/shard_map/ppermute | solution.py:503
  25.8 1.3 %collective-permute-start.8 = (bf16[7,16,1024]{2,1,0:T(8,128)(2,1)S(1)}, bf16[7,16,1024]{2,1,0:T(8,128)(2,1)S(1)}, u32[]{:S(2)}, u32[]{:S(2)}) collective-permute-start(bf16[7,16,1024]{2,1,0:T(8,128)(2,1)S(1)} %get-tuple-element.33), channel_id=1, source_target_pairs={{0,24},{8,16},{16,8},{24,0},{1,25},{9,17},{17,9},{25,1},{2,26},{10... | collective-permute-start | bytes 688136 | tf_op jit(solution)/shard_map/ppermute | solution.py:503
  27.2 0.5 %collective-permute-start.6 = (bf16[7,16,1024]{2,1,0:T(8,128)(2,1)S(1)}, bf16[7,16,1024]{2,1,0:T(8,128)(2,1)S(1)}, u32[]{:S(2)}, u32[]{:S(2)}) collective-permute-start(bf16[7,16,1024]{2,1,0:T(8,128)(2,1)S(1)} %get-tuple-element.31.tie_ref), channel_id=1, source_target_pairs={{0,8},{8,0},{16,24},{24,16},{1,9},{9,1},{17,25},{25,17},{2,10},{10... | collective-permute-start | bytes 688136 | tf_op jit(solution)/shard_map/ppermute | solution.py:503
  27.7 5.3 %expert_backward.1 = bf16[128,1536]{1,0:T(8,128)(2,1)} custom-call(f32[6,1,32]{2,1,0:T(1,128)} %bitcast.17, bf16[128,1536]{1,0:T(8,128)(2,1)} %bitcast.11, bf16[768,4096]{1,0:T(8,128)(2,1)} %bitcast.9, bf16[7,16,1024]{2,1,0:T(8,128)(2,1)S(1)} %get-tuple-element.31.tie_ref, bf16[4,4,16,1024]{3,2,1,0:T(8,128)(2,1)S(1)} %get-tuple-element.29.mine, ...), custom_call_target="tpu_custom_call" | custom-call | flops 1024 | bytes 1024 | tf_op jit(solution)/shard_map/expert_backward/pallas_call | solution.py:354
  33.0 3.4 %all-to-all-done.ret_hbm = bf16[8,16,4096]{2,1,0:T(8,128)(2,1)} async-done(((bf16[8,16,4096]{2,1,0:T(8,128)(2,1)}), bf16[8,16,4096]{2,1,0:T(8,128)(2,1)}, u32[]{:S(2)}, u32[]{:S(2)}) %all-to-all-start) | async-done | bytes 1048608 | tf_op jit(solution)/shard_map/all_to_all | solution.py:525
  36.4 3.6 %combine.1 = (bf16[128,4096]{1,0:T(8,128)(2,1)}, f32[8,128]{1,0:T(8,128)}) custom-call(s32[8,128]{1,0:T(8,128)} %bitcast.15, f32[128,128]{1,0:T(8,128)} %get-tuple-element.19.own_hbm, bf16[128,4096]{1,0:T(8,128)(2,1)} %dout_hbm.3, bf16[8,16,4096]{2,1,0:T(8,128)(2,1)} %all-to-all-done.ret_hbm), custom_call_target="tpu_custom_call" | custom-call | flops 1024 | bytes 1024 | tf_op jit(solution)/shard_map/combine/pallas_call | solution.py:420
  40.0 2.8 %collective-permute-done.7.refs_1_ = bf16[7,16,1024]{2,1,0:T(8,128)(2,1)S(1)} collective-permute-done((bf16[7,16,1024]{2,1,0:T(8,128)(2,1)S(1)}, bf16[7,16,1024]{2,1,0:T(8,128)(2,1)S(1)}, u32[]{:S(2)}, u32[]{:S(2)}) %collective-permute-start.7) | collective-permute-done | bytes 229408 | tf_op jit(solution)/shard_map/ppermute | solution.py:503
  42.8 2.2 %collective-permute-done.6.refs_0_ = bf16[7,16,1024]{2,1,0:T(8,128)(2,1)S(1)} collective-permute-done((bf16[7,16,1024]{2,1,0:T(8,128)(2,1)S(1)}, bf16[7,16,1024]{2,1,0:T(8,128)(2,1)S(1)}, u32[]{:S(2)}, u32[]{:S(2)}) %collective-permute-start.6) | collective-permute-done | bytes 229408 | tf_op jit(solution)/shard_map/ppermute | solution.py:503
  45.0 1.8 %weight_grad.1 = bf16[1024,768]{1,0:T(8,128)(2,1)} custom-call(f32[8,128]{1,0:T(8,128)} %get-tuple-element.22.tie_ref, bf16[4,4,16,1024]{3,2,1,0:T(8,128)(2,1)S(1)} %get-tuple-element.29.mine, bf16[4,4,16,1024]{3,2,1,0:T(8,128)(2,1)S(1)} %collective-permute-done.5.swapped, bf16[128,768]{1,0:T(8,128)(2,1)S(1)} %get-tuple-element.20.hidden_ref, ...), custom_call_target="tpu_custom_call" | custom-call | flops 1024 | bytes 1024 | tf_op jit(solution)/shard_map/weight_grad/pallas_call | solution.py:484
  (5 shorter events, 0.1 us)
Async XLA Ops:
  2.7 18.2 %collective-permute-start = (bf16[2,4,16,1024]{3,2,1,0:T(8,128)(2,1)S(1)}, bf16[2,4,16,1024]{3,2,1,0:T(8,128)(2,1)S(1)}, u32[]{:S(2)}, u32[]{:S(2)}) collective-permute-start(bf16[2,4,16,1024]{3,2,1,0:T(8,128)(2,1)S(1)} %get-tuple-element.24), channel_id=1, source_target_pairs={{0,2},{1,3},{2,0},{3,1},{4,6},{5,7},{6,4},{7,5},{8,10},{9,11},{10,... | collective-permute-start | bytes 786440 | tf_op jit(solution)/shard_map/ppermute | solution.py:503
  5.7 15.3 %collective-permute-start.1 = (bf16[2,4,16,1024]{3,2,1,0:T(8,128)(2,1)S(1)}, bf16[2,4,16,1024]{3,2,1,0:T(8,128)(2,1)S(1)}, u32[]{:S(2)}, u32[]{:S(2)}) collective-permute-start(bf16[2,4,16,1024]{3,2,1,0:T(8,128)(2,1)S(1)} %get-tuple-element.25), channel_id=1, source_target_pairs={{0,4},{1,5},{2,6},{3,7},{4,0},{5,1},{6,2},{7,3},{8,12},{9,13},{10,... | collective-permute-start | bytes 786440 | tf_op jit(solution)/shard_map/ppermute | solution.py:503
  7.3 13.7 %collective-permute-start.2 = (bf16[2,4,16,1024]{3,2,1,0:T(8,128)(2,1)S(1)}, bf16[2,4,16,1024]{3,2,1,0:T(8,128)(2,1)S(1)}, u32[]{:S(2)}, u32[]{:S(2)}) collective-permute-start(bf16[2,4,16,1024]{3,2,1,0:T(8,128)(2,1)S(1)} %get-tuple-element.26), channel_id=1, source_target_pairs={{0,6},{1,7},{2,4},{3,5},{4,2},{5,3},{6,0},{7,1},{8,14},{9,15},{10,... | collective-permute-start | bytes 786440 | tf_op jit(solution)/shard_map/ppermute | solution.py:503
  7.3 14.1 %collective-permute-start.3 = (bf16[32,16,256]{2,1,0:T(8,128)(2,1)S(1)}, bf16[32,16,256]{2,1,0:T(8,128)(2,1)S(1)}, u32[]{:S(2)}, u32[]{:S(2)}) collective-permute-start(bf16[32,16,256]{2,1,0:T(8,128)(2,1)S(1)} %get-tuple-element.27), channel_id=1, source_target_pairs={{0,16},{8,24},{16,0},{24,8},{1,17},{9,25},{17,1},{25,9},{2,18},{10... | collective-permute-start | bytes 786440 | tf_op jit(solution)/shard_map/ppermute | solution.py:503
  10.3 10.6 %collective-permute-start.4 = (bf16[28,16,256]{2,1,0:T(8,128)(2,1)S(1)}, bf16[28,16,256]{2,1,0:T(8,128)(2,1)S(1)}, u32[]{:S(2)}, u32[]{:S(2)}) collective-permute-start(bf16[28,16,256]{2,1,0:T(8,128)(2,1)S(1)} %get-tuple-element.28), channel_id=1, source_target_pairs={{0,8},{8,0},{16,24},{24,16},{1,9},{9,1},{17,25},{25,17},{2,10},{10... | collective-permute-start | bytes 688136 | tf_op jit(solution)/shard_map/ppermute | solution.py:503
  16.7 19.7 %all-to-all-start = ((bf16[8,16,4096]{2,1,0:T(8,128)(2,1)}), bf16[8,16,4096]{2,1,0:T(8,128)(2,1)}, u32[]{:S(2)}, u32[]{:S(2)}) async-start(bf16[8,16,4096]{2,1,0:T(8,128)(2,1)} %expert_forward.1.refs_4_), calls=%async_computation | async-start | bytes 2097152 | tf_op jit(solution)/shard_map/all_to_all | solution.py:525
  21.5 2.0 %collective-permute-start.5 = (bf16[4,4,16,1024]{3,2,1,0:T(8,128)(2,1)S(1)}, bf16[4,4,16,1024]{3,2,1,0:T(8,128)(2,1)S(1)}, u32[]{:S(2)}, u32[]{:S(2)}) collective-permute-start(bf16[4,4,16,1024]{3,2,1,0:T(8,128)(2,1)S(1)} %get-tuple-element.30), channel_id=1, source_target_pairs={{0,1},{1,0},{2,3},{3,2},{4,5},{5,4},{6,7},{7,6},{8,9},{9,8},{10,11... | collective-permute-start | bytes 1572872 | tf_op jit(solution)/shard_map/ppermute | solution.py:503
  21.6 18.5 %collective-permute-start.9 = (bf16[32,16,256]{2,1,0:T(8,128)(2,1)S(1)}, bf16[32,16,256]{2,1,0:T(8,128)(2,1)S(1)}, u32[]{:S(2)}, u32[]{:S(2)}) collective-permute-start(bf16[32,16,256]{2,1,0:T(8,128)(2,1)S(1)} %collective-permute-done.3.refs_5_.refs_4_), channel_id=1, source_target_pairs={{0,8},{8,0},{16,24},{24,16},{1,9},{9,1},{17,25},{25,17},{2,10},{10... | collective-permute-start | bytes 786440 | tf_op jit(solution)/shard_map/ppermute | solution.py:503
  23.5 19.3 %collective-permute-start.7 = (bf16[7,16,1024]{2,1,0:T(8,128)(2,1)S(1)}, bf16[7,16,1024]{2,1,0:T(8,128)(2,1)S(1)}, u32[]{:S(2)}, u32[]{:S(2)}) collective-permute-start(bf16[7,16,1024]{2,1,0:T(8,128)(2,1)S(1)} %get-tuple-element.32), channel_id=1, source_target_pairs={{0,16},{8,24},{16,0},{24,8},{1,17},{9,25},{17,1},{25,9},{2,18},{10... | collective-permute-start | bytes 688136 | tf_op jit(solution)/shard_map/ppermute | solution.py:503
  25.8 17.0 %collective-permute-start.8 = (bf16[7,16,1024]{2,1,0:T(8,128)(2,1)S(1)}, bf16[7,16,1024]{2,1,0:T(8,128)(2,1)S(1)}, u32[]{:S(2)}, u32[]{:S(2)}) collective-permute-start(bf16[7,16,1024]{2,1,0:T(8,128)(2,1)S(1)} %get-tuple-element.33), channel_id=1, source_target_pairs={{0,24},{8,16},{16,8},{24,0},{1,25},{9,17},{17,9},{25,1},{2,26},{10... | collective-permute-start | bytes 688136 | tf_op jit(solution)/shard_map/ppermute | solution.py:503
  27.2 17.8 %collective-permute-start.6 = (bf16[7,16,1024]{2,1,0:T(8,128)(2,1)S(1)}, bf16[7,16,1024]{2,1,0:T(8,128)(2,1)S(1)}, u32[]{:S(2)}, u32[]{:S(2)}) collective-permute-start(bf16[7,16,1024]{2,1,0:T(8,128)(2,1)S(1)} %get-tuple-element.31.tie_ref), channel_id=1, source_target_pairs={{0,8},{8,0},{16,24},{24,16},{1,9},{9,1},{17,25},{25,17},{2,10},{10... | collective-permute-start | bytes 688136 | tf_op jit(solution)/shard_map/ppermute | solution.py:503

commit v11 on v10

--- a/solution.py
+++ b/solution.py
@@ -10,6 +10,7 @@
 QB = 128
 CAP = 16
 TILE = 256
+AHEAD = 3
 
 bf16 = jnp.bfloat16
 f32 = jnp.float32
@@ -39,6 +40,11 @@
         groups //= 2
         bits.append(groups)
     return bits
+
+
+def message_tiles(flight, groups, bit, hid, share):
+    far = 1 if 2 * bit == groups else 0
+    return flight * (hid // TILE) + bit * (share // TILE) + far
 
 
 def block_place(me, r, flight):
@@ -124,6 +130,7 @@
                 first = flight * (hid // TILE) + (j - bit) * (share // TILE)
                 for q in range(share // TILE):
                     messages[bit][first + q] = part[:CAP, q * TILE : (q + 1) * TILE]
+    messages[bits[0]][messages[bits[0]].shape[0] - 1] = jnp.zeros((CAP, TILE), bf16)
     for copy in gates:
         copy.wait()
     for r in range(flight):
@@ -149,7 +156,7 @@
         out_shape=(pltpu.HBM((slots, tokens), f32), pltpu.VMEM((rows, double // 2), bf16))
         + (pltpu.VMEM((2, groups, CAP, share), bf16),) * half
         + tuple(
-            pltpu.VMEM((flight * (double // 2 // TILE) + bit * (share // TILE), CAP, TILE), bf16)
+            pltpu.VMEM((message_tiles(flight, groups, bit, double // 2, share), CAP, TILE), bf16)
             for bit in bits_of(groups)
         ),
         in_specs=[HBM] * 6,
@@ -184,7 +191,7 @@
         for c in range(steps)
     ]
     small = pltpu.make_async_copy(scale_hbm, scale, scale_sem)
-    for copy in [small] + loads:
+    for copy in [small] + loads[:AHEAD]:
         copy.start()
     for r in range(flight):
         place = pl.multiple_of(block_place(me, r, flight) * CAP, CAP)
@@ -194,6 +201,8 @@
     for c in range(steps):
         cols = pl.ds(c * block, block)
         loads[c].wait()
+        if c + AHEAD < steps:
+            loads[c + AHEAD].start()
         total = [None] * (block // QB)
         for i in range(hid // QB):
             part = jnp.dot(

time: 47.6 us -> 47.4 us (level)
    ppermute x10, waiting for transfers between devices: 6.12 us -> 5.08 us  [swap(): return lax.ppermute(value, axis, [(i, i ^ j) for i in range(size)])]
    all_to_all x1, waiting for transfers between devices: 3.41 us -> 4 us  [shards(): lax.all_to_all(expert_out, 'expert', split_axis=0, concat_axis=0, tiled=T...]
  transfers between devices with their start and end apart: 11 -> 11, of which waited for: 5 -> 4; matrix products, arithmetic and copies ran while one was open for 0% -> 0% of each run, Pallas kernels for 29% -> 30%
where the time goes in v11:
time: 47.4 us; the launch traced here: 47.1 us
  starting transfers between devices  19.1 us (40%)
  Pallas kernels  18.1 us (38%)
  waiting for transfers between devices  9.08 us (19%)
  between operations  0.73 us (2%)
    ppermute x10, starting transfers between devices, swap(): return lax.ppermute(value, axis, [(i, i ^ j) for i in range(size)])  14.8 us
    pallas_call x1, Pallas kernels, backward(): pl.pallas_call(functools.partial(backward_kernel, flight, groups), out_sh...  5.26 us
    pallas_call x1, Pallas kernels, forward(): pl.pallas_call(functools.partial(forward_kernel, flight, block), out_shap...  5.22 us
    ppermute x10, waiting for transfers between devices, swap(): return lax.ppermute(value, axis, [(i, i ^ j) for i in range(size)])  5.08 us
    all_to_all x1, starting transfers between devices, shards(): lax.all_to_all(expert_out, 'expert', split_axis=0, concat_axis=0, tiled=T...  4.27 us
    all_to_all x1, waiting for transfers between devices, shards(): lax.all_to_all(expert_out, 'expert', split_axis=0, concat_axis=0, tiled=T...  4 us
    pallas_call x1, Pallas kernels, combine(): pl.pallas_call(functools.partial(combine_kernel, block), out_shape=(pltpu...  3.63 us
    pallas_call x1, Pallas kernels, dispatch(): pl.pallas_call(functools.partial(dispatch_kernel, flight, groups), out_sh...  2.09 us
  transfers between devices with their start and end apart: 11, of which 4 were waited for; matrix products, arithmetic and copies ran while one was open for 0% of the time, Pallas kernels for 30%

profile of v11, /device:TPU:0, one launch (start us, length us, event | category | flops | bytes accessed | tf_op | source)
XLA Modules:
  0.0 47.1 jit_solution(12462787311768704040)
XLA Ops:
  0.6 2.1 %dispatch.1 = (f32[128,128]{1,0:T(8,128)}, bf16[128,768]{1,0:T(8,128)(2,1)S(1)}, bf16[2,4,16,1024]{3,2,1,0:T(8,128)(2,1)S(1)}, bf16[2,4,16,1024]{3,2,1,0:T(8,128...) custom-call(bf16[128,1536]{1,0:T(8,128)(2,1)} %bitcast.10, ...), custom_call_target="tpu_custom_call" | custom-call | flops 1024 | bytes 1024 | tf_op jit(solution)/shard_map/dispatch/pallas_call | solution.py:154
  2.7 4.1 %collective-permute-start.3 = (bf16[33,16,256]{2,1,0:T(8,128)(2,1)S(1)}, bf16[33,16,256]{2,1,0:T(8,128)(2,1)S(1)}, u32[]{:S(2)}, u32[]{:S(2)}) collective-permute-start(bf16[33,16,256]{2,1,0:T(8,128)(2,1)S(1)} %get-tuple-element.27), channel_id=1, source_target_pairs={{0,16},{8,24},{16,0},{24,8},{1,17},{9,25},{17,1},{25,9},{2,18},{10... | collective-permute-start | bytes 811016 | tf_op jit(solution)/shard_map/ppermute | solution.py:512
  6.8 1.5 %collective-permute-start = (bf16[2,4,16,1024]{3,2,1,0:T(8,128)(2,1)S(1)}, bf16[2,4,16,1024]{3,2,1,0:T(8,128)(2,1)S(1)}, u32[]{:S(2)}, u32[]{:S(2)}) collective-permute-start(bf16[2,4,16,1024]{3,2,1,0:T(8,128)(2,1)S(1)} %get-tuple-element.24), channel_id=1, source_target_pairs={{0,2},{1,3},{2,0},{3,1},{4,6},{5,7},{6,4},{7,5},{8,10},{9,11},{10,... | collective-permute-start | bytes 786440 | tf_op jit(solution)/shard_map/ppermute | solution.py:512
  8.3 1.5 %collective-permute-start.1 = (bf16[2,4,16,1024]{3,2,1,0:T(8,128)(2,1)S(1)}, bf16[2,4,16,1024]{3,2,1,0:T(8,128)(2,1)S(1)}, u32[]{:S(2)}, u32[]{:S(2)}) collective-permute-start(bf16[2,4,16,1024]{3,2,1,0:T(8,128)(2,1)S(1)} %get-tuple-element.25), channel_id=1, source_target_pairs={{0,4},{1,5},{2,6},{3,7},{4,0},{5,1},{6,2},{7,3},{8,12},{9,13},{10,... | collective-permute-start | bytes 786440 | tf_op jit(solution)/shard_map/ppermute | solution.py:512
  9.8 0.5 %collective-permute-start.2 = (bf16[2,4,16,1024]{3,2,1,0:T(8,128)(2,1)S(1)}, bf16[2,4,16,1024]{3,2,1,0:T(8,128)(2,1)S(1)}, u32[]{:S(2)}, u32[]{:S(2)}) collective-permute-start(bf16[2,4,16,1024]{3,2,1,0:T(8,128)(2,1)S(1)} %get-tuple-element.26), channel_id=1, source_target_pairs={{0,6},{1,7},{2,4},{3,5},{4,2},{5,3},{6,0},{7,1},{8,14},{9,15},{10,... | collective-permute-start | bytes 786440 | tf_op jit(solution)/shard_map/ppermute | solution.py:512
  10.3 1.6 %collective-permute-start.4 = (bf16[28,16,256]{2,1,0:T(8,128)(2,1)S(1)}, bf16[28,16,256]{2,1,0:T(8,128)(2,1)S(1)}, u32[]{:S(2)}, u32[]{:S(2)}) collective-permute-start(bf16[28,16,256]{2,1,0:T(8,128)(2,1)S(1)} %get-tuple-element.28), channel_id=1, source_target_pairs={{0,8},{8,0},{16,24},{24,16},{1,9},{9,1},{17,25},{25,17},{2,10},{10... | collective-permute-start | bytes 688136 | tf_op jit(solution)/shard_map/ppermute | solution.py:512
  11.9 5.2 %expert_forward.1.refs_4_ = bf16[8,16,4096]{2,1,0:T(8,128)(2,1)} custom-call(bf16[128,768]{1,0:T(8,128)(2,1)S(1)} %get-tuple-element.20.hidden_ref, f32[6,1,32]{2,1,0:T(1,128)} %bitcast.16, bf16[768,4096]{1,0:T(8,128)(2,1)} %bitcast.8), custom_call_target="tpu_custom_call" | custom-call | flops 1024 | bytes 1024 | tf_op jit(solution)/shard_map/expert_forward/pallas_call | solution.py:230
  17.1 4.3 %all-to-all-start = ((bf16[8,16,4096]{2,1,0:T(8,128)(2,1)}), bf16[8,16,4096]{2,1,0:T(8,128)(2,1)}, u32[]{:S(2)}, u32[]{:S(2)}) async-start(bf16[8,16,4096]{2,1,0:T(8,128)(2,1)} %expert_forward.1.refs_4_), calls=%async_computation | async-start | bytes 2097152 | tf_op jit(solution)/shard_map/all_to_all | solution.py:534
  21.4 0.0 collective-permute-done.4.refs_6_.refs_3_
  21.4 0.0 collective-permute-done.refs_1_
  21.4 0.0 collective-permute-done.1.refs_2_
  21.4 0.1 sort_rows.1
  21.5 0.4 collective-permute-start.5
  22.0 1.3 %collective-permute-start.9 = (bf16[33,16,256]{2,1,0:T(8,128)(2,1)S(1)}, bf16[33,16,256]{2,1,0:T(8,128)(2,1)S(1)}, u32[]{:S(2)}, u32[]{:S(2)}) collective-permute-start(bf16[33,16,256]{2,1,0:T(8,128)(2,1)S(1)} %collective-permute-done.3.refs_5_.refs_4_), channel_id=1, source_target_pairs={{0,8},{8,0},{16,24},{24,16},{1,9},{9,1},{17,25},{25,17},{2,10},{10... | collective-permute-start | bytes 811016 | tf_op jit(solution)/shard_map/ppermute | solution.py:512
  23.2 0.3 collective-permute-done.5.swapped
  23.6 1.0 %collective-permute-start.7 = (bf16[7,16,1024]{2,1,0:T(8,128)(2,1)S(1)}, bf16[7,16,1024]{2,1,0:T(8,128)(2,1)S(1)}, u32[]{:S(2)}, u32[]{:S(2)}) collective-permute-start(bf16[7,16,1024]{2,1,0:T(8,128)(2,1)S(1)} %get-tuple-element.32), channel_id=1, source_target_pairs={{0,16},{8,24},{16,0},{24,8},{1,17},{9,25},{17,1},{25,9},{2,18},{10... | collective-permute-start | bytes 688136 | tf_op jit(solution)/shard_map/ppermute | solution.py:512
  24.5 3.0 %collective-permute-start.8 = (bf16[7,16,1024]{2,1,0:T(8,128)(2,1)S(1)}, bf16[7,16,1024]{2,1,0:T(8,128)(2,1)S(1)}, u32[]{:S(2)}, u32[]{:S(2)}) collective-permute-start(bf16[7,16,1024]{2,1,0:T(8,128)(2,1)S(1)} %get-tuple-element.33), channel_id=1, source_target_pairs={{0,24},{8,16},{16,8},{24,0},{1,25},{9,17},{17,9},{25,1},{2,26},{10... | collective-permute-start | bytes 688136 | tf_op jit(solution)/shard_map/ppermute | solution.py:512
  27.5 5.3 %expert_backward.1 = bf16[128,1536]{1,0:T(8,128)(2,1)} custom-call(f32[6,1,32]{2,1,0:T(1,128)} %bitcast.17, bf16[128,1536]{1,0:T(8,128)(2,1)} %bitcast.11, bf16[768,4096]{1,0:T(8,128)(2,1)} %bitcast.9, bf16[7,16,1024]{2,1,0:T(8,128)(2,1)S(1)} %get-tuple-element.31.tie_ref, bf16[4,4,16,1024]{3,2,1,0:T(8,128)(2,1)S(1)} %get-tuple-element.29.mine, ...), custom_call_target="tpu_custom_call" | custom-call | flops 1024 | bytes 1024 | tf_op jit(solution)/shard_map/expert_backward/pallas_call | solution.py:363
  32.8 4.0 %all-to-all-done.ret_hbm = bf16[8,16,4096]{2,1,0:T(8,128)(2,1)} async-done(((bf16[8,16,4096]{2,1,0:T(8,128)(2,1)}), bf16[8,16,4096]{2,1,0:T(8,128)(2,1)}, u32[]{:S(2)}, u32[]{:S(2)}) %all-to-all-start) | async-done | bytes 1048608 | tf_op jit(solution)/shard_map/all_to_all | solution.py:534
  36.8 3.6 %combine.1 = (bf16[128,4096]{1,0:T(8,128)(2,1)}, f32[8,128]{1,0:T(8,128)}) custom-call(s32[8,128]{1,0:T(8,128)} %bitcast.15, f32[128,128]{1,0:T(8,128)} %get-tuple-element.19.own_hbm, bf16[128,4096]{1,0:T(8,128)(2,1)} %dout_hbm.3, bf16[8,16,4096]{2,1,0:T(8,128)(2,1)} %all-to-all-done.ret_hbm), custom_call_target="tpu_custom_call" | custom-call | flops 1024 | bytes 1024 | tf_op jit(solution)/shard_map/combine/pallas_call | solution.py:429
  40.5 2.4 %collective-permute-done.7.refs_1_ = bf16[7,16,1024]{2,1,0:T(8,128)(2,1)S(1)} collective-permute-done((bf16[7,16,1024]{2,1,0:T(8,128)(2,1)S(1)}, bf16[7,16,1024]{2,1,0:T(8,128)(2,1)S(1)}, u32[]{:S(2)}, u32[]{:S(2)}) %collective-permute-start.7) | collective-permute-done | bytes 229408 | tf_op jit(solution)/shard_map/ppermute | solution.py:512
  42.9 0.0 collective-permute-done.8.refs_2_
  42.9 2.4 %collective-permute-done.6.refs_0_ = bf16[7,16,1024]{2,1,0:T(8,128)(2,1)S(1)} collective-permute-done((bf16[7,16,1024]{2,1,0:T(8,128)(2,1)S(1)}, bf16[7,16,1024]{2,1,0:T(8,128)(2,1)S(1)}, u32[]{:S(2)}, u32[]{:S(2)}) %collective-permute-start.6) | collective-permute-done | bytes 229408 | tf_op jit(solution)/shard_map/ppermute | solution.py:512
  45.2 1.8 %weight_grad.1 = bf16[1024,768]{1,0:T(8,128)(2,1)} custom-call(f32[8,128]{1,0:T(8,128)} %get-tuple-element.22.tie_ref, bf16[4,4,16,1024]{3,2,1,0:T(8,128)(2,1)S(1)} %get-tuple-element.29.mine, bf16[4,4,16,1024]{3,2,1,0:T(8,128)(2,1)S(1)} %collective-permute-done.5.swapped, bf16[128,768]{1,0:T(8,128)(2,1)S(1)} %get-tuple-element.20.hidden_ref, ...), custom_call_target="tpu_custom_call" | custom-call | flops 1024 | bytes 1024 | tf_op jit(solution)/shard_map/weight_grad/pallas_call | solution.py:493
  (5 shorter events, 0.1 us)
Async XLA Ops:
  2.7 18.7 %collective-permute-start.3 = (bf16[33,16,256]{2,1,0:T(8,128)(2,1)S(1)}, bf16[33,16,256]{2,1,0:T(8,128)(2,1)S(1)}, u32[]{:S(2)}, u32[]{:S(2)}) collective-permute-start(bf16[33,16,256]{2,1,0:T(8,128)(2,1)S(1)} %get-tuple-element.27), channel_id=1, source_target_pairs={{0,16},{8,24},{16,0},{24,8},{1,17},{9,25},{17,1},{25,9},{2,18},{10... | collective-permute-start | bytes 811016 | tf_op jit(solution)/shard_map/ppermute | solution.py:512
  6.8 14.6 %collective-permute-start = (bf16[2,4,16,1024]{3,2,1,0:T(8,128)(2,1)S(1)}, bf16[2,4,16,1024]{3,2,1,0:T(8,128)(2,1)S(1)}, u32[]{:S(2)}, u32[]{:S(2)}) collective-permute-start(bf16[2,4,16,1024]{3,2,1,0:T(8,128)(2,1)S(1)} %get-tuple-element.24), channel_id=1, source_target_pairs={{0,2},{1,3},{2,0},{3,1},{4,6},{5,7},{6,4},{7,5},{8,10},{9,11},{10,... | collective-permute-start | bytes 786440 | tf_op jit(solution)/shard_map/ppermute | solution.py:512
  8.3 13.1 %collective-permute-start.1 = (bf16[2,4,16,1024]{3,2,1,0:T(8,128)(2,1)S(1)}, bf16[2,4,16,1024]{3,2,1,0:T(8,128)(2,1)S(1)}, u32[]{:S(2)}, u32[]{:S(2)}) collective-permute-start(bf16[2,4,16,1024]{3,2,1,0:T(8,128)(2,1)S(1)} %get-tuple-element.25), channel_id=1, source_target_pairs={{0,4},{1,5},{2,6},{3,7},{4,0},{5,1},{6,2},{7,3},{8,12},{9,13},{10,... | collective-permute-start | bytes 786440 | tf_op jit(solution)/shard_map/ppermute | solution.py:512
  9.8 11.6 %collective-permute-start.2 = (bf16[2,4,16,1024]{3,2,1,0:T(8,128)(2,1)S(1)}, bf16[2,4,16,1024]{3,2,1,0:T(8,128)(2,1)S(1)}, u32[]{:S(2)}, u32[]{:S(2)}) collective-permute-start(bf16[2,4,16,1024]{3,2,1,0:T(8,128)(2,1)S(1)} %get-tuple-element.26), channel_id=1, source_target_pairs={{0,6},{1,7},{2,4},{3,5},{4,2},{5,3},{6,0},{7,1},{8,14},{9,15},{10,... | collective-permute-start | bytes 786440 | tf_op jit(solution)/shard_map/ppermute | solution.py:512
  10.3 11.1 %collective-permute-start.4 = (bf16[28,16,256]{2,1,0:T(8,128)(2,1)S(1)}, bf16[28,16,256]{2,1,0:T(8,128)(2,1)S(1)}, u32[]{:S(2)}, u32[]{:S(2)}) collective-permute-start(bf16[28,16,256]{2,1,0:T(8,128)(2,1)S(1)} %get-tuple-element.28), channel_id=1, source_target_pairs={{0,8},{8,0},{16,24},{24,16},{1,9},{9,1},{17,25},{25,17},{2,10},{10... | collective-permute-start | bytes 688136 | tf_op jit(solution)/shard_map/ppermute | solution.py:512
  17.1 19.7 %all-to-all-start = ((bf16[8,16,4096]{2,1,0:T(8,128)(2,1)}), bf16[8,16,4096]{2,1,0:T(8,128)(2,1)}, u32[]{:S(2)}, u32[]{:S(2)}) async-start(bf16[8,16,4096]{2,1,0:T(8,128)(2,1)} %expert_forward.1.refs_4_), calls=%async_computation | async-start | bytes 2097152 | tf_op jit(solution)/shard_map/all_to_all | solution.py:534
  21.5 2.0 %collective-permute-start.5 = (bf16[4,4,16,1024]{3,2,1,0:T(8,128)(2,1)S(1)}, bf16[4,4,16,1024]{3,2,1,0:T(8,128)(2,1)S(1)}, u32[]{:S(2)}, u32[]{:S(2)}) collective-permute-start(bf16[4,4,16,1024]{3,2,1,0:T(8,128)(2,1)S(1)} %get-tuple-element.30), channel_id=1, source_target_pairs={{0,1},{1,0},{2,3},{3,2},{4,5},{5,4},{6,7},{7,6},{8,9},{9,8},{10,11... | collective-permute-start | bytes 1572872 | tf_op jit(solution)/shard_map/ppermute | solution.py:512
  22.0 18.5 %collective-permute-start.9 = (bf16[33,16,256]{2,1,0:T(8,128)(2,1)S(1)}, bf16[33,16,256]{2,1,0:T(8,128)(2,1)S(1)}, u32[]{:S(2)}, u32[]{:S(2)}) collective-permute-start(bf16[33,16,256]{2,1,0:T(8,128)(2,1)S(1)} %collective-permute-done.3.refs_5_.refs_4_), channel_id=1, source_target_pairs={{0,8},{8,0},{16,24},{24,16},{1,9},{9,1},{17,25},{25,17},{2,10},{10... | collective-permute-start | bytes 811016 | tf_op jit(solution)/shard_map/ppermute | solution.py:512
  23.6 19.3 %collective-permute-start.7 = (bf16[7,16,1024]{2,1,0:T(8,128)(2,1)S(1)}, bf16[7,16,1024]{2,1,0:T(8,128)(2,1)S(1)}, u32[]{:S(2)}, u32[]{:S(2)}) collective-permute-start(bf16[7,16,1024]{2,1,0:T(8,128)(2,1)S(1)} %get-tuple-element.32), channel_id=1, source_target_pairs={{0,16},{8,24},{16,0},{24,8},{1,17},{9,25},{17,1},{25,9},{2,18},{10... | collective-permute-start | bytes 688136 | tf_op jit(solution)/shard_map/ppermute | solution.py:512
  24.5 18.3 %collective-permute-start.8 = (bf16[7,16,1024]{2,1,0:T(8,128)(2,1)S(1)}, bf16[7,16,1024]{2,1,0:T(8,128)(2,1)S(1)}, u32[]{:S(2)}, u32[]{:S(2)}) collective-permute-start(bf16[7,16,1024]{2,1,0:T(8,128)(2,1)S(1)} %get-tuple-element.33), channel_id=1, source_target_pairs={{0,24},{8,16},{16,8},{24,0},{1,25},{9,17},{17,9},{25,1},{2,26},{10... | collective-permute-start | bytes 688136 | tf_op jit(solution)/shard_map/ppermute | solution.py:512
  27.5 17.7 %collective-permute-start.6 = (bf16[7,16,1024]{2,1,0:T(8,128)(2,1)S(1)}, bf16[7,16,1024]{2,1,0:T(8,128)(2,1)S(1)}, u32[]{:S(2)}, u32[]{:S(2)}) collective-permute-start(bf16[7,16,1024]{2,1,0:T(8,128)(2,1)S(1)} %get-tuple-element.31.tie_ref), channel_id=1, source_target_pairs={{0,8},{8,0},{16,24},{24,16},{1,9},{9,1},{17,25},{25,17},{2,10},{10... | collective-permute-start | bytes 688136 | tf_op jit(solution)/shard_map/ppermute | solution.py:512

commit v12 on v11

--- a/solution.py
+++ b/solution.py
@@ -10,7 +10,7 @@
 QB = 128
 CAP = 16
 TILE = 256
-AHEAD = 3
+PART = 256
 
 bf16 = jnp.bfloat16
 f32 = jnp.float32
@@ -191,7 +191,7 @@
         for c in range(steps)
     ]
     small = pltpu.make_async_copy(scale_hbm, scale, scale_sem)
-    for copy in [small] + loads[:AHEAD]:
+    for copy in [small] + loads:
         copy.start()
     for r in range(flight):
         place = pl.multiple_of(block_place(me, r, flight) * CAP, CAP)
@@ -201,21 +201,21 @@
     for c in range(steps):
         cols = pl.ds(c * block, block)
         loads[c].wait()
-        if c + AHEAD < steps:
-            loads[c + AHEAD].start()
-        total = [None] * (block // QB)
-        for i in range(hid // QB):
-            part = jnp.dot(
-                hidden[:, i * QB : (i + 1) * QB],
-                quant[c, i * QB : (i + 1) * QB, :],
-                preferred_element_type=f32,
-            )
-            for j in range(block // QB):
-                scaled = part[:, j * QB : (j + 1) * QB] * scale[i, 0, c * (block // QB) + j]
-                total[j] = scaled if i == 0 else total[j] + scaled
-        for j in range(block // QB):
-            at = pl.ds(c * block + j * QB, QB)
-            out[:, :, at] = total[j].astype(bf16).reshape(flight, CAP, QB)
+        for p in range(0, block, PART):
+            total = [None] * (PART // QB)
+            for i in range(hid // QB):
+                part = jnp.dot(
+                    hidden[:, i * QB : (i + 1) * QB],
+                    quant[c, i * QB : (i + 1) * QB, p : p + PART],
+                    preferred_element_type=f32,
+                )
+                for j in range(PART // QB):
+                    factor = scale[i, 0, (c * block + p) // QB + j]
+                    scaled = part[:, j * QB : (j + 1) * QB] * factor
+                    total[j] = scaled if i == 0 else total[j] + scaled
+            for j in range(PART // QB):
+                at = pl.ds(c * block + p + j * QB, QB)
+                out[:, :, at] = total[j].astype(bf16).reshape(flight, CAP, QB)
         stores.append(
             pltpu.make_async_copy(out.at[:, :, cols], out_hbm.at[:, :, cols], out_sems.at[c])
         )
@@ -247,24 +247,32 @@
     )(hidden, hbm(scale), hbm(quant))
 
 
-def sort_kernel(half, *refs):
-    chips, (sibling, mine) = refs[:half], refs[-2:]
+def sort_kernel(half, keep, picks, *refs):
+    chips, messages = refs[:half], refs[half : half + len(picks)]
+    sibling, mine, *passed = refs[-2 - len(picks) :]
     for c in range(half):
         sibling[c] = chips[c][1]
         mine[c] = chips[c][0]
-
-
-def sort_rows(chips, ties):
+    for message, out, pick in zip(messages, passed, picks):
+        tall = out.shape[0] - keep
+        out[:keep] = message[:keep]
+        out[keep:] = message[keep + pick * tall : keep + (pick + 1) * tall]
+
+
+def sort_rows(chips, messages, picks, ties, hid):
     half = len(chips)
-    return pl.pallas_call(
-        functools.partial(sort_kernel, half),
-        out_shape=(pltpu.VMEM((half,) + chips[0].shape[1:], bf16),) * 2,
-        in_specs=[VMEM] * half + [ANY] * len(ties),
-        out_specs=(VMEM, VMEM),
+    _, groups, cap, share = chips[0].shape
+    keep = 2 * half * (hid // TILE)
+    return pl.pallas_call(
+        functools.partial(sort_kernel, half, keep, picks),
+        out_shape=(pltpu.VMEM((half, groups, cap, share), bf16),) * 2
+        + (pltpu.VMEM((keep + share // TILE, cap, TILE), bf16),) * len(messages),
+        in_specs=[VMEM] * (half + len(messages)) + [ANY] * len(ties),
+        out_specs=(VMEM,) * (2 + len(messages)),
         compiler_params=params(2 * half * CAP),
         cost_estimate=SMALL,
         name="sort_rows",
-    )(*chips, *ties)
+    )(*chips, *messages, *ties)
 
 
 def split_kernel(mine, swapped, *pieces):
@@ -457,7 +465,7 @@
     wide = hidden_ref.shape[1] // TILE
     hidden[:slots, :] = hidden_ref[...]
     for j in range(1, groups):
-        bit = max(b for b in bits_of(groups) if b <= j)
+        bit = j if j % 2 else max(b for b in bits_of(groups) if b <= j)
         message = messages[j - 1]
         for r in range(flight):
             for q in range(wide):
@@ -523,16 +531,22 @@
     )
     half, bits = flight // 2, bits_of(groups)
     chips = rest[:1] + [swap(rest[c], "expert", 2 * c) for c in range(1, half)]
-    messages, early = {}, []
+    messages = {}
     for bit, message in zip(bits, rest[half:]):
-        for j in sorted(messages):
-            messages[j ^ bit] = swap(messages[j], "dp", bit)
+        if bit > 1:
+            for j in sorted(messages):
+                messages[j ^ bit] = swap(messages[j], "dp", bit)
         messages[bit] = swap(message, "dp", bit)
-        early.append(messages[bit])
-    messages = [messages[j] for j in range(1, groups)]
+    even = list(range(2, groups, 2))
+    picks = [j + 1 - max(bit for bit in bits if bit <= j) for j in even]
     expert_out = forward(scale, hidden, w_quant[0], flight)
     returned = lax.all_to_all(expert_out, "expert", split_axis=0, concat_axis=0, tiled=True)
-    sibling, mine = sort_rows(chips, [hbm(expert_out)] + early)
+    sibling, mine, *passed = sort_rows(
+        chips, [messages[j] for j in even], picks, [hbm(expert_out), messages[1]], hidden.shape[1]
+    )
+    for j, message in zip(even, passed):
+        messages[j + 1] = swap(message, "dp", 1)
+    messages = [messages[j] for j in range(1, groups)]
     swapped = swap(sibling, "expert", 1)
     pieces = split(mine, swapped)
     parts = [swap(pieces[j - 1], "dp", j) for j in range(1, groups)]

time: 47.4 us -> 47.4 us (level)
  the two profiles are of different devices: /device:TPU:0 before, /device:TPU:10 now
where the time goes in v12:
time: 47.4 us; the launch traced here: 47.2 us
  Pallas kernels  18.4 us (39%)
  starting transfers between devices  16.6 us (35%)
  waiting for transfers between devices  11.5 us (24%)
  between operations  0.7 us (1%)
    ppermute x10, starting transfers between devices, swap(): return lax.ppermute(value, axis, [(i, i ^ j) for i in range(size)])  11.9 us
    ppermute x10, waiting for transfers between devices, swap(): return lax.ppermute(value, axis, [(i, i ^ j) for i in range(size)])  10.8 us
    pallas_call x1, Pallas kernels, backward(): pl.pallas_call(functools.partial(backward_kernel, flight, groups), out_sh...  5.25 us
    pallas_call x1, Pallas kernels, forward(): pl.pallas_call(functools.partial(forward_kernel, flight, block), out_shap...  4.81 us
    all_to_all x1, starting transfers between devices, shards(): lax.all_to_all(expert_out, 'expert', split_axis=0, concat_axis=0, tiled=T...  4.68 us
    pallas_call x1, Pallas kernels, combine(): pl.pallas_call(functools.partial(combine_kernel, block), out_shape=(pltpu...  3.63 us
    pallas_call x1, Pallas kernels, dispatch(): pl.pallas_call(functools.partial(dispatch_kernel, flight, groups), out_sh...  2.09 us
    pallas_call x1, Pallas kernels, weight_grad(): pl.pallas_call(functools.partial(weight_grad_kernel, groups, block), out_...  1.82 us
  transfers between devices with their start and end apart: 11, of which 5 were waited for; matrix products, arithmetic and copies ran while one was open for 0% of the time, Pallas kernels for 31%

profile of v12, /device:TPU:10, one launch (start us, length us, event | category | flops | bytes accessed | tf_op | source)
XLA Modules:
  0.0 47.2 jit_solution(15220005646435136367)
XLA Ops:
  0.6 2.1 %dispatch.1 = (f32[128,128]{1,0:T(8,128)}, bf16[128,768]{1,0:T(8,128)(2,1)S(1)}, bf16[2,4,16,1024]{3,2,1,0:T(8,128)(2,1)S(1)}, bf16[2,4,16,1024]{3,2,1,0:T(8,128...) custom-call(bf16[128,1536]{1,0:T(8,128)(2,1)} %bitcast.10, ...), custom_call_target="tpu_custom_call" | custom-call | flops 1024 | bytes 1024 | tf_op jit(solution)/shard_map/dispatch/pallas_call | solution.py:154
  2.7 2.7 %collective-permute-start.3 = (bf16[33,16,256]{2,1,0:T(8,128)(2,1)S(1)}, bf16[33,16,256]{2,1,0:T(8,128)(2,1)S(1)}, u32[]{:S(2)}, u32[]{:S(2)}) collective-permute-start(bf16[33,16,256]{2,1,0:T(8,128)(2,1)S(1)} %get-tuple-element.28), channel_id=1, source_target_pairs={{0,16},{8,24},{16,0},{24,8},{1,17},{9,25},{17,1},{25,9},{2,18},{10... | collective-permute-start | bytes 811016 | tf_op jit(solution)/shard_map/ppermute | solution.py:520
  5.4 0.5 %collective-permute-start = (bf16[2,4,16,1024]{3,2,1,0:T(8,128)(2,1)S(1)}, bf16[2,4,16,1024]{3,2,1,0:T(8,128)(2,1)S(1)}, u32[]{:S(2)}, u32[]{:S(2)}) collective-permute-start(bf16[2,4,16,1024]{3,2,1,0:T(8,128)(2,1)S(1)} %get-tuple-element.25), channel_id=1, source_target_pairs={{0,2},{1,3},{2,0},{3,1},{4,6},{5,7},{6,4},{7,5},{8,10},{9,11},{10,... | collective-permute-start | bytes 786440 | tf_op jit(solution)/shard_map/ppermute | solution.py:520
  5.9 1.5 %collective-permute-start.1 = (bf16[2,4,16,1024]{3,2,1,0:T(8,128)(2,1)S(1)}, bf16[2,4,16,1024]{3,2,1,0:T(8,128)(2,1)S(1)}, u32[]{:S(2)}, u32[]{:S(2)}) collective-permute-start(bf16[2,4,16,1024]{3,2,1,0:T(8,128)(2,1)S(1)} %get-tuple-element.26), channel_id=1, source_target_pairs={{0,4},{1,5},{2,6},{3,7},{4,0},{5,1},{6,2},{7,3},{8,12},{9,13},{10,... | collective-permute-start | bytes 786440 | tf_op jit(solution)/shard_map/ppermute | solution.py:520
  7.4 1.4 %collective-permute-start.2 = (bf16[2,4,16,1024]{3,2,1,0:T(8,128)(2,1)S(1)}, bf16[2,4,16,1024]{3,2,1,0:T(8,128)(2,1)S(1)}, u32[]{:S(2)}, u32[]{:S(2)}) collective-permute-start(bf16[2,4,16,1024]{3,2,1,0:T(8,128)(2,1)S(1)} %get-tuple-element.27), channel_id=1, source_target_pairs={{0,6},{1,7},{2,4},{3,5},{4,2},{5,3},{6,0},{7,1},{8,14},{9,15},{10,... | collective-permute-start | bytes 786440 | tf_op jit(solution)/shard_map/ppermute | solution.py:520
  8.9 0.4 collective-permute-start.4
  9.3 4.8 %expert_forward.1.refs_5_ = bf16[8,16,4096]{2,1,0:T(8,128)(2,1)} custom-call(bf16[128,768]{1,0:T(8,128)(2,1)S(1)} %get-tuple-element.21.hidden_ref, f32[6,1,32]{2,1,0:T(1,128)} %bitcast.16, bf16[768,4096]{1,0:T(8,128)(2,1)} %bitcast.8), custom_call_target="tpu_custom_call" | custom-call | flops 1024 | bytes 1024 | tf_op jit(solution)/shard_map/expert_forward/pallas_call | solution.py:230
  14.1 4.7 %all-to-all-start = ((bf16[8,16,4096]{2,1,0:T(8,128)(2,1)}), bf16[8,16,4096]{2,1,0:T(8,128)(2,1)}, u32[]{:S(2)}, u32[]{:S(2)}) async-start(bf16[8,16,4096]{2,1,0:T(8,128)(2,1)} %expert_forward.1.refs_5_), calls=%async_computation | async-start | bytes 2097152 | tf_op jit(solution)/shard_map/all_to_all | solution.py:543
  18.8 0.0 collective-permute-done.1.refs_2_
  18.8 0.9 %collective-permute-done.2.refs_3_ = bf16[2,4,16,1024]{3,2,1,0:T(8,128)(2,1)S(1)} collective-permute-done((bf16[2,4,16,1024]{3,2,1,0:T(8,128)(2,1)S(1)}, bf16[2,4,16,1024]{3,2,1,0:T(8,128)(2,1)S(1)}, u32[]{:S(2)}, u32[]{:S(2)}) %collective-permute-start.2) | collective-permute-done | bytes 262176 | tf_op jit(solution)/shard_map/ppermute | solution.py:520
  19.7 0.1 sort_rows.1
  19.8 0.1 collective-permute-start.5
  19.9 0.9 %collective-permute-start.9 = (bf16[28,16,256]{2,1,0:T(8,128)(2,1)S(1)}, bf16[28,16,256]{2,1,0:T(8,128)(2,1)S(1)}, u32[]{:S(2)}, u32[]{:S(2)}) collective-permute-start(bf16[28,16,256]{2,1,0:T(8,128)(2,1)S(1)} %get-tuple-element.35), channel_id=1, source_target_pairs={{0,8},{8,0},{16,24},{24,16},{1,9},{9,1},{17,25},{25,17},{2,10},{10... | collective-permute-start | bytes 688136 | tf_op jit(solution)/shard_map/ppermute | solution.py:520
  20.8 1.0 %collective-permute-done.5.swapped = bf16[4,4,16,1024]{3,2,1,0:T(8,128)(2,1)S(1)} collective-permute-done((bf16[4,4,16,1024]{3,2,1,0:T(8,128)(2,1)S(1)}, bf16[4,4,16,1024]{3,2,1,0:T(8,128)(2,1)S(1)}, u32[]{:S(2)}, u32[]{:S(2)}) %collective-permute-start.5) | collective-permute-done | bytes 524320 | tf_op jit(solution)/shard_map/ppermute | solution.py:520
  21.8 0.7 %split.1 = (bf16[7,16,1024]{2,1,0:T(8,128)(2,1)S(1)}, bf16[7,16,1024]{2,1,0:T(8,128)(2,1)}, bf16[7,16,1024]{2,1,0:T(8,128)(2,1)S(1)}) custom-call(bf16[4,4,16,1024]{3,2,1,0:T(8,128)(2,1)S(1)} %get-tuple-element.30.mine, bf16[4,4,16,1024]{3,2,1,0:T(8,128)(2,1)S(1)} %collective-permute-done.5.swapped), custom_call_target="tpu_custom_call" | custom-call | flops 1024 | bytes 1024 | tf_op jit(solution)/shard_map/split/pallas_call | solution.py:287
  22.5 1.5 %collective-permute-start.7 = (bf16[7,16,1024]{2,1,0:T(8,128)(2,1)}, bf16[7,16,1024]{2,1,0:T(8,128)(2,1)S(1)}, u32[]{:S(2)}, u32[]{:S(2)}) collective-permute-start(bf16[7,16,1024]{2,1,0:T(8,128)(2,1)} %get-tuple-element.33), channel_id=1, source_target_pairs={{0,16},{8,24},{16,0},{24,8},{1,17},{9,25},{17,1},{25,9},{2,18},{10... | collective-permute-start | bytes 688136 | tf_op jit(solution)/shard_map/ppermute | solution.py:520
  24.0 0.7 %collective-permute-start.8 = (bf16[7,16,1024]{2,1,0:T(8,128)(2,1)S(1)}, bf16[7,16,1024]{2,1,0:T(8,128)(2,1)S(1)}, u32[]{:S(2)}, u32[]{:S(2)}) collective-permute-start(bf16[7,16,1024]{2,1,0:T(8,128)(2,1)S(1)} %get-tuple-element.34), channel_id=1, source_target_pairs={{0,24},{8,16},{16,8},{24,0},{1,25},{9,17},{17,9},{25,1},{2,26},{10... | collective-permute-start | bytes 688136 | tf_op jit(solution)/shard_map/ppermute | solution.py:520
  24.7 2.2 %collective-permute-start.6 = (bf16[7,16,1024]{2,1,0:T(8,128)(2,1)S(1)}, bf16[7,16,1024]{2,1,0:T(8,128)(2,1)S(1)}, u32[]{:S(2)}, u32[]{:S(2)}) collective-permute-start(bf16[7,16,1024]{2,1,0:T(8,128)(2,1)S(1)} %get-tuple-element.32.tie_ref), channel_id=1, source_target_pairs={{0,8},{8,0},{16,24},{24,16},{1,9},{9,1},{17,25},{25,17},{2,10},{10... | collective-permute-start | bytes 688136 | tf_op jit(solution)/shard_map/ppermute | solution.py:520
  26.9 5.2 %expert_backward.1 = bf16[128,1536]{1,0:T(8,128)(2,1)} custom-call(f32[6,1,32]{2,1,0:T(1,128)} %bitcast.17, bf16[128,1536]{1,0:T(8,128)(2,1)} %bitcast.11, bf16[768,4096]{1,0:T(8,128)(2,1)} %bitcast.9, bf16[7,16,1024]{2,1,0:T(8,128)(2,1)S(1)} %get-tuple-element.32.tie_ref, bf16[4,4,16,1024]{3,2,1,0:T(8,128)(2,1)S(1)} %get-tuple-element.30.mine, ...), custom_call_target="tpu_custom_call" | custom-call | flops 1024 | bytes 1024 | tf_op jit(solution)/shard_map/expert_backward/pallas_call | solution.py:371
  32.2 0.7 %all-to-all-done.ret_hbm = bf16[8,16,4096]{2,1,0:T(8,128)(2,1)} async-done(((bf16[8,16,4096]{2,1,0:T(8,128)(2,1)}), bf16[8,16,4096]{2,1,0:T(8,128)(2,1)}, u32[]{:S(2)}, u32[]{:S(2)}) %all-to-all-start) | async-done | bytes 1048608 | tf_op jit(solution)/shard_map/all_to_all | solution.py:543
  32.8 3.6 %combine.1 = (bf16[128,4096]{1,0:T(8,128)(2,1)}, f32[8,128]{1,0:T(8,128)}) custom-call(s32[8,128]{1,0:T(8,128)} %bitcast.15, f32[128,128]{1,0:T(8,128)} %get-tuple-element.20.own_hbm, bf16[128,4096]{1,0:T(8,128)(2,1)} %dout_hbm.3, bf16[8,16,4096]{2,1,0:T(8,128)(2,1)} %all-to-all-done.ret_hbm), custom_call_target="tpu_custom_call" | custom-call | flops 1024 | bytes 1024 | tf_op jit(solution)/shard_map/combine/pallas_call | solution.py:437
  36.5 3.7 %collective-permute-done.7.refs_1_ = bf16[7,16,1024]{2,1,0:T(8,128)(2,1)S(1)} collective-permute-done((bf16[7,16,1024]{2,1,0:T(8,128)(2,1)}, bf16[7,16,1024]{2,1,0:T(8,128)(2,1)S(1)}, u32[]{:S(2)}, u32[]{:S(2)}) %collective-permute-start.7) | collective-permute-done | bytes 229408 | tf_op jit(solution)/shard_map/ppermute | solution.py:520
  40.2 5.2 %collective-permute-done.8.refs_2_ = bf16[7,16,1024]{2,1,0:T(8,128)(2,1)S(1)} collective-permute-done((bf16[7,16,1024]{2,1,0:T(8,128)(2,1)S(1)}, bf16[7,16,1024]{2,1,0:T(8,128)(2,1)S(1)}, u32[]{:S(2)}, u32[]{:S(2)}) %collective-permute-start.8) | collective-permute-done | bytes 229408 | tf_op jit(solution)/shard_map/ppermute | solution.py:520
  45.4 1.8 %weight_grad.1 = bf16[1024,768]{1,0:T(8,128)(2,1)} custom-call(f32[8,128]{1,0:T(8,128)} %get-tuple-element.23.tie_ref, bf16[4,4,16,1024]{3,2,1,0:T(8,128)(2,1)S(1)} %get-tuple-element.30.mine, bf16[4,4,16,1024]{3,2,1,0:T(8,128)(2,1)S(1)} %collective-permute-done.5.swapped, bf16[128,768]{1,0:T(8,128)(2,1)S(1)} %get-tuple-element.21.hidden_ref, ...), custom_call_target="tpu_custom_call" | custom-call | flops 1024 | bytes 1024 | tf_op jit(solution)/shard_map/weight_grad/pallas_call | solution.py:501
  (5 shorter events, 0.0 us)
Async XLA Ops:
  2.7 17.0 %collective-permute-start.3 = (bf16[33,16,256]{2,1,0:T(8,128)(2,1)S(1)}, bf16[33,16,256]{2,1,0:T(8,128)(2,1)S(1)}, u32[]{:S(2)}, u32[]{:S(2)}) collective-permute-start(bf16[33,16,256]{2,1,0:T(8,128)(2,1)S(1)} %get-tuple-element.28), channel_id=1, source_target_pairs={{0,16},{8,24},{16,0},{24,8},{1,17},{9,25},{17,1},{25,9},{2,18},{10... | collective-permute-start | bytes 811016 | tf_op jit(solution)/shard_map/ppermute | solution.py:520
  5.4 13.4 %collective-permute-start = (bf16[2,4,16,1024]{3,2,1,0:T(8,128)(2,1)S(1)}, bf16[2,4,16,1024]{3,2,1,0:T(8,128)(2,1)S(1)}, u32[]{:S(2)}, u32[]{:S(2)}) collective-permute-start(bf16[2,4,16,1024]{3,2,1,0:T(8,128)(2,1)S(1)} %get-tuple-element.25), channel_id=1, source_target_pairs={{0,2},{1,3},{2,0},{3,1},{4,6},{5,7},{6,4},{7,5},{8,10},{9,11},{10,... | collective-permute-start | bytes 786440 | tf_op jit(solution)/shard_map/ppermute | solution.py:520
  5.9 12.9 %collective-permute-start.1 = (bf16[2,4,16,1024]{3,2,1,0:T(8,128)(2,1)S(1)}, bf16[2,4,16,1024]{3,2,1,0:T(8,128)(2,1)S(1)}, u32[]{:S(2)}, u32[]{:S(2)}) collective-permute-start(bf16[2,4,16,1024]{3,2,1,0:T(8,128)(2,1)S(1)} %get-tuple-element.26), channel_id=1, source_target_pairs={{0,4},{1,5},{2,6},{3,7},{4,0},{5,1},{6,2},{7,3},{8,12},{9,13},{10,... | collective-permute-start | bytes 786440 | tf_op jit(solution)/shard_map/ppermute | solution.py:520
  7.4 12.3 %collective-permute-start.2 = (bf16[2,4,16,1024]{3,2,1,0:T(8,128)(2,1)S(1)}, bf16[2,4,16,1024]{3,2,1,0:T(8,128)(2,1)S(1)}, u32[]{:S(2)}, u32[]{:S(2)}) collective-permute-start(bf16[2,4,16,1024]{3,2,1,0:T(8,128)(2,1)S(1)} %get-tuple-element.27), channel_id=1, source_target_pairs={{0,6},{1,7},{2,4},{3,5},{4,2},{5,3},{6,0},{7,1},{8,14},{9,15},{10,... | collective-permute-start | bytes 786440 | tf_op jit(solution)/shard_map/ppermute | solution.py:520
  8.9 9.9 %collective-permute-start.4 = (bf16[28,16,256]{2,1,0:T(8,128)(2,1)S(1)}, bf16[28,16,256]{2,1,0:T(8,128)(2,1)S(1)}, u32[]{:S(2)}, u32[]{:S(2)}) collective-permute-start(bf16[28,16,256]{2,1,0:T(8,128)(2,1)S(1)} %get-tuple-element.29), channel_id=1, source_target_pairs={{0,8},{8,0},{16,24},{24,16},{1,9},{9,1},{17,25},{25,17},{2,10},{10... | collective-permute-start | bytes 688136 | tf_op jit(solution)/shard_map/ppermute | solution.py:520
  14.1 18.7 %all-to-all-start = ((bf16[8,16,4096]{2,1,0:T(8,128)(2,1)}), bf16[8,16,4096]{2,1,0:T(8,128)(2,1)}, u32[]{:S(2)}, u32[]{:S(2)}) async-start(bf16[8,16,4096]{2,1,0:T(8,128)(2,1)} %expert_forward.1.refs_5_), calls=%async_computation | async-start | bytes 2097152 | tf_op jit(solution)/shard_map/all_to_all | solution.py:543
  19.8 2.0 %collective-permute-start.5 = (bf16[4,4,16,1024]{3,2,1,0:T(8,128)(2,1)S(1)}, bf16[4,4,16,1024]{3,2,1,0:T(8,128)(2,1)S(1)}, u32[]{:S(2)}, u32[]{:S(2)}) collective-permute-start(bf16[4,4,16,1024]{3,2,1,0:T(8,128)(2,1)S(1)} %get-tuple-element.31), channel_id=1, source_target_pairs={{0,1},{1,0},{2,3},{3,2},{4,5},{5,4},{6,7},{7,6},{8,9},{9,8},{10,11... | collective-permute-start | bytes 1572872 | tf_op jit(solution)/shard_map/ppermute | solution.py:520
  19.9 16.6 %collective-permute-start.9 = (bf16[28,16,256]{2,1,0:T(8,128)(2,1)S(1)}, bf16[28,16,256]{2,1,0:T(8,128)(2,1)S(1)}, u32[]{:S(2)}, u32[]{:S(2)}) collective-permute-start(bf16[28,16,256]{2,1,0:T(8,128)(2,1)S(1)} %get-tuple-element.35), channel_id=1, source_target_pairs={{0,8},{8,0},{16,24},{24,16},{1,9},{9,1},{17,25},{25,17},{2,10},{10... | collective-permute-start | bytes 688136 | tf_op jit(solution)/shard_map/ppermute | solution.py:520
  22.5 17.7 %collective-permute-start.7 = (bf16[7,16,1024]{2,1,0:T(8,128)(2,1)}, bf16[7,16,1024]{2,1,0:T(8,128)(2,1)S(1)}, u32[]{:S(2)}, u32[]{:S(2)}) collective-permute-start(bf16[7,16,1024]{2,1,0:T(8,128)(2,1)} %get-tuple-element.33), channel_id=1, source_target_pairs={{0,16},{8,24},{16,0},{24,8},{1,17},{9,25},{17,1},{25,9},{2,18},{10... | collective-permute-start | bytes 688136 | tf_op jit(solution)/shard_map/ppermute | solution.py:520
  24.0 21.4 %collective-permute-start.8 = (bf16[7,16,1024]{2,1,0:T(8,128)(2,1)S(1)}, bf16[7,16,1024]{2,1,0:T(8,128)(2,1)S(1)}, u32[]{:S(2)}, u32[]{:S(2)}) collective-permute-start(bf16[7,16,1024]{2,1,0:T(8,128)(2,1)S(1)} %get-tuple-element.34), channel_id=1, source_target_pairs={{0,24},{8,16},{16,8},{24,0},{1,25},{9,17},{17,9},{25,1},{2,26},{10... | collective-permute-start | bytes 688136 | tf_op jit(solution)/shard_map/ppermute | solution.py:520
  24.7 20.7 %collective-permute-start.6 = (bf16[7,16,1024]{2,1,0:T(8,128)(2,1)S(1)}, bf16[7,16,1024]{2,1,0:T(8,128)(2,1)S(1)}, u32[]{:S(2)}, u32[]{:S(2)}) collective-permute-start(bf16[7,16,1024]{2,1,0:T(8,128)(2,1)S(1)} %get-tuple-element.32.tie_ref), channel_id=1, source_target_pairs={{0,8},{8,0},{16,24},{24,16},{1,9},{9,1},{17,25},{25,17},{2,10},{10... | collective-permute-start | bytes 688136 | tf_op jit(solution)/shard_map/ppermute | solution.py:520

commit v13 on v12

--- a/solution.py
+++ b/solution.py
@@ -55,16 +55,16 @@
 def dispatch_kernel(flight, groups, gate_up_hbm, cap_hbm, hot_hbm, ids_hbm, probs_hbm, dout_hbm, *refs):
     half = flight // 2
     bits = bits_of(groups)
-    outs = 2 + half + len(bits)
-    own_hbm, hidden_ref, *chips = refs[: 2 + half]
-    messages = dict(zip(bits, refs[2 + half : outs]))
+    outs = 1 + half + len(bits)
+    own_hbm, *chips = refs[: 1 + half]
+    messages = dict(zip(bits, refs[1 + half : outs]))
     gate_up, cap_ref, hot_ref, ids_ref, probs_ref, dout, own_ref = refs[outs : outs + 7]
     gate_sems, own_sem, small_sems, in_sems = refs[outs + 7 :]
     topk, tokens = ids_ref.shape
     slots = flight * CAP
     me, group = lax.axis_index("expert"), lax.axis_index("dp")
     share = dout_hbm.shape[1] // groups
-    hid = hidden_ref.shape[1]
+    hid = gate_up_hbm.shape[1] // 2
     small = [
         pltpu.make_async_copy(src, dst, small_sems.at[i])
         for i, (src, dst) in enumerate(
@@ -138,7 +138,6 @@
         gate = gate_up[at, :hid].astype(f32)
         up = gate_up[at, hid:].astype(f32)
         block = (gate * jax.nn.sigmoid(gate) * up).astype(bf16)
-        hidden_ref[at, :] = block
         for bit in bits:
             for q in range(hid // TILE):
                 messages[bit][r * (hid // TILE) + q] = block[:, q * TILE : (q + 1) * TILE]
@@ -153,14 +152,14 @@
     half = flight // 2
     return pl.pallas_call(
         functools.partial(dispatch_kernel, flight, groups),
-        out_shape=(pltpu.HBM((slots, tokens), f32), pltpu.VMEM((rows, double // 2), bf16))
+        out_shape=(pltpu.HBM((slots, tokens), f32),)
         + (pltpu.VMEM((2, groups, CAP, share), bf16),) * half
         + tuple(
             pltpu.VMEM((message_tiles(flight, groups, bit, double // 2, share), CAP, TILE), bf16)
             for bit in bits_of(groups)
         ),
         in_specs=[HBM] * 6,
-        out_specs=(HBM, VMEM) + (VMEM,) * (half + len(bits_of(groups))),
+        out_specs=(HBM,) + (VMEM,) * (half + len(bits_of(groups))),
         scratch_shapes=[
             pltpu.VMEM((rows, double), bf16),
             pltpu.SMEM(capacity.shape, jnp.int32),
@@ -181,26 +180,38 @@
 
 
 def forward_kernel(
-    flight, block, hidden_ref, scale_hbm, quant_hbm, out_hbm,
-    scale, hidden, quant, out, scale_sem, in_sems, out_sems
+    flight, block, gate_up_hbm, scale_hbm, quant_hbm, out_hbm,
+    gate_up, scale, hidden, quant, out, small_sems, in_sems, out_sems
 ):
     steps, hid, _ = quant.shape
-    me = lax.axis_index("expert")
+    tall = hid // in_sems.shape[1]
     loads = [
-        pltpu.make_async_copy(quant_hbm.at[:, pl.ds(c * block, block)], quant.at[c], in_sems.at[c])
+        [
+            pltpu.make_async_copy(
+                quant_hbm.at[pl.ds(t * tall, tall), pl.ds(c * block, block)],
+                quant.at[c, pl.ds(t * tall, tall)],
+                in_sems.at[c, t],
+            )
+            for t in range(hid // tall)
+        ]
         for c in range(steps)
     ]
-    small = pltpu.make_async_copy(scale_hbm, scale, scale_sem)
-    for copy in [small] + loads:
+    small = [
+        pltpu.make_async_copy(gate_up_hbm, gate_up, small_sems.at[0]),
+        pltpu.make_async_copy(scale_hbm, scale, small_sems.at[1]),
+    ]
+    for copy in sum(loads, small):
         copy.start()
-    for r in range(flight):
-        place = pl.multiple_of(block_place(me, r, flight) * CAP, CAP)
-        hidden[pl.ds(place, CAP), :] = hidden_ref[pl.ds(r * CAP, CAP), :]
-    small.wait()
+    for copy in small:
+        copy.wait()
+    gate = gate_up[:, :hid].astype(f32)
+    up = gate_up[:, hid:].astype(f32)
+    hidden[...] = (gate * jax.nn.sigmoid(gate) * up).astype(bf16)
     stores = []
     for c in range(steps):
         cols = pl.ds(c * block, block)
-        loads[c].wait()
+        for copy in loads[c]:
+            copy.wait()
         for p in range(0, block, PART):
             total = [None] * (PART // QB)
             for i in range(hid // QB):
@@ -224,27 +235,29 @@
         copy.wait()
 
 
-def forward(scale, hidden, quant, flight, block=512):
+def forward(scale, gate_up, quant, flight, block=1024, parts=3):
+    slots, double = gate_up.shape
     hid, width = quant.shape
     steps = width // block
     return pl.pallas_call(
         functools.partial(forward_kernel, flight, block),
         out_shape=pltpu.HBM((flight, CAP, width), bf16),
-        in_specs=[VMEM, HBM, HBM],
+        in_specs=[HBM, HBM, HBM],
         out_specs=HBM,
         scratch_shapes=[
+            pltpu.VMEM((slots, double), bf16),
             pltpu.SMEM(scale.shape, f32),
-            pltpu.VMEM(hidden.shape, bf16),
+            pltpu.VMEM((slots, hid), bf16),
             pltpu.VMEM((steps, hid, block), bf16),
             pltpu.VMEM((flight, CAP, width), bf16),
-            pltpu.SemaphoreType.DMA,
-            pltpu.SemaphoreType.DMA((steps,)),
+            pltpu.SemaphoreType.DMA((2,)),
+            pltpu.SemaphoreType.DMA((steps, parts)),
             pltpu.SemaphoreType.DMA((steps,)),
         ],
         compiler_params=params(flight * CAP),
         cost_estimate=SMALL,
         name="expert_forward",
-    )(hidden, hbm(scale), hbm(quant))
+    )(hbm(gate_up), hbm(scale), hbm(quant))
 
 
 def sort_kernel(half, keep, picks, *refs):
@@ -296,7 +309,7 @@
 
 
 def backward_kernel(
-    flight, groups, scale_hbm, gate_up_hbm, quant_hbm, tie_ref, mine, swapped, out_hbm,
+    flight, groups, scale_hbm, gate_up_hbm, quant_hbm, tie_ref, mine, swapped, out_hbm, hidden_ref,
     scale, gate_up, rows, quant, acc, out, scale_sem, gate_sems, in_sems, out_sems
 ):
     half = flight // 2
@@ -352,7 +365,9 @@
     sig = jax.nn.sigmoid(gate)
     d_hidden = acc[...]
     out[:, :hid] = (d_hidden * up * sig * (1.0 + gate * (1.0 - sig))).astype(bf16)
-    out[:, hid:] = (d_hidden * (gate * sig)).astype(bf16)
+    silu = gate * sig
+    out[:, hid:] = (d_hidden * silu).astype(bf16)
+    hidden_ref[...] = (silu * up).astype(bf16)
     stores = [
         pltpu.make_async_copy(out.at[pl.ds(r * CAP, CAP)], out_hbm.at[place(r)], out_sems.at[r])
         for r in range(flight)
@@ -370,9 +385,9 @@
     flight = 2 * half
     return pl.pallas_call(
         functools.partial(backward_kernel, flight, groups),
-        out_shape=pltpu.HBM((slots, double), bf16),
+        out_shape=(pltpu.HBM((slots, double), bf16), pltpu.VMEM((slots, hid), bf16)),
         in_specs=[HBM, HBM, HBM, ANY, VMEM, VMEM],
-        out_specs=HBM,
+        out_specs=(HBM, VMEM),
         scratch_shapes=[
             pltpu.SMEM(scale.shape, f32),
             pltpu.VMEM((slots, double), bf16),
@@ -526,7 +541,7 @@
     gate_up = gate_up[0, 0]
     ids, probs = route_ids.T, route_probs.T
     scale = w_scale.transpose(1, 0, 2)
-    own, hidden, *rest = dispatch(
+    own, *rest = dispatch(
         gate_up, capacity, hot_lists, ids, probs, d_out, flight, groups
     )
     half, bits = flight // 2, bits_of(groups)
@@ -539,10 +554,10 @@
         messages[bit] = swap(message, "dp", bit)
     even = list(range(2, groups, 2))
     picks = [j + 1 - max(bit for bit in bits if bit <= j) for j in even]
-    expert_out = forward(scale, hidden, w_quant[0], flight)
+    expert_out = forward(scale, gate_up, w_quant[0], flight)
     returned = lax.all_to_all(expert_out, "expert", split_axis=0, concat_axis=0, tiled=True)
     sibling, mine, *passed = sort_rows(
-        chips, [messages[j] for j in even], picks, [hbm(expert_out), messages[1]], hidden.shape[1]
+        chips, [messages[j] for j in even], picks, [hbm(expert_out), messages[1]], gate_up.shape[1] // 2
     )
     for j, message in zip(even, passed):
         messages[j + 1] = swap(message, "dp", 1)
@@ -550,7 +565,7 @@
     swapped = swap(sibling, "expert", 1)
     pieces = split(mine, swapped)
     parts = [swap(pieces[j - 1], "dp", j) for j in range(1, groups)]
-    d_gate_up = backward(scale, gate_up, w_quant[0], pieces[0], mine, swapped)
+    d_gate_up, hidden = backward(scale, gate_up, w_quant[0], pieces[0], mine, swapped)
     combined, d_probs = combine(ids, own, d_out, returned)
     d_weight = weight_grad(d_probs, mine, swapped, hidden, parts, messages)
     return (combined, d_probs.T, d_gate_up[None, None], d_weight[None])

time: 47.4 us -> 48.7 us (1.027)
  the two profiles are of different devices: /device:TPU:10 before, /device:TPU:8 now
where the time goes in v13:
time: 48.7 us; the launch traced here: 48.4 us
  Pallas kernels  19.4 us (40%)
  starting transfers between devices  15.9 us (33%)
  waiting for transfers between devices  12.4 us (25%)
  between operations  0.73 us (1%)
    ppermute x10, starting transfers between devices, swap(): return lax.ppermute(value, axis, [(i, i ^ j) for i in range(size)])  11.6 us
    ppermute x10, waiting for transfers between devices, swap(): return lax.ppermute(value, axis, [(i, i ^ j) for i in range(size)])  9.09 us
    pallas_call x1, Pallas kernels, forward(): pl.pallas_call(functools.partial(forward_kernel, flight, block), out_shap...  5.84 us
    pallas_call x1, Pallas kernels, backward(): pl.pallas_call(functools.partial(backward_kernel, flight, groups), out_sh...  5.26 us
    all_to_all x1, starting transfers between devices, shards(): lax.all_to_all(expert_out, 'expert', split_axis=0, concat_axis=0, tiled=T...  4.26 us
    pallas_call x1, Pallas kernels, combine(): pl.pallas_call(functools.partial(combine_kernel, block), out_shape=(pltpu...  3.63 us
    all_to_all x1, waiting for transfers between devices, shards(): lax.all_to_all(expert_out, 'expert', split_axis=0, concat_axis=0, tiled=T...  3.32 us
    pallas_call x1, Pallas kernels, dispatch(): pl.pallas_call(functools.partial(dispatch_kernel, flight, groups), out_sh...  2.09 us
  transfers between devices with their start and end apart: 11, of which 4 were waited for; matrix products, arithmetic and copies ran while one was open for 0% of the time, Pallas kernels for 32%

profile of v13, /device:TPU:8, one launch (start us, length us, event | category | flops | bytes accessed | tf_op | source)
XLA Modules:
  0.0 48.4 jit_solution(10827270866254460872)
XLA Ops:
  0.6 2.1 %dispatch.1 = (f32[128,128]{1,0:T(8,128)}, bf16[2,4,16,1024]{3,2,1,0:T(8,128)(2,1)S(1)}, bf16[2,4,16,1024]{3,2,1,0:T(8,128)(2,1)S(1)}, bf16[2,4,16,1024]{3,2,1,0...) custom-call(bf16[128,1536]{1,0:T(8,128)(2,1)} %bitcast.10, ...), custom_call_target="tpu_custom_call" | custom-call | flops 1024 | bytes 1024 | tf_op jit(solution)/shard_map/dispatch/pallas_call | solution.py:153
  2.7 2.7 %collective-permute-start.3 = (bf16[33,16,256]{2,1,0:T(8,128)(2,1)S(1)}, bf16[33,16,256]{2,1,0:T(8,128)(2,1)S(1)}, u32[]{:S(2)}, u32[]{:S(2)}) collective-permute-start(bf16[33,16,256]{2,1,0:T(8,128)(2,1)S(1)} %get-tuple-element.28), channel_id=1, source_target_pairs={{0,16},{8,24},{16,0},{24,8},{1,17},{9,25},{17,1},{25,9},{2,18},{10... | collective-permute-start | bytes 811016 | tf_op jit(solution)/shard_map/ppermute | solution.py:535
  5.4 1.5 %collective-permute-start = (bf16[2,4,16,1024]{3,2,1,0:T(8,128)(2,1)S(1)}, bf16[2,4,16,1024]{3,2,1,0:T(8,128)(2,1)S(1)}, u32[]{:S(2)}, u32[]{:S(2)}) collective-permute-start(bf16[2,4,16,1024]{3,2,1,0:T(8,128)(2,1)S(1)} %get-tuple-element.25), channel_id=1, source_target_pairs={{0,2},{1,3},{2,0},{3,1},{4,6},{5,7},{6,4},{7,5},{8,10},{9,11},{10,... | collective-permute-start | bytes 786440 | tf_op jit(solution)/shard_map/ppermute | solution.py:535
  6.9 1.5 %collective-permute-start.1 = (bf16[2,4,16,1024]{3,2,1,0:T(8,128)(2,1)S(1)}, bf16[2,4,16,1024]{3,2,1,0:T(8,128)(2,1)S(1)}, u32[]{:S(2)}, u32[]{:S(2)}) collective-permute-start(bf16[2,4,16,1024]{3,2,1,0:T(8,128)(2,1)S(1)} %get-tuple-element.26), channel_id=1, source_target_pairs={{0,4},{1,5},{2,6},{3,7},{4,0},{5,1},{6,2},{7,3},{8,12},{9,13},{10,... | collective-permute-start | bytes 786440 | tf_op jit(solution)/shard_map/ppermute | solution.py:535
  8.4 0.5 collective-permute-start.2
  8.9 0.4 collective-permute-start.4
  9.3 5.8 %expert_forward.1.refs_5_ = bf16[8,16,4096]{2,1,0:T(8,128)(2,1)} custom-call(bf16[128,1536]{1,0:T(8,128)(2,1)} %bitcast.11, f32[6,1,32]{2,1,0:T(1,128)} %bitcast.16, bf16[768,4096]{1,0:T(8,128)(2,1)} %bitcast.8), custom_call_target="tpu_custom_call" | custom-call | flops 1024 | bytes 1024 | tf_op jit(solution)/shard_map/expert_forward/pallas_call | solution.py:242
  15.2 4.3 %all-to-all-start = ((bf16[8,16,4096]{2,1,0:T(8,128)(2,1)}), bf16[8,16,4096]{2,1,0:T(8,128)(2,1)}, u32[]{:S(2)}, u32[]{:S(2)}) async-start(bf16[8,16,4096]{2,1,0:T(8,128)(2,1)} %expert_forward.1.refs_5_), calls=%async_computation | async-start | bytes 2097152 | tf_op jit(solution)/shard_map/all_to_all | solution.py:558
  19.4 0.0 collective-permute-done.4.refs_6_.refs_3_
  19.5 0.5 %collective-permute-done.1.refs_2_ = bf16[2,4,16,1024]{3,2,1,0:T(8,128)(2,1)S(1)} collective-permute-done((bf16[2,4,16,1024]{3,2,1,0:T(8,128)(2,1)S(1)}, bf16[2,4,16,1024]{3,2,1,0:T(8,128)(2,1)S(1)}, u32[]{:S(2)}, u32[]{:S(2)}) %collective-permute-start.1) | collective-permute-done | bytes 262176 | tf_op jit(solution)/shard_map/ppermute | solution.py:535
  20.0 0.0 collective-permute-done.3.refs_4_
  20.0 0.1 sort_rows.1
  20.1 0.1 collective-permute-start.5
  20.1 1.4 %collective-permute-start.9 = (bf16[28,16,256]{2,1,0:T(8,128)(2,1)S(1)}, bf16[28,16,256]{2,1,0:T(8,128)(2,1)S(1)}, u32[]{:S(2)}, u32[]{:S(2)}) collective-permute-start(bf16[28,16,256]{2,1,0:T(8,128)(2,1)S(1)} %get-tuple-element.37), channel_id=1, source_target_pairs={{0,8},{8,0},{16,24},{24,16},{1,9},{9,1},{17,25},{25,17},{2,10},{10... | collective-permute-start | bytes 688136 | tf_op jit(solution)/shard_map/ppermute | solution.py:535
  21.6 0.5 collective-permute-done.5.swapped
  22.0 0.7 %split.1 = (bf16[7,16,1024]{2,1,0:T(8,128)(2,1)S(1)}, bf16[7,16,1024]{2,1,0:T(8,128)(2,1)}, bf16[7,16,1024]{2,1,0:T(8,128)(2,1)S(1)}) custom-call(bf16[4,4,16,1024]{3,2,1,0:T(8,128)(2,1)S(1)} %get-tuple-element.30.mine, bf16[4,4,16,1024]{3,2,1,0:T(8,128)(2,1)S(1)} %collective-permute-done.5.swapped), custom_call_target="tpu_custom_call" | custom-call | flops 1024 | bytes 1024 | tf_op jit(solution)/shard_map/split/pallas_call | solution.py:300
  22.8 1.1 %collective-permute-start.6 = (bf16[7,16,1024]{2,1,0:T(8,128)(2,1)S(1)}, bf16[7,16,1024]{2,1,0:T(8,128)(2,1)S(1)}, u32[]{:S(2)}, u32[]{:S(2)}) collective-permute-start(bf16[7,16,1024]{2,1,0:T(8,128)(2,1)S(1)} %get-tuple-element.32.tie_ref), channel_id=1, source_target_pairs={{0,8},{8,0},{16,24},{24,16},{1,9},{9,1},{17,25},{25,17},{2,10},{10... | collective-permute-start | bytes 688136 | tf_op jit(solution)/shard_map/ppermute | solution.py:535
  23.9 0.3 collective-permute-start.7
  24.2 2.0 %collective-permute-start.8 = (bf16[7,16,1024]{2,1,0:T(8,128)(2,1)S(1)}, bf16[7,16,1024]{2,1,0:T(8,128)(2,1)S(1)}, u32[]{:S(2)}, u32[]{:S(2)}) collective-permute-start(bf16[7,16,1024]{2,1,0:T(8,128)(2,1)S(1)} %get-tuple-element.36), channel_id=1, source_target_pairs={{0,24},{8,16},{16,8},{24,0},{1,25},{9,17},{17,9},{25,1},{2,26},{10... | collective-permute-start | bytes 688136 | tf_op jit(solution)/shard_map/ppermute | solution.py:535
  26.3 5.3 %expert_backward.1 = (bf16[128,1536]{1,0:T(8,128)(2,1)}, bf16[128,768]{1,0:T(8,128)(2,1)S(1)}) custom-call(f32[6,1,32]{2,1,0:T(1,128)} %bitcast.17, bf16[128,1536]{1,0:T(8,128)(2,1)} %bitcast.12, bf16[768,4096]{1,0:T(8,128)(2,1)} %bitcast.9, bf16[7,16,1024]{2,1,0:T(8,128)(2,1)S(1)} %get-tuple-element.32.tie_ref, ...), custom_call_target="tpu_custom_call" | custom-call | flops 1024 | bytes 1024 | tf_op jit(solution)/shard_map/expert_backward/pallas_call | solution.py:386
  31.5 3.3 %all-to-all-done.ret_hbm = bf16[8,16,4096]{2,1,0:T(8,128)(2,1)} async-done(((bf16[8,16,4096]{2,1,0:T(8,128)(2,1)}), bf16[8,16,4096]{2,1,0:T(8,128)(2,1)}, u32[]{:S(2)}, u32[]{:S(2)}) %all-to-all-start) | async-done | bytes 1048608 | tf_op jit(solution)/shard_map/all_to_all | solution.py:558
  34.9 3.6 %combine.1 = (bf16[128,4096]{1,0:T(8,128)(2,1)}, f32[8,128]{1,0:T(8,128)}) custom-call(s32[8,128]{1,0:T(8,128)} %bitcast.15, f32[128,128]{1,0:T(8,128)} %get-tuple-element.21.own_hbm, bf16[128,4096]{1,0:T(8,128)(2,1)} %dout_hbm.3, bf16[8,16,4096]{2,1,0:T(8,128)(2,1)} %all-to-all-done.ret_hbm), custom_call_target="tpu_custom_call" | custom-call | flops 1024 | bytes 1024 | tf_op jit(solution)/shard_map/combine/pallas_call | solution.py:452
  38.5 8.1 %collective-permute-done.8.refs_2_ = bf16[7,16,1024]{2,1,0:T(8,128)(2,1)S(1)} collective-permute-done((bf16[7,16,1024]{2,1,0:T(8,128)(2,1)S(1)}, bf16[7,16,1024]{2,1,0:T(8,128)(2,1)S(1)}, u32[]{:S(2)}, u32[]{:S(2)}) %collective-permute-start.8) | collective-permute-done | bytes 229408 | tf_op jit(solution)/shard_map/ppermute | solution.py:535
  46.6 1.8 %weight_grad.1 = bf16[1024,768]{1,0:T(8,128)(2,1)} custom-call(f32[8,128]{1,0:T(8,128)} %get-tuple-element.23.tie_ref, bf16[4,4,16,1024]{3,2,1,0:T(8,128)(2,1)S(1)} %get-tuple-element.30.mine, bf16[4,4,16,1024]{3,2,1,0:T(8,128)(2,1)S(1)} %collective-permute-done.5.swapped, bf16[128,768]{1,0:T(8,128)(2,1)S(1)} %get-tuple-element.34.hidden_ref, ...), custom_call_target="tpu_custom_call" | custom-call | flops 1024 | bytes 1024 | tf_op jit(solution)/shard_map/weight_grad/pallas_call | solution.py:516
  (5 shorter events, 0.0 us)
Async XLA Ops:
  2.7 17.3 %collective-permute-start.3 = (bf16[33,16,256]{2,1,0:T(8,128)(2,1)S(1)}, bf16[33,16,256]{2,1,0:T(8,128)(2,1)S(1)}, u32[]{:S(2)}, u32[]{:S(2)}) collective-permute-start(bf16[33,16,256]{2,1,0:T(8,128)(2,1)S(1)} %get-tuple-element.28), channel_id=1, source_target_pairs={{0,16},{8,24},{16,0},{24,8},{1,17},{9,25},{17,1},{25,9},{2,18},{10... | collective-permute-start | bytes 811016 | tf_op jit(solution)/shard_map/ppermute | solution.py:535
  5.4 14.1 %collective-permute-start = (bf16[2,4,16,1024]{3,2,1,0:T(8,128)(2,1)S(1)}, bf16[2,4,16,1024]{3,2,1,0:T(8,128)(2,1)S(1)}, u32[]{:S(2)}, u32[]{:S(2)}) collective-permute-start(bf16[2,4,16,1024]{3,2,1,0:T(8,128)(2,1)S(1)} %get-tuple-element.25), channel_id=1, source_target_pairs={{0,2},{1,3},{2,0},{3,1},{4,6},{5,7},{6,4},{7,5},{8,10},{9,11},{10,... | collective-permute-start | bytes 786440 | tf_op jit(solution)/shard_map/ppermute | solution.py:535
  6.9 13.1 %collective-permute-start.1 = (bf16[2,4,16,1024]{3,2,1,0:T(8,128)(2,1)S(1)}, bf16[2,4,16,1024]{3,2,1,0:T(8,128)(2,1)S(1)}, u32[]{:S(2)}, u32[]{:S(2)}) collective-permute-start(bf16[2,4,16,1024]{3,2,1,0:T(8,128)(2,1)S(1)} %get-tuple-element.26), channel_id=1, source_target_pairs={{0,4},{1,5},{2,6},{3,7},{4,0},{5,1},{6,2},{7,3},{8,12},{9,13},{10,... | collective-permute-start | bytes 786440 | tf_op jit(solution)/shard_map/ppermute | solution.py:535
  8.4 11.6 %collective-permute-start.2 = (bf16[2,4,16,1024]{3,2,1,0:T(8,128)(2,1)S(1)}, bf16[2,4,16,1024]{3,2,1,0:T(8,128)(2,1)S(1)}, u32[]{:S(2)}, u32[]{:S(2)}) collective-permute-start(bf16[2,4,16,1024]{3,2,1,0:T(8,128)(2,1)S(1)} %get-tuple-element.27), channel_id=1, source_target_pairs={{0,6},{1,7},{2,4},{3,5},{4,2},{5,3},{6,0},{7,1},{8,14},{9,15},{10,... | collective-permute-start | bytes 786440 | tf_op jit(solution)/shard_map/ppermute | solution.py:535
  8.9 10.6 %collective-permute-start.4 = (bf16[28,16,256]{2,1,0:T(8,128)(2,1)S(1)}, bf16[28,16,256]{2,1,0:T(8,128)(2,1)S(1)}, u32[]{:S(2)}, u32[]{:S(2)}) collective-permute-start(bf16[28,16,256]{2,1,0:T(8,128)(2,1)S(1)} %get-tuple-element.29), channel_id=1, source_target_pairs={{0,8},{8,0},{16,24},{24,16},{1,9},{9,1},{17,25},{25,17},{2,10},{10... | collective-permute-start | bytes 688136 | tf_op jit(solution)/shard_map/ppermute | solution.py:535
  15.2 19.7 %all-to-all-start = ((bf16[8,16,4096]{2,1,0:T(8,128)(2,1)}), bf16[8,16,4096]{2,1,0:T(8,128)(2,1)}, u32[]{:S(2)}, u32[]{:S(2)}) async-start(bf16[8,16,4096]{2,1,0:T(8,128)(2,1)} %expert_forward.1.refs_5_), calls=%async_computation | async-start | bytes 2097152 | tf_op jit(solution)/shard_map/all_to_all | solution.py:558
  20.1 2.0 %collective-permute-start.5 = (bf16[4,4,16,1024]{3,2,1,0:T(8,128)(2,1)S(1)}, bf16[4,4,16,1024]{3,2,1,0:T(8,128)(2,1)S(1)}, u32[]{:S(2)}, u32[]{:S(2)}) collective-permute-start(bf16[4,4,16,1024]{3,2,1,0:T(8,128)(2,1)S(1)} %get-tuple-element.31), channel_id=1, source_target_pairs={{0,1},{1,0},{2,3},{3,2},{4,5},{5,4},{6,7},{7,6},{8,9},{9,8},{10,11... | collective-permute-start | bytes 1572872 | tf_op jit(solution)/shard_map/ppermute | solution.py:535
  20.1 18.3 %collective-permute-start.9 = (bf16[28,16,256]{2,1,0:T(8,128)(2,1)S(1)}, bf16[28,16,256]{2,1,0:T(8,128)(2,1)S(1)}, u32[]{:S(2)}, u32[]{:S(2)}) collective-permute-start(bf16[28,16,256]{2,1,0:T(8,128)(2,1)S(1)} %get-tuple-element.37), channel_id=1, source_target_pairs={{0,8},{8,0},{16,24},{24,16},{1,9},{9,1},{17,25},{25,17},{2,10},{10... | collective-permute-start | bytes 688136 | tf_op jit(solution)/shard_map/ppermute | solution.py:535
  22.8 15.7 %collective-permute-start.6 = (bf16[7,16,1024]{2,1,0:T(8,128)(2,1)S(1)}, bf16[7,16,1024]{2,1,0:T(8,128)(2,1)S(1)}, u32[]{:S(2)}, u32[]{:S(2)}) collective-permute-start(bf16[7,16,1024]{2,1,0:T(8,128)(2,1)S(1)} %get-tuple-element.32.tie_ref), channel_id=1, source_target_pairs={{0,8},{8,0},{16,24},{24,16},{1,9},{9,1},{17,25},{25,17},{2,10},{10... | collective-permute-start | bytes 688136 | tf_op jit(solution)/shard_map/ppermute | solution.py:535
  23.9 14.6 %collective-permute-start.7 = (bf16[7,16,1024]{2,1,0:T(8,128)(2,1)}, bf16[7,16,1024]{2,1,0:T(8,128)(2,1)S(1)}, u32[]{:S(2)}, u32[]{:S(2)}) collective-permute-start(bf16[7,16,1024]{2,1,0:T(8,128)(2,1)} %get-tuple-element.35), channel_id=1, source_target_pairs={{0,16},{8,24},{16,0},{24,8},{1,17},{9,25},{17,1},{25,9},{2,18},{10... | collective-permute-start | bytes 688136 | tf_op jit(solution)/shard_map/ppermute | solution.py:535
  24.2 22.4 %collective-permute-start.8 = (bf16[7,16,1024]{2,1,0:T(8,128)(2,1)S(1)}, bf16[7,16,1024]{2,1,0:T(8,128)(2,1)S(1)}, u32[]{:S(2)}, u32[]{:S(2)}) collective-permute-start(bf16[7,16,1024]{2,1,0:T(8,128)(2,1)S(1)} %get-tuple-element.36), channel_id=1, source_target_pairs={{0,24},{8,16},{16,8},{24,0},{1,25},{9,17},{17,9},{25,1},{2,26},{10... | collective-permute-start | bytes 688136 | tf_op jit(solution)/shard_map/ppermute | solution.py:535

commit v14 on v12

--- a/solution.py
+++ b/solution.py
@@ -296,10 +296,13 @@
 
 
 def backward_kernel(
-    flight, groups, scale_hbm, gate_up_hbm, quant_hbm, tie_ref, mine, swapped, out_hbm,
-    scale, gate_up, rows, quant, acc, out, scale_sem, gate_sems, in_sems, out_sems
+    flight, groups, scale_hbm, gate_up_hbm, quant_hbm, message_hbm, tie_ref, mine, swapped,
+    out_hbm, message_ref,
+    scale, gate_up, rows, quant, acc, out, small_sems, gate_sems, in_sems, out_sems
 ):
     half = flight // 2
+    message_copy = pltpu.make_async_copy(message_hbm, message_ref, small_sems.at[1])
+    message_copy.start()
     me, group = lax.axis_index("expert"), lax.axis_index("dp")
     slots, hid = acc.shape
     share = quant.shape[2]
@@ -321,7 +324,7 @@
         )
         for r in range(flight)
     ]
-    small = pltpu.make_async_copy(scale_hbm, scale, scale_sem)
+    small = pltpu.make_async_copy(scale_hbm, scale, small_sems.at[0])
     for copy in [small] + loads + gates:
         copy.start()
     for c in range(half):
@@ -361,18 +364,19 @@
         copy.start()
     for copy in stores:
         copy.wait()
-
-
-def backward(scale, gate_up, quant, tie, mine, swapped):
+    message_copy.wait()
+
+
+def backward(scale, gate_up, quant, message, tie, mine, swapped):
     slots, double = gate_up.shape
     hid, width = quant.shape
     half, groups, cap, share = swapped.shape
     flight = 2 * half
     return pl.pallas_call(
         functools.partial(backward_kernel, flight, groups),
-        out_shape=pltpu.HBM((slots, double), bf16),
-        in_specs=[HBM, HBM, HBM, ANY, VMEM, VMEM],
-        out_specs=HBM,
+        out_shape=(pltpu.HBM((slots, double), bf16), pltpu.VMEM(message.shape, bf16)),
+        in_specs=[HBM, HBM, HBM, HBM, ANY, VMEM, VMEM],
+        out_specs=(HBM, VMEM),
         scratch_shapes=[
             pltpu.SMEM(scale.shape, f32),
             pltpu.VMEM((slots, double), bf16),
@@ -380,7 +384,7 @@
             pltpu.VMEM((groups, hid, share), bf16),
             pltpu.VMEM((slots, hid), f32),
             pltpu.VMEM((slots, double), bf16),
-            pltpu.SemaphoreType.DMA,
+            pltpu.SemaphoreType.DMA((2,)),
             pltpu.SemaphoreType.DMA((flight,)),
             pltpu.SemaphoreType.DMA((groups,)),
             pltpu.SemaphoreType.DMA((flight,)),
@@ -388,7 +392,7 @@
         compiler_params=params(slots),
         cost_estimate=SMALL,
         name="expert_backward",
-    )(hbm(scale), hbm(gate_up), hbm(quant), tie, mine, swapped)
+    )(hbm(scale), hbm(gate_up), hbm(quant), hbm(message), tie, mine, swapped)
 
 
 def combine_kernel(
@@ -542,7 +546,7 @@
     expert_out = forward(scale, hidden, w_quant[0], flight)
     returned = lax.all_to_all(expert_out, "expert", split_axis=0, concat_axis=0, tiled=True)
     sibling, mine, *passed = sort_rows(
-        chips, [messages[j] for j in even], picks, [hbm(expert_out), messages[1]], hidden.shape[1]
+        chips, [messages[j] for j in even], picks, [hbm(expert_out), hbm(messages[1])], hidden.shape[1]
     )
     for j, message in zip(even, passed):
         messages[j + 1] = swap(message, "dp", 1)
@@ -550,7 +554,9 @@
     swapped = swap(sibling, "expert", 1)
     pieces = split(mine, swapped)
     parts = [swap(pieces[j - 1], "dp", j) for j in range(1, groups)]
-    d_gate_up = backward(scale, gate_up, w_quant[0], pieces[0], mine, swapped)
+    d_gate_up, messages[0] = backward(
+        scale, gate_up, w_quant[0], messages[0], pieces[0], mine, swapped
+    )
     combined, d_probs = combine(ids, own, d_out, returned)
     d_weight = weight_grad(d_probs, mine, swapped, hidden, parts, messages)
     return (combined, d_probs.T, d_gate_up[None, None], d_weight[None])

time: 47.4 us -> 48.7 us (1.027)
  the two profiles are of different devices: /device:TPU:10 before, /device:TPU:12 now
where the time goes in v14:
time: 48.7 us; the launch traced here: 48.5 us
  Pallas kernels  18.5 us (38%)
  starting transfers between devices  16 us (33%)
  waiting for transfers between devices  13.3 us (27%)
  between operations  0.71 us (1%)
    ppermute x10, waiting for transfers between devices, swap(): return lax.ppermute(value, axis, [(i, i ^ j) for i in range(size)])  12 us
    ppermute x10, starting transfers between devices, swap(): return lax.ppermute(value, axis, [(i, i ^ j) for i in range(size)])  11.4 us
    pallas_call x1, Pallas kernels, backward(): pl.pallas_call(functools.partial(backward_kernel, flight, groups), out_sh...  5.28 us
    pallas_call x1, Pallas kernels, forward(): pl.pallas_call(functools.partial(forward_kernel, flight, block), out_shap...  4.8 us
    all_to_all x1, starting transfers between devices, shards(): lax.all_to_all(expert_out, 'expert', split_axis=0, concat_axis=0, tiled=T...  4.66 us
    pallas_call x1, Pallas kernels, combine(): pl.pallas_call(functools.partial(combine_kernel, block), out_shape=(pltpu...  3.63 us
    pallas_call x1, Pallas kernels, dispatch(): pl.pallas_call(functools.partial(dispatch_kernel, flight, groups), out_sh...  2.09 us
    pallas_call x1, Pallas kernels, weight_grad(): pl.pallas_call(functools.partial(weight_grad_kernel, groups, block), out_...  1.82 us
  transfers between devices with their start and end apart: 11, of which 6 were waited for; matrix products, arithmetic and copies ran while one was open for 0% of the time, Pallas kernels for 30%

profile of v14, /device:TPU:12, one launch (start us, length us, event | category | flops | bytes accessed | tf_op | source)
XLA Modules:
  0.0 48.5 jit_solution(4469120240118725498)
XLA Ops:
  0.6 2.1 %dispatch.1 = (f32[128,128]{1,0:T(8,128)}, bf16[128,768]{1,0:T(8,128)(2,1)S(1)}, bf16[2,4,16,1024]{3,2,1,0:T(8,128)(2,1)S(1)}, bf16[2,4,16,1024]{3,2,1,0:T(8,128...) custom-call(bf16[128,1536]{1,0:T(8,128)(2,1)} %bitcast.10, ...), custom_call_target="tpu_custom_call" | custom-call | flops 1024 | bytes 1024 | tf_op jit(solution)/shard_map/dispatch/pallas_call | solution.py:154
  2.7 2.7 %collective-permute-start.4 = (bf16[33,16,256]{2,1,0:T(8,128)(2,1)S(1)}, bf16[33,16,256]{2,1,0:T(8,128)(2,1)S(1)}, u32[]{:S(2)}, u32[]{:S(2)}) collective-permute-start(bf16[33,16,256]{2,1,0:T(8,128)(2,1)S(1)} %get-tuple-element.31), channel_id=1, source_target_pairs={{0,16},{8,24},{16,0},{24,8},{1,17},{9,25},{17,1},{25,9},{2,18},{10... | collective-permute-start | bytes 811016 | tf_op jit(solution)/shard_map/ppermute | solution.py:524
  5.4 1.5 %collective-permute-start.1 = (bf16[2,4,16,1024]{3,2,1,0:T(8,128)(2,1)S(1)}, bf16[2,4,16,1024]{3,2,1,0:T(8,128)(2,1)S(1)}, u32[]{:S(2)}, u32[]{:S(2)}) collective-permute-start(bf16[2,4,16,1024]{3,2,1,0:T(8,128)(2,1)S(1)} %get-tuple-element.28), channel_id=1, source_target_pairs={{0,2},{1,3},{2,0},{3,1},{4,6},{5,7},{6,4},{7,5},{8,10},{9,11},{10,... | collective-permute-start | bytes 786440 | tf_op jit(solution)/shard_map/ppermute | solution.py:524
  6.9 0.5 %collective-permute-start.2 = (bf16[2,4,16,1024]{3,2,1,0:T(8,128)(2,1)S(1)}, bf16[2,4,16,1024]{3,2,1,0:T(8,128)(2,1)S(1)}, u32[]{:S(2)}, u32[]{:S(2)}) collective-permute-start(bf16[2,4,16,1024]{3,2,1,0:T(8,128)(2,1)S(1)} %get-tuple-element.29), channel_id=1, source_target_pairs={{0,4},{1,5},{2,6},{3,7},{4,0},{5,1},{6,2},{7,3},{8,12},{9,13},{10,... | collective-permute-start | bytes 786440 | tf_op jit(solution)/shard_map/ppermute | solution.py:524
  7.4 1.5 %collective-permute-start.3 = (bf16[2,4,16,1024]{3,2,1,0:T(8,128)(2,1)S(1)}, bf16[2,4,16,1024]{3,2,1,0:T(8,128)(2,1)S(1)}, u32[]{:S(2)}, u32[]{:S(2)}) collective-permute-start(bf16[2,4,16,1024]{3,2,1,0:T(8,128)(2,1)S(1)} %get-tuple-element.30), channel_id=1, source_target_pairs={{0,6},{1,7},{2,4},{3,5},{4,2},{5,3},{6,0},{7,1},{8,14},{9,15},{10,... | collective-permute-start | bytes 786440 | tf_op jit(solution)/shard_map/ppermute | solution.py:524
  8.9 0.4 collective-permute-start
  9.3 4.8 %expert_forward.1.refs_5_ = bf16[8,16,4096]{2,1,0:T(8,128)(2,1)} custom-call(bf16[128,768]{1,0:T(8,128)(2,1)S(1)} %get-tuple-element.23.hidden_ref, f32[6,1,32]{2,1,0:T(1,128)} %bitcast.15, bf16[768,4096]{1,0:T(8,128)(2,1)} %bitcast.8), custom_call_target="tpu_custom_call" | custom-call | flops 1024 | bytes 1024 | tf_op jit(solution)/shard_map/expert_forward/pallas_call | solution.py:230
  14.1 4.7 %all-to-all-start = ((bf16[8,16,4096]{2,1,0:T(8,128)(2,1)}), bf16[8,16,4096]{2,1,0:T(8,128)(2,1)}, u32[]{:S(2)}, u32[]{:S(2)}) async-start(bf16[8,16,4096]{2,1,0:T(8,128)(2,1)} %expert_forward.1.refs_5_), calls=%async_computation | async-start | bytes 2097152 | tf_op jit(solution)/shard_map/all_to_all | solution.py:547
  18.8 1.2 %collective-permute-done.2.refs_2_ = bf16[2,4,16,1024]{3,2,1,0:T(8,128)(2,1)S(1)} collective-permute-done((bf16[2,4,16,1024]{3,2,1,0:T(8,128)(2,1)S(1)}, bf16[2,4,16,1024]{3,2,1,0:T(8,128)(2,1)S(1)}, u32[]{:S(2)}, u32[]{:S(2)}) %collective-permute-start.2) | collective-permute-done | bytes 262176 | tf_op jit(solution)/shard_map/ppermute | solution.py:524
  20.0 0.1 sort_rows.1
  20.1 0.1 collective-permute-start.5
  20.2 1.2 %collective-permute-start.9 = (bf16[28,16,256]{2,1,0:T(8,128)(2,1)S(1)}, bf16[28,16,256]{2,1,0:T(8,128)(2,1)S(1)}, u32[]{:S(2)}, u32[]{:S(2)}) collective-permute-start(bf16[28,16,256]{2,1,0:T(8,128)(2,1)S(1)} %get-tuple-element.39), channel_id=1, source_target_pairs={{0,8},{8,0},{16,24},{24,16},{1,9},{9,1},{17,25},{25,17},{2,10},{10... | collective-permute-start | bytes 688136 | tf_op jit(solution)/shard_map/ppermute | solution.py:524
  21.4 0.7 %collective-permute-done.5.swapped = bf16[4,4,16,1024]{3,2,1,0:T(8,128)(2,1)S(1)} collective-permute-done((bf16[4,4,16,1024]{3,2,1,0:T(8,128)(2,1)S(1)}, bf16[4,4,16,1024]{3,2,1,0:T(8,128)(2,1)S(1)}, u32[]{:S(2)}, u32[]{:S(2)}) %collective-permute-start.5) | collective-permute-done | bytes 524320 | tf_op jit(solution)/shard_map/ppermute | solution.py:524
  22.1 0.8 %split.1 = (bf16[7,16,1024]{2,1,0:T(8,128)(2,1)S(1)}, bf16[7,16,1024]{2,1,0:T(8,128)(2,1)}, bf16[7,16,1024]{2,1,0:T(8,128)(2,1)S(1)}) custom-call(bf16[4,4,16,1024]{3,2,1,0:T(8,128)(2,1)S(1)} %get-tuple-element.32.mine, bf16[4,4,16,1024]{3,2,1,0:T(8,128)(2,1)S(1)} %collective-permute-done.5.swapped), custom_call_target="tpu_custom_call" | custom-call | flops 1024 | bytes 1024 | tf_op jit(solution)/shard_map/split/pallas_call | solution.py:287
  22.8 1.1 %collective-permute-start.6 = (bf16[7,16,1024]{2,1,0:T(8,128)(2,1)S(1)}, bf16[7,16,1024]{2,1,0:T(8,128)(2,1)S(1)}, u32[]{:S(2)}, u32[]{:S(2)}) collective-permute-start(bf16[7,16,1024]{2,1,0:T(8,128)(2,1)S(1)} %get-tuple-element.34.tie_ref), channel_id=1, source_target_pairs={{0,8},{8,0},{16,24},{24,16},{1,9},{9,1},{17,25},{25,17},{2,10},{10... | collective-permute-start | bytes 688136 | tf_op jit(solution)/shard_map/ppermute | solution.py:524
  23.9 1.0 %collective-permute-start.7 = (bf16[7,16,1024]{2,1,0:T(8,128)(2,1)}, bf16[7,16,1024]{2,1,0:T(8,128)(2,1)S(1)}, u32[]{:S(2)}, u32[]{:S(2)}) collective-permute-start(bf16[7,16,1024]{2,1,0:T(8,128)(2,1)} %get-tuple-element.36), channel_id=1, source_target_pairs={{0,16},{8,24},{16,0},{24,8},{1,17},{9,25},{17,1},{25,9},{2,18},{10... | collective-permute-start | bytes 688136 | tf_op jit(solution)/shard_map/ppermute | solution.py:524
  24.9 1.5 %collective-permute-start.8 = (bf16[7,16,1024]{2,1,0:T(8,128)(2,1)S(1)}, bf16[7,16,1024]{2,1,0:T(8,128)(2,1)S(1)}, u32[]{:S(2)}, u32[]{:S(2)}) collective-permute-start(bf16[7,16,1024]{2,1,0:T(8,128)(2,1)S(1)} %get-tuple-element.37), channel_id=1, source_target_pairs={{0,24},{8,16},{16,8},{24,0},{1,25},{9,17},{17,9},{25,1},{2,26},{10... | collective-permute-start | bytes 688136 | tf_op jit(solution)/shard_map/ppermute | solution.py:524
  26.3 5.3 %expert_backward.1 = (bf16[128,1536]{1,0:T(8,128)(2,1)}, bf16[28,16,256]{2,1,0:T(8,128)(2,1)S(1)}) custom-call(f32[6,1,32]{2,1,0:T(1,128)} %bitcast.16, bf16[128,1536]{1,0:T(8,128)(2,1)} %bitcast.11, bf16[768,4096]{1,0:T(8,128)(2,1)} %bitcast.9, bf16[28,16,256]{2,1,0:T(8,128)(2,1)} %copy-done, bf16[7,16,1024]{2,1,0:T(8,128)(2,1)S(1)} %get-tuple-element.34.tie_ref, ...), custom_call_target="tpu_custom_call" | custom-call | flops 1024 | bytes 1024 | tf_op jit(solution)/shard_map/expert_backward/pallas_call | solution.py:375
  31.6 1.2 %all-to-all-done.ret_hbm = bf16[8,16,4096]{2,1,0:T(8,128)(2,1)} async-done(((bf16[8,16,4096]{2,1,0:T(8,128)(2,1)}), bf16[8,16,4096]{2,1,0:T(8,128)(2,1)}, u32[]{:S(2)}, u32[]{:S(2)}) %all-to-all-start) | async-done | bytes 1048608 | tf_op jit(solution)/shard_map/all_to_all | solution.py:547
  32.8 3.6 %combine.1 = (bf16[128,4096]{1,0:T(8,128)(2,1)}, f32[8,128]{1,0:T(8,128)}) custom-call(s32[8,128]{1,0:T(8,128)} %bitcast.14, f32[128,128]{1,0:T(8,128)} %get-tuple-element.22.own_hbm, bf16[128,4096]{1,0:T(8,128)(2,1)} %dout_hbm.3, bf16[8,16,4096]{2,1,0:T(8,128)(2,1)} %all-to-all-done.ret_hbm), custom_call_target="tpu_custom_call" | custom-call | flops 1024 | bytes 1024 | tf_op jit(solution)/shard_map/combine/pallas_call | solution.py:441
  36.5 0.1 collective-permute-done.6.refs_0_
  36.6 1.9 %collective-permute-done.7.refs_1_ = bf16[7,16,1024]{2,1,0:T(8,128)(2,1)S(1)} collective-permute-done((bf16[7,16,1024]{2,1,0:T(8,128)(2,1)}, bf16[7,16,1024]{2,1,0:T(8,128)(2,1)S(1)}, u32[]{:S(2)}, u32[]{:S(2)}) %collective-permute-start.7) | collective-permute-done | bytes 229408 | tf_op jit(solution)/shard_map/ppermute | solution.py:524
  38.5 8.2 %collective-permute-done.8.refs_2_ = bf16[7,16,1024]{2,1,0:T(8,128)(2,1)S(1)} collective-permute-done((bf16[7,16,1024]{2,1,0:T(8,128)(2,1)S(1)}, bf16[7,16,1024]{2,1,0:T(8,128)(2,1)S(1)}, u32[]{:S(2)}, u32[]{:S(2)}) %collective-permute-start.8) | collective-permute-done | bytes 229408 | tf_op jit(solution)/shard_map/ppermute | solution.py:524
  46.6 1.8 %weight_grad.1 = bf16[1024,768]{1,0:T(8,128)(2,1)} custom-call(f32[8,128]{1,0:T(8,128)} %get-tuple-element.25.tie_ref, bf16[4,4,16,1024]{3,2,1,0:T(8,128)(2,1)S(1)} %get-tuple-element.32.mine, bf16[4,4,16,1024]{3,2,1,0:T(8,128)(2,1)S(1)} %collective-permute-done.5.swapped, bf16[128,768]{1,0:T(8,128)(2,1)S(1)} %get-tuple-element.23.hidden_ref, ...), custom_call_target="tpu_custom_call" | custom-call | flops 1024 | bytes 1024 | tf_op jit(solution)/shard_map/weight_grad/pallas_call | solution.py:505
  (7 shorter events, 0.0 us)
Async XLA Ops:
  2.7 17.3 %collective-permute-start.4 = (bf16[33,16,256]{2,1,0:T(8,128)(2,1)S(1)}, bf16[33,16,256]{2,1,0:T(8,128)(2,1)S(1)}, u32[]{:S(2)}, u32[]{:S(2)}) collective-permute-start(bf16[33,16,256]{2,1,0:T(8,128)(2,1)S(1)} %get-tuple-element.31), channel_id=1, source_target_pairs={{0,16},{8,24},{16,0},{24,8},{1,17},{9,25},{17,1},{25,9},{2,18},{10... | collective-permute-start | bytes 811016 | tf_op jit(solution)/shard_map/ppermute | solution.py:524
  5.4 13.4 %collective-permute-start.1 = (bf16[2,4,16,1024]{3,2,1,0:T(8,128)(2,1)S(1)}, bf16[2,4,16,1024]{3,2,1,0:T(8,128)(2,1)S(1)}, u32[]{:S(2)}, u32[]{:S(2)}) collective-permute-start(bf16[2,4,16,1024]{3,2,1,0:T(8,128)(2,1)S(1)} %get-tuple-element.28), channel_id=1, source_target_pairs={{0,2},{1,3},{2,0},{3,1},{4,6},{5,7},{6,4},{7,5},{8,10},{9,11},{10,... | collective-permute-start | bytes 786440 | tf_op jit(solution)/shard_map/ppermute | solution.py:524
  6.9 13.1 %collective-permute-start.2 = (bf16[2,4,16,1024]{3,2,1,0:T(8,128)(2,1)S(1)}, bf16[2,4,16,1024]{3,2,1,0:T(8,128)(2,1)S(1)}, u32[]{:S(2)}, u32[]{:S(2)}) collective-permute-start(bf16[2,4,16,1024]{3,2,1,0:T(8,128)(2,1)S(1)} %get-tuple-element.29), channel_id=1, source_target_pairs={{0,4},{1,5},{2,6},{3,7},{4,0},{5,1},{6,2},{7,3},{8,12},{9,13},{10,... | collective-permute-start | bytes 786440 | tf_op jit(solution)/shard_map/ppermute | solution.py:524
  7.4 12.6 %collective-permute-start.3 = (bf16[2,4,16,1024]{3,2,1,0:T(8,128)(2,1)S(1)}, bf16[2,4,16,1024]{3,2,1,0:T(8,128)(2,1)S(1)}, u32[]{:S(2)}, u32[]{:S(2)}) collective-permute-start(bf16[2,4,16,1024]{3,2,1,0:T(8,128)(2,1)S(1)} %get-tuple-element.30), channel_id=1, source_target_pairs={{0,6},{1,7},{2,4},{3,5},{4,2},{5,3},{6,0},{7,1},{8,14},{9,15},{10,... | collective-permute-start | bytes 786440 | tf_op jit(solution)/shard_map/ppermute | solution.py:524
  8.9 9.9 %collective-permute-start = (bf16[28,16,256]{2,1,0:T(8,128)(2,1)S(1)}, bf16[28,16,256]{2,1,0:T(8,128)(2,1)S(1)}, u32[]{:S(2)}, u32[]{:S(2)}) collective-permute-start(bf16[28,16,256]{2,1,0:T(8,128)(2,1)S(1)} %get-tuple-element.26), channel_id=1, source_target_pairs={{0,8},{8,0},{16,24},{24,16},{1,9},{9,1},{17,25},{25,17},{2,10},{10... | collective-permute-start | bytes 688136 | tf_op jit(solution)/shard_map/ppermute | solution.py:524
  14.1 18.7 %all-to-all-start = ((bf16[8,16,4096]{2,1,0:T(8,128)(2,1)}), bf16[8,16,4096]{2,1,0:T(8,128)(2,1)}, u32[]{:S(2)}, u32[]{:S(2)}) async-start(bf16[8,16,4096]{2,1,0:T(8,128)(2,1)} %expert_forward.1.refs_5_), calls=%async_computation | async-start | bytes 2097152 | tf_op jit(solution)/shard_map/all_to_all | solution.py:547
  18.8 1.2 %copy-start = (bf16[28,16,256]{2,1,0:T(8,128)(2,1)}, bf16[28,16,256]{2,1,0:T(8,128)(2,1)S(1)}, u32[]{:S(2)}) copy-start(bf16[28,16,256]{2,1,0:T(8,128)(2,1)S(1)} %collective-permute-done.refs_6_.message_hbm) | copy-start | bytes 688132
  20.1 2.0 %collective-permute-start.5 = (bf16[4,4,16,1024]{3,2,1,0:T(8,128)(2,1)S(1)}, bf16[4,4,16,1024]{3,2,1,0:T(8,128)(2,1)S(1)}, u32[]{:S(2)}, u32[]{:S(2)}) collective-permute-start(bf16[4,4,16,1024]{3,2,1,0:T(8,128)(2,1)S(1)} %get-tuple-element.33), channel_id=1, source_target_pairs={{0,1},{1,0},{2,3},{3,2},{4,5},{5,4},{6,7},{7,6},{8,9},{9,8},{10,11... | collective-permute-start | bytes 1572872 | tf_op jit(solution)/shard_map/ppermute | solution.py:524
  20.2 16.3 %collective-permute-start.9 = (bf16[28,16,256]{2,1,0:T(8,128)(2,1)S(1)}, bf16[28,16,256]{2,1,0:T(8,128)(2,1)S(1)}, u32[]{:S(2)}, u32[]{:S(2)}) collective-permute-start(bf16[28,16,256]{2,1,0:T(8,128)(2,1)S(1)} %get-tuple-element.39), channel_id=1, source_target_pairs={{0,8},{8,0},{16,24},{24,16},{1,9},{9,1},{17,25},{25,17},{2,10},{10... | collective-permute-start | bytes 688136 | tf_op jit(solution)/shard_map/ppermute | solution.py:524
  22.8 13.8 %collective-permute-start.6 = (bf16[7,16,1024]{2,1,0:T(8,128)(2,1)S(1)}, bf16[7,16,1024]{2,1,0:T(8,128)(2,1)S(1)}, u32[]{:S(2)}, u32[]{:S(2)}) collective-permute-start(bf16[7,16,1024]{2,1,0:T(8,128)(2,1)S(1)} %get-tuple-element.34.tie_ref), channel_id=1, source_target_pairs={{0,8},{8,0},{16,24},{24,16},{1,9},{9,1},{17,25},{25,17},{2,10},{10... | collective-permute-start | bytes 688136 | tf_op jit(solution)/shard_map/ppermute | solution.py:524
  23.9 14.6 %collective-permute-start.7 = (bf16[7,16,1024]{2,1,0:T(8,128)(2,1)}, bf16[7,16,1024]{2,1,0:T(8,128)(2,1)S(1)}, u32[]{:S(2)}, u32[]{:S(2)}) collective-permute-start(bf16[7,16,1024]{2,1,0:T(8,128)(2,1)} %get-tuple-element.36), channel_id=1, source_target_pairs={{0,16},{8,24},{16,0},{24,8},{1,17},{9,25},{17,1},{25,9},{2,18},{10... | collective-permute-start | bytes 688136 | tf_op jit(solution)/shard_map/ppermute | solution.py:524
  24.9 21.8 %collective-permute-start.8 = (bf16[7,16,1024]{2,1,0:T(8,128)(2,1)S(1)}, bf16[7,16,1024]{2,1,0:T(8,128)(2,1)S(1)}, u32[]{:S(2)}, u32[]{:S(2)}) collective-permute-start(bf16[7,16,1024]{2,1,0:T(8,128)(2,1)S(1)} %get-tuple-element.37), channel_id=1, source_target_pairs={{0,24},{8,16},{16,8},{24,0},{1,25},{9,17},{17,9},{25,1},{2,26},{10... | collective-permute-start | bytes 688136 | tf_op jit(solution)/shard_map/ppermute | solution.py:524

commit v15 on v12

--- a/solution.py
+++ b/solution.py
@@ -23,7 +23,7 @@
 
 
 def params(slots):
-    return pltpu.CompilerParams(vmem_limit_bytes=(12 + slots // 32) * 1024 * 1024)
+    return pltpu.CompilerParams(vmem_limit_bytes=3 * (slots // 32) * 1024 * 1024)
 
 
 def hbm(value):

time: 47.4 us -> 47.4 us (level)
  no operation moved by 1% of the time
where the time goes in v15:
time: 47.4 us; the launch traced here: 47.2 us
  Pallas kernels  18.4 us (39%)
  starting transfers between devices  16.6 us (35%)
  waiting for transfers between devices  11.5 us (24%)
  between operations  0.7 us (1%)
    ppermute x10, starting transfers between devices, swap(): return lax.ppermute(value, axis, [(i, i ^ j) for i in range(size)])  11.9 us
    ppermute x10, waiting for transfers between devices, swap(): return lax.ppermute(value, axis, [(i, i ^ j) for i in range(size)])  10.8 us
    pallas_call x1, Pallas kernels, backward(): pl.pallas_call(functools.partial(backward_kernel, flight, groups), out_sh...  5.25 us
    pallas_call x1, Pallas kernels, forward(): pl.pallas_call(functools.partial(forward_kernel, flight, block), out_shap...  4.81 us
    all_to_all x1, starting transfers between devices, shards(): lax.all_to_all(expert_out, 'expert', split_axis=0, concat_axis=0, tiled=T...  4.68 us
    pallas_call x1, Pallas kernels, combine(): pl.pallas_call(functools.partial(combine_kernel, block), out_shape=(pltpu...  3.63 us
    pallas_call x1, Pallas kernels, dispatch(): pl.pallas_call(functools.partial(dispatch_kernel, flight, groups), out_sh...  2.09 us
    pallas_call x1, Pallas kernels, weight_grad(): pl.pallas_call(functools.partial(weight_grad_kernel, groups, block), out_...  1.82 us
  transfers between devices with their start and end apart: 11, of which 5 were waited for; matrix products, arithmetic and copies ran while one was open for 0% of the time, Pallas kernels for 31%

profile of v15, /device:TPU:10, one launch (start us, length us, event | category | flops | bytes accessed | tf_op | source)
XLA Modules:
  0.0 47.2 jit_solution(13815976372388824497)
XLA Ops:
  0.6 2.1 %dispatch.1 = (f32[128,128]{1,0:T(8,128)}, bf16[128,768]{1,0:T(8,128)(2,1)S(1)}, bf16[2,4,16,1024]{3,2,1,0:T(8,128)(2,1)S(1)}, bf16[2,4,16,1024]{3,2,1,0:T(8,128...) custom-call(bf16[128,1536]{1,0:T(8,128)(2,1)} %bitcast.10, ...), custom_call_target="tpu_custom_call" | custom-call | flops 1024 | bytes 1024 | tf_op jit(solution)/shard_map/dispatch/pallas_call | solution.py:154
  2.7 2.7 %collective-permute-start.3 = (bf16[33,16,256]{2,1,0:T(8,128)(2,1)S(1)}, bf16[33,16,256]{2,1,0:T(8,128)(2,1)S(1)}, u32[]{:S(2)}, u32[]{:S(2)}) collective-permute-start(bf16[33,16,256]{2,1,0:T(8,128)(2,1)S(1)} %get-tuple-element.28), channel_id=1, source_target_pairs={{0,16},{8,24},{16,0},{24,8},{1,17},{9,25},{17,1},{25,9},{2,18},{10... | collective-permute-start | bytes 811016 | tf_op jit(solution)/shard_map/ppermute | solution.py:520
  5.4 0.5 %collective-permute-start = (bf16[2,4,16,1024]{3,2,1,0:T(8,128)(2,1)S(1)}, bf16[2,4,16,1024]{3,2,1,0:T(8,128)(2,1)S(1)}, u32[]{:S(2)}, u32[]{:S(2)}) collective-permute-start(bf16[2,4,16,1024]{3,2,1,0:T(8,128)(2,1)S(1)} %get-tuple-element.25), channel_id=1, source_target_pairs={{0,2},{1,3},{2,0},{3,1},{4,6},{5,7},{6,4},{7,5},{8,10},{9,11},{10,... | collective-permute-start | bytes 786440 | tf_op jit(solution)/shard_map/ppermute | solution.py:520
  5.9 1.5 %collective-permute-start.1 = (bf16[2,4,16,1024]{3,2,1,0:T(8,128)(2,1)S(1)}, bf16[2,4,16,1024]{3,2,1,0:T(8,128)(2,1)S(1)}, u32[]{:S(2)}, u32[]{:S(2)}) collective-permute-start(bf16[2,4,16,1024]{3,2,1,0:T(8,128)(2,1)S(1)} %get-tuple-element.26), channel_id=1, source_target_pairs={{0,4},{1,5},{2,6},{3,7},{4,0},{5,1},{6,2},{7,3},{8,12},{9,13},{10,... | collective-permute-start | bytes 786440 | tf_op jit(solution)/shard_map/ppermute | solution.py:520
  7.4 1.4 %collective-permute-start.2 = (bf16[2,4,16,1024]{3,2,1,0:T(8,128)(2,1)S(1)}, bf16[2,4,16,1024]{3,2,1,0:T(8,128)(2,1)S(1)}, u32[]{:S(2)}, u32[]{:S(2)}) collective-permute-start(bf16[2,4,16,1024]{3,2,1,0:T(8,128)(2,1)S(1)} %get-tuple-element.27), channel_id=1, source_target_pairs={{0,6},{1,7},{2,4},{3,5},{4,2},{5,3},{6,0},{7,1},{8,14},{9,15},{10,... | collective-permute-start | bytes 786440 | tf_op jit(solution)/shard_map/ppermute | solution.py:520
  8.9 0.4 collective-permute-start.4
  9.3 4.8 %expert_forward.1.refs_5_ = bf16[8,16,4096]{2,1,0:T(8,128)(2,1)} custom-call(bf16[128,768]{1,0:T(8,128)(2,1)S(1)} %get-tuple-element.21.hidden_ref, f32[6,1,32]{2,1,0:T(1,128)} %bitcast.16, bf16[768,4096]{1,0:T(8,128)(2,1)} %bitcast.8), custom_call_target="tpu_custom_call" | custom-call | flops 1024 | bytes 1024 | tf_op jit(solution)/shard_map/expert_forward/pallas_call | solution.py:230
  14.1 4.7 %all-to-all-start = ((bf16[8,16,4096]{2,1,0:T(8,128)(2,1)}), bf16[8,16,4096]{2,1,0:T(8,128)(2,1)}, u32[]{:S(2)}, u32[]{:S(2)}) async-start(bf16[8,16,4096]{2,1,0:T(8,128)(2,1)} %expert_forward.1.refs_5_), calls=%async_computation | async-start | bytes 2097152 | tf_op jit(solution)/shard_map/all_to_all | solution.py:543
  18.8 0.0 collective-permute-done.1.refs_2_
  18.8 0.9 %collective-permute-done.2.refs_3_ = bf16[2,4,16,1024]{3,2,1,0:T(8,128)(2,1)S(1)} collective-permute-done((bf16[2,4,16,1024]{3,2,1,0:T(8,128)(2,1)S(1)}, bf16[2,4,16,1024]{3,2,1,0:T(8,128)(2,1)S(1)}, u32[]{:S(2)}, u32[]{:S(2)}) %collective-permute-start.2) | collective-permute-done | bytes 262176 | tf_op jit(solution)/shard_map/ppermute | solution.py:520
  19.7 0.1 sort_rows.1
  19.8 0.1 collective-permute-start.5
  19.9 0.9 %collective-permute-start.9 = (bf16[28,16,256]{2,1,0:T(8,128)(2,1)S(1)}, bf16[28,16,256]{2,1,0:T(8,128)(2,1)S(1)}, u32[]{:S(2)}, u32[]{:S(2)}) collective-permute-start(bf16[28,16,256]{2,1,0:T(8,128)(2,1)S(1)} %get-tuple-element.35), channel_id=1, source_target_pairs={{0,8},{8,0},{16,24},{24,16},{1,9},{9,1},{17,25},{25,17},{2,10},{10... | collective-permute-start | bytes 688136 | tf_op jit(solution)/shard_map/ppermute | solution.py:520
  20.8 1.0 %collective-permute-done.5.swapped = bf16[4,4,16,1024]{3,2,1,0:T(8,128)(2,1)S(1)} collective-permute-done((bf16[4,4,16,1024]{3,2,1,0:T(8,128)(2,1)S(1)}, bf16[4,4,16,1024]{3,2,1,0:T(8,128)(2,1)S(1)}, u32[]{:S(2)}, u32[]{:S(2)}) %collective-permute-start.5) | collective-permute-done | bytes 524320 | tf_op jit(solution)/shard_map/ppermute | solution.py:520
  21.8 0.7 %split.1 = (bf16[7,16,1024]{2,1,0:T(8,128)(2,1)S(1)}, bf16[7,16,1024]{2,1,0:T(8,128)(2,1)}, bf16[7,16,1024]{2,1,0:T(8,128)(2,1)S(1)}) custom-call(bf16[4,4,16,1024]{3,2,1,0:T(8,128)(2,1)S(1)} %get-tuple-element.30.mine, bf16[4,4,16,1024]{3,2,1,0:T(8,128)(2,1)S(1)} %collective-permute-done.5.swapped), custom_call_target="tpu_custom_call" | custom-call | flops 1024 | bytes 1024 | tf_op jit(solution)/shard_map/split/pallas_call | solution.py:287
  22.5 1.5 %collective-permute-start.7 = (bf16[7,16,1024]{2,1,0:T(8,128)(2,1)}, bf16[7,16,1024]{2,1,0:T(8,128)(2,1)S(1)}, u32[]{:S(2)}, u32[]{:S(2)}) collective-permute-start(bf16[7,16,1024]{2,1,0:T(8,128)(2,1)} %get-tuple-element.33), channel_id=1, source_target_pairs={{0,16},{8,24},{16,0},{24,8},{1,17},{9,25},{17,1},{25,9},{2,18},{10... | collective-permute-start | bytes 688136 | tf_op jit(solution)/shard_map/ppermute | solution.py:520
  24.0 0.7 %collective-permute-start.8 = (bf16[7,16,1024]{2,1,0:T(8,128)(2,1)S(1)}, bf16[7,16,1024]{2,1,0:T(8,128)(2,1)S(1)}, u32[]{:S(2)}, u32[]{:S(2)}) collective-permute-start(bf16[7,16,1024]{2,1,0:T(8,128)(2,1)S(1)} %get-tuple-element.34), channel_id=1, source_target_pairs={{0,24},{8,16},{16,8},{24,0},{1,25},{9,17},{17,9},{25,1},{2,26},{10... | collective-permute-start | bytes 688136 | tf_op jit(solution)/shard_map/ppermute | solution.py:520
  24.7 2.2 %collective-permute-start.6 = (bf16[7,16,1024]{2,1,0:T(8,128)(2,1)S(1)}, bf16[7,16,1024]{2,1,0:T(8,128)(2,1)S(1)}, u32[]{:S(2)}, u32[]{:S(2)}) collective-permute-start(bf16[7,16,1024]{2,1,0:T(8,128)(2,1)S(1)} %get-tuple-element.32.tie_ref), channel_id=1, source_target_pairs={{0,8},{8,0},{16,24},{24,16},{1,9},{9,1},{17,25},{25,17},{2,10},{10... | collective-permute-start | bytes 688136 | tf_op jit(solution)/shard_map/ppermute | solution.py:520
  26.9 5.2 %expert_backward.1 = bf16[128,1536]{1,0:T(8,128)(2,1)} custom-call(f32[6,1,32]{2,1,0:T(1,128)} %bitcast.17, bf16[128,1536]{1,0:T(8,128)(2,1)} %bitcast.11, bf16[768,4096]{1,0:T(8,128)(2,1)} %bitcast.9, bf16[7,16,1024]{2,1,0:T(8,128)(2,1)S(1)} %get-tuple-element.32.tie_ref, bf16[4,4,16,1024]{3,2,1,0:T(8,128)(2,1)S(1)} %get-tuple-element.30.mine, ...), custom_call_target="tpu_custom_call" | custom-call | flops 1024 | bytes 1024 | tf_op jit(solution)/shard_map/expert_backward/pallas_call | solution.py:371
  32.2 0.7 %all-to-all-done.ret_hbm = bf16[8,16,4096]{2,1,0:T(8,128)(2,1)} async-done(((bf16[8,16,4096]{2,1,0:T(8,128)(2,1)}), bf16[8,16,4096]{2,1,0:T(8,128)(2,1)}, u32[]{:S(2)}, u32[]{:S(2)}) %all-to-all-start) | async-done | bytes 1048608 | tf_op jit(solution)/shard_map/all_to_all | solution.py:543
  32.8 3.6 %combine.1 = (bf16[128,4096]{1,0:T(8,128)(2,1)}, f32[8,128]{1,0:T(8,128)}) custom-call(s32[8,128]{1,0:T(8,128)} %bitcast.15, f32[128,128]{1,0:T(8,128)} %get-tuple-element.20.own_hbm, bf16[128,4096]{1,0:T(8,128)(2,1)} %dout_hbm.3, bf16[8,16,4096]{2,1,0:T(8,128)(2,1)} %all-to-all-done.ret_hbm), custom_call_target="tpu_custom_call" | custom-call | flops 1024 | bytes 1024 | tf_op jit(solution)/shard_map/combine/pallas_call | solution.py:437
  36.5 3.7 %collective-permute-done.7.refs_1_ = bf16[7,16,1024]{2,1,0:T(8,128)(2,1)S(1)} collective-permute-done((bf16[7,16,1024]{2,1,0:T(8,128)(2,1)}, bf16[7,16,1024]{2,1,0:T(8,128)(2,1)S(1)}, u32[]{:S(2)}, u32[]{:S(2)}) %collective-permute-start.7) | collective-permute-done | bytes 229408 | tf_op jit(solution)/shard_map/ppermute | solution.py:520
  40.2 5.2 %collective-permute-done.8.refs_2_ = bf16[7,16,1024]{2,1,0:T(8,128)(2,1)S(1)} collective-permute-done((bf16[7,16,1024]{2,1,0:T(8,128)(2,1)S(1)}, bf16[7,16,1024]{2,1,0:T(8,128)(2,1)S(1)}, u32[]{:S(2)}, u32[]{:S(2)}) %collective-permute-start.8) | collective-permute-done | bytes 229408 | tf_op jit(solution)/shard_map/ppermute | solution.py:520
  45.4 1.8 %weight_grad.1 = bf16[1024,768]{1,0:T(8,128)(2,1)} custom-call(f32[8,128]{1,0:T(8,128)} %get-tuple-element.23.tie_ref, bf16[4,4,16,1024]{3,2,1,0:T(8,128)(2,1)S(1)} %get-tuple-element.30.mine, bf16[4,4,16,1024]{3,2,1,0:T(8,128)(2,1)S(1)} %collective-permute-done.5.swapped, bf16[128,768]{1,0:T(8,128)(2,1)S(1)} %get-tuple-element.21.hidden_ref, ...), custom_call_target="tpu_custom_call" | custom-call | flops 1024 | bytes 1024 | tf_op jit(solution)/shard_map/weight_grad/pallas_call | solution.py:501
  (5 shorter events, 0.0 us)
Async XLA Ops:
  2.7 17.0 %collective-permute-start.3 = (bf16[33,16,256]{2,1,0:T(8,128)(2,1)S(1)}, bf16[33,16,256]{2,1,0:T(8,128)(2,1)S(1)}, u32[]{:S(2)}, u32[]{:S(2)}) collective-permute-start(bf16[33,16,256]{2,1,0:T(8,128)(2,1)S(1)} %get-tuple-element.28), channel_id=1, source_target_pairs={{0,16},{8,24},{16,0},{24,8},{1,17},{9,25},{17,1},{25,9},{2,18},{10... | collective-permute-start | bytes 811016 | tf_op jit(solution)/shard_map/ppermute | solution.py:520
  5.4 13.4 %collective-permute-start = (bf16[2,4,16,1024]{3,2,1,0:T(8,128)(2,1)S(1)}, bf16[2,4,16,1024]{3,2,1,0:T(8,128)(2,1)S(1)}, u32[]{:S(2)}, u32[]{:S(2)}) collective-permute-start(bf16[2,4,16,1024]{3,2,1,0:T(8,128)(2,1)S(1)} %get-tuple-element.25), channel_id=1, source_target_pairs={{0,2},{1,3},{2,0},{3,1},{4,6},{5,7},{6,4},{7,5},{8,10},{9,11},{10,... | collective-permute-start | bytes 786440 | tf_op jit(solution)/shard_map/ppermute | solution.py:520
  5.9 12.9 %collective-permute-start.1 = (bf16[2,4,16,1024]{3,2,1,0:T(8,128)(2,1)S(1)}, bf16[2,4,16,1024]{3,2,1,0:T(8,128)(2,1)S(1)}, u32[]{:S(2)}, u32[]{:S(2)}) collective-permute-start(bf16[2,4,16,1024]{3,2,1,0:T(8,128)(2,1)S(1)} %get-tuple-element.26), channel_id=1, source_target_pairs={{0,4},{1,5},{2,6},{3,7},{4,0},{5,1},{6,2},{7,3},{8,12},{9,13},{10,... | collective-permute-start | bytes 786440 | tf_op jit(solution)/shard_map/ppermute | solution.py:520
  7.4 12.3 %collective-permute-start.2 = (bf16[2,4,16,1024]{3,2,1,0:T(8,128)(2,1)S(1)}, bf16[2,4,16,1024]{3,2,1,0:T(8,128)(2,1)S(1)}, u32[]{:S(2)}, u32[]{:S(2)}) collective-permute-start(bf16[2,4,16,1024]{3,2,1,0:T(8,128)(2,1)S(1)} %get-tuple-element.27), channel_id=1, source_target_pairs={{0,6},{1,7},{2,4},{3,5},{4,2},{5,3},{6,0},{7,1},{8,14},{9,15},{10,... | collective-permute-start | bytes 786440 | tf_op jit(solution)/shard_map/ppermute | solution.py:520
  8.9 9.9 %collective-permute-start.4 = (bf16[28,16,256]{2,1,0:T(8,128)(2,1)S(1)}, bf16[28,16,256]{2,1,0:T(8,128)(2,1)S(1)}, u32[]{:S(2)}, u32[]{:S(2)}) collective-permute-start(bf16[28,16,256]{2,1,0:T(8,128)(2,1)S(1)} %get-tuple-element.29), channel_id=1, source_target_pairs={{0,8},{8,0},{16,24},{24,16},{1,9},{9,1},{17,25},{25,17},{2,10},{10... | collective-permute-start | bytes 688136 | tf_op jit(solution)/shard_map/ppermute | solution.py:520
  14.1 18.7 %all-to-all-start = ((bf16[8,16,4096]{2,1,0:T(8,128)(2,1)}), bf16[8,16,4096]{2,1,0:T(8,128)(2,1)}, u32[]{:S(2)}, u32[]{:S(2)}) async-start(bf16[8,16,4096]{2,1,0:T(8,128)(2,1)} %expert_forward.1.refs_5_), calls=%async_computation | async-start | bytes 2097152 | tf_op jit(solution)/shard_map/all_to_all | solution.py:543
  19.8 2.0 %collective-permute-start.5 = (bf16[4,4,16,1024]{3,2,1,0:T(8,128)(2,1)S(1)}, bf16[4,4,16,1024]{3,2,1,0:T(8,128)(2,1)S(1)}, u32[]{:S(2)}, u32[]{:S(2)}) collective-permute-start(bf16[4,4,16,1024]{3,2,1,0:T(8,128)(2,1)S(1)} %get-tuple-element.31), channel_id=1, source_target_pairs={{0,1},{1,0},{2,3},{3,2},{4,5},{5,4},{6,7},{7,6},{8,9},{9,8},{10,11... | collective-permute-start | bytes 1572872 | tf_op jit(solution)/shard_map/ppermute | solution.py:520
  19.9 16.6 %collective-permute-start.9 = (bf16[28,16,256]{2,1,0:T(8,128)(2,1)S(1)}, bf16[28,16,256]{2,1,0:T(8,128)(2,1)S(1)}, u32[]{:S(2)}, u32[]{:S(2)}) collective-permute-start(bf16[28,16,256]{2,1,0:T(8,128)(2,1)S(1)} %get-tuple-element.35), channel_id=1, source_target_pairs={{0,8},{8,0},{16,24},{24,16},{1,9},{9,1},{17,25},{25,17},{2,10},{10... | collective-permute-start | bytes 688136 | tf_op jit(solution)/shard_map/ppermute | solution.py:520
  22.5 17.7 %collective-permute-start.7 = (bf16[7,16,1024]{2,1,0:T(8,128)(2,1)}, bf16[7,16,1024]{2,1,0:T(8,128)(2,1)S(1)}, u32[]{:S(2)}, u32[]{:S(2)}) collective-permute-start(bf16[7,16,1024]{2,1,0:T(8,128)(2,1)} %get-tuple-element.33), channel_id=1, source_target_pairs={{0,16},{8,24},{16,0},{24,8},{1,17},{9,25},{17,1},{25,9},{2,18},{10... | collective-permute-start | bytes 688136 | tf_op jit(solution)/shard_map/ppermute | solution.py:520
  24.0 21.4 %collective-permute-start.8 = (bf16[7,16,1024]{2,1,0:T(8,128)(2,1)S(1)}, bf16[7,16,1024]{2,1,0:T(8,128)(2,1)S(1)}, u32[]{:S(2)}, u32[]{:S(2)}) collective-permute-start(bf16[7,16,1024]{2,1,0:T(8,128)(2,1)S(1)} %get-tuple-element.34), channel_id=1, source_target_pairs={{0,24},{8,16},{16,8},{24,0},{1,25},{9,17},{17,9},{25,1},{2,26},{10... | collective-permute-start | bytes 688136 | tf_op jit(solution)/shard_map/ppermute | solution.py:520
  24.7 20.7 %collective-permute-start.6 = (bf16[7,16,1024]{2,1,0:T(8,128)(2,1)S(1)}, bf16[7,16,1024]{2,1,0:T(8,128)(2,1)S(1)}, u32[]{:S(2)}, u32[]{:S(2)}) collective-permute-start(bf16[7,16,1024]{2,1,0:T(8,128)(2,1)S(1)} %get-tuple-element.32.tie_ref), channel_id=1, source_target_pairs={{0,8},{8,0},{16,24},{24,16},{1,9},{9,1},{17,25},{25,17},{2,10},{10... | collective-permute-start | bytes 688136 | tf_op jit(solution)/shard_map/ppermute | solution.py:520

commit v16 on v11

--- a/solution.py
+++ b/solution.py
@@ -10,7 +10,6 @@
 QB = 128
 CAP = 16
 TILE = 256
-AHEAD = 3
 
 bf16 = jnp.bfloat16
 f32 = jnp.float32
@@ -191,7 +190,7 @@
         for c in range(steps)
     ]
     small = pltpu.make_async_copy(scale_hbm, scale, scale_sem)
-    for copy in [small] + loads[:AHEAD]:
+    for copy in [small] + loads:
         copy.start()
     for r in range(flight):
         place = pl.multiple_of(block_place(me, r, flight) * CAP, CAP)
@@ -201,8 +200,6 @@
     for c in range(steps):
         cols = pl.ds(c * block, block)
         loads[c].wait()
-        if c + AHEAD < steps:
-            loads[c + AHEAD].start()
         total = [None] * (block // QB)
         for i in range(hid // QB):
             part = jnp.dot(

time: 47.4 us -> 47.3 us (level)
    ppermute x10, waiting for transfers between devices: 5.08 us -> 5.94 us  [swap(): return lax.ppermute(value, axis, [(i, i ^ j) for i in range(size)])]
  transfers between devices with their start and end apart: 11 -> 11, of which waited for: 4 -> 6; matrix products, arithmetic and copies ran while one was open for 0% -> 0% of each run, Pallas kernels for 30% -> 29%
where the time goes in v16:
time: 47.3 us; the launch traced here: 47 us
  starting transfers between devices  19.1 us (40%)
  Pallas kernels  17.7 us (37%)
  waiting for transfers between devices  9.5 us (20%)
  between operations  0.71 us (2%)
    ppermute x10, starting transfers between devices, swap(): return lax.ppermute(value, axis, [(i, i ^ j) for i in range(size)])  14.9 us
    ppermute x10, waiting for transfers between devices, swap(): return lax.ppermute(value, axis, [(i, i ^ j) for i in range(size)])  5.94 us
    pallas_call x1, Pallas kernels, backward(): pl.pallas_call(functools.partial(backward_kernel, flight, groups), out_sh...  5.26 us
    pallas_call x1, Pallas kernels, forward(): pl.pallas_call(functools.partial(forward_kernel, flight, block), out_shap...  4.78 us
    all_to_all x1, starting transfers between devices, shards(): lax.all_to_all(expert_out, 'expert', split_axis=0, concat_axis=0, tiled=T...  4.27 us
    pallas_call x1, Pallas kernels, combine(): pl.pallas_call(functools.partial(combine_kernel, block), out_shape=(pltpu...  3.63 us
    all_to_all x1, waiting for transfers between devices, shards(): lax.all_to_all(expert_out, 'expert', split_axis=0, concat_axis=0, tiled=T...  3.57 us
    pallas_call x1, Pallas kernels, dispatch(): pl.pallas_call(functools.partial(dispatch_kernel, flight, groups), out_sh...  2.09 us
  transfers between devices with their start and end apart: 11, of which 6 were waited for; matrix products, arithmetic and copies ran while one was open for 0% of the time, Pallas kernels for 29%

profile of v16, /device:TPU:0, one launch (start us, length us, event | category | flops | bytes accessed | tf_op | source)
XLA Modules:
  0.0 47.0 jit_solution(13079297045901258370)
XLA Ops:
  0.6 2.1 %dispatch.1 = (f32[128,128]{1,0:T(8,128)}, bf16[128,768]{1,0:T(8,128)(2,1)S(1)}, bf16[2,4,16,1024]{3,2,1,0:T(8,128)(2,1)S(1)}, bf16[2,4,16,1024]{3,2,1,0:T(8,128...) custom-call(bf16[128,1536]{1,0:T(8,128)(2,1)} %bitcast.10, ...), custom_call_target="tpu_custom_call" | custom-call | flops 1024 | bytes 1024 | tf_op jit(solution)/shard_map/dispatch/pallas_call | solution.py:153
  2.7 4.1 %collective-permute-start.3 = (bf16[33,16,256]{2,1,0:T(8,128)(2,1)S(1)}, bf16[33,16,256]{2,1,0:T(8,128)(2,1)S(1)}, u32[]{:S(2)}, u32[]{:S(2)}) collective-permute-start(bf16[33,16,256]{2,1,0:T(8,128)(2,1)S(1)} %get-tuple-element.27), channel_id=1, source_target_pairs={{0,16},{8,24},{16,0},{24,8},{1,17},{9,25},{17,1},{25,9},{2,18},{10... | collective-permute-start | bytes 811016 | tf_op jit(solution)/shard_map/ppermute | solution.py:509
  6.8 1.5 %collective-permute-start = (bf16[2,4,16,1024]{3,2,1,0:T(8,128)(2,1)S(1)}, bf16[2,4,16,1024]{3,2,1,0:T(8,128)(2,1)S(1)}, u32[]{:S(2)}, u32[]{:S(2)}) collective-permute-start(bf16[2,4,16,1024]{3,2,1,0:T(8,128)(2,1)S(1)} %get-tuple-element.24), channel_id=1, source_target_pairs={{0,2},{1,3},{2,0},{3,1},{4,6},{5,7},{6,4},{7,5},{8,10},{9,11},{10,... | collective-permute-start | bytes 786440 | tf_op jit(solution)/shard_map/ppermute | solution.py:509
  8.3 1.5 %collective-permute-start.1 = (bf16[2,4,16,1024]{3,2,1,0:T(8,128)(2,1)S(1)}, bf16[2,4,16,1024]{3,2,1,0:T(8,128)(2,1)S(1)}, u32[]{:S(2)}, u32[]{:S(2)}) collective-permute-start(bf16[2,4,16,1024]{3,2,1,0:T(8,128)(2,1)S(1)} %get-tuple-element.25), channel_id=1, source_target_pairs={{0,4},{1,5},{2,6},{3,7},{4,0},{5,1},{6,2},{7,3},{8,12},{9,13},{10,... | collective-permute-start | bytes 786440 | tf_op jit(solution)/shard_map/ppermute | solution.py:509
  9.8 0.5 %collective-permute-start.2 = (bf16[2,4,16,1024]{3,2,1,0:T(8,128)(2,1)S(1)}, bf16[2,4,16,1024]{3,2,1,0:T(8,128)(2,1)S(1)}, u32[]{:S(2)}, u32[]{:S(2)}) collective-permute-start(bf16[2,4,16,1024]{3,2,1,0:T(8,128)(2,1)S(1)} %get-tuple-element.26), channel_id=1, source_target_pairs={{0,6},{1,7},{2,4},{3,5},{4,2},{5,3},{6,0},{7,1},{8,14},{9,15},{10,... | collective-permute-start | bytes 786440 | tf_op jit(solution)/shard_map/ppermute | solution.py:509
  10.3 1.6 %collective-permute-start.4 = (bf16[28,16,256]{2,1,0:T(8,128)(2,1)S(1)}, bf16[28,16,256]{2,1,0:T(8,128)(2,1)S(1)}, u32[]{:S(2)}, u32[]{:S(2)}) collective-permute-start(bf16[28,16,256]{2,1,0:T(8,128)(2,1)S(1)} %get-tuple-element.28), channel_id=1, source_target_pairs={{0,8},{8,0},{16,24},{24,16},{1,9},{9,1},{17,25},{25,17},{2,10},{10... | collective-permute-start | bytes 688136 | tf_op jit(solution)/shard_map/ppermute | solution.py:509
  11.9 4.8 %expert_forward.1.refs_4_ = bf16[8,16,4096]{2,1,0:T(8,128)(2,1)} custom-call(bf16[128,768]{1,0:T(8,128)(2,1)S(1)} %get-tuple-element.20.hidden_ref, f32[6,1,32]{2,1,0:T(1,128)} %bitcast.16, bf16[768,4096]{1,0:T(8,128)(2,1)} %bitcast.8), custom_call_target="tpu_custom_call" | custom-call | flops 1024 | bytes 1024 | tf_op jit(solution)/shard_map/expert_forward/pallas_call | solution.py:227
  16.7 4.3 %all-to-all-start = ((bf16[8,16,4096]{2,1,0:T(8,128)(2,1)}), bf16[8,16,4096]{2,1,0:T(8,128)(2,1)}, u32[]{:S(2)}, u32[]{:S(2)}) async-start(bf16[8,16,4096]{2,1,0:T(8,128)(2,1)} %expert_forward.1.refs_4_), calls=%async_computation | async-start | bytes 2097152 | tf_op jit(solution)/shard_map/all_to_all | solution.py:531
  21.0 0.2 collective-permute-done.4.refs_6_.refs_3_
  21.2 0.2 collective-permute-done.1.refs_2_
  21.4 0.0 collective-permute-done.2.refs_3_
  21.4 0.0 collective-permute-done.3.refs_5_.refs_4_
  21.4 0.1 sort_rows.1
  21.5 0.1 collective-permute-start.5
  21.6 1.6 %collective-permute-start.9 = (bf16[33,16,256]{2,1,0:T(8,128)(2,1)S(1)}, bf16[33,16,256]{2,1,0:T(8,128)(2,1)S(1)}, u32[]{:S(2)}, u32[]{:S(2)}) collective-permute-start(bf16[33,16,256]{2,1,0:T(8,128)(2,1)S(1)} %collective-permute-done.3.refs_5_.refs_4_), channel_id=1, source_target_pairs={{0,8},{8,0},{16,24},{24,16},{1,9},{9,1},{17,25},{25,17},{2,10},{10... | collective-permute-start | bytes 811016 | tf_op jit(solution)/shard_map/ppermute | solution.py:509
  23.2 0.3 collective-permute-done.5.swapped
  23.5 1.0 %collective-permute-start.7 = (bf16[7,16,1024]{2,1,0:T(8,128)(2,1)S(1)}, bf16[7,16,1024]{2,1,0:T(8,128)(2,1)S(1)}, u32[]{:S(2)}, u32[]{:S(2)}) collective-permute-start(bf16[7,16,1024]{2,1,0:T(8,128)(2,1)S(1)} %get-tuple-element.32), channel_id=1, source_target_pairs={{0,16},{8,24},{16,0},{24,8},{1,17},{9,25},{17,1},{25,9},{2,18},{10... | collective-permute-start | bytes 688136 | tf_op jit(solution)/shard_map/ppermute | solution.py:509
  24.5 3.0 %collective-permute-start.8 = (bf16[7,16,1024]{2,1,0:T(8,128)(2,1)S(1)}, bf16[7,16,1024]{2,1,0:T(8,128)(2,1)S(1)}, u32[]{:S(2)}, u32[]{:S(2)}) collective-permute-start(bf16[7,16,1024]{2,1,0:T(8,128)(2,1)S(1)} %get-tuple-element.33), channel_id=1, source_target_pairs={{0,24},{8,16},{16,8},{24,0},{1,25},{9,17},{17,9},{25,1},{2,26},{10... | collective-permute-start | bytes 688136 | tf_op jit(solution)/shard_map/ppermute | solution.py:509
  27.5 5.3 %expert_backward.1 = bf16[128,1536]{1,0:T(8,128)(2,1)} custom-call(f32[6,1,32]{2,1,0:T(1,128)} %bitcast.17, bf16[128,1536]{1,0:T(8,128)(2,1)} %bitcast.11, bf16[768,4096]{1,0:T(8,128)(2,1)} %bitcast.9, bf16[7,16,1024]{2,1,0:T(8,128)(2,1)S(1)} %get-tuple-element.31.tie_ref, bf16[4,4,16,1024]{3,2,1,0:T(8,128)(2,1)S(1)} %get-tuple-element.29.mine, ...), custom_call_target="tpu_custom_call" | custom-call | flops 1024 | bytes 1024 | tf_op jit(solution)/shard_map/expert_backward/pallas_call | solution.py:360
  32.8 3.6 %all-to-all-done.ret_hbm = bf16[8,16,4096]{2,1,0:T(8,128)(2,1)} async-done(((bf16[8,16,4096]{2,1,0:T(8,128)(2,1)}), bf16[8,16,4096]{2,1,0:T(8,128)(2,1)}, u32[]{:S(2)}, u32[]{:S(2)}) %all-to-all-start) | async-done | bytes 1048608 | tf_op jit(solution)/shard_map/all_to_all | solution.py:531
  36.4 3.6 %combine.1 = (bf16[128,4096]{1,0:T(8,128)(2,1)}, f32[8,128]{1,0:T(8,128)}) custom-call(s32[8,128]{1,0:T(8,128)} %bitcast.15, f32[128,128]{1,0:T(8,128)} %get-tuple-element.19.own_hbm, bf16[128,4096]{1,0:T(8,128)(2,1)} %dout_hbm.3, bf16[8,16,4096]{2,1,0:T(8,128)(2,1)} %all-to-all-done.ret_hbm), custom_call_target="tpu_custom_call" | custom-call | flops 1024 | bytes 1024 | tf_op jit(solution)/shard_map/combine/pallas_call | solution.py:426
  40.0 2.8 %collective-permute-done.7.refs_1_ = bf16[7,16,1024]{2,1,0:T(8,128)(2,1)S(1)} collective-permute-done((bf16[7,16,1024]{2,1,0:T(8,128)(2,1)S(1)}, bf16[7,16,1024]{2,1,0:T(8,128)(2,1)S(1)}, u32[]{:S(2)}, u32[]{:S(2)}) %collective-permute-start.7) | collective-permute-done | bytes 229408 | tf_op jit(solution)/shard_map/ppermute | solution.py:509
  42.9 2.4 %collective-permute-done.6.refs_0_ = bf16[7,16,1024]{2,1,0:T(8,128)(2,1)S(1)} collective-permute-done((bf16[7,16,1024]{2,1,0:T(8,128)(2,1)S(1)}, bf16[7,16,1024]{2,1,0:T(8,128)(2,1)S(1)}, u32[]{:S(2)}, u32[]{:S(2)}) %collective-permute-start.6) | collective-permute-done | bytes 229408 | tf_op jit(solution)/shard_map/ppermute | solution.py:509
  45.2 1.8 %weight_grad.1 = bf16[1024,768]{1,0:T(8,128)(2,1)} custom-call(f32[8,128]{1,0:T(8,128)} %get-tuple-element.22.tie_ref, bf16[4,4,16,1024]{3,2,1,0:T(8,128)(2,1)S(1)} %get-tuple-element.29.mine, bf16[4,4,16,1024]{3,2,1,0:T(8,128)(2,1)S(1)} %collective-permute-done.5.swapped, bf16[128,768]{1,0:T(8,128)(2,1)S(1)} %get-tuple-element.20.hidden_ref, ...), custom_call_target="tpu_custom_call" | custom-call | flops 1024 | bytes 1024 | tf_op jit(solution)/shard_map/weight_grad/pallas_call | solution.py:490
  (5 shorter events, 0.1 us)
Async XLA Ops:
  2.7 18.7 %collective-permute-start.3 = (bf16[33,16,256]{2,1,0:T(8,128)(2,1)S(1)}, bf16[33,16,256]{2,1,0:T(8,128)(2,1)S(1)}, u32[]{:S(2)}, u32[]{:S(2)}) collective-permute-start(bf16[33,16,256]{2,1,0:T(8,128)(2,1)S(1)} %get-tuple-element.27), channel_id=1, source_target_pairs={{0,16},{8,24},{16,0},{24,8},{1,17},{9,25},{17,1},{25,9},{2,18},{10... | collective-permute-start | bytes 811016 | tf_op jit(solution)/shard_map/ppermute | solution.py:509
  6.8 14.3 %collective-permute-start = (bf16[2,4,16,1024]{3,2,1,0:T(8,128)(2,1)S(1)}, bf16[2,4,16,1024]{3,2,1,0:T(8,128)(2,1)S(1)}, u32[]{:S(2)}, u32[]{:S(2)}) collective-permute-start(bf16[2,4,16,1024]{3,2,1,0:T(8,128)(2,1)S(1)} %get-tuple-element.24), channel_id=1, source_target_pairs={{0,2},{1,3},{2,0},{3,1},{4,6},{5,7},{6,4},{7,5},{8,10},{9,11},{10,... | collective-permute-start | bytes 786440 | tf_op jit(solution)/shard_map/ppermute | solution.py:509
  8.3 13.1 %collective-permute-start.1 = (bf16[2,4,16,1024]{3,2,1,0:T(8,128)(2,1)S(1)}, bf16[2,4,16,1024]{3,2,1,0:T(8,128)(2,1)S(1)}, u32[]{:S(2)}, u32[]{:S(2)}) collective-permute-start(bf16[2,4,16,1024]{3,2,1,0:T(8,128)(2,1)S(1)} %get-tuple-element.25), channel_id=1, source_target_pairs={{0,4},{1,5},{2,6},{3,7},{4,0},{5,1},{6,2},{7,3},{8,12},{9,13},{10,... | collective-permute-start | bytes 786440 | tf_op jit(solution)/shard_map/ppermute | solution.py:509
  9.8 11.6 %collective-permute-start.2 = (bf16[2,4,16,1024]{3,2,1,0:T(8,128)(2,1)S(1)}, bf16[2,4,16,1024]{3,2,1,0:T(8,128)(2,1)S(1)}, u32[]{:S(2)}, u32[]{:S(2)}) collective-permute-start(bf16[2,4,16,1024]{3,2,1,0:T(8,128)(2,1)S(1)} %get-tuple-element.26), channel_id=1, source_target_pairs={{0,6},{1,7},{2,4},{3,5},{4,2},{5,3},{6,0},{7,1},{8,14},{9,15},{10,... | collective-permute-start | bytes 786440 | tf_op jit(solution)/shard_map/ppermute | solution.py:509
  10.3 10.9 %collective-permute-start.4 = (bf16[28,16,256]{2,1,0:T(8,128)(2,1)S(1)}, bf16[28,16,256]{2,1,0:T(8,128)(2,1)S(1)}, u32[]{:S(2)}, u32[]{:S(2)}) collective-permute-start(bf16[28,16,256]{2,1,0:T(8,128)(2,1)S(1)} %get-tuple-element.28), channel_id=1, source_target_pairs={{0,8},{8,0},{16,24},{24,16},{1,9},{9,1},{17,25},{25,17},{2,10},{10... | collective-permute-start | bytes 688136 | tf_op jit(solution)/shard_map/ppermute | solution.py:509
  16.7 19.7 %all-to-all-start = ((bf16[8,16,4096]{2,1,0:T(8,128)(2,1)}), bf16[8,16,4096]{2,1,0:T(8,128)(2,1)}, u32[]{:S(2)}, u32[]{:S(2)}) async-start(bf16[8,16,4096]{2,1,0:T(8,128)(2,1)} %expert_forward.1.refs_4_), calls=%async_computation | async-start | bytes 2097152 | tf_op jit(solution)/shard_map/all_to_all | solution.py:531
  21.5 2.0 %collective-permute-start.5 = (bf16[4,4,16,1024]{3,2,1,0:T(8,128)(2,1)S(1)}, bf16[4,4,16,1024]{3,2,1,0:T(8,128)(2,1)S(1)}, u32[]{:S(2)}, u32[]{:S(2)}) collective-permute-start(bf16[4,4,16,1024]{3,2,1,0:T(8,128)(2,1)S(1)} %get-tuple-element.30), channel_id=1, source_target_pairs={{0,1},{1,0},{2,3},{3,2},{4,5},{5,4},{6,7},{7,6},{8,9},{9,8},{10,11... | collective-permute-start | bytes 1572872 | tf_op jit(solution)/shard_map/ppermute | solution.py:509
  21.6 18.4 %collective-permute-start.9 = (bf16[33,16,256]{2,1,0:T(8,128)(2,1)S(1)}, bf16[33,16,256]{2,1,0:T(8,128)(2,1)S(1)}, u32[]{:S(2)}, u32[]{:S(2)}) collective-permute-start(bf16[33,16,256]{2,1,0:T(8,128)(2,1)S(1)} %collective-permute-done.3.refs_5_.refs_4_), channel_id=1, source_target_pairs={{0,8},{8,0},{16,24},{24,16},{1,9},{9,1},{17,25},{25,17},{2,10},{10... | collective-permute-start | bytes 811016 | tf_op jit(solution)/shard_map/ppermute | solution.py:509
  23.5 19.3 %collective-permute-start.7 = (bf16[7,16,1024]{2,1,0:T(8,128)(2,1)S(1)}, bf16[7,16,1024]{2,1,0:T(8,128)(2,1)S(1)}, u32[]{:S(2)}, u32[]{:S(2)}) collective-permute-start(bf16[7,16,1024]{2,1,0:T(8,128)(2,1)S(1)} %get-tuple-element.32), channel_id=1, source_target_pairs={{0,16},{8,24},{16,0},{24,8},{1,17},{9,25},{17,1},{25,9},{2,18},{10... | collective-permute-start | bytes 688136 | tf_op jit(solution)/shard_map/ppermute | solution.py:509
  24.5 18.3 %collective-permute-start.8 = (bf16[7,16,1024]{2,1,0:T(8,128)(2,1)S(1)}, bf16[7,16,1024]{2,1,0:T(8,128)(2,1)S(1)}, u32[]{:S(2)}, u32[]{:S(2)}) collective-permute-start(bf16[7,16,1024]{2,1,0:T(8,128)(2,1)S(1)} %get-tuple-element.33), channel_id=1, source_target_pairs={{0,24},{8,16},{16,8},{24,0},{1,25},{9,17},{17,9},{25,1},{2,26},{10... | collective-permute-start | bytes 688136 | tf_op jit(solution)/shard_map/ppermute | solution.py:509
  27.5 17.7 %collective-permute-start.6 = (bf16[7,16,1024]{2,1,0:T(8,128)(2,1)S(1)}, bf16[7,16,1024]{2,1,0:T(8,128)(2,1)S(1)}, u32[]{:S(2)}, u32[]{:S(2)}) collective-permute-start(bf16[7,16,1024]{2,1,0:T(8,128)(2,1)S(1)} %get-tuple-element.31.tie_ref), channel_id=1, source_target_pairs={{0,8},{8,0},{16,24},{24,16},{1,9},{9,1},{17,25},{25,17},{2,10},{10... | collective-permute-start | bytes 688136 | tf_op jit(solution)/shard_map/ppermute | solution.py:509

commit v17 on v16

--- a/solution.py
+++ b/solution.py
@@ -264,6 +264,37 @@
     )(*chips, *ties)
 
 
+def cut_kernel(keep, picks, *refs):
+    count = len(picks)
+    messages, outs, sems = refs[:count], refs[count + 1 : 2 * count + 1], refs[-1]
+    copies = []
+    for n, (message, out, pick) in enumerate(zip(messages, outs, picks)):
+        tall = out.shape[0] - keep
+        first = keep + pick * tall
+        for k, (src, dst) in enumerate(
+            [(pl.ds(0, keep), pl.ds(0, keep)), (pl.ds(first, tall), pl.ds(keep, tall))]
+        ):
+            copies.append(pltpu.make_async_copy(message.at[src], out.at[dst], sems.at[n, k]))
+    for copy in copies:
+        copy.start()
+    for copy in copies:
+        copy.wait()
+
+
+def cut(messages, picks, tie, keep, tall):
+    count = len(messages)
+    return pl.pallas_call(
+        functools.partial(cut_kernel, keep, picks),
+        out_shape=(pltpu.HBM((keep + tall, CAP, TILE), bf16),) * count,
+        in_specs=[ANY] * (count + 1),
+        out_specs=(HBM,) * count,
+        scratch_shapes=[pltpu.SemaphoreType.DMA((count, 2))],
+        compiler_params=params(4 * QB),
+        cost_estimate=SMALL,
+        name="cut",
+    )(*messages, tie)
+
+
 def split_kernel(mine, swapped, *pieces):
     half = mine.shape[0]
     for j, piece in enumerate(pieces, 1):
@@ -454,7 +485,7 @@
     wide = hidden_ref.shape[1] // TILE
     hidden[:slots, :] = hidden_ref[...]
     for j in range(1, groups):
-        bit = max(b for b in bits_of(groups) if b <= j)
+        bit = j if j % 2 else max(b for b in bits_of(groups) if b <= j)
         message = messages[j - 1]
         for r in range(flight):
             for q in range(wide):
@@ -522,15 +553,21 @@
     chips = rest[:1] + [swap(rest[c], "expert", 2 * c) for c in range(1, half)]
     messages, early = {}, []
     for bit, message in zip(bits, rest[half:]):
-        for j in sorted(messages):
-            messages[j ^ bit] = swap(messages[j], "dp", bit)
+        if bit > 1:
+            for j in sorted(messages):
+                messages[j ^ bit] = swap(messages[j], "dp", bit)
         messages[bit] = swap(message, "dp", bit)
         early.append(messages[bit])
-    messages = [messages[j] for j in range(1, groups)]
+    even = list(range(2, groups, 2))
+    picks = [j + 1 - max(bit for bit in bits if bit <= j) for j in even]
     expert_out = forward(scale, hidden, w_quant[0], flight)
     returned = lax.all_to_all(expert_out, "expert", split_axis=0, concat_axis=0, tiled=True)
     sibling, mine = sort_rows(chips, [hbm(expert_out)] + early)
     swapped = swap(sibling, "expert", 1)
+    keep, tall = flight * (hidden.shape[1] // TILE), d_out.shape[1] // groups // TILE
+    for j, message in zip(even, cut([messages[j] for j in even], picks, mine, keep, tall)):
+        messages[j + 1] = swap(message, "dp", 1)
+    messages = [messages[j] for j in range(1, groups)]
     pieces = split(mine, swapped)
     parts = [swap(pieces[j - 1], "dp", j) for j in range(1, groups)]
     d_gate_up = backward(scale, gate_up, w_quant[0], pieces[0], mine, swapped)

time: 47.3 us -> 47.4 us (level)
  Pallas kernels: 17.7 us -> 18.4 us
    pallas_call x0 -> x1, Pallas kernels: none -> 0.7 us  [cut(): pl.pallas_call(functools.partial(cut_kernel, keep, picks), out_shape=(plt...]
  transfers between devices with their start and end apart: 11 -> 11, of which waited for: 6 -> 5; matrix products, arithmetic and copies ran while one was open for 0% -> 0% of each run, Pallas kernels for 29% -> 31%
where the time goes in v17:
time: 47.4 us; the launch traced here: 47.1 us
  starting transfers between devices  18.7 us (39%)
  Pallas kernels  18.4 us (39%)
  waiting for transfers between devices  9.35 us (20%)
  between operations  0.71 us (1%)
    ppermute x10, starting transfers between devices, swap(): return lax.ppermute(value, axis, [(i, i ^ j) for i in range(size)])  14.4 us
    ppermute x10, waiting for transfers between devices, swap(): return lax.ppermute(value, axis, [(i, i ^ j) for i in range(size)])  5.77 us
    pallas_call x1, Pallas kernels, backward(): pl.pallas_call(functools.partial(backward_kernel, flight, groups), out_sh...  5.25 us
    pallas_call x1, Pallas kernels, forward(): pl.pallas_call(functools.partial(forward_kernel, flight, block), out_shap...  4.78 us
    all_to_all x1, starting transfers between devices, shards(): lax.all_to_all(expert_out, 'expert', split_axis=0, concat_axis=0, tiled=T...  4.27 us
    pallas_call x1, Pallas kernels, combine(): pl.pallas_call(functools.partial(combine_kernel, block), out_shape=(pltpu...  3.63 us
    all_to_all x1, waiting for transfers between devices, shards(): lax.all_to_all(expert_out, 'expert', split_axis=0, concat_axis=0, tiled=T...  3.58 us
    pallas_call x1, Pallas kernels, dispatch(): pl.pallas_call(functools.partial(dispatch_kernel, flight, groups), out_sh...  2.09 us
  transfers between devices with their start and end apart: 11, of which 5 were waited for; matrix products, arithmetic and copies ran while one was open for 0% of the time, Pallas kernels for 31%

profile of v17, /device:TPU:0, one launch (start us, length us, event | category | flops | bytes accessed | tf_op | source)
XLA Modules:
  0.0 47.1 jit_solution(2104779898988497702)
XLA Ops:
  0.6 2.1 %dispatch.1 = (f32[128,128]{1,0:T(8,128)}, bf16[128,768]{1,0:T(8,128)(2,1)S(1)}, bf16[2,4,16,1024]{3,2,1,0:T(8,128)(2,1)S(1)}, bf16[2,4,16,1024]{3,2,1,0:T(8,128...) custom-call(bf16[128,1536]{1,0:T(8,128)(2,1)} %bitcast.10, ...), custom_call_target="tpu_custom_call" | custom-call | flops 1024 | bytes 1024 | tf_op jit(solution)/shard_map/dispatch/pallas_call | solution.py:153
  2.7 4.1 %collective-permute-start.3 = (bf16[33,16,256]{2,1,0:T(8,128)(2,1)S(1)}, bf16[33,16,256]{2,1,0:T(8,128)(2,1)S(1)}, u32[]{:S(2)}, u32[]{:S(2)}) collective-permute-start(bf16[33,16,256]{2,1,0:T(8,128)(2,1)S(1)} %get-tuple-element.27), channel_id=1, source_target_pairs={{0,16},{8,24},{16,0},{24,8},{1,17},{9,25},{17,1},{25,9},{2,18},{10... | collective-permute-start | bytes 811016 | tf_op jit(solution)/shard_map/ppermute | solution.py:540
  6.8 1.5 %collective-permute-start = (bf16[2,4,16,1024]{3,2,1,0:T(8,128)(2,1)S(1)}, bf16[2,4,16,1024]{3,2,1,0:T(8,128)(2,1)S(1)}, u32[]{:S(2)}, u32[]{:S(2)}) collective-permute-start(bf16[2,4,16,1024]{3,2,1,0:T(8,128)(2,1)S(1)} %get-tuple-element.24), channel_id=1, source_target_pairs={{0,2},{1,3},{2,0},{3,1},{4,6},{5,7},{6,4},{7,5},{8,10},{9,11},{10,... | collective-permute-start | bytes 786440 | tf_op jit(solution)/shard_map/ppermute | solution.py:540
  8.3 1.5 %collective-permute-start.1 = (bf16[2,4,16,1024]{3,2,1,0:T(8,128)(2,1)S(1)}, bf16[2,4,16,1024]{3,2,1,0:T(8,128)(2,1)S(1)}, u32[]{:S(2)}, u32[]{:S(2)}) collective-permute-start(bf16[2,4,16,1024]{3,2,1,0:T(8,128)(2,1)S(1)} %get-tuple-element.25), channel_id=1, source_target_pairs={{0,4},{1,5},{2,6},{3,7},{4,0},{5,1},{6,2},{7,3},{8,12},{9,13},{10,... | collective-permute-start | bytes 786440 | tf_op jit(solution)/shard_map/ppermute | solution.py:540
  9.8 0.5 %collective-permute-start.2 = (bf16[2,4,16,1024]{3,2,1,0:T(8,128)(2,1)S(1)}, bf16[2,4,16,1024]{3,2,1,0:T(8,128)(2,1)S(1)}, u32[]{:S(2)}, u32[]{:S(2)}) collective-permute-start(bf16[2,4,16,1024]{3,2,1,0:T(8,128)(2,1)S(1)} %get-tuple-element.26), channel_id=1, source_target_pairs={{0,6},{1,7},{2,4},{3,5},{4,2},{5,3},{6,0},{7,1},{8,14},{9,15},{10,... | collective-permute-start | bytes 786440 | tf_op jit(solution)/shard_map/ppermute | solution.py:540
  10.3 1.6 %collective-permute-start.4 = (bf16[28,16,256]{2,1,0:T(8,128)(2,1)S(1)}, bf16[28,16,256]{2,1,0:T(8,128)(2,1)S(1)}, u32[]{:S(2)}, u32[]{:S(2)}) collective-permute-start(bf16[28,16,256]{2,1,0:T(8,128)(2,1)S(1)} %get-tuple-element.28), channel_id=1, source_target_pairs={{0,8},{8,0},{16,24},{24,16},{1,9},{9,1},{17,25},{25,17},{2,10},{10... | collective-permute-start | bytes 688136 | tf_op jit(solution)/shard_map/ppermute | solution.py:540
  11.9 4.8 %expert_forward.1.refs_4_ = bf16[8,16,4096]{2,1,0:T(8,128)(2,1)} custom-call(bf16[128,768]{1,0:T(8,128)(2,1)S(1)} %get-tuple-element.20.hidden_ref, f32[6,1,32]{2,1,0:T(1,128)} %bitcast.16, bf16[768,4096]{1,0:T(8,128)(2,1)} %bitcast.8), custom_call_target="tpu_custom_call" | custom-call | flops 1024 | bytes 1024 | tf_op jit(solution)/shard_map/expert_forward/pallas_call | solution.py:227
  16.7 4.3 %all-to-all-start = ((bf16[8,16,4096]{2,1,0:T(8,128)(2,1)}), bf16[8,16,4096]{2,1,0:T(8,128)(2,1)}, u32[]{:S(2)}, u32[]{:S(2)}) async-start(bf16[8,16,4096]{2,1,0:T(8,128)(2,1)} %expert_forward.1.refs_4_), calls=%async_computation | async-start | bytes 2097152 | tf_op jit(solution)/shard_map/all_to_all | solution.py:564
  21.0 0.2 collective-permute-done.4.refs_6_.refs_3_
  21.2 0.2 collective-permute-done.1.refs_2_
  21.4 0.0 collective-permute-done.2.refs_3_
  21.4 0.1 sort_rows.1
  21.5 0.1 collective-permute-start.5
  21.6 0.7 %cut.1 = bf16[28,16,256]{2,1,0:T(8,128)(2,1)} custom-call(bf16[33,16,256]{2,1,0:T(8,128)(2,1)S(1)} %collective-permute-done.3.refs_5_.refs_0_.refs_4_, bf16[4,4,16,1024]{3,2,1,0:T(8,128)(2,1)S(1)} %get-tuple-element.29.mine.refs_1_), custom_call_target="tpu_custom_call" | custom-call | flops 1024 | bytes 1024 | tf_op jit(solution)/shard_map/cut/pallas_call | solution.py:286
  22.3 1.6 %collective-permute-start.9 = (bf16[28,16,256]{2,1,0:T(8,128)(2,1)}, bf16[28,16,256]{2,1,0:T(8,128)(2,1)S(1)}, u32[]{:S(2)}, u32[]{:S(2)}) collective-permute-start(bf16[28,16,256]{2,1,0:T(8,128)(2,1)} %cut.1), channel_id=1, source_target_pairs={{0,8},{8,0},{16,24},{24,16},{1,9},{9,1},{17,25},{25,17},{2,10},{10... | collective-permute-start | bytes 688136 | tf_op jit(solution)/shard_map/ppermute | solution.py:540
  24.0 1.3 %collective-permute-start.7 = (bf16[7,16,1024]{2,1,0:T(8,128)(2,1)S(1)}, bf16[7,16,1024]{2,1,0:T(8,128)(2,1)S(1)}, u32[]{:S(2)}, u32[]{:S(2)}) collective-permute-start(bf16[7,16,1024]{2,1,0:T(8,128)(2,1)S(1)} %get-tuple-element.32), channel_id=1, source_target_pairs={{0,16},{8,24},{16,0},{24,8},{1,17},{9,25},{17,1},{25,9},{2,18},{10... | collective-permute-start | bytes 688136 | tf_op jit(solution)/shard_map/ppermute | solution.py:540
  25.2 2.3 %collective-permute-start.8 = (bf16[7,16,1024]{2,1,0:T(8,128)(2,1)S(1)}, bf16[7,16,1024]{2,1,0:T(8,128)(2,1)S(1)}, u32[]{:S(2)}, u32[]{:S(2)}) collective-permute-start(bf16[7,16,1024]{2,1,0:T(8,128)(2,1)S(1)} %get-tuple-element.33), channel_id=1, source_target_pairs={{0,24},{8,16},{16,8},{24,0},{1,25},{9,17},{17,9},{25,1},{2,26},{10... | collective-permute-start | bytes 688136 | tf_op jit(solution)/shard_map/ppermute | solution.py:540
  27.5 0.0 collective-permute-start.6
  27.5 5.2 %expert_backward.1 = bf16[128,1536]{1,0:T(8,128)(2,1)} custom-call(f32[6,1,32]{2,1,0:T(1,128)} %bitcast.17, bf16[128,1536]{1,0:T(8,128)(2,1)} %bitcast.11, bf16[768,4096]{1,0:T(8,128)(2,1)} %bitcast.9, bf16[7,16,1024]{2,1,0:T(8,128)(2,1)S(1)} %get-tuple-element.31.tie_ref, bf16[4,4,16,1024]{3,2,1,0:T(8,128)(2,1)S(1)} %get-tuple-element.29.mine.refs_1_, ...), custom_call_target="tpu_custom_call" | custom-call | flops 1024 | bytes 1024 | tf_op jit(solution)/shard_map/expert_backward/pallas_call | solution.py:391
  32.8 3.6 %all-to-all-done.ret_hbm = bf16[8,16,4096]{2,1,0:T(8,128)(2,1)} async-done(((bf16[8,16,4096]{2,1,0:T(8,128)(2,1)}), bf16[8,16,4096]{2,1,0:T(8,128)(2,1)}, u32[]{:S(2)}, u32[]{:S(2)}) %all-to-all-start) | async-done | bytes 1048608 | tf_op jit(solution)/shard_map/all_to_all | solution.py:564
  36.4 3.6 %combine.1 = (bf16[128,4096]{1,0:T(8,128)(2,1)}, f32[8,128]{1,0:T(8,128)}) custom-call(s32[8,128]{1,0:T(8,128)} %bitcast.15, f32[128,128]{1,0:T(8,128)} %get-tuple-element.19.own_hbm, bf16[128,4096]{1,0:T(8,128)(2,1)} %dout_hbm.3, bf16[8,16,4096]{2,1,0:T(8,128)(2,1)} %all-to-all-done.ret_hbm), custom_call_target="tpu_custom_call" | custom-call | flops 1024 | bytes 1024 | tf_op jit(solution)/shard_map/combine/pallas_call | solution.py:457
  40.0 3.3 %collective-permute-done.7.refs_1_ = bf16[7,16,1024]{2,1,0:T(8,128)(2,1)S(1)} collective-permute-done((bf16[7,16,1024]{2,1,0:T(8,128)(2,1)S(1)}, bf16[7,16,1024]{2,1,0:T(8,128)(2,1)S(1)}, u32[]{:S(2)}, u32[]{:S(2)}) %collective-permute-start.7) | collective-permute-done | bytes 229408 | tf_op jit(solution)/shard_map/ppermute | solution.py:540
  43.3 2.0 %collective-permute-done.6.refs_0_ = bf16[7,16,1024]{2,1,0:T(8,128)(2,1)S(1)} collective-permute-done((bf16[7,16,1024]{2,1,0:T(8,128)(2,1)S(1)}, bf16[7,16,1024]{2,1,0:T(8,128)(2,1)S(1)}, u32[]{:S(2)}, u32[]{:S(2)}) %collective-permute-start.6) | collective-permute-done | bytes 229408 | tf_op jit(solution)/shard_map/ppermute | solution.py:540
  45.3 1.8 %weight_grad.1 = bf16[1024,768]{1,0:T(8,128)(2,1)} custom-call(f32[8,128]{1,0:T(8,128)} %get-tuple-element.22.tie_ref, bf16[4,4,16,1024]{3,2,1,0:T(8,128)(2,1)S(1)} %get-tuple-element.29.mine.refs_1_, bf16[4,4,16,1024]{3,2,1,0:T(8,128)(2,1)S(1)} %collective-permute-done.5.swapped, bf16[128,768]{1,0:T(8,128)(2,1)S(1)} %get-tuple-element.20.hidden_ref, ...), custom_call_target="tpu_custom_call" | custom-call | flops 1024 | bytes 1024 | tf_op jit(solution)/shard_map/weight_grad/pallas_call | solution.py:521
  (6 shorter events, 0.1 us)
Async XLA Ops:
  2.7 18.7 %collective-permute-start.3 = (bf16[33,16,256]{2,1,0:T(8,128)(2,1)S(1)}, bf16[33,16,256]{2,1,0:T(8,128)(2,1)S(1)}, u32[]{:S(2)}, u32[]{:S(2)}) collective-permute-start(bf16[33,16,256]{2,1,0:T(8,128)(2,1)S(1)} %get-tuple-element.27), channel_id=1, source_target_pairs={{0,16},{8,24},{16,0},{24,8},{1,17},{9,25},{17,1},{25,9},{2,18},{10... | collective-permute-start | bytes 811016 | tf_op jit(solution)/shard_map/ppermute | solution.py:540
  6.8 14.3 %collective-permute-start = (bf16[2,4,16,1024]{3,2,1,0:T(8,128)(2,1)S(1)}, bf16[2,4,16,1024]{3,2,1,0:T(8,128)(2,1)S(1)}, u32[]{:S(2)}, u32[]{:S(2)}) collective-permute-start(bf16[2,4,16,1024]{3,2,1,0:T(8,128)(2,1)S(1)} %get-tuple-element.24), channel_id=1, source_target_pairs={{0,2},{1,3},{2,0},{3,1},{4,6},{5,7},{6,4},{7,5},{8,10},{9,11},{10,... | collective-permute-start | bytes 786440 | tf_op jit(solution)/shard_map/ppermute | solution.py:540
  8.3 13.1 %collective-permute-start.1 = (bf16[2,4,16,1024]{3,2,1,0:T(8,128)(2,1)S(1)}, bf16[2,4,16,1024]{3,2,1,0:T(8,128)(2,1)S(1)}, u32[]{:S(2)}, u32[]{:S(2)}) collective-permute-start(bf16[2,4,16,1024]{3,2,1,0:T(8,128)(2,1)S(1)} %get-tuple-element.25), channel_id=1, source_target_pairs={{0,4},{1,5},{2,6},{3,7},{4,0},{5,1},{6,2},{7,3},{8,12},{9,13},{10,... | collective-permute-start | bytes 786440 | tf_op jit(solution)/shard_map/ppermute | solution.py:540
  9.8 11.6 %collective-permute-start.2 = (bf16[2,4,16,1024]{3,2,1,0:T(8,128)(2,1)S(1)}, bf16[2,4,16,1024]{3,2,1,0:T(8,128)(2,1)S(1)}, u32[]{:S(2)}, u32[]{:S(2)}) collective-permute-start(bf16[2,4,16,1024]{3,2,1,0:T(8,128)(2,1)S(1)} %get-tuple-element.26), channel_id=1, source_target_pairs={{0,6},{1,7},{2,4},{3,5},{4,2},{5,3},{6,0},{7,1},{8,14},{9,15},{10,... | collective-permute-start | bytes 786440 | tf_op jit(solution)/shard_map/ppermute | solution.py:540
  10.3 10.9 %collective-permute-start.4 = (bf16[28,16,256]{2,1,0:T(8,128)(2,1)S(1)}, bf16[28,16,256]{2,1,0:T(8,128)(2,1)S(1)}, u32[]{:S(2)}, u32[]{:S(2)}) collective-permute-start(bf16[28,16,256]{2,1,0:T(8,128)(2,1)S(1)} %get-tuple-element.28), channel_id=1, source_target_pairs={{0,8},{8,0},{16,24},{24,16},{1,9},{9,1},{17,25},{25,17},{2,10},{10... | collective-permute-start | bytes 688136 | tf_op jit(solution)/shard_map/ppermute | solution.py:540
  16.7 19.7 %all-to-all-start = ((bf16[8,16,4096]{2,1,0:T(8,128)(2,1)}), bf16[8,16,4096]{2,1,0:T(8,128)(2,1)}, u32[]{:S(2)}, u32[]{:S(2)}) async-start(bf16[8,16,4096]{2,1,0:T(8,128)(2,1)} %expert_forward.1.refs_4_), calls=%async_computation | async-start | bytes 2097152 | tf_op jit(solution)/shard_map/all_to_all | solution.py:564
  21.5 2.4 %collective-permute-start.5 = (bf16[4,4,16,1024]{3,2,1,0:T(8,128)(2,1)S(1)}, bf16[4,4,16,1024]{3,2,1,0:T(8,128)(2,1)S(1)}, u32[]{:S(2)}, u32[]{:S(2)}) collective-permute-start(bf16[4,4,16,1024]{3,2,1,0:T(8,128)(2,1)S(1)} %get-tuple-element.30), channel_id=1, source_target_pairs={{0,1},{1,0},{2,3},{3,2},{4,5},{5,4},{6,7},{7,6},{8,9},{9,8},{10,11... | collective-permute-start | bytes 1572872 | tf_op jit(solution)/shard_map/ppermute | solution.py:540
  22.3 17.7 %collective-permute-start.9 = (bf16[28,16,256]{2,1,0:T(8,128)(2,1)}, bf16[28,16,256]{2,1,0:T(8,128)(2,1)S(1)}, u32[]{:S(2)}, u32[]{:S(2)}) collective-permute-start(bf16[28,16,256]{2,1,0:T(8,128)(2,1)} %cut.1), channel_id=1, source_target_pairs={{0,8},{8,0},{16,24},{24,16},{1,9},{9,1},{17,25},{25,17},{2,10},{10... | collective-permute-start | bytes 688136 | tf_op jit(solution)/shard_map/ppermute | solution.py:540
  24.0 19.3 %collective-permute-start.7 = (bf16[7,16,1024]{2,1,0:T(8,128)(2,1)S(1)}, bf16[7,16,1024]{2,1,0:T(8,128)(2,1)S(1)}, u32[]{:S(2)}, u32[]{:S(2)}) collective-permute-start(bf16[7,16,1024]{2,1,0:T(8,128)(2,1)S(1)} %get-tuple-element.32), channel_id=1, source_target_pairs={{0,16},{8,24},{16,0},{24,8},{1,17},{9,25},{17,1},{25,9},{2,18},{10... | collective-permute-start | bytes 688136 | tf_op jit(solution)/shard_map/ppermute | solution.py:540
  25.2 18.1 %collective-permute-start.8 = (bf16[7,16,1024]{2,1,0:T(8,128)(2,1)S(1)}, bf16[7,16,1024]{2,1,0:T(8,128)(2,1)S(1)}, u32[]{:S(2)}, u32[]{:S(2)}) collective-permute-start(bf16[7,16,1024]{2,1,0:T(8,128)(2,1)S(1)} %get-tuple-element.33), channel_id=1, source_target_pairs={{0,24},{8,16},{16,8},{24,0},{1,25},{9,17},{17,9},{25,1},{2,26},{10... | collective-permute-start | bytes 688136 | tf_op jit(solution)/shard_map/ppermute | solution.py:540
  27.5 17.8 %collective-permute-start.6 = (bf16[7,16,1024]{2,1,0:T(8,128)(2,1)S(1)}, bf16[7,16,1024]{2,1,0:T(8,128)(2,1)S(1)}, u32[]{:S(2)}, u32[]{:S(2)}) collective-permute-start(bf16[7,16,1024]{2,1,0:T(8,128)(2,1)S(1)} %get-tuple-element.31.tie_ref), channel_id=1, source_target_pairs={{0,8},{8,0},{16,24},{24,16},{1,9},{9,1},{17,25},{25,17},{2,10},{10... | collective-permute-start | bytes 688136 | tf_op jit(solution)/shard_map/ppermute | solution.py:540

commit v18 on v16

--- a/solution.py
+++ b/solution.py
@@ -484,7 +484,7 @@
         copy.wait()
 
 
-def weight_grad(tie, mine, swapped, hidden, parts, messages, block=256):
+def weight_grad(tie, mine, swapped, hidden, parts, messages, block=512):
     half, groups, cap, share = swapped.shape
     slots, hid = hidden.shape
     return pl.pallas_call(

time: 47.3 us -> 47.4 us (level)
  no operation moved by 1% of the time
where the time goes in v18:
time: 47.4 us; the launch traced here: 47.2 us
  starting transfers between devices  19.1 us (40%)
  Pallas kernels  17.8 us (38%)
  waiting for transfers between devices  9.5 us (20%)
  between operations  0.71 us (1%)
    ppermute x10, starting transfers between devices, swap(): return lax.ppermute(value, axis, [(i, i ^ j) for i in range(size)])  14.9 us
    ppermute x10, waiting for transfers between devices, swap(): return lax.ppermute(value, axis, [(i, i ^ j) for i in range(size)])  5.94 us
    pallas_call x1, Pallas kernels, backward(): pl.pallas_call(functools.partial(backward_kernel, flight, groups), out_sh...  5.26 us
    pallas_call x1, Pallas kernels, forward(): pl.pallas_call(functools.partial(forward_kernel, flight, block), out_shap...  4.78 us
    all_to_all x1, starting transfers between devices, shards(): lax.all_to_all(expert_out, 'expert', split_axis=0, concat_axis=0, tiled=T...  4.27 us
    pallas_call x1, Pallas kernels, combine(): pl.pallas_call(functools.partial(combine_kernel, block), out_shape=(pltpu...  3.63 us
    all_to_all x1, waiting for transfers between devices, shards(): lax.all_to_all(expert_out, 'expert', split_axis=0, concat_axis=0, tiled=T...  3.57 us
    pallas_call x1, Pallas kernels, dispatch(): pl.pallas_call(functools.partial(dispatch_kernel, flight, groups), out_sh...  2.09 us
  transfers between devices with their start and end apart: 11, of which 6 were waited for; matrix products, arithmetic and copies ran while one was open for 0% of the time, Pallas kernels for 29%

profile of v18, /device:TPU:0, one launch (start us, length us, event | category | flops | bytes accessed | tf_op | source)
XLA Modules:
  0.0 47.2 jit_solution(1270996755064193125)
XLA Ops:
  0.6 2.1 %dispatch.1 = (f32[128,128]{1,0:T(8,128)}, bf16[128,768]{1,0:T(8,128)(2,1)S(1)}, bf16[2,4,16,1024]{3,2,1,0:T(8,128)(2,1)S(1)}, bf16[2,4,16,1024]{3,2,1,0:T(8,128...) custom-call(bf16[128,1536]{1,0:T(8,128)(2,1)} %bitcast.10, ...), custom_call_target="tpu_custom_call" | custom-call | flops 1024 | bytes 1024 | tf_op jit(solution)/shard_map/dispatch/pallas_call | solution.py:153
  2.7 4.1 %collective-permute-start.3 = (bf16[33,16,256]{2,1,0:T(8,128)(2,1)S(1)}, bf16[33,16,256]{2,1,0:T(8,128)(2,1)S(1)}, u32[]{:S(2)}, u32[]{:S(2)}) collective-permute-start(bf16[33,16,256]{2,1,0:T(8,128)(2,1)S(1)} %get-tuple-element.27), channel_id=1, source_target_pairs={{0,16},{8,24},{16,0},{24,8},{1,17},{9,25},{17,1},{25,9},{2,18},{10... | collective-permute-start | bytes 811016 | tf_op jit(solution)/shard_map/ppermute | solution.py:509
  6.8 1.5 %collective-permute-start = (bf16[2,4,16,1024]{3,2,1,0:T(8,128)(2,1)S(1)}, bf16[2,4,16,1024]{3,2,1,0:T(8,128)(2,1)S(1)}, u32[]{:S(2)}, u32[]{:S(2)}) collective-permute-start(bf16[2,4,16,1024]{3,2,1,0:T(8,128)(2,1)S(1)} %get-tuple-element.24), channel_id=1, source_target_pairs={{0,2},{1,3},{2,0},{3,1},{4,6},{5,7},{6,4},{7,5},{8,10},{9,11},{10,... | collective-permute-start | bytes 786440 | tf_op jit(solution)/shard_map/ppermute | solution.py:509
  8.3 1.5 %collective-permute-start.1 = (bf16[2,4,16,1024]{3,2,1,0:T(8,128)(2,1)S(1)}, bf16[2,4,16,1024]{3,2,1,0:T(8,128)(2,1)S(1)}, u32[]{:S(2)}, u32[]{:S(2)}) collective-permute-start(bf16[2,4,16,1024]{3,2,1,0:T(8,128)(2,1)S(1)} %get-tuple-element.25), channel_id=1, source_target_pairs={{0,4},{1,5},{2,6},{3,7},{4,0},{5,1},{6,2},{7,3},{8,12},{9,13},{10,... | collective-permute-start | bytes 786440 | tf_op jit(solution)/shard_map/ppermute | solution.py:509
  9.8 0.5 %collective-permute-start.2 = (bf16[2,4,16,1024]{3,2,1,0:T(8,128)(2,1)S(1)}, bf16[2,4,16,1024]{3,2,1,0:T(8,128)(2,1)S(1)}, u32[]{:S(2)}, u32[]{:S(2)}) collective-permute-start(bf16[2,4,16,1024]{3,2,1,0:T(8,128)(2,1)S(1)} %get-tuple-element.26), channel_id=1, source_target_pairs={{0,6},{1,7},{2,4},{3,5},{4,2},{5,3},{6,0},{7,1},{8,14},{9,15},{10,... | collective-permute-start | bytes 786440 | tf_op jit(solution)/shard_map/ppermute | solution.py:509
  10.3 1.6 %collective-permute-start.4 = (bf16[28,16,256]{2,1,0:T(8,128)(2,1)S(1)}, bf16[28,16,256]{2,1,0:T(8,128)(2,1)S(1)}, u32[]{:S(2)}, u32[]{:S(2)}) collective-permute-start(bf16[28,16,256]{2,1,0:T(8,128)(2,1)S(1)} %get-tuple-element.28), channel_id=1, source_target_pairs={{0,8},{8,0},{16,24},{24,16},{1,9},{9,1},{17,25},{25,17},{2,10},{10... | collective-permute-start | bytes 688136 | tf_op jit(solution)/shard_map/ppermute | solution.py:509
  11.9 4.8 %expert_forward.1.refs_4_ = bf16[8,16,4096]{2,1,0:T(8,128)(2,1)} custom-call(bf16[128,768]{1,0:T(8,128)(2,1)S(1)} %get-tuple-element.20.hidden_ref, f32[6,1,32]{2,1,0:T(1,128)} %bitcast.16, bf16[768,4096]{1,0:T(8,128)(2,1)} %bitcast.8), custom_call_target="tpu_custom_call" | custom-call | flops 1024 | bytes 1024 | tf_op jit(solution)/shard_map/expert_forward/pallas_call | solution.py:227
  16.7 4.3 %all-to-all-start = ((bf16[8,16,4096]{2,1,0:T(8,128)(2,1)}), bf16[8,16,4096]{2,1,0:T(8,128)(2,1)}, u32[]{:S(2)}, u32[]{:S(2)}) async-start(bf16[8,16,4096]{2,1,0:T(8,128)(2,1)} %expert_forward.1.refs_4_), calls=%async_computation | async-start | bytes 2097152 | tf_op jit(solution)/shard_map/all_to_all | solution.py:531
  21.0 0.2 collective-permute-done.4.refs_6_.refs_3_
  21.2 0.0 collective-permute-done.refs_1_
  21.2 0.2 collective-permute-done.1.refs_2_
  21.4 0.0 collective-permute-done.2.refs_3_
  21.4 0.1 sort_rows.1
  21.5 0.1 collective-permute-start.5
  21.6 1.6 %collective-permute-start.9 = (bf16[33,16,256]{2,1,0:T(8,128)(2,1)S(1)}, bf16[33,16,256]{2,1,0:T(8,128)(2,1)S(1)}, u32[]{:S(2)}, u32[]{:S(2)}) collective-permute-start(bf16[33,16,256]{2,1,0:T(8,128)(2,1)S(1)} %collective-permute-done.3.refs_5_.refs_4_), channel_id=1, source_target_pairs={{0,8},{8,0},{16,24},{24,16},{1,9},{9,1},{17,25},{25,17},{2,10},{10... | collective-permute-start | bytes 811016 | tf_op jit(solution)/shard_map/ppermute | solution.py:509
  23.2 0.3 collective-permute-done.5.swapped
  23.5 1.0 %collective-permute-start.7 = (bf16[7,16,1024]{2,1,0:T(8,128)(2,1)S(1)}, bf16[7,16,1024]{2,1,0:T(8,128)(2,1)S(1)}, u32[]{:S(2)}, u32[]{:S(2)}) collective-permute-start(bf16[7,16,1024]{2,1,0:T(8,128)(2,1)S(1)} %get-tuple-element.32), channel_id=1, source_target_pairs={{0,16},{8,24},{16,0},{24,8},{1,17},{9,25},{17,1},{25,9},{2,18},{10... | collective-permute-start | bytes 688136 | tf_op jit(solution)/shard_map/ppermute | solution.py:509
  24.5 3.0 %collective-permute-start.8 = (bf16[7,16,1024]{2,1,0:T(8,128)(2,1)S(1)}, bf16[7,16,1024]{2,1,0:T(8,128)(2,1)S(1)}, u32[]{:S(2)}, u32[]{:S(2)}) collective-permute-start(bf16[7,16,1024]{2,1,0:T(8,128)(2,1)S(1)} %get-tuple-element.33), channel_id=1, source_target_pairs={{0,24},{8,16},{16,8},{24,0},{1,25},{9,17},{17,9},{25,1},{2,26},{10... | collective-permute-start | bytes 688136 | tf_op jit(solution)/shard_map/ppermute | solution.py:509
  27.5 5.3 %expert_backward.1 = bf16[128,1536]{1,0:T(8,128)(2,1)} custom-call(f32[6,1,32]{2,1,0:T(1,128)} %bitcast.17, bf16[128,1536]{1,0:T(8,128)(2,1)} %bitcast.11, bf16[768,4096]{1,0:T(8,128)(2,1)} %bitcast.9, bf16[7,16,1024]{2,1,0:T(8,128)(2,1)S(1)} %get-tuple-element.31.tie_ref, bf16[4,4,16,1024]{3,2,1,0:T(8,128)(2,1)S(1)} %get-tuple-element.29.mine, ...), custom_call_target="tpu_custom_call" | custom-call | flops 1024 | bytes 1024 | tf_op jit(solution)/shard_map/expert_backward/pallas_call | solution.py:360
  32.8 3.6 %all-to-all-done.ret_hbm = bf16[8,16,4096]{2,1,0:T(8,128)(2,1)} async-done(((bf16[8,16,4096]{2,1,0:T(8,128)(2,1)}), bf16[8,16,4096]{2,1,0:T(8,128)(2,1)}, u32[]{:S(2)}, u32[]{:S(2)}) %all-to-all-start) | async-done | bytes 1048608 | tf_op jit(solution)/shard_map/all_to_all | solution.py:531
  36.4 3.6 %combine.1 = (bf16[128,4096]{1,0:T(8,128)(2,1)}, f32[8,128]{1,0:T(8,128)}) custom-call(s32[8,128]{1,0:T(8,128)} %bitcast.15, f32[128,128]{1,0:T(8,128)} %get-tuple-element.19.own_hbm, bf16[128,4096]{1,0:T(8,128)(2,1)} %dout_hbm.3, bf16[8,16,4096]{2,1,0:T(8,128)(2,1)} %all-to-all-done.ret_hbm), custom_call_target="tpu_custom_call" | custom-call | flops 1024 | bytes 1024 | tf_op jit(solution)/shard_map/combine/pallas_call | solution.py:426
  40.0 2.8 %collective-permute-done.7.refs_1_ = bf16[7,16,1024]{2,1,0:T(8,128)(2,1)S(1)} collective-permute-done((bf16[7,16,1024]{2,1,0:T(8,128)(2,1)S(1)}, bf16[7,16,1024]{2,1,0:T(8,128)(2,1)S(1)}, u32[]{:S(2)}, u32[]{:S(2)}) %collective-permute-start.7) | collective-permute-done | bytes 229408 | tf_op jit(solution)/shard_map/ppermute | solution.py:509
  42.9 2.4 %collective-permute-done.6.refs_0_ = bf16[7,16,1024]{2,1,0:T(8,128)(2,1)S(1)} collective-permute-done((bf16[7,16,1024]{2,1,0:T(8,128)(2,1)S(1)}, bf16[7,16,1024]{2,1,0:T(8,128)(2,1)S(1)}, u32[]{:S(2)}, u32[]{:S(2)}) %collective-permute-start.6) | collective-permute-done | bytes 229408 | tf_op jit(solution)/shard_map/ppermute | solution.py:509
  45.2 1.9 %weight_grad.1 = bf16[1024,768]{1,0:T(8,128)(2,1)} custom-call(f32[8,128]{1,0:T(8,128)} %get-tuple-element.22.tie_ref, bf16[4,4,16,1024]{3,2,1,0:T(8,128)(2,1)S(1)} %get-tuple-element.29.mine, bf16[4,4,16,1024]{3,2,1,0:T(8,128)(2,1)S(1)} %collective-permute-done.5.swapped, bf16[128,768]{1,0:T(8,128)(2,1)S(1)} %get-tuple-element.20.hidden_ref, ...), custom_call_target="tpu_custom_call" | custom-call | flops 1024 | bytes 1024 | tf_op jit(solution)/shard_map/weight_grad/pallas_call | solution.py:490
  (5 shorter events, 0.1 us)
Async XLA Ops:
  2.7 18.7 %collective-permute-start.3 = (bf16[33,16,256]{2,1,0:T(8,128)(2,1)S(1)}, bf16[33,16,256]{2,1,0:T(8,128)(2,1)S(1)}, u32[]{:S(2)}, u32[]{:S(2)}) collective-permute-start(bf16[33,16,256]{2,1,0:T(8,128)(2,1)S(1)} %get-tuple-element.27), channel_id=1, source_target_pairs={{0,16},{8,24},{16,0},{24,8},{1,17},{9,25},{17,1},{25,9},{2,18},{10... | collective-permute-start | bytes 811016 | tf_op jit(solution)/shard_map/ppermute | solution.py:509
  6.8 14.3 %collective-permute-start = (bf16[2,4,16,1024]{3,2,1,0:T(8,128)(2,1)S(1)}, bf16[2,4,16,1024]{3,2,1,0:T(8,128)(2,1)S(1)}, u32[]{:S(2)}, u32[]{:S(2)}) collective-permute-start(bf16[2,4,16,1024]{3,2,1,0:T(8,128)(2,1)S(1)} %get-tuple-element.24), channel_id=1, source_target_pairs={{0,2},{1,3},{2,0},{3,1},{4,6},{5,7},{6,4},{7,5},{8,10},{9,11},{10,... | collective-permute-start | bytes 786440 | tf_op jit(solution)/shard_map/ppermute | solution.py:509
  8.3 13.1 %collective-permute-start.1 = (bf16[2,4,16,1024]{3,2,1,0:T(8,128)(2,1)S(1)}, bf16[2,4,16,1024]{3,2,1,0:T(8,128)(2,1)S(1)}, u32[]{:S(2)}, u32[]{:S(2)}) collective-permute-start(bf16[2,4,16,1024]{3,2,1,0:T(8,128)(2,1)S(1)} %get-tuple-element.25), channel_id=1, source_target_pairs={{0,4},{1,5},{2,6},{3,7},{4,0},{5,1},{6,2},{7,3},{8,12},{9,13},{10,... | collective-permute-start | bytes 786440 | tf_op jit(solution)/shard_map/ppermute | solution.py:509
  9.8 11.6 %collective-permute-start.2 = (bf16[2,4,16,1024]{3,2,1,0:T(8,128)(2,1)S(1)}, bf16[2,4,16,1024]{3,2,1,0:T(8,128)(2,1)S(1)}, u32[]{:S(2)}, u32[]{:S(2)}) collective-permute-start(bf16[2,4,16,1024]{3,2,1,0:T(8,128)(2,1)S(1)} %get-tuple-element.26), channel_id=1, source_target_pairs={{0,6},{1,7},{2,4},{3,5},{4,2},{5,3},{6,0},{7,1},{8,14},{9,15},{10,... | collective-permute-start | bytes 786440 | tf_op jit(solution)/shard_map/ppermute | solution.py:509
  10.3 10.9 %collective-permute-start.4 = (bf16[28,16,256]{2,1,0:T(8,128)(2,1)S(1)}, bf16[28,16,256]{2,1,0:T(8,128)(2,1)S(1)}, u32[]{:S(2)}, u32[]{:S(2)}) collective-permute-start(bf16[28,16,256]{2,1,0:T(8,128)(2,1)S(1)} %get-tuple-element.28), channel_id=1, source_target_pairs={{0,8},{8,0},{16,24},{24,16},{1,9},{9,1},{17,25},{25,17},{2,10},{10... | collective-permute-start | bytes 688136 | tf_op jit(solution)/shard_map/ppermute | solution.py:509
  16.7 19.7 %all-to-all-start = ((bf16[8,16,4096]{2,1,0:T(8,128)(2,1)}), bf16[8,16,4096]{2,1,0:T(8,128)(2,1)}, u32[]{:S(2)}, u32[]{:S(2)}) async-start(bf16[8,16,4096]{2,1,0:T(8,128)(2,1)} %expert_forward.1.refs_4_), calls=%async_computation | async-start | bytes 2097152 | tf_op jit(solution)/shard_map/all_to_all | solution.py:531
  21.5 2.0 %collective-permute-start.5 = (bf16[4,4,16,1024]{3,2,1,0:T(8,128)(2,1)S(1)}, bf16[4,4,16,1024]{3,2,1,0:T(8,128)(2,1)S(1)}, u32[]{:S(2)}, u32[]{:S(2)}) collective-permute-start(bf16[4,4,16,1024]{3,2,1,0:T(8,128)(2,1)S(1)} %get-tuple-element.30), channel_id=1, source_target_pairs={{0,1},{1,0},{2,3},{3,2},{4,5},{5,4},{6,7},{7,6},{8,9},{9,8},{10,11... | collective-permute-start | bytes 1572872 | tf_op jit(solution)/shard_map/ppermute | solution.py:509
  21.6 18.4 %collective-permute-start.9 = (bf16[33,16,256]{2,1,0:T(8,128)(2,1)S(1)}, bf16[33,16,256]{2,1,0:T(8,128)(2,1)S(1)}, u32[]{:S(2)}, u32[]{:S(2)}) collective-permute-start(bf16[33,16,256]{2,1,0:T(8,128)(2,1)S(1)} %collective-permute-done.3.refs_5_.refs_4_), channel_id=1, source_target_pairs={{0,8},{8,0},{16,24},{24,16},{1,9},{9,1},{17,25},{25,17},{2,10},{10... | collective-permute-start | bytes 811016 | tf_op jit(solution)/shard_map/ppermute | solution.py:509
  23.5 19.3 %collective-permute-start.7 = (bf16[7,16,1024]{2,1,0:T(8,128)(2,1)S(1)}, bf16[7,16,1024]{2,1,0:T(8,128)(2,1)S(1)}, u32[]{:S(2)}, u32[]{:S(2)}) collective-permute-start(bf16[7,16,1024]{2,1,0:T(8,128)(2,1)S(1)} %get-tuple-element.32), channel_id=1, source_target_pairs={{0,16},{8,24},{16,0},{24,8},{1,17},{9,25},{17,1},{25,9},{2,18},{10... | collective-permute-start | bytes 688136 | tf_op jit(solution)/shard_map/ppermute | solution.py:509
  24.5 18.3 %collective-permute-start.8 = (bf16[7,16,1024]{2,1,0:T(8,128)(2,1)S(1)}, bf16[7,16,1024]{2,1,0:T(8,128)(2,1)S(1)}, u32[]{:S(2)}, u32[]{:S(2)}) collective-permute-start(bf16[7,16,1024]{2,1,0:T(8,128)(2,1)S(1)} %get-tuple-element.33), channel_id=1, source_target_pairs={{0,24},{8,16},{16,8},{24,0},{1,25},{9,17},{17,9},{25,1},{2,26},{10... | collective-permute-start | bytes 688136 | tf_op jit(solution)/shard_map/ppermute | solution.py:509
  27.5 17.7 %collective-permute-start.6 = (bf16[7,16,1024]{2,1,0:T(8,128)(2,1)S(1)}, bf16[7,16,1024]{2,1,0:T(8,128)(2,1)S(1)}, u32[]{:S(2)}, u32[]{:S(2)}) collective-permute-start(bf16[7,16,1024]{2,1,0:T(8,128)(2,1)S(1)} %get-tuple-element.31.tie_ref), channel_id=1, source_target_pairs={{0,8},{8,0},{16,24},{24,16},{1,9},{9,1},{17,25},{25,17},{2,10},{10... | collective-permute-start | bytes 688136 | tf_op jit(solution)/shard_map/ppermute | solution.py:509
